TPU v7x, 32 devices: a whole 2x2x4 slice. The times are simulated.
32 devices in a mesh: rows: 16 (over z, y, core), cols: 2 (over x).
Axes of the slice: x: 2, y: 2, z: 4, core: 2. Of those that a mesh axis runs over, the one named last changes fastest.
Arguments:
- patches: bfloat16 [8, 160, 40, 256], P(None, 'rows', 'cols'), may hold values from -6 to 6
- target: bfloat16 [8, 160, 40, 256], P(None, 'rows', 'cols'), may hold values from -6 to 6
- kept_mask: int32 [8, 160, 40], P(None, 'rows', 'cols'), may hold values from 0 to 1, as said below
- ln1_gain: float32 [256], replicated, may hold values from 0.5 to 1.5
- ln1_bias: float32 [256], replicated, may hold values from -1.75 to 1.75
- qkv_weight: bfloat16 [256, 768], replicated, may hold values from -0.375 to 0.375
- query_bias: float32 [256], replicated, may hold values from -3 to 3
- value_bias: float32 [256], replicated, may hold values from -3 to 3
- rel_table: float32 [8, 361], replicated, may hold values from -4 to 4
- proj_weight: bfloat16 [256, 256], replicated, may hold values from -1.5 to 1.5
- proj_bias: float32 [256], replicated, may hold values from -1.75 to 1.75
- ln2_gain: float32 [256], replicated, may hold values from 0.5 to 1.5
- ln2_bias: float32 [256], replicated, may hold values from -1.75 to 1.75
- fc1_weight: bfloat16 [256, 1024], replicated, may hold values from -0.375 to 0.375
- fc1_bias: float32 [1024], replicated, may hold values from -3 to 3
- fc2_weight: bfloat16 [1024, 256], replicated, may hold values from -0.1875 to 0.1875
- fc2_bias: float32 [256], replicated, may hold values from -1.75 to 1.75
Outputs:
- output: bfloat16 [8, 160, 40, 256], P(None, 'rows', 'cols')
- patches_grad: float32 [8, 160, 40, 256], P(None, 'rows', 'cols')
- ln1_gain_grad: float32 [256], replicated
- ln1_bias_grad: float32 [256], replicated
- qkv_weight_grad: float32 [256, 768], replicated
- query_bias_grad: float32 [256], replicated
- value_bias_grad: float32 [256], replicated
- rel_table_grad: float32 [8, 361], replicated
- proj_weight_grad: float32 [256, 256], replicated
- proj_bias_grad: float32 [256], replicated
- ln2_gain_grad: float32 [256], replicated
- ln2_bias_grad: float32 [256], replicated
- fc1_weight_grad: float32 [256, 1024], replicated
- fc1_bias_grad: float32 [1024], replicated
- fc2_weight_grad: float32 [1024, 256], replicated
- fc2_bias_grad: float32 [256], replicated
Inputs may be any that keep to these rules, and one draw needn't show every extreme that they name: `kept_mask`: 1 marks a patch that counts in the loss; at least one patch is kept.
All inputs are finite; a program needn't handle non-finite values.
Results may differ from a plain program's by a relative error of at most 0.012.
Values may be sent and summed in bfloat16 or wider, within the bound.
No kernel may reach another device: no remote copies, remote signals or barrier semaphores. Data moves between devices by JAX's collectives and lax.ppermute only.
A program may use at most 128 MiB of HBM per device.

v0:
```python
import math

import jax
import jax.numpy as jnp
from jax import lax
from jax.sharding import PartitionSpec as P

WIN = 10
SHIFT = 5


EPS = 1e-05
HIGH = lax.Precision.HIGHEST


def passed_along(block, axis, distance):
    devices = range(lax.axis_size(axis))
    route = [((i - distance) % len(devices), i) for i in devices]
    return lax.ppermute(block, axis, route)


def shortened(shard):
    return jax.tree.map(lambda a: a.astype(jnp.bfloat16) if a.dtype == jnp.float32 else a, shard)


def to_windows(field):
    count_p, height, width, chans = field.shape
    blocks = field.reshape(count_p, height // WIN, WIN, width // WIN, WIN, chans)
    return blocks.transpose(0, 1, 3, 2, 4, 5).reshape(-1, WIN * WIN, chans)


def from_windows(field, count_p, height, width):
    chans = field.shape[-1]
    blocks = field.reshape(count_p, height // WIN, width // WIN, WIN, WIN, chans)
    return blocks.transpose(0, 1, 3, 2, 4, 5).reshape(count_p, height, width, chans)


def enter_input(field):
    lower = passed_along(field[:, :SHIFT], "rows", -1)
    field = jnp.concatenate([field[:, SHIFT:], lower], 1)
    right = passed_along(field[:, :, :SHIFT], "cols", -1)
    return jnp.concatenate([field[:, :, SHIFT:], right], 2)


def enter_target(field):
    lower = passed_along(field[:, :SHIFT], "rows", -1)
    field = jnp.concatenate([field[:, SHIFT:], lower], 1)
    right = passed_along(field[:, :, :SHIFT], "cols", -1)
    return jnp.concatenate([field[:, :, SHIFT:], right], 2)


def leave_output(field):
    upper = passed_along(field[:, -SHIFT:], "rows", 1)
    field = jnp.concatenate([upper, field[:, :-SHIFT]], 1)
    left_part = passed_along(field[:, :, -SHIFT:], "cols", 1)
    return jnp.concatenate([left_part, field[:, :, :-SHIFT]], 2)


def leave_grad(field):
    upper = passed_along(field[:, -SHIFT:].astype(jnp.bfloat16), "rows", 1).astype(jnp.float32)
    field = jnp.concatenate([upper, field[:, :-SHIFT]], 1)
    left_part = passed_along(shortened(field[:, :, -SHIFT:]), "cols", 1)
    return jnp.concatenate([left_part, field[:, :, :-SHIFT]], 2)


def shift_mask(height, width):
    rows_all = height * lax.axis_size("rows")
    cols_all = width * lax.axis_size("cols")
    row_global = lax.axis_index("rows") * height + jnp.arange(height, dtype=jnp.int32)
    col_global = lax.axis_index("cols") * width + jnp.arange(width, dtype=jnp.int32)
    row_region = (row_global >= rows_all - WIN).astype(jnp.int32) + (
        row_global >= rows_all - SHIFT
    ).astype(jnp.int32)
    col_region = (col_global >= cols_all - WIN).astype(jnp.int32) + (
        col_global >= cols_all - SHIFT
    ).astype(jnp.int32)
    labels = row_region[:, None] * 3 + col_region[None, :]
    label_win = to_windows(labels[None, :, :, None])[..., 0]
    return jnp.where(label_win[:, :, None] == label_win[:, None, :], 0.0, -100.0).astype(
        jnp.float32
    )


def relative_hots():
    offsets = jnp.arange(WIN)[:, None] - jnp.arange(WIN)[None, :] + WIN - 1
    return (offsets[:, :, None] == jnp.arange(2 * WIN - 1)[None, None, :]).astype(jnp.float32)


def normalize(field):
    center = field - jnp.mean(field, -1, keepdims=True)
    inv_std = lax.rsqrt(jnp.mean(center * center, -1, keepdims=True) + EPS)
    return (center * inv_std, inv_std)


def norm_back(upstream, normed, inv_std):
    return inv_std * (
        upstream
        - jnp.mean(upstream, -1, keepdims=True)
        - normed * jnp.mean(upstream * normed, -1, keepdims=True)
    )


def gelu_slope(value):
    return 0.5 * (1.0 + lax.erf(value / math.sqrt(2.0))) + value * jnp.exp(
        -0.5 * value * value
    ) / math.sqrt(2.0 * math.pi)


def forward_pass(frame_win, mask_win, rel_bias, weights):
    (
        ln1_gain,
        ln1_bias,
        qkv_weight,
        query_bias,
        value_bias,
        proj_weight,
        proj_bias,
        ln2_gain,
        ln2_bias,
        fc1_weight,
        fc1_bias,
        fc2_weight,
        fc2_bias,
    ) = weights
    wins, length, width = frame_win.shape
    heads = rel_bias.shape[0]
    head_dim = width // heads
    inputs = frame_win.astype(jnp.float32)
    normed1, inv1 = normalize(inputs)
    attn_in = (normed1 * ln1_gain + ln1_bias).astype(jnp.bfloat16)
    projected = jnp.einsum("wld,de->wle", attn_in, qkv_weight, preferred_element_type=jnp.float32)
    queries = (
        (projected[..., :width] + query_bias)
        .astype(jnp.bfloat16)
        .reshape(wins, length, heads, head_dim)
    )
    keys_all = (
        projected[..., width : 2 * width]
        .astype(jnp.bfloat16)
        .reshape(wins, length, heads, head_dim)
    )
    values = (
        (projected[..., 2 * width :] + value_bias)
        .astype(jnp.bfloat16)
        .reshape(wins, length, heads, head_dim)
    )
    logits = jnp.einsum("wihd,wjhd->whij", queries, keys_all, preferred_element_type=jnp.float32)
    scores = logits * head_dim ** (-0.5) + rel_bias[None] + mask_win[:, None]
    top_score = jnp.max(scores, -1, keepdims=True)
    expo = jnp.exp(scores - top_score)
    probs = expo / jnp.sum(expo, -1, keepdims=True)
    probs_low = probs.astype(jnp.bfloat16)
    mixed = jnp.einsum("whij,wjhd->wihd", probs_low, values, preferred_element_type=jnp.float32)
    mixed = mixed.reshape(wins, length, width).astype(jnp.bfloat16)
    branch = (
        jnp.einsum("wld,de->wle", mixed, proj_weight, preferred_element_type=jnp.float32)
        + proj_bias
    )
    resid = inputs + branch
    normed2, inv2 = normalize(resid)
    mlp_in = (normed2 * ln2_gain + ln2_bias).astype(jnp.bfloat16)
    pre_act = (
        jnp.einsum("wld,df->wlf", mlp_in, fc1_weight, preferred_element_type=jnp.float32) + fc1_bias
    )
    hidden = jax.nn.gelu(pre_act, approximate=False).astype(jnp.bfloat16)
    result = (
        resid
        + jnp.einsum("wlf,fd->wld", hidden, fc2_weight, preferred_element_type=jnp.float32)
        + fc2_bias
    )
    return {
        "normed1": normed1,
        "inv1": inv1,
        "attn_in": attn_in,
        "queries": queries,
        "keys_all": keys_all,
        "values": values,
        "probs": probs,
        "probs_low": probs_low,
        "mixed": mixed,
        "normed2": normed2,
        "inv2": inv2,
        "mlp_in": mlp_in,
        "pre_act": pre_act,
        "hidden": hidden,
        "result": result,
    }


def mlp_backward(saved, grad_out, weights):
    (
        ln1_gain,
        ln1_bias,
        qkv_weight,
        query_bias,
        value_bias,
        proj_weight,
        proj_bias,
        ln2_gain,
        ln2_bias,
        fc1_weight,
        fc1_bias,
        fc2_weight,
        fc2_bias,
    ) = weights
    grad_low = grad_out.astype(jnp.bfloat16)
    fc2_bias_grad = jnp.sum(grad_low.astype(jnp.float32), axis=(0, 1))
    fc2_weight_grad = jnp.einsum(
        "wlf,wld->fd", saved["hidden"], grad_low, preferred_element_type=jnp.float32
    )
    hidden_grad = jnp.einsum(
        "wld,fd->wlf", grad_low, fc2_weight, preferred_element_type=jnp.float32
    )
    pre_grad = (hidden_grad * gelu_slope(saved["pre_act"])).astype(jnp.bfloat16)
    fc1_bias_grad = jnp.sum(pre_grad.astype(jnp.float32), axis=(0, 1))
    fc1_weight_grad = jnp.einsum(
        "wld,wlf->df", saved["mlp_in"], pre_grad, preferred_element_type=jnp.float32
    )
    mlp_in_grad = jnp.einsum(
        "wlf,df->wld", pre_grad, fc1_weight, preferred_element_type=jnp.float32
    )
    ln2_gain_grad = jnp.sum(mlp_in_grad * saved["normed2"], axis=(0, 1))
    ln2_bias_grad = jnp.sum(mlp_in_grad, axis=(0, 1))
    resid_grad = grad_out + norm_back(mlp_in_grad * ln2_gain, saved["normed2"], saved["inv2"])
    return (
        (
            ln2_gain_grad,
            ln2_bias_grad,
            fc1_weight_grad,
            fc1_bias_grad,
            fc2_weight_grad,
            fc2_bias_grad,
        ),
        resid_grad,
    )


def attn_backward(saved, resid_grad, weights, hots, heads):
    (
        ln1_gain,
        ln1_bias,
        qkv_weight,
        query_bias,
        value_bias,
        proj_weight,
        proj_bias,
        ln2_gain,
        ln2_bias,
        fc1_weight,
        fc1_bias,
        fc2_weight,
        fc2_bias,
    ) = weights
    wins, length, width = resid_grad.shape
    head_dim = width // heads
    branch_grad = resid_grad.astype(jnp.bfloat16)
    proj_bias_grad = jnp.sum(branch_grad.astype(jnp.float32), axis=(0, 1))
    proj_weight_grad = jnp.einsum(
        "wld,wle->de", saved["mixed"], branch_grad, preferred_element_type=jnp.float32
    )
    mixed_grad = jnp.einsum(
        "wle,de->wld", branch_grad, proj_weight, preferred_element_type=jnp.float32
    )
    mixed_grad = mixed_grad.astype(jnp.bfloat16).reshape(wins, length, heads, head_dim)
    probs = saved["probs"]
    probs_grad = jnp.einsum(
        "wihd,wjhd->whij", mixed_grad, saved["values"], preferred_element_type=jnp.float32
    )
    values_grad = jnp.einsum(
        "whij,wihd->wjhd", saved["probs_low"], mixed_grad, preferred_element_type=jnp.float32
    )
    score_grad = probs * (probs_grad - jnp.sum(probs * probs_grad, -1, keepdims=True))
    bias_grad = jnp.sum(score_grad, 0).reshape(heads, WIN, WIN, WIN, WIN)
    rel_table_grad = jnp.einsum(
        "hikjl,ija,klb->hab", bias_grad, hots, hots, precision=HIGH
    ).reshape(heads, -1)
    logit_grad = (score_grad * head_dim ** (-0.5)).astype(jnp.bfloat16)
    query_grad = jnp.einsum(
        "whij,wjhd->wihd", logit_grad, saved["keys_all"], preferred_element_type=jnp.float32
    )
    key_grad = jnp.einsum(
        "whij,wihd->wjhd", logit_grad, saved["queries"], preferred_element_type=jnp.float32
    )
    query_low = query_grad.astype(jnp.bfloat16).reshape(wins, length, width)
    key_low = key_grad.astype(jnp.bfloat16).reshape(wins, length, width)
    value_low = values_grad.astype(jnp.bfloat16).reshape(wins, length, width)
    query_bias_grad = jnp.sum(query_low.astype(jnp.float32), axis=(0, 1))
    value_bias_grad = jnp.sum(value_low.astype(jnp.float32), axis=(0, 1))
    joined_grad = jnp.concatenate([query_low, key_low, value_low], -1)
    qkv_weight_grad = jnp.einsum(
        "wld,wle->de", saved["attn_in"], joined_grad, preferred_element_type=jnp.float32
    )
    attn_in_grad = jnp.einsum(
        "wle,de->wld", joined_grad, qkv_weight, preferred_element_type=jnp.float32
    )
    ln1_gain_grad = jnp.sum(attn_in_grad * saved["normed1"], axis=(0, 1))
    ln1_bias_grad = jnp.sum(attn_in_grad, axis=(0, 1))
    input_grad = resid_grad + norm_back(attn_in_grad * ln1_gain, saved["normed1"], saved["inv1"])
    grads = (
        ln1_gain_grad,
        ln1_bias_grad,
        qkv_weight_grad,
        query_bias_grad,
        value_bias_grad,
        rel_table_grad,
        proj_weight_grad,
        proj_bias_grad,
    )
    return (grads, input_grad)


def shards(
    patches,
    target,
    kept_mask,
    ln1_gain,
    ln1_bias,
    qkv_weight,
    query_bias,
    value_bias,
    rel_table,
    proj_weight,
    proj_bias,
    ln2_gain,
    ln2_bias,
    fc1_weight,
    fc1_bias,
    fc2_weight,
    fc2_bias,
):
    count_p, height, width_p, _ = patches.shape
    heads = rel_table.shape[0]
    weights = (
        ln1_gain,
        ln1_bias,
        qkv_weight,
        query_bias,
        value_bias,
        proj_weight,
        proj_bias,
        ln2_gain,
        ln2_bias,
        fc1_weight,
        fc1_bias,
        fc2_weight,
        fc2_bias,
    )
    hots = relative_hots()
    table_grid = rel_table.reshape(heads, 2 * WIN - 1, 2 * WIN - 1)
    rel_bias = jnp.einsum("hab,ija,klb->hikjl", table_grid, hots, hots, precision=HIGH).reshape(
        heads, WIN * WIN, WIN * WIN
    )
    mask_win = jnp.tile(shift_mask(height, width_p), (count_p, 1, 1))
    first = forward_pass(to_windows(enter_input(patches)), mask_win, rel_bias, weights)
    out_field = from_windows(first["result"], count_p, height, width_p).astype(jnp.bfloat16)
    output = leave_output(out_field)
    kept_total = lax.psum(jnp.sum(kept_mask.astype(jnp.float32)), ("rows", "cols"))
    total = count_p * height * lax.axis_size("rows") * width_p * lax.axis_size("cols")
    masked = target * kept_mask.astype(jnp.bfloat16)[..., None]
    masked_frame = enter_target(masked)
    grad_out = to_windows(masked_frame).astype(jnp.float32) * (total / kept_total)
    again, grad_out = lax.optimization_barrier((patches, grad_out))
    saved = forward_pass(to_windows(enter_input(again)), mask_win, rel_bias, weights)
    mlp_grads, resid_grad = mlp_backward(saved, grad_out, weights)
    ln2_gain_grad, ln2_bias_grad, fc1_weight_grad, fc1_bias_grad, fc2_weight_grad, fc2_bias_grad = (
        mlp_grads
    )
    attn_grads, input_grad = attn_backward(saved, resid_grad, weights, hots, heads)
    (
        ln1_gain_grad,
        ln1_bias_grad,
        qkv_weight_grad,
        query_bias_grad,
        value_bias_grad,
        rel_table_grad,
        proj_weight_grad,
        proj_bias_grad,
    ) = attn_grads
    (
        ln1_gain_grad,
        ln1_bias_grad,
        qkv_weight_grad,
        query_bias_grad,
        value_bias_grad,
        rel_table_grad,
        proj_weight_grad,
        proj_bias_grad,
        ln2_gain_grad,
        ln2_bias_grad,
        fc1_weight_grad,
        fc1_bias_grad,
        fc2_weight_grad,
        fc2_bias_grad,
    ) = lax.psum(
        (
            ln1_gain_grad,
            ln1_bias_grad,
            qkv_weight_grad,
            query_bias_grad,
            value_bias_grad,
            rel_table_grad,
            proj_weight_grad,
            proj_bias_grad,
            ln2_gain_grad,
            ln2_bias_grad,
            fc1_weight_grad,
            fc1_bias_grad,
            fc2_weight_grad,
            fc2_bias_grad,
        ),
        ("rows", "cols"),
    )
    grad_field = from_windows(input_grad, count_p, height, width_p)
    patches_grad = leave_grad(grad_field)
    return (
        output,
        patches_grad,
        ln1_gain_grad,
        ln1_bias_grad,
        qkv_weight_grad,
        query_bias_grad,
        value_bias_grad,
        rel_table_grad,
        proj_weight_grad,
        proj_bias_grad,
        ln2_gain_grad,
        ln2_bias_grad,
        fc1_weight_grad,
        fc1_bias_grad,
        fc2_weight_grad,
        fc2_bias_grad,
    )


def solution(mesh):
    return jax.shard_map(
        shards,
        mesh=mesh,
        in_specs=(
            P(None, "rows", "cols", None),
            P(None, "rows", "cols", None),
            P(None, "rows", "cols"),
            P(),
            P(),
            P(),
            P(),
            P(),
            P(),
            P(),
            P(),
            P(),
            P(),
            P(),
            P(),
            P(),
            P(),
        ),
        out_specs=(
            P(None, "rows", "cols", None),
            P(None, "rows", "cols", None),
            P(),
            P(),
            P(),
            P(),
            P(),
            P(),
            P(),
            P(),
            P(),
            P(),
            P(),
            P(),
            P(),
            P(),
        ),
        check_vma=False,
    )
```

profile of v0, /device:TPU:0, one launch (start us, length us, event | category | flops | bytes accessed | tf_op | source)
XLA Modules:
  0.0 478.3 jit_solution(4365714909131413174)
XLA Ops:
  10.5 5.4 %collective-permute-start.4 = (bf16[8,5,20,256]{3,0,2,1:T(8,128)(2,1)}, bf16[8,5,20,256]{3,0,2,1:T(8,128)(2,1)S(1)}, u32[]{:S(2)}, u32[]{:S(2)}) collective-permute-start(bf16[8,5,20,256]{3,0,2,1:T(8,128)(2,1)} %get-tuple-element.61), channel_id=1, source_target_pairs={{2,0},{4,2},{6,4},{8,6},{10,8},{12,10},{14,12},{16,14},{18,16},{20... | collective-permute-start | bytes 1228808 | tf_op jit(solution)/shard_map/ppermute | solution.py:19
  20.5 4.8 %convolution_bitcast_fusion = f32[8,10,10,10,10]{4,3,2,0,1:T(8,128)} fusion(f32[10,10,8,19,1]{3,1,4,2,0:T(8,128)S(1)} %convolution_bitcast_fusion.4, s32[10,10]{1,0:T(8,128)S(1)} %subtract_add_fusion), kind=kOutput, calls=%fused_computation.79 | convolution fusion | flops 18241900 | bytes 381200 | tf_op jit(solution)/shard_map/hab,ija,klb->hikjl/dot_general | solution.py:350
  25.4 37.1 %psum.105 = f32[]{:T(128)} all-reduce(f32[]{:T(128)} %convert_reduce_fusion.5), channel_id=1, replica_groups=mesh['rows'=16,'cols'=2] {'rows','cols'}, use_global_device_ids=true, to_apply=%region_7.8 | all-reduce | flops 1 | bytes 8 | tf_op jit(solution)/shard_map/psum | solution.py:357
  62.5 11.8 %copy.240 = f32[8,10,10,10,10]{2,1,4,3,0:T(8,128)} copy(f32[8,10,10,10,10]{4,3,2,0,1:T(8,128)} %convolution_bitcast_fusion) | data formatting | bytes 640000 | tf_op jit(solution)/shard_map/add | solution.py:148
  74.3 5.1 %reshape.333 = f32[8,100,100]{1,2,0:T(8,128)} reshape(f32[8,10,10,10,10]{2,1,4,3,0:T(8,128)} %copy.240) | data formatting | bytes 640000 | tf_op jit(solution)/shard_map/add | solution.py:148
  80.9 2.3 collective-permute-start.5
  84.0 5.2 %collective-permute-done.5 = bf16[8,10,5,256]{3,0,2,1:T(8,128)(2,1)S(1)} collective-permute-done((bf16[8,10,5,256]{3,0,2,1:T(8,128)(2,1)S(1)}, bf16[8,10,5,256]{3,0,2,1:T(8,128)(2,1)S(1)}, u32[]{:S(2)}, u32[]{:S(2)}) %collective-permute-start.5) | collective-permute-done | bytes 204832 | tf_op jit(solution)/shard_map/ppermute | solution.py:19
  89.4 2.4 copy.296
  91.8 2.4 mul.237
  94.2 1.8 fusion.210
  96.1 1.7 convert_reduce_fusion.4
  97.9 3.7 collective-permute-done.6
  101.6 2.1 collective-permute-start.7
  106.1 1.8 copy.297
  107.8 2.7 reshape.312
  110.9 1.8 copy.295
  113.2 2.6 fusion.205
  119.9 4.7 multiply_reduce_fusion.8
  125.3 2.6 fusion.81
  128.1 2.0 fusion.208
  130.0 2.4 reshape.313
  133.1 6.0 %multiply_reduce_fusion.7 = f32[8,2,10,10]{1,0,3,2:T(8,128)} fusion(f32[8,2,10,10]{1,0,3,2:T(8,128)S(1)} %copy.200, f32[8,1,10,2,10,256]{5,0,4,3,2,1:T(8,128)} %copy-done.10), kind=kLoop, calls=%fused_computation.126 | loop fusion | flops 1227200 | bytes 1651200 | tf_op jit(solution)/shard_map/reduce_sum | solution.py:91
  140.8 2.7 fusion.113
  144.5 2.0 fusion.207
  147.8 2.3 copy.207
  150.1 4.1 fusion.57
  154.2 1.9 copy.204
  156.1 4.5 fusion.56
  160.6 2.6 copy.206
  163.2 2.6 copy.183
  165.7 2.7 copy.185
  169.5 8.0 %fusion.213 = (f32[16,8,100]{2,1,0:T(8,128)S(1)}, f32[16,8,100,100]{2,3,1,0:T(8,128)}) fusion(f32[16,100,100]{1,2,0:T(8,128)} %bitcast.204, f32[8,100,100]{1,2,0:T(8,128)} %reshape.333, bf16[16,100,8,32]{1,3,2,0:T(8,128)(2,1)} %bitcast.197, bf16[16,100,8,32]{1,3,2,0:T(8,128)(2,1)} %bitcast.200), kind=kOutput, calls=%fused_computation.307 | convolution fusion | flops 88320096 | bytes 7769600 | tf_op jit(solution)/shard_map/sub | solution.py:150
  177.5 4.4 fusion.60
  185.2 8.0 %fusion.215 = (f32[16,8,100]{2,1,0:T(8,128)S(1)}, f32[16,8,100,100]{2,3,1,0:T(8,128)}) fusion(f32[16,100,100]{1,2,0:T(8,128)} %bitcast.205, f32[8,100,100]{1,2,0:T(8,128)} %reshape.333, bf16[16,100,8,32]{1,3,2,0:T(8,128)(2,1)} %bitcast.194, bf16[16,100,8,32]{1,3,2,0:T(8,128)(2,1)} %bitcast.198), kind=kOutput, calls=%fused_computation.309 | convolution fusion | flops 88320096 | bytes 7769600 | tf_op jit(solution)/shard_map/sub | solution.py:150
  193.3 4.0 fusion.61
  200.8 6.8 %fusion.41 = (u16[100,1024]{1,0:T(8,128)(2,1)}, u16[100,1024]{1,0:T(8,128)(2,1)}, u16[100,1024]{1,0:T(8,128)(2,1)}, u16[100,1024]{1,0:T(8,128)(2,1)}, f32[16,100,1024]{2,1,0:T(8,128)S(1)}) fusion(f32[1024]{0:T(1024)S(1)} %copy-done.43, f32[16,100,1024]{2,1,0:T(8,128)S(1)} %fusion.82, bf16[256,1024]{1,0:T(8,128)(2,1)S(1)} %copy-done, ...), kind=kOutput, calls=%fused_computation.75 | convolution fusion | flops 886374400 | bytes 16108032 | tf_op jit(solution)/shard_map/wld,df->wlf/dot_general | solution.py:163
  207.6 4.8 %convert_reduce_fusion = (f32[1024]{0:T(1024)}, bf16[16,100,1024]{2,1,0:T(8,128)(2,1)S(1)}) fusion(f32[16,100,1024]{2,1,0:T(8,128)S(1)} %get-tuple-element.76, f32[1024]{0:T(1024)S(1)} %copy-done.43, bf16[1024,256]{1,0:T(8,128)(2,1)S(1)} %copy-done.41, bf16[16,100,256]{2,0,1:T(8,128)(2,1)S(1)} %copy-done.23), kind=kOutput, calls=%fused_computation.40 | convolution fusion | flops 860158976 | bytes 11182080 | tf_op jit(solution)/shard_map/wld,fd->wlf/dot_general | solution.py:211
  212.4 2.6 convolution_bitcast_fusion.1
  215.0 2.2 multiply_reduce_fusion.1
  217.2 2.1 convert_reduce_fusion.3
  221.9 2.3 copy.213
  224.2 6.8 %convert_reduce_fusion.1 = (f32[8,32]{1,0:T(8,128)}, bf16[16,8,32,100]{3,2,1,0:T(8,128)(2,1)}) fusion(bf16[16,100,8,32]{1,3,2,0:T(8,128)(2,1)} %bitcast.188, f32[16,8,100,100]{2,3,1,0:T(8,128)} %get-tuple-element.73, f32[16,8,100]{2,1,0:T(8,128)S(1)} %get-tuple-element.72), kind=kOutput, calls=%fused_computation.81 | convolution fusion | flops 85708544 | bytes 6810624 | tf_op jit(solution)/shard_map/whij,wihd->wjhd/dot_general | solution.py:269
  231.0 4.8 %fusion.220 = f32[16,8,100,100]{2,3,1,0:T(8,128)} fusion(bf16[16,100,8,32]{1,3,2,0:T(8,128)(2,1)S(1)} %bitcast.190, bf16[16,100,8,32]{1,3,2,0:T(8,128)(2,1)S(1)} %bitcast.186), kind=kOutput, calls=%fused_computation.312 | convolution fusion | flops 81920000 | bytes 6758400 | tf_op jit(solution)/shard_map/wihd,wjhd->whij/dot_general | solution.py:266
  235.8 12.5 %convolution_convert_fusion = bf16[16,8,32,100]{3,2,1,0:T(8,128)(2,1)} fusion(bf16[16,100,8,32]{1,3,2,0:T(8,128)(2,1)} %bitcast.195, f32[16,8,100,100]{2,3,1,0:T(8,128)} %fusion.220, f32[16,8,100,100]{2,3,1,0:T(8,128)} %get-tuple-element.73, f32[16,8,100]{2,1,0:T(8,128)S(1)} %get-tuple-element.72), kind=kOutput, calls=%fused_computation.133 | convolution fusion | flops 91302496 | bytes 11929600 | tf_op jit(solution)/shard_map/whij,wihd->wjhd/dot_general | solution.py:281
  248.2 11.3 %convert_reduce_fusion.2 = (f32[8,32]{1,0:T(8,128)S(1)}, bf16[16,8,32,100]{3,2,1,0:T(8,128)(2,1)}) fusion(bf16[16,100,8,32]{1,3,2,0:T(8,128)(2,1)S(1)} %bitcast.199, f32[16,8,100,100]{2,3,1,0:T(8,128)} %fusion.220, f32[16,8,100,100]{2,3,1,0:T(8,128)} %get-tuple-element.73, f32[16,8,100]{2,1,0:T(8,128)S(1)} %get-tuple-element.72), kind=kOutput, calls=%fused_computation.82 | convolution fusion | flops 92121440 | bytes 11930624 | tf_op jit(solution)/shard_map/whij,wjhd->wihd/dot_general | solution.py:278
  261.1 2.3 copy.217
  263.4 2.4 copy.218
  265.8 4.3 convolution_bitcast_fusion.2
  270.2 3.2 multiply_reduce_fusion.2
  273.4 17.3 %add_convert_fusion.2 = bf16[16,100,256]{2,1,0:T(8,128)(2,1)S(1)} fusion(f32[16,100,256]{2,1,0:T(8,128)S(1)} %copy-done.7, f32[16,100,1024]{2,1,0:T(8,128)S(1)} %bitcast.175, f32[1024]{0:T(1024)S(1)} %copy-done.43, u16[100,1024]{1,0:T(8,128)(2,1)S(1)} %copy-done.46, u16[100,1024]{1,0:T(8,128)(2,1)S(1)} %copy-done.47, f32[256]{0:T(256)S(1)} %copy-done.44, ...), kind=kOutput, calls=%fused_computation.105 | convolution fusion | flops 956416000 | bytes 9950208 | tf_op jit(solution)/shard_map/wlf,fd->wld/dot_general | solution.py:168
  295.1 2.8 multiply_add_fusion
  298.5 2.1 reshape.308
  303.2 19.8 %fusion.69 = f32[1024,256]{1,0:T(8,128)} fusion(f32[16,100,1024]{2,1,0:T(8,128)} %copy-done.45, f32[1024]{0:T(1024)S(1)} %copy-done.43, u16[100,1024]{1,0:T(8,128)(2,1)} %get-tuple-element.21, u16[100,1024]{1,0:T(8,128)(2,1)} %get-tuple-element.20, bf16[16,100,256]{2,0,1:T(8,128)(2,1)} %get-tuple-element.49), kind=kOutput, calls=%fused_computation.139 | convolution fusion | flops 955187200 | bytes 8835072 | tf_op jit(solution)/shard_map/wlf,wld->fd/dot_general | solution.py:208
  323.0 8.9 %fusion.219 = f32[8,100,100]{1,2,0:T(8,128)} fusion(bf16[16,100,8,32]{1,3,2,0:T(8,128)(2,1)} %bitcast.189, bf16[16,100,8,32]{1,3,2,0:T(8,128)(2,1)} %bitcast.187, f32[16,8,100,100]{2,3,1,0:T(8,128)} %get-tuple-element.73, f32[16,8,100]{2,1,0:T(8,128)S(1)} %get-tuple-element.72), kind=kOutput, calls=%fused_computation.311 | convolution fusion | flops 171452896 | bytes 7129600 | tf_op jit(solution)/shard_map/sub | solution.py:272
  332.0 5.0 %reshape.334 = f32[8,10,10,10,10]{2,1,4,3,0:T(8,128)} reshape(f32[8,100,100]{1,2,0:T(8,128)} %fusion.219) | data formatting | bytes 640000 | tf_op jit(solution)/shard_map/reshape | solution.py:273
  337.0 12.5 %copy.236 = f32[8,10,10,10,10]{4,3,1,2,0:T(8,128)} copy(f32[8,10,10,10,10]{2,1,4,3,0:T(8,128)} %reshape.334) | data formatting | bytes 640000 | tf_op jit(solution)/shard_map/reshape | solution.py:273
  354.1 8.2 %convolution_bitcast_fusion.3 = f32[19,8,10,10]{0,3,2,1:T(8,128)S(1)} fusion(f32[8,10,10,10,10]{4,3,1,2,0:T(8,128)} %copy.236, s32[10,10]{1,0:T(8,128)S(1)} %copy-done.26), kind=kOutput, calls=%fused_computation.141 | convolution fusion | flops 18241900 | bytes 381200 | tf_op jit(solution)/shard_map/hikjl,ija,klb->hab/dot_general | solution.py:274
  363.4 41.6 %all-reduce = (f32[256]{0:T(256)}, f32[256]{0:T(256)}, f32[256]{0:T(256)}, f32[256]{0:T(256)}, f32[8,361]{1,0:T(8,128)}, /*index=5*/f32[256]{0:T(256)}, f32[256]...) all-reduce(f32[256]{0:T(256)S(1)} %get-tuple-element.26, ...), channel_id=1, replica_groups=mesh['rows'=16,'cols'=2] {'rows','cols'}, use_global_device_ids=true, to_apply=%region_20.21 | all-reduce | flops 5960 | bytes 47680 | tf_op jit(solution)/shard_map/psum | solution.py:394
  405.9 2.0 fusion.91
  409.3 53.7 %all-reduce.4.cloned.1.call-done = (f32[256,768]{1,0:T(8,128)}, f32[256,256]{1,0:T(8,128)}, f32[256,1024]{1,0:T(8,128)}, f32[1024,256]{1,0:T(8,128)}) async-done(((f32[256,768]{1,0:T(8,128)}, f32[256,256]{1,0:T(8,128)}, f32[256,1024]{1,0:T(8,128)}, f32[1024,256]{1,0:T(8,128)}), (f32[256,768]{1,0:T(8,128)}, f32[256,256]{1,0:T(8,128)}, f32[256,1024]{1,0:T(8,128)}, ...) | async-done | bytes 3145744 | tf_op jit(solution)/shard_map/psum | solution.py:394
  463.0 2.1 copy.302
  465.0 1.7 copy.303
  466.7 2.3 copy.304
  469.0 2.3 copy.305
  (198 shorter events, 49.9 us)
Async XLA Ops:
  7.2 192.2 %copy-start = (bf16[256,1024]{1,0:T(8,128)(2,1)S(1)}, bf16[256,1024]{1,0:T(8,128)(2,1)}, u32[]{:S(2)}) copy-start(bf16[256,1024]{1,0:T(8,128)(2,1)} %param.30) | copy-start | bytes 1572868
  7.2 455.8 %all-reduce.4.cloned.1.call-start = ((), (), s32[]{:S(2)}) async-start(), calls=%async_computation | async-start | bytes 6291456 | tf_op jit(solution)/shard_map/psum | solution.py:394
  10.5 70.4 %collective-permute-start.4 = (bf16[8,5,20,256]{3,0,2,1:T(8,128)(2,1)}, bf16[8,5,20,256]{3,0,2,1:T(8,128)(2,1)S(1)}, u32[]{:S(2)}, u32[]{:S(2)}) collective-permute-start(bf16[8,5,20,256]{3,0,2,1:T(8,128)(2,1)} %get-tuple-element.61), channel_id=1, source_target_pairs={{2,0},{4,2},{6,4},{8,6},{10,8},{12,10},{14,12},{16,14},{18,16},{20... | collective-permute-start | bytes 1228808 | tf_op jit(solution)/shard_map/ppermute | solution.py:19
  17.1 66.1 %collective-permute-start = (bf16[8,5,20,256]{3,0,2,1:T(8,128)(2,1)S(1)}, bf16[8,5,20,256]{3,0,2,1:T(8,128)(2,1)S(1)}, u32[]{:S(2)}, u32[]{:S(2)}) collective-permute-start(bf16[8,5,20,256]{3,0,2,1:T(8,128)(2,1)S(1)} %get-tuple-element.63), channel_id=1, source_target_pairs={{2,0},{4,2},{6,4},{8,6},{10,8},{12,10},{14,12},{16,14},{18,16},{20... | collective-permute-start | bytes 1228808 | tf_op jit(solution)/shard_map/ppermute | solution.py:19
  19.2 55.1 %copy-start.25 = (s32[10,10]{1,0:T(8,128)}, s32[10,10]{1,0:T(8,128)S(1)}, u32[]{:S(2)}) copy-start(s32[10,10]{1,0:T(8,128)S(1)} %subtract_add_fusion) | copy-start | bytes 1204
  80.9 8.3 %collective-permute-start.5 = (bf16[8,10,5,256]{3,0,2,1:T(8,128)(2,1)S(1)}, bf16[8,10,5,256]{3,0,2,1:T(8,128)(2,1)S(1)}, u32[]{:S(2)}, u32[]{:S(2)}) collective-permute-start(bf16[8,10,5,256]{3,0,2,1:T(8,128)(2,1)S(1)} %pad_maximum_fusion.8), channel_id=1, source_target_pairs={{1,0},{0,1},{3,2},{2,3},{5,4},{4,5},{7,6},{6,7},{9,8},{8,9},{11,10... | collective-permute-start | bytes 614408 | tf_op jit(solution)/shard_map/ppermute | solution.py:19
  83.9 19.7 %collective-permute-start.1 = (bf16[8,10,5,256]{3,0,2,1:T(8,128)(2,1)}, bf16[8,10,5,256]{3,0,2,1:T(8,128)(2,1)}, u32[]{:S(2)}, u32[]{:S(2)}) collective-permute-start(bf16[8,10,5,256]{3,0,2,1:T(8,128)(2,1)} %pad_maximum_fusion.10), channel_id=1, source_target_pairs={{1,0},{0,1},{3,2},{2,3},{5,4},{4,5},{7,6},{6,7},{9,8},{8,9},{11,10... | collective-permute-start | bytes 614408 | tf_op jit(solution)/shard_map/ppermute | solution.py:19
  94.2 13.6 %copy-start.8 = (f32[16,100,256]{2,0,1:T(8,128)}, f32[16,100,256]{2,0,1:T(8,128)S(1)}, u32[]{:S(2)}) copy-start(f32[16,100,256]{2,0,1:T(8,128)S(1)} %mul.237) | copy-start | bytes 4915204
  96.0 5.5 %collective-permute-start.6 = (bf16[8,5,20,256]{3,0,2,1:T(8,128)(2,1)S(1)}, bf16[8,5,20,256]{3,0,2,1:T(8,128)(2,1)S(1)}, u32[]{:S(2)}, u32[]{:S(2)}) collective-permute-start(bf16[8,5,20,256]{3,0,2,1:T(8,128)(2,1)S(1)} %get-tuple-element.59), channel_id=1, source_target_pairs={{2,0},{4,2},{6,4},{8,6},{10,8},{12,10},{14,12},{16,14},{18,16},{20... | collective-permute-start | bytes 1228808 | tf_op jit(solution)/shard_map/ppermute | solution.py:19
  101.5 3.1 copy-start.16
  101.6 9.1 %collective-permute-start.7 = (bf16[8,10,5,256]{3,0,2,1:T(8,128)(2,1)S(1)}, bf16[8,10,5,256]{3,0,2,1:T(8,128)(2,1)S(1)}, u32[]{:S(2)}, u32[]{:S(2)}) collective-permute-start(bf16[8,10,5,256]{3,0,2,1:T(8,128)(2,1)S(1)} %pad_maximum_fusion.7), channel_id=1, source_target_pairs={{1,0},{0,1},{3,2},{2,3},{5,4},{4,5},{7,6},{6,7},{9,8},{8,9},{11,10... | collective-permute-start | bytes 614408 | tf_op jit(solution)/shard_map/ppermute | solution.py:19
  104.7 5.9 %copy-start.17 = (bf16[8,5,20,256]{3,0,2,1:T(8,128)(2,1)S(1)}, bf16[8,5,20,256]{3,0,2,1:T(8,128)(2,1)}, u32[]{:S(2)}) copy-start(bf16[8,5,20,256]{3,0,2,1:T(8,128)(2,1)} %copy-done.16) | copy-start | bytes 1228804
  110.5 14.8 %copy-start.3 = (f32[16,100,256]{2,0,1:T(8,128)}, f32[16,100,256]{2,0,1:T(8,128)S(1)}, u32[]{:S(2)}) copy-start(f32[16,100,256]{2,0,1:T(8,128)S(1)} %reshape.312) | copy-start | bytes 4915204
  110.6 2.6 copy-start.11
  110.9 1.8 copy-start.10
  143.5 6.7 %copy-start.39 = (f32[256]{0:T(256)S(1)}, f32[256]{0:T(256)}, u32[]{:S(2)}) copy-start(f32[256]{0:T(256)} %param.24) | copy-start | bytes 3076
  146.5 9.6 %copy-start.40 = (f32[256]{0:T(256)S(1)}, f32[256]{0:T(256)}, u32[]{:S(2)}) copy-start(f32[256]{0:T(256)} %param.23) | copy-start | bytes 3076
  154.2 14.3 %copy-start.24 = (f32[2,100,100]{1,2,0:T(8,128)S(1)}, f32[2,100,100]{1,2,0:T(8,128)}, u32[]{:S(2)}) copy-start(f32[2,100,100]{1,2,0:T(8,128)} %compare_select_fusion) | copy-start | bytes 240004
  156.1 74.9 %copy-start.13 = (bf16[16,100,256]{1,2,0:T(8,128)(2,1)}, bf16[16,100,256]{1,2,0:T(8,128)(2,1)S(1)}, u32[]{:S(2)}) copy-start(bf16[16,100,256]{1,2,0:T(8,128)(2,1)S(1)} %copy.204) | copy-start | bytes 2457604
  177.5 4.4 copy-start.4
  177.5 4.4 copy-start.19
  177.5 4.4 copy-start.29
  183.4 1.2 copy-start.5
  193.3 6.1 %copy-start.30 = (f32[256]{0:T(256)S(1)}, f32[256]{0:T(256)}, u32[]{:S(2)}) copy-start(f32[256]{0:T(256)} %param.28) | copy-start | bytes 3076
  193.3 6.1 %copy-start.36 = (f32[256]{0:T(256)S(1)}, f32[256]{0:T(256)}, u32[]{:S(2)}) copy-start(f32[256]{0:T(256)} %param.29) | copy-start | bytes 3076
  197.2 2.2 copy-start.6
  197.2 3.5 copy-start.43
  200.8 6.8 %copy-start.12 = (f32[16,100,1024]{2,1,0:T(8,128)}, f32[16,100,1024]{2,1,0:T(8,128)S(1)}, u32[]{:S(2)}) copy-start(f32[16,100,1024]{2,1,0:T(8,128)S(1)} %fusion.82) | copy-start | bytes 19660804
  200.8 6.8 %copy-start.23 = (bf16[16,100,256]{2,0,1:T(8,128)(2,1)S(1)}, bf16[16,100,256]{2,0,1:T(8,128)(2,1)}, u32[]{:S(2)}) copy-start(bf16[16,100,256]{2,0,1:T(8,128)(2,1)} %get-tuple-element.49) | copy-start | bytes 2457604
  200.8 6.8 %copy-start.41 = (bf16[1024,256]{1,0:T(8,128)(2,1)S(1)}, bf16[1024,256]{1,0:T(8,128)(2,1)}, u32[]{:S(2)}) copy-start(bf16[1024,256]{1,0:T(8,128)(2,1)} %param.32) | copy-start | bytes 1572868
  207.5 4.8 %copy-start.45 = (f32[16,100,1024]{2,1,0:T(8,128)}, f32[16,100,1024]{2,1,0:T(8,128)S(1)}, u32[]{:S(2)}) copy-start(f32[16,100,1024]{2,1,0:T(8,128)S(1)} %get-tuple-element.76) | copy-start | bytes 19660804
  215.0 2.2 copy-start.9
  219.3 1.3 copy-start.2
  224.2 6.8 %copy-start.14 = (bf16[16,100,256]{1,2,0:T(8,128)(2,1)S(1)}, bf16[16,100,256]{1,2,0:T(8,128)(2,1)}, u32[]{:S(2)}) copy-start(bf16[16,100,256]{1,2,0:T(8,128)(2,1)} %copy.213) | copy-start | bytes 2457604
  235.8 12.5 %copy-start.20 = (bf16[16,100,256]{1,2,0:T(8,128)(2,1)S(1)}, bf16[16,100,256]{1,2,0:T(8,128)(2,1)}, u32[]{:S(2)}) copy-start(bf16[16,100,256]{1,2,0:T(8,128)(2,1)} %copy.207) | copy-start | bytes 2457604
  248.2 17.5 %copy-start.27 = (f32[16,100]{1,0:T(8,128)S(1)}, f32[16,100]{1,0:T(8,128)}, u32[]{:S(2)}) copy-start(f32[16,100]{1,0:T(8,128)} %div.78) | copy-start | bytes 19204
  248.2 17.5 %copy-start.28 = (f32[256]{0:T(256)S(1)}, f32[256]{0:T(256)}, u32[]{:S(2)}) copy-start(f32[256]{0:T(256)} %param.20) | copy-start | bytes 3076
  248.2 17.5 %copy-start.31 = (f32[256]{0:T(256)S(1)}, f32[256]{0:T(256)}, u32[]{:S(2)}) copy-start(f32[256]{0:T(256)} %param.21) | copy-start | bytes 3076
  263.4 6.7 %copy-start.18 = (bf16[256,768]{1,0:T(8,128)(2,1)S(1)}, bf16[256,768]{1,0:T(8,128)(2,1)}, u32[]{:S(2)}) copy-start(bf16[256,768]{1,0:T(8,128)(2,1)} %param.22) | copy-start | bytes 1179652
  265.8 4.3 copy-start.21
  265.8 4.3 copy-start.22
  265.8 7.6 %slice-start = ((s8[6815744]{0:T(1024)(128)(4,1)}), s8[4194304]{0:T(1024)(128)(4,1)S(1)}, s32[]{:S(2)}) async-start(s8[6815744]{0:T(1024)(128)(4,1)} %bitcast.174), calls=%async_computation.1 | async-start | bytes 8388608
  270.1 3.3 copy-start.7
  270.1 3.3 slice-start.1
  270.1 3.3 copy-start.42
  270.1 3.3 copy-start.44
  270.2 3.2 copy-start.46
  270.2 3.2 copy-start.47
  294.2 55.4 %collective-permute-start.2 = (bf16[8,5,20,256]{3,0,2,1:T(8,128)(2,1)}, bf16[8,5,20,256]{3,0,2,1:T(8,128)(2,1)S(1)}, u32[]{:S(2)}, u32[]{:S(2)}) collective-permute-start(bf16[8,5,20,256]{3,0,2,1:T(8,128)(2,1)} %get-tuple-element.56), channel_id=1, source_target_pairs={{30,0},{0,2},{2,4},{4,6},{6,8},{8,10},{10,12},{12,14},{14,16},{16,... | collective-permute-start | bytes 1228808 | tf_op jit(solution)/shard_map/ppermute | solution.py:19
  303.1 48.5 %collective-permute-start.8 = (bf16[8,5,20,256]{3,0,2,1:T(8,128)(2,1)}, bf16[8,5,20,256]{3,0,2,1:T(8,128)(2,1)}, u32[]{:S(2)}, u32[]{:S(2)}) collective-permute-start(bf16[8,5,20,256]{3,0,2,1:T(8,128)(2,1)} %slice.159), channel_id=1, source_target_pairs={{30,0},{0,2},{2,4},{4,6},{6,8},{8,10},{10,12},{12,14},{14,16},{16,... | collective-permute-start | bytes 1228808 | tf_op jit(solution)/shard_map/ppermute | solution.py:19
  337.0 17.1 %copy-start.26 = (s32[10,10]{1,0:T(8,128)S(1)}, s32[10,10]{1,0:T(8,128)}, u32[]{:S(2)}) copy-start(s32[10,10]{1,0:T(8,128)} %copy-done.25) | copy-start | bytes 1204
  349.5 12.9 %copy-start.34 = (f32[8,32]{1,0:T(8,128)S(1)}, f32[8,32]{1,0:T(8,128)}, u32[]{:S(2)}) copy-start(f32[8,32]{1,0:T(8,128)} %get-tuple-element.81) | copy-start | bytes 3076
  349.5 13.8 %copy-start.32 = (f32[256]{0:T(256)S(1)}, f32[256]{0:T(256)}, u32[]{:S(2)}) copy-start(f32[256]{0:T(256)} %get-tuple-element.48) | copy-start | bytes 3076
  349.5 13.8 %copy-start.33 = (f32[256]{0:T(256)S(1)}, f32[256]{0:T(256)}, u32[]{:S(2)}) copy-start(f32[256]{0:T(256)} %get-tuple-element.50) | copy-start | bytes 3076
  349.5 13.8 %copy-start.35 = (f32[1024]{0:T(1024)S(1)}, f32[1024]{0:T(1024)}, u32[]{:S(2)}) copy-start(f32[1024]{0:T(1024)} %get-tuple-element.83) | copy-start | bytes 12292
  349.5 13.8 %copy-start.37 = (f32[256]{0:T(256)S(1)}, f32[256]{0:T(256)}, u32[]{:S(2)}) copy-start(f32[256]{0:T(256)} %get-tuple-element.24) | copy-start | bytes 3076
  349.6 13.8 %copy-start.38 = (f32[256]{0:T(256)S(1)}, f32[256]{0:T(256)}, u32[]{:S(2)}) copy-start(f32[256]{0:T(256)} %get-tuple-element.30) | copy-start | bytes 3076
  349.6 3.8 copy-start.15
  350.3 55.6 %collective-permute-start.3 = (bf16[8,10,5,256]{3,0,2,1:T(8,128)(2,1)}, bf16[8,10,5,256]{3,0,2,1:T(8,128)(2,1)}, u32[]{:S(2)}, u32[]{:S(2)}) collective-permute-start(bf16[8,10,5,256]{3,0,2,1:T(8,128)(2,1)} %pad_maximum_fusion.9), channel_id=1, source_target_pairs={{1,0},{0,1},{3,2},{2,3},{5,4},{4,5},{7,6},{6,7},{9,8},{8,9},{11,10... | collective-permute-start | bytes 614408 | tf_op jit(solution)/shard_map/ppermute | solution.py:19
  353.4 51.6 %collective-permute-start.9 = (bf16[8,10,5,256]{3,0,2,1:T(8,128)(2,1)}, bf16[8,10,5,256]{3,0,2,1:T(8,128)(2,1)}, u32[]{:S(2)}, u32[]{:S(2)}) collective-permute-start(bf16[8,10,5,256]{3,0,2,1:T(8,128)(2,1)} %fusion.111), channel_id=1, source_target_pairs={{1,0},{0,1},{3,2},{2,3},{5,4},{4,5},{7,6},{6,7},{9,8},{8,9},{11,10... | collective-permute-start | bytes 614408 | tf_op jit(solution)/shard_map/ppermute | solution.py:19
  354.1 117.1 %copy-start.1 = (bf16[256,1024]{1,0:T(8,128)(2,1)S(1)}, bf16[256,1024]{1,0:T(8,128)(2,1)}, u32[]{:S(2)}) copy-start(bf16[256,1024]{1,0:T(8,128)(2,1)} %param.30) | copy-start | bytes 1572868
Sparse Core Ops, SparseCore 0:
  323.2 139.7 all-reduce.3
where the time goes:
time: 487 us; the launch traced here: 478 us
  matrix products  156 us (32%)
  local copies, waits for them, and re-layouts  107 us (22%)
  blocking collectives  78.6 us (16%)
  waiting for transfers between devices  62.6 us (13%)
  other arithmetic  44.6 us (9%)
  between operations  15.9 us (3%)
  starting transfers between devices  13.8 us (3%)
    psum x1, waiting for transfers between devices, shards(): lax.psum((ln1_gain_grad, ln1_bias_grad, qkv_weight_grad, query_bias_grad,...  53.7 us
    psum x1, blocking collectives, shards(): lax.psum((ln1_gain_grad, ln1_bias_grad, qkv_weight_grad, query_bias_grad,...  41.6 us
    psum x1, blocking collectives, shards(): lax.psum(jnp.sum(kept_mask.astype(jnp.float32)), ('rows', 'cols'))  37.1 us
    dot_general x1, matrix products, mlp_backward(): jnp.einsum('wlf,wld->fd', saved['hidden'], grad_low, preferred_element_ty...  19.8 us
    reshape x2, local copies, waits for them, and re-layouts, attn_backward(): bias_grad = jnp.sum(score_grad, 0).reshape(heads, WIN, WIN, WIN, WIN)  17.5 us
    dot_general x1, matrix products, forward_pass(): jnp.einsum('wlf,fd->wld', hidden, fc2_weight, preferred_element_type=jnp....  17.3 us
    add x2, local copies, waits for them, and re-layouts, forward_pass(): scores = logits * head_dim ** (-0.5) + rel_bias[None] + mask_win[:, None]  16.9 us
    sub x2, matrix products, forward_pass(): expo = jnp.exp(scores - top_score)  16.1 us
  transfers between devices with their start and end apart: 11, of which 3 were waited for; matrix products, arithmetic and copies ran while one was open for 24% of the time, Pallas kernels for 0%

commit v1 on v0

v1 whole, which is shorter than its diff:
```python
import math

import jax
import jax.numpy as jnp
from jax import lax
from jax.experimental import pallas as pl
from jax.experimental.pallas import tpu as pltpu
from jax.sharding import PartitionSpec as P

WIN = 10
SHIFT = 5
EPS = 1e-05
HIGH = lax.Precision.HIGHEST
F32 = jnp.float32
BF16 = jnp.bfloat16

SPAN = 2 * WIN - 1
TOK = WIN * WIN
ROWS = 104
KEYS = 128
GROUP = 4
RELS = 384
NEVER = -1e30
VMEM_LIMIT = 60 * 1024 * 1024


def dot(a, b):
    return lax.dot_general(a, b, (((1,), (0,)), ((), ())), preferred_element_type=F32)


def dot_bt(a, b):
    return lax.dot_general(a, b, (((1,), (1,)), ((), ())), preferred_element_type=F32)


def dot_at(a, b):
    return lax.dot_general(a, b, (((0,), (0,)), ((), ())), preferred_element_type=F32)


def normalize(x):
    center = x - jnp.sum(x, -1, keepdims=True) * (1.0 / x.shape[-1])
    inv = lax.rsqrt(jnp.sum(center * center, -1, keepdims=True) * (1.0 / x.shape[-1]) + EPS)
    return center * inv, inv


def norm_back(up, normed, inv):
    scale = 1.0 / up.shape[-1]
    mean_up = jnp.sum(up, -1, keepdims=True) * scale
    mean_un = jnp.sum(up * normed, -1, keepdims=True) * scale
    return inv * (up - mean_up - normed * mean_un)


def fold(x):
    return jnp.sum(x.reshape(x.shape[0] // 8, 8, x.shape[1]), 0)


def gather_windows(raster, windows, own, low, right, corner):
    for r in range(WIN):
        if r < WIN - SHIFT:
            main, side = own[0, r + SHIFT], right[0, r]
        else:
            main, side = low[0, r - SHIFT], corner[0, r - SHIFT]
        raster[r, 0 : 2 * WIN, :] = main.astype(F32)
        raster[r, 2 * WIN : 2 * WIN + SHIFT, :] = side.astype(F32)
    for r in range(WIN):
        for w in range(2):
            at = SHIFT + w * WIN
            windows[w * ROWS + r * WIN : w * ROWS + (r + 1) * WIN, :] = raster[r, at : at + WIN, :]


def scatter_windows(raster, windows, out):
    for r in range(WIN):
        for w in range(2):
            raster[r, w * WIN : (w + 1) * WIN, :] = windows[
                w * ROWS + r * WIN : w * ROWS + (r + 1) * WIN, :
            ]
    for r in range(WIN):
        out[0, r] = raster[r, 0 : 2 * WIN, :].astype(out.dtype)


def head_masks(rows, dtype):
    lane = lax.broadcasted_iota(jnp.int32, (rows, KEYS), 1)
    width = KEYS // GROUP
    return [
        ((lane >= k * width) & (lane < (k + 1) * width)).astype(F32).astype(dtype)
        for k in range(GROUP)
    ]


def split_rows(x):
    high = x.astype(BF16)
    return high, (x - high.astype(F32)).astype(BF16)


def forward_kernel(
    own, low, right, corner, t_own, t_low, t_right, t_corner, count,
    qkv_w, proj_w, fc1_w, fc2_w, bias,
    g1, b1, qb, vb, pb, g2, b2, f1b, f2b,
    frame_out, xw_out, qkv_out, p_out, dy_out, do_out, sums_out,
    raster, xw, tw, rw, fc1_acc, fc2_acc, proj_acc, fc1_sum, small_sum,
):
    page = pl.program_id(0)

    @pl.when(page == 0)
    def _():
        for buf in (xw, tw, rw, fc1_acc, fc2_acc, proj_acc, fc1_sum, small_sum):
            buf[...] = jnp.zeros_like(buf)

    d = g1.shape[-1]
    heads = d // (KEYS // GROUP)
    scale = (d // heads) ** (-0.5)
    gather_windows(raster, xw, own, low, right, corner)
    gather_windows(raster, tw, t_own, t_low, t_right, t_corner)
    x = xw[...]
    xw_out[0] = x.astype(BF16)
    normed, _ = normalize(x)
    attn_in = (normed * g1[...] + b1[...]).astype(BF16)
    proj = dot(attn_in, qkv_w[...])
    q_all = proj[:, :d] + qb[...]
    k_all = proj[:, d : 2 * d]
    v_all = proj[:, 2 * d :] + vb[...]
    masks = head_masks(KEYS, BF16)
    filler = jnp.zeros((KEYS - ROWS, d), F32)
    mixed = []
    for w in range(2):
        rows = slice(w * ROWS, (w + 1) * ROWS)
        q = jnp.concatenate([q_all[rows], filler], 0).astype(BF16)
        k = jnp.concatenate([k_all[rows], filler], 0).astype(BF16)
        v = jnp.concatenate([v_all[rows], filler], 0).astype(BF16)
        qkv_out[w, :, :d] = q
        qkv_out[w, :, d : 2 * d] = k
        qkv_out[w, :, 2 * d :] = v
        parts = []
        for g in range(heads // GROUP):
            lanes = slice(g * KEYS, (g + 1) * KEYS)
            kg, vg = k[:, lanes], v[:, lanes]
            k_stack = jnp.concatenate([kg * m for m in masks], 0)
            v_stack = jnp.concatenate([vg * m for m in masks], 0)
            wide = slice(g * GROUP * KEYS, (g + 1) * GROUP * KEYS)
            s = dot_bt(q[:ROWS, lanes], k_stack) * scale + bias[w, :, wide]
            probs = []
            for h in range(GROUP):
                sh = s[:, h * KEYS : (h + 1) * KEYS]
                e = jnp.exp(sh - jnp.max(sh, -1, keepdims=True))
                probs.append(e * (1.0 / jnp.sum(e, -1, keepdims=True)))
            p = jnp.concatenate(probs, 1).astype(BF16)
            p_out[w, :, wide] = p
            parts.append(dot(p, v_stack))
        mixed.append(jnp.concatenate(parts, 1))
    o = jnp.concatenate(mixed, 0).astype(BF16)
    y = x + dot(o, proj_w[...]) + pb[...]
    normed2, inv2 = normalize(y)
    c = (normed2 * g2[...] + b2[...]).astype(BF16)
    h = dot(c, fc1_w[...]) + f1b[...]
    e = jnp.exp(h * h * -0.5)
    phi = 0.5 * (1.0 + lax.erf(h * math.sqrt(0.5)))
    gelu = (h * phi).astype(BF16)
    slope = phi + h * e * (1.0 / math.sqrt(2.0 * math.pi))
    rw[...] = y + dot(gelu, fc2_w[...]) + f2b[...]
    scatter_windows(raster, rw, frame_out)

    dr = tw[...]
    drb = dr.astype(BF16)
    dh = (dot_bt(drb, fc2_w[...]) * slope).astype(BF16)
    fc2_acc[...] += dot_at(drb, gelu)
    fc1_acc[...] += dot_at(c, dh)
    dc = dot_bt(dh, fc1_w[...])
    dy = dr + norm_back(dc * g2[...], normed2, inv2)
    dz = dy.astype(BF16)
    proj_acc[...] += dot_at(o, dz)
    do = dot_bt(dz, proj_w[...])
    for w in range(2):
        do_out[w] = do[w * ROWS : (w + 1) * ROWS].astype(BF16)
    dy_out[0] = dy
    fc1_sum[...] += fold(dh.astype(F32))
    small_sum[0] += fold(dc * normed2)
    small_sum[1] += fold(dc)
    small_sum[2] += fold(dr)
    small_sum[3] += fold(dz.astype(F32))

    @pl.when(page == pl.num_programs(0) - 1)
    def _():
        ff = fc1_w.shape[1] // d
        for j in range(ff):
            sums_out[j * d : (j + 1) * d, :] = fc1_acc[:, j * d : (j + 1) * d].astype(BF16)
            sums_out[(ff + j) * d : (ff + j + 1) * d, :] = fc2_acc[:, j * d : (j + 1) * d].T.astype(
                BF16
            )
        at = 2 * ff * d
        sums_out[at : at + d, :] = proj_acc[...].astype(BF16)
        rows = [jnp.sum(fc1_sum[:, j * d : (j + 1) * d], 0, keepdims=True) for j in range(ff)]
        rows += [jnp.sum(small_sum[k], 0, keepdims=True) for k in range(4)]
        rows.append(jnp.full((1, d), count[0], F32))
        rows.append(jnp.zeros((16 - len(rows), d), F32))
        high, low_part = split_rows(jnp.concatenate(rows, 0))
        at += d
        sums_out[at : at + 16, :] = high
        sums_out[at + 16 : at + 32, :] = low_part
        if sums_out.shape[0] > at + 32:
            sums_out[at + 32 :, :] = jnp.zeros((sums_out.shape[0] - at - 32, d), BF16)


def backward_kernel(
    xw, qkv, p_in, dy_in, do_in, qkv_w, g1, b1, hot,
    frame_out, sums_out,
    raster, dxw, qkv_acc, rel_acc, col_sum, small_sum,
):
    page = pl.program_id(0)

    @pl.when(page == 0)
    def _():
        for buf in (qkv_acc, rel_acc, col_sum, small_sum):
            buf[...] = jnp.zeros_like(buf)

    d = g1.shape[-1]
    heads = d // (KEYS // GROUP)
    scale = (d // heads) ** (-0.5)
    masks = head_masks(KEYS, BF16)
    row_masks = head_masks(ROWS, F32)
    dqs, dks, dvs = [], [], []
    for w in range(2):
        q = qkv[w, :, :d]
        k = qkv[w, :, d : 2 * d]
        v = qkv[w, :, 2 * d :]
        do = do_in[w]
        dq, dk, dv = [], [], []
        for g in range(heads // GROUP):
            lanes = slice(g * KEYS, (g + 1) * KEYS)
            kg, vg = k[:, lanes], v[:, lanes]
            k_stack = jnp.concatenate([kg * m for m in masks], 0)
            v_stack = jnp.concatenate([vg * m for m in masks], 0)
            dog = do[:, lanes]
            qf = q[:, lanes].astype(F32)[:ROWS]
            dof = dog.astype(F32)
            q_stack = jnp.concatenate([qf * m for m in row_masks], 0).astype(BF16)
            do_stack = jnp.concatenate([dof * m for m in row_masks], 0).astype(BF16)
            wide = slice(g * GROUP * KEYS, (g + 1) * GROUP * KEYS)
            dp = dot_bt(dog, v_stack)
            p = p_in[w, :, wide].astype(F32)
            t = p * dp
            ds = []
            for h in range(GROUP):
                at = slice(h * KEYS, (h + 1) * KEYS)
                th = t[:, at]
                ds.append(th - p[:, at] * jnp.sum(th, -1, keepdims=True))
            for h in range(GROUP):
                at = (g * GROUP + h) * KEYS
                rel_acc[:, at : at + KEYS] += ds[h]
            dts = [x * scale for x in ds]
            dt = jnp.concatenate(dts, 1).astype(BF16)
            dt_stack = jnp.concatenate(dts, 0).astype(BF16)
            p_stack = jnp.concatenate(
                [p[:, h * KEYS : (h + 1) * KEYS] for h in range(GROUP)], 0
            ).astype(BF16)
            dq.append(dot(dt, k_stack))
            dk.append(dot_at(dt_stack, q_stack)[:ROWS])
            dv.append(dot_at(p_stack, do_stack)[:ROWS])
        dqs.append(jnp.concatenate(dq, 1))
        dks.append(jnp.concatenate(dk, 1))
        dvs.append(jnp.concatenate(dv, 1))
    joined = jnp.concatenate(
        [jnp.concatenate(dqs, 0), jnp.concatenate(dks, 0), jnp.concatenate(dvs, 0)], 1
    ).astype(BF16)
    normed, inv = normalize(xw[0].astype(F32))
    attn_in = (normed * g1[...] + b1[...]).astype(BF16)
    qkv_acc[...] += dot_at(attn_in, joined)
    col_sum[...] += fold(joined.astype(F32))
    da = dot_bt(joined, qkv_w[...])
    small_sum[0] += fold(da * normed)
    small_sum[1] += fold(da)
    dxw[...] = dy_in[0] + norm_back(da * g1[...], normed, inv)
    scatter_windows(raster, dxw, frame_out)

    @pl.when(page == pl.num_programs(0) - 1)
    def _():
        for j in range(3):
            sums_out[j * d : (j + 1) * d, :] = qkv_acc[:, j * d : (j + 1) * d].astype(BF16)
        stack = jnp.concatenate([rel_acc[:, h * KEYS : (h + 1) * KEYS] for h in range(heads)], 0)
        high, rest = split_rows(stack)
        u = dot(high, hot[...]) + dot(rest, hot[...])
        row = lax.broadcasted_iota(jnp.int32, (ROWS, RELS), 0)
        place = row
        for k in range(1, WIN):
            place = place + jnp.where(row >= k * WIN, WIN - 1, 0)
        place = jnp.concatenate([place] * heads, 0)
        for bit in range(8):
            moved = pltpu.roll(u, 1 << bit, 1)
            u = jnp.where((place & (1 << bit)) != 0, moved, u)
        rel = jnp.concatenate(
            [jnp.sum(u[h * ROWS : (h + 1) * ROWS], 0, keepdims=True) for h in range(heads)], 0
        )
        rows = [jnp.sum(small_sum[k], 0, keepdims=True) for k in range(2)]
        rows.append(jnp.sum(col_sum[:, :d], 0, keepdims=True))
        rows.append(jnp.sum(col_sum[:, 2 * d :], 0, keepdims=True))
        rows.append(jnp.zeros((4, d), F32))
        rows.append(rel[:, :d])
        rows.append(jnp.concatenate([rel[:, d:], jnp.zeros((heads, 2 * d - RELS), F32)], 1))
        rows.append(jnp.zeros((8, d), F32))
        high, rest = split_rows(jnp.concatenate(rows, 0))
        at = 3 * d
        sums_out[at : at + 32, :] = high
        sums_out[at + 32 : at + 64, :] = rest
        if sums_out.shape[0] > at + 64:
            sums_out[at + 64 :, :] = jnp.zeros((sums_out.shape[0] - at - 64, d), BF16)


def finish_forward_kernel(total, sums, fc1, fc2, proj, smalls, scale_out):
    d = proj.shape[0]
    ff = fc1.shape[1] // d
    at = (2 * ff + 1) * d
    rows = sums[at : at + 16, :].astype(F32) + sums[at + 16 : at + 32, :].astype(F32)
    scale = total / rows[ff + 4 : ff + 5, :]
    smalls[...] = rows * scale
    scale_out[...] = scale
    for j in range(ff):
        fc1[:, j * d : (j + 1) * d] = sums[j * d : (j + 1) * d, :].astype(F32) * scale
        fc2[j * d : (j + 1) * d, :] = sums[(ff + j) * d : (ff + j + 1) * d, :].astype(F32) * scale
    proj[...] = sums[2 * ff * d : (2 * ff + 1) * d, :].astype(F32) * scale


def finish_backward_kernel(sums, scale_in, qkv, smalls):
    d = scale_in.shape[1]
    scale = scale_in[...]
    for j in range(3):
        qkv[:, j * d : (j + 1) * d] = sums[j * d : (j + 1) * d, :].astype(F32) * scale
    at = 3 * d
    rows = sums[at : at + 32, :].astype(F32) + sums[at + 32 : at + 64, :].astype(F32)
    smalls[...] = rows * scale


def permute(block, target):
    rows, cols = lax.axis_size("rows"), lax.axis_size("cols")
    route = []
    for r in range(rows):
        for c in range(cols):
            tr, tc = target(r, c)
            route.append((r * cols + c, (tr % rows) * cols + tc % cols))
    return lax.ppermute(block, ("rows", "cols"), route)


def flip_by(parts, index):
    stack = jnp.stack(parts, 0)
    n = len(parts)
    bit = 1
    while bit < n:
        view = stack.reshape((n // (2 * bit), 2, bit) + stack.shape[1:])
        view = jnp.where((index & bit) != 0, view[:, ::-1], view)
        stack = view.reshape(stack.shape)
        bit *= 2
    return stack


def tree_sum(parts):
    parts = [p.astype(F32) for p in parts]
    while len(parts) > 1:
        parts = [parts[i] + parts[i + 1] for i in range(0, len(parts), 2)]
    return parts[0].astype(BF16)


def sum_over_devices(x):
    rows, cols = lax.axis_size("rows"), lax.axis_size("cols")
    r, c = lax.axis_index("rows"), lax.axis_index("cols")
    planes = 2 * cols
    depth = rows // 4
    n, d = x.shape
    core = r & 1
    spot = ((r >> 1) & 1) * cols + c
    halves = x.reshape(2, n // 2, d)
    mine = lax.dynamic_index_in_dim(halves, core, 0, False)
    other = permute(
        lax.dynamic_index_in_dim(halves, 1 - core, 0, False), lambda r, c: (r ^ 1, c)
    )
    half = tree_sum([mine, other]).reshape(planes, n // (2 * planes), d)

    def plane_hop(k):
        return lambda r, c: (r ^ (2 * (k // cols)), c ^ (k % cols))

    got = [lax.dynamic_index_in_dim(half, spot, 0, False)]
    for k in range(1, planes):
        got.append(permute(lax.dynamic_index_in_dim(half, spot ^ k, 0, False), plane_hop(k)))
    piece = tree_sum(got)
    got = [piece]
    for k in range(1, depth):
        got.append(permute(piece, lambda r, c, k=k: (r ^ (4 * k), c)))
    piece = tree_sum(got)
    got = [piece]
    for k in range(1, planes):
        got.append(permute(piece, plane_hop(k)))
    half = flip_by(got, spot).reshape(n // 2, d)
    other = permute(half, lambda r, c: (r ^ 1, c))
    return flip_by([half, other], core).reshape(n, d)


def strips(field):
    low = permute(field[:, :SHIFT], lambda r, c: (r - 1, c))
    right = permute(field[:, SHIFT:, :SHIFT], lambda r, c: (r, c - 1))
    corner = permute(field[:, :SHIFT, :SHIFT], lambda r, c: (r - 1, c - 1))
    return low, right, corner


def leave(field, scale=None):
    upper = permute(field[:, SHIFT:, :-SHIFT].astype(BF16), lambda r, c: (r + 1, c))
    left = permute(field[:, :SHIFT, -SHIFT:].astype(BF16), lambda r, c: (r, c + 1))
    corner = permute(field[:, SHIFT:, -SHIFT:].astype(BF16), lambda r, c: (r + 1, c + 1))
    dtype = field.dtype
    top = jnp.concatenate([corner.astype(dtype), upper.astype(dtype)], 2)
    low = jnp.concatenate([left.astype(dtype), field[:, :SHIFT, :-SHIFT]], 2)
    whole = jnp.concatenate([top, low], 1)
    return whole if scale is None else whole * scale


def region_labels(height, width):
    rows_all = height * lax.axis_size("rows")
    cols_all = width * lax.axis_size("cols")
    row = lax.axis_index("rows") * height + jnp.arange(height, dtype=jnp.int32)
    col = lax.axis_index("cols") * width + jnp.arange(width, dtype=jnp.int32)
    row_region = (row >= rows_all - WIN).astype(jnp.int32) + (row >= rows_all - SHIFT).astype(
        jnp.int32
    )
    col_region = (col >= cols_all - WIN).astype(jnp.int32) + (col >= cols_all - SHIFT).astype(
        jnp.int32
    )
    return row_region[:, None] * 3 + col_region[None, :]


def attention_bias(rel_table, height, width):
    heads = rel_table.shape[0]
    offsets = jnp.arange(WIN)[:, None] - jnp.arange(WIN)[None, :] + WIN - 1
    hots = (offsets[:, :, None] == jnp.arange(SPAN)[None, None, :]).astype(F32)
    grid = rel_table.reshape(heads, SPAN, SPAN)
    rel = jnp.einsum("hab,ija,klb->ikhjl", grid, hots, hots, precision=HIGH).reshape(
        TOK, heads, TOK
    )
    labels = region_labels(height, width).reshape(WIN, width // WIN, WIN)
    labels = labels.transpose(1, 0, 2).reshape(width // WIN, TOK)
    mask = jnp.where(labels[:, :, None] == labels[:, None, :], 0.0, -100.0).astype(F32)
    full = rel[None] + mask[:, :, None, :]
    full = jnp.pad(
        full, ((0, 0), (0, ROWS - TOK), (0, 0), (0, KEYS - TOK)), constant_values=NEVER
    )
    return full.reshape(width // WIN, ROWS, heads * KEYS)


def whole(a):
    return pl.BlockSpec(a.shape, lambda i: (0,) * len(a.shape), pipeline_mode=pl.Buffered(1))


def paged(shape, count=1):
    return pl.BlockSpec((count,) + shape[1:], lambda i: (i,) + (0,) * (len(shape) - 1))


def held(shape):
    return pl.BlockSpec(shape, lambda i: (0,) * len(shape))


def shards(
    patches, target, kept_mask, ln1_gain, ln1_bias, qkv_weight, query_bias, value_bias, rel_table,
    proj_weight, proj_bias, ln2_gain, ln2_bias, fc1_weight, fc1_bias, fc2_weight, fc2_bias,
):
    pages, height, width, d = patches.shape
    heads = rel_table.shape[0]
    ff = fc1_weight.shape[1]
    rows, cols = lax.axis_size("rows"), lax.axis_size("cols")
    step = 64 * cols
    params = pltpu.CompilerParams(
        dimension_semantics=("arbitrary",), vmem_limit_bytes=VMEM_LIMIT
    )

    p_strips = strips(patches)
    masked = target * kept_mask.astype(BF16)[..., None]
    t_strips = strips(masked)
    count = jnp.sum(kept_mask.astype(F32)).reshape(1)
    bias = attention_bias(rel_table, height, width)
    vec = lambda a: a.reshape(1, -1)

    paged_in = [patches, *p_strips, masked, *t_strips]
    weights = [qkv_weight, proj_weight, fc1_weight, fc2_weight, bias]
    vectors = [
        vec(a)
        for a in (
            ln1_gain, ln1_bias, query_bias, value_bias, proj_bias, ln2_gain, ln2_bias, fc1_bias,
            fc2_bias,
        )
    ]
    n1 = -(-(2 * ff + d + 32) // step) * step
    n2 = -(-(3 * d + 64) // step) * step
    outs = [
        jax.ShapeDtypeStruct((pages, height, width, d), BF16),
        jax.ShapeDtypeStruct((pages, 2 * ROWS, d), BF16),
        jax.ShapeDtypeStruct((2 * pages, KEYS, 3 * d), BF16),
        jax.ShapeDtypeStruct((2 * pages, ROWS, heads * KEYS), BF16),
        jax.ShapeDtypeStruct((pages, 2 * ROWS, d), F32),
        jax.ShapeDtypeStruct((2 * pages, ROWS, d), BF16),
        jax.ShapeDtypeStruct((n1, d), BF16),
    ]
    frame, xw, qkv, probs, dy, do, sums1 = pl.pallas_call(
        forward_kernel,
        grid=(pages,),
        in_specs=[paged(a.shape) for a in paged_in]
        + [pl.BlockSpec(memory_space=pltpu.SMEM)]
        + [whole(a) for a in weights + vectors],
        out_specs=[
            paged(outs[0].shape), paged(outs[1].shape), paged(outs[2].shape, 2),
            paged(outs[3].shape, 2), paged(outs[4].shape), paged(outs[5].shape, 2),
            held(outs[6].shape),
        ],
        out_shape=outs,
        scratch_shapes=[
            pltpu.VMEM((WIN, 32, d), F32),
            pltpu.VMEM((2 * ROWS, d), F32),
            pltpu.VMEM((2 * ROWS, d), F32),
            pltpu.VMEM((2 * ROWS, d), F32),
            pltpu.VMEM((d, ff), F32),
            pltpu.VMEM((d, ff), F32),
            pltpu.VMEM((d, d), F32),
            pltpu.VMEM((8, ff), F32),
            pltpu.VMEM((4, 8, d), F32),
        ],
        compiler_params=params,
        name="forward_and_mlp_backward",
    )(*paged_in, count, *weights, *vectors)

    total1 = sum_over_devices(sums1)
    output = leave(frame)

    place = jnp.arange(KEYS)
    spot = (SPAN * (WIN - 1) + WIN - 1) - (place // WIN * SPAN + place % WIN)
    hot = ((spot[:, None] == jnp.arange(RELS)[None, :]) & (place < TOK)[:, None]).astype(BF16)
    outs = [
        jax.ShapeDtypeStruct((pages, height, width, d), F32),
        jax.ShapeDtypeStruct((n2, d), BF16),
    ]
    grad_frame, sums2 = pl.pallas_call(
        backward_kernel,
        grid=(pages,),
        in_specs=[
            paged(xw.shape), paged(qkv.shape, 2), paged(probs.shape, 2), paged(dy.shape),
            paged(do.shape, 2),
        ]
        + [whole(a) for a in (qkv_weight, vectors[0], vectors[1], hot)],
        out_specs=[paged(outs[0].shape), held(outs[1].shape)],
        out_shape=outs,
        scratch_shapes=[
            pltpu.VMEM((WIN, 32, d), F32),
            pltpu.VMEM((2 * ROWS, d), F32),
            pltpu.VMEM((d, 3 * d), F32),
            pltpu.VMEM((ROWS, heads * KEYS), F32),
            pltpu.VMEM((8, 3 * d), F32),
            pltpu.VMEM((2, 8, d), F32),
        ],
        compiler_params=params,
        name="attention_backward",
    )(xw, qkv, probs, dy, do, qkv_weight, vectors[0], vectors[1], hot)

    total2 = sum_over_devices(sums2)
    total = float(pages * height * rows * width * cols)
    outs = [
        jax.ShapeDtypeStruct(s, F32) for s in ((d, ff), (ff, d), (d, d), (16, d), (1, d))
    ]
    fc1_grad, fc2_grad, proj_grad, smalls1, scale = pl.pallas_call(
        lambda *refs: finish_forward_kernel(total, *refs),
        out_shape=outs,
        compiler_params=pltpu.CompilerParams(vmem_limit_bytes=VMEM_LIMIT),
        name="finish_mlp_sums",
    )(total1)
    outs = [jax.ShapeDtypeStruct(s, F32) for s in ((d, 3 * d), (32, d))]
    qkv_grad, smalls2 = pl.pallas_call(
        finish_backward_kernel,
        out_shape=outs,
        compiler_params=pltpu.CompilerParams(vmem_limit_bytes=VMEM_LIMIT),
        name="finish_attention_sums",
    )(total2, scale)
    patches_grad = leave(grad_frame, scale[0, 0])
    k = ff // d
    rel = jnp.concatenate([smalls2[8 : 8 + heads], smalls2[16 : 16 + heads]], 1)
    rel_grad = rel[:, : SPAN * SPAN]
    return (
        output,
        patches_grad,
        smalls2[0],
        smalls2[1],
        qkv_grad,
        smalls2[2],
        smalls2[3],
        rel_grad,
        proj_grad,
        smalls1[k + 3],
        smalls1[k],
        smalls1[k + 1],
        fc1_grad,
        smalls1[:k].reshape(ff),
        fc2_grad,
        smalls1[k + 2],
    )


def solution(mesh):
    field = P(None, "rows", "cols", None)
    return jax.shard_map(
        shards,
        mesh=mesh,
        in_specs=(field, field, P(None, "rows", "cols")) + (P(),) * 14,
        out_specs=(field, field) + (P(),) * 14,
        check_vma=False,
    )
```

time: 487 us -> 184 us (0.38); the launches traced: 478 us -> 183 us
  matrix products: 156 us -> 3.32 us
  local copies, waits for them, and re-layouts: 107 us -> 24 us
  blocking collectives: 78.6 us -> 0 us
  Pallas kernels: 0 us -> 63 us
  starting transfers between devices: 13.8 us -> 48 us
  other arithmetic: 44.6 us -> 11 us
  waiting for transfers between devices: 62.6 us -> 32.2 us
  between operations: 15.9 us -> 1.12 us
    dot_general x25 -> x2, matrix products: 131 us -> 3.32 us  [attention_bias(): jnp.einsum('hab,ija,klb->ikhjl', grid, hots, hots, precision=HIGH)]
    psum x2 -> x0, blocking collectives: 78.6 us -> none  [the longest x1 41.6 us: shards(): lax.psum((ln1_gain_grad, ln1_bias_grad, qkv_weight_grad, query_bias_grad,...]
    pallas_call x0 -> x4, Pallas kernels: none -> 63 us  [the longest x1 34.8 us: shards(): pl.pallas_call(forward_kernel, grid=(pages,), in_specs=[paged(a.shape) fo...]
    psum x1 -> x0, waiting for transfers between devices: 53.7 us -> none  [shards(): lax.psum((ln1_gain_grad, ln1_bias_grad, qkv_weight_grad, query_bias_grad,...]
    ppermute x10 -> x34, starting transfers between devices: 13.8 us -> 48 us  [permute(): return lax.ppermute(block, ('rows', 'cols'), route)]
    reshape x8 -> x2, local copies, waits for them, and re-layouts: 26.7 us -> 1.14 us  [the longest x1 1.05 us: attention_bias(): return full.reshape(width // WIN, ROWS, heads * KEYS)]
    sub x3 -> x0, matrix products: 25 us -> none  [the longest x2 16.1 us: forward_pass(): expo = jnp.exp(scores - top_score)]
    convert_element_type x13 -> x1, local copies, waits for them, and re-layouts: 23.5 us -> 0.01 us  [shards(): masked = target * kept_mask.astype(BF16)[..., None]]
  transfers between devices with their start and end apart: 11 -> 34, of which waited for: 3 -> 13; matrix products, arithmetic and copies ran while one was open for 24% -> 12% of each run, Pallas kernels for 0% -> 0%
where the time goes in v1:
time: 184 us; the launch traced here: 183 us
  Pallas kernels  63 us (34%)
  starting transfers between devices  48 us (26%)
  waiting for transfers between devices  32.2 us (18%)
  local copies, waits for them, and re-layouts  24 us (13%)
  other arithmetic  11 us (6%)
  matrix products  3.32 us (2%)
    ppermute x34, starting transfers between devices, permute(): return lax.ppermute(block, ('rows', 'cols'), route)  48 us
    pallas_call x1, Pallas kernels, shards(): pl.pallas_call(forward_kernel, grid=(pages,), in_specs=[paged(a.shape) fo...  34.8 us
    ppermute x34, waiting for transfers between devices, permute(): return lax.ppermute(block, ('rows', 'cols'), route)  32.2 us
    pallas_call x1, Pallas kernels, shards(): pl.pallas_call(backward_kernel, grid=(pages,), in_specs=[paged(xw.shape),...  23.5 us
    unnamed x27, local copies, waits for them, and re-layouts  5.62 us
    add x1, local copies, waits for them, and re-layouts, attention_bias(): full = rel[None] + mask[:, :, None, :]  4.57 us
  transfers between devices with their start and end apart: 34, of which 13 were waited for; matrix products, arithmetic and copies ran while one was open for 12% of the time, Pallas kernels for 0%

profile of v1, /device:TPU:0, one launch (start us, length us, event | category | flops | bytes accessed | tf_op | source)
XLA Modules:
  0.0 182.6 jit_solution(2440754729439470786)
XLA Ops:
  0.7 0.9 convert_element_type.136
  1.5 1.5 copy_multiply_fusion.t_own
  3.0 0.8 fusion.25
  3.8 2.9 %collective-permute-start.4 = (bf16[8,5,5,256]{3,2,1,0:T(8,128)(2,1)}, bf16[8,5,5,256]{3,2,1,0:T(8,128)(2,1)}, u32[]{:S(2)}, u32[]{:S(2)}) collective-permute-start(bf16[8,5,5,256]{3,2,1,0:T(8,128)(2,1)} %get-tuple-element.87), channel_id=1, source_target_pairs={{0,1},{1,0},{2,3},{3,2},{4,5},{5,4},{6,7},{7,6},{8,9},{9,8},{10,11... | collective-permute-start | bytes 307208 | tf_op jit(solution)/shard_map/ppermute | solution.py:337
  6.8 3.7 %collective-permute-start.5 = (bf16[8,5,5,256]{3,2,1,0:T(8,128)(2,1)}, bf16[8,5,5,256]{3,2,1,0:T(8,128)(2,1)}, u32[]{:S(2)}, u32[]{:S(2)}) collective-permute-start(bf16[8,5,5,256]{3,2,1,0:T(8,128)(2,1)} %get-tuple-element.86), channel_id=1, source_target_pairs={{0,31},{1,30},{2,1},{3,0},{4,3},{5,2},{6,5},{7,4},{8,7},{9,6},{10,... | collective-permute-start | bytes 307208 | tf_op jit(solution)/shard_map/ppermute | solution.py:337
  10.7 0.8 fusion.26
  11.5 1.5 collective-permute-start.1
  13.0 0.9 collective-permute-start.3
  15.0 2.9 %convolution_bitcast_fusion = f32[10,10,8,10,10]{4,3,1,2,0:T(8,128)S(1)} fusion(f32[10,10,8,19,1]{3,1,4,2,0:T(8,128)S(1)} %convolution_bitcast_fusion.1, s32[10,10]{1,0:T(8,128)S(1)} %subtract_add_fusion), kind=kOutput, calls=%fused_computation | convolution fusion | flops 18241900 | bytes 381200 | tf_op jit(solution)/shard_map/hab,ija,klb->ikhjl/dot_general | solution.py:430
  17.9 3.5 %copy.46 = f32[10,10,8,10,10]{4,3,2,1,0:T(8,128)} copy(f32[10,10,8,10,10]{4,3,1,2,0:T(8,128)S(1)} %convolution_bitcast_fusion) | data formatting | bytes 640000 | tf_op jit(solution)/shard_map/hab,ija,klb->ikhjl/transpose | solution.py:430
  21.4 4.6 %add.181 = f32[100,8,100]{2,1,0:T(8,128)S(1)} reshape(f32[10,10,8,10,10]{4,3,2,1,0:T(8,128)} %copy.46) | data formatting | bytes 640000 | tf_op jit(solution)/shard_map/add | solution.py:436
  26.1 0.8 fusion.7.hot
  26.9 1.0 reshape.183.bias
  28.5 0.6 convert_reduce_fusion
  29.1 3.8 %collective-permute-done.2.corner = bf16[8,5,5,256]{3,2,1,0:T(8,128)(2,1)S(1)} collective-permute-done((bf16[8,5,5,256]{3,2,1,0:T(8,128)(2,1)S(1)}, bf16[8,5,5,256]{3,2,1,0:T(8,128)(2,1)S(1)}, u32[]{:S(2)}, u32[]{:S(2)}) %collective-permute-start.2) | collective-permute-done | bytes 102432 | tf_op jit(solution)/shard_map/ppermute | solution.py:337
  32.9 0.7 copy-done.7
  33.8 34.8 %forward_and_mlp_backward.1 = (bf16[8,10,20,256]{3,2,1,0:T(8,128)(2,1)}, bf16[8,208,256]{2,1,0:T(8,128)(2,1)}, bf16[16,128,768]{2,1,0:T(8,128)(2,1)}, bf16[16,10...) custom-call(bf16[8,10,20,256]{3,2,1,0:T(8,128)(2,1)} %copy-done.1, ...), custom_call_target="tpu_custom_call" | custom-call | tf_op jit(solution)/shard_map/forward_and_mlp_backward/pallas_call | solution.py:495
  68.5 23.5 %attention_backward.1 = (f32[8,10,20,256]{3,2,1,0:T(8,128)}, bf16[896,256]{1,0:T(8,128)(2,1)}) custom-call(bf16[8,208,256]{2,1,0:T(8,128)(2,1)} %get-tuple-element.33.xw, bf16[16,128,768]{2,1,0:T(8,128)(2,1)} %get-tuple-element.34.qkv, bf16[16,104,1024]{2,1,0:T(8,128)(2,1)} %get-tuple-element.35.p_in, f32[8,208,256]{2,1,0:T(8,128)} %get-tuple-element.36.dy_in, ...), custom_call_target="tpu_custom_call" | custom-call | tf_op jit(solution)/shard_map/attention_backward/pallas_call | solution.py:532
  92.1 1.0 dynamic-slice_bitcast_fusion.1
  93.0 2.1 %collective-permute-start.23 = (bf16[448,256]{1,0:T(8,128)(2,1)S(1)}, bf16[448,256]{1,0:T(8,128)(2,1)S(1)}, u32[]{:S(2)}, u32[]{:S(2)}) collective-permute-start(bf16[448,256]{1,0:T(8,128)(2,1)S(1)} %dynamic-slice_bitcast_fusion.1), channel_id=1, source_target_pairs={{0,2},{1,3},{2,0},{3,1},{4,6},{5,7},{6,4},{7,5},{8,10},{9,11},{10,... | collective-permute-start | bytes 688136 | tf_op jit(solution)/shard_map/ppermute | solution.py:337
  95.3 1.7 convert.10
  97.1 0.6 collective-permute-start.24
  98.1 2.6 %collective-permute-start.26 = (bf16[112,256]{1,0:T(8,128)(2,1)S(1)}, bf16[112,256]{1,0:T(8,128)(2,1)S(1)}, u32[]{:S(2)}, u32[]{:S(2)}) collective-permute-start(bf16[112,256]{1,0:T(8,128)(2,1)S(1)} %get-tuple-element.94), channel_id=1, source_target_pairs={{0,5},{1,4},{2,7},{3,6},{4,1},{5,0},{6,3},{7,2},{8,13},{9,12},{10,... | collective-permute-start | bytes 172040 | tf_op jit(solution)/shard_map/ppermute | solution.py:337
  100.8 0.6 collective-permute-start.11
  101.5 1.0 collective-permute-done.25
  102.5 1.1 collective-permute-done.26
  103.7 3.0 %collective-permute-start.28 = (bf16[112,256]{1,0:T(8,128)(2,1)S(1)}, bf16[112,256]{1,0:T(8,128)(2,1)S(1)}, u32[]{:S(2)}, u32[]{:S(2)}) collective-permute-start(bf16[112,256]{1,0:T(8,128)(2,1)S(1)} %fusion.9), channel_id=1, source_target_pairs={{0,16},{1,17},{2,18},{3,19},{4,20},{5,21},{6,22},{7,23},{8,24},{9,... | collective-permute-start | bytes 172040 | tf_op jit(solution)/shard_map/ppermute | solution.py:337
  106.7 1.4 collective-permute-start.29
  108.1 0.7 collective-permute-done.28
  108.8 3.8 %collective-permute-done.29 = bf16[112,256]{1,0:T(8,128)(2,1)S(1)} collective-permute-done((bf16[112,256]{1,0:T(8,128)(2,1)S(1)}, bf16[112,256]{1,0:T(8,128)(2,1)S(1)}, u32[]{:S(2)}, u32[]{:S(2)}) %collective-permute-start.29) | collective-permute-done | bytes 57376 | tf_op jit(solution)/shard_map/ppermute | solution.py:337
  112.7 1.8 %collective-permute-start.30 = (bf16[112,256]{1,0:T(8,128)(2,1)S(1)}, bf16[112,256]{1,0:T(8,128)(2,1)S(1)}, u32[]{:S(2)}, u32[]{:S(2)}) collective-permute-start(bf16[112,256]{1,0:T(8,128)(2,1)S(1)} %add_convert_fusion.1), channel_id=1, source_target_pairs={{0,1},{1,0},{2,3},{3,2},{4,5},{5,4},{6,7},{7,6},{8,9},{9,8},{10,11... | collective-permute-start | bytes 172040 | tf_op jit(solution)/shard_map/ppermute | solution.py:337
  114.5 1.7 collective-permute-start.32
  116.5 1.8 %collective-permute-start.13 = (bf16[304,256]{1,0:T(8,128)(2,1)S(1)}, bf16[304,256]{1,0:T(8,128)(2,1)S(1)}, u32[]{:S(2)}, u32[]{:S(2)}) collective-permute-start(bf16[304,256]{1,0:T(8,128)(2,1)S(1)} %get-tuple-element.90), channel_id=1, source_target_pairs={{0,1},{1,0},{2,3},{3,2},{4,5},{5,4},{6,7},{7,6},{8,9},{9,8},{10,11... | collective-permute-start | bytes 466952 | tf_op jit(solution)/shard_map/ppermute | solution.py:337
  118.3 1.7 collective-permute-start.15
  120.2 1.1 slice.97
  121.5 1.4 collective-permute-start.10
  122.9 2.4 %collective-permute-done.14 = bf16[304,256]{1,0:T(8,128)(2,1)S(1)} collective-permute-done((bf16[304,256]{1,0:T(8,128)(2,1)S(1)}, bf16[304,256]{1,0:T(8,128)(2,1)S(1)}, u32[]{:S(2)}, u32[]{:S(2)}) %collective-permute-start.14) | collective-permute-done | bytes 155680 | tf_op jit(solution)/shard_map/ppermute | solution.py:337
  125.4 2.8 %collective-permute-start.17 = (bf16[304,256]{1,0:T(8,128)(2,1)S(1)}, bf16[304,256]{1,0:T(8,128)(2,1)S(1)}, u32[]{:S(2)}, u32[]{:S(2)}) collective-permute-start(bf16[304,256]{1,0:T(8,128)(2,1)S(1)} %fusion.4), channel_id=1, source_target_pairs={{0,16},{1,17},{2,18},{3,19},{4,20},{5,21},{6,22},{7,23},{8,24},{9,... | collective-permute-start | bytes 466952 | tf_op jit(solution)/shard_map/ppermute | solution.py:337
  128.2 1.6 collective-permute-start.18
  129.8 1.3 collective-permute-done.16
  131.1 7.7 %collective-permute-done.17 = bf16[304,256]{1,0:T(8,128)(2,1)S(1)} collective-permute-done((bf16[304,256]{1,0:T(8,128)(2,1)S(1)}, bf16[304,256]{1,0:T(8,128)(2,1)S(1)}, u32[]{:S(2)}, u32[]{:S(2)}) %collective-permute-start.17) | collective-permute-done | bytes 155680 | tf_op jit(solution)/shard_map/ppermute | solution.py:337
  138.9 0.7 collective-permute-start.19
  139.6 5.7 %collective-permute-start.20 = (bf16[304,256]{1,0:T(8,128)(2,1)S(1)}, bf16[304,256]{1,0:T(8,128)(2,1)S(1)}, u32[]{:S(2)}, u32[]{:S(2)}) collective-permute-start(bf16[304,256]{1,0:T(8,128)(2,1)S(1)} %add_convert_fusion), channel_id=1, source_target_pairs={{0,4},{1,5},{2,6},{3,7},{4,0},{5,1},{6,2},{7,3},{8,12},{9,13},{10,... | collective-permute-start | bytes 466952 | tf_op jit(solution)/shard_map/ppermute | solution.py:337
  145.3 1.4 collective-permute-start.21
  146.9 4.2 %collective-permute-done.20 = bf16[304,256]{1,0:T(8,128)(2,1)S(1)} collective-permute-done((bf16[304,256]{1,0:T(8,128)(2,1)S(1)}, bf16[304,256]{1,0:T(8,128)(2,1)S(1)}, u32[]{:S(2)}, u32[]{:S(2)}) %collective-permute-start.20) | collective-permute-done | bytes 155680 | tf_op jit(solution)/shard_map/ppermute | solution.py:337
  151.3 2.1 %collective-permute-done.21 = bf16[304,256]{1,0:T(8,128)(2,1)S(1)} collective-permute-done((bf16[304,256]{1,0:T(8,128)(2,1)S(1)}, bf16[304,256]{1,0:T(8,128)(2,1)S(1)}, u32[]{:S(2)}, u32[]{:S(2)}) %collective-permute-start.21) | collective-permute-done | bytes 155680 | tf_op jit(solution)/shard_map/ppermute | solution.py:337
  153.4 4.0 %collective-permute-start.8 = (bf16[8,5,5,256]{3,2,1,0:T(8,128)(2,1)S(1)}, bf16[8,5,5,256]{3,2,1,0:T(8,128)(2,1)S(1)}, u32[]{:S(2)}, u32[]{:S(2)}) collective-permute-start(bf16[8,5,5,256]{3,2,1,0:T(8,128)(2,1)S(1)} %get-tuple-element.83), channel_id=1, source_target_pairs={{0,1},{1,0},{2,3},{3,2},{4,5},{5,4},{6,7},{7,6},{8,9},{9,8},{10,11... | collective-permute-start | bytes 307208 | tf_op jit(solution)/shard_map/ppermute | solution.py:337
  157.7 1.9 %collective-permute-done.6 = bf16[8,5,5,256]{3,2,1,0:T(8,128)(2,1)S(1)} collective-permute-done((bf16[8,5,5,256]{3,2,1,0:T(8,128)(2,1)S(1)}, bf16[8,5,5,256]{3,2,1,0:T(8,128)(2,1)S(1)}, u32[]{:S(2)}, u32[]{:S(2)}) %collective-permute-start.6) | collective-permute-done | bytes 102432 | tf_op jit(solution)/shard_map/ppermute | solution.py:337
  159.6 2.5 %collective-permute-start.33 = (bf16[448,256]{1,0:T(8,128)(2,1)S(1)}, bf16[448,256]{1,0:T(8,128)(2,1)S(1)}, u32[]{:S(2)}, u32[]{:S(2)}) collective-permute-start(bf16[448,256]{1,0:T(8,128)(2,1)S(1)} %bitcast.105), channel_id=1, source_target_pairs={{0,2},{1,3},{2,0},{3,1},{4,6},{5,7},{6,4},{7,5},{8,10},{9,11},{10,... | collective-permute-start | bytes 688136 | tf_op jit(solution)/shard_map/ppermute | solution.py:337
  162.0 2.1 %collective-permute-done.8 = bf16[8,5,5,256]{3,2,1,0:T(8,128)(2,1)S(1)} collective-permute-done((bf16[8,5,5,256]{3,2,1,0:T(8,128)(2,1)S(1)}, bf16[8,5,5,256]{3,2,1,0:T(8,128)(2,1)S(1)}, u32[]{:S(2)}, u32[]{:S(2)}) %collective-permute-start.8) | collective-permute-done | bytes 102432 | tf_op jit(solution)/shard_map/ppermute | solution.py:337
  164.6 1.2 copy.48
  166.0 0.9 reverse_select_fusion.3
  167.0 1.3 reverse_select_fusion
  168.3 2.8 %finish_mlp_sums.1 = (f32[256,1024]{1,0:T(8,128)}, f32[1024,256]{1,0:T(8,128)}, f32[256,256]{1,0:T(8,128)}, f32[16,256]{1,0:T(8,128)}, f32[1,256]{1,0:T(1,128)}) custom-call(bf16[2432,256]{1,0:T(8,128)(2,1)} %bitcast.96), custom_call_target="tpu_custom_call" | custom-call | tf_op jit(solution)/shard_map/finish_mlp_sums/pallas_call | solution.py:559
  171.1 2.0 %finish_attention_sums.1 = (f32[256,768]{1,0:T(8,128)}, f32[32,256]{1,0:T(8,128)}) custom-call(bf16[896,256]{1,0:T(8,128)(2,1)} %bitcast.102, f32[1,256]{1,0:T(1,128)} %get-tuple-element.40.scale_in), custom_call_target="tpu_custom_call" | custom-call | tf_op jit(solution)/shard_map/finish_attention_sums/pallas_call | solution.py:566
  173.0 0.7 fusion.27
  173.7 1.4 fusion.28
  175.2 1.2 slice.98
  176.3 0.7 slice_bitcast_fusion
  177.0 1.4 fusion.29
  178.5 0.9 maximum_multiply_fusion
  179.3 2.1 %copy.49 = f32[8,10,20,256]{3,0,2,1:T(8,128)} copy(f32[8,10,20,256]{3,2,1,0:T(8,128)S(1)} %maximum_multiply_fusion) | data formatting | bytes 3276800
  181.5 0.6 copy.53
  182.0 0.6 pad_maximum_fusion.4
  (98 shorter events, 5.3 us)
Async XLA Ops:
  0.6 9.8 %copy-start.4 = (bf16[8,10,20,256]{3,0,2,1:T(8,128)(2,1)S(1)}, bf16[8,10,20,256]{3,0,2,1:T(8,128)(2,1)}, u32[]{:S(2)}) copy-start(bf16[8,10,20,256]{3,0,2,1:T(8,128)(2,1)} %param.17) | copy-start | bytes 2457604
  3.0 10.0 %copy-start = (bf16[8,10,20,256]{3,2,1,0:T(8,128)(2,1)}, bf16[8,10,20,256]{3,2,1,0:T(8,128)(2,1)S(1)}, u32[]{:S(2)}) copy-start(bf16[8,10,20,256]{3,2,1,0:T(8,128)(2,1)S(1)} %copy_multiply_fusion.t_own) | copy-start | bytes 2457604
  3.8 24.1 %collective-permute-start.4 = (bf16[8,5,5,256]{3,2,1,0:T(8,128)(2,1)}, bf16[8,5,5,256]{3,2,1,0:T(8,128)(2,1)}, u32[]{:S(2)}, u32[]{:S(2)}) collective-permute-start(bf16[8,5,5,256]{3,2,1,0:T(8,128)(2,1)} %get-tuple-element.87), channel_id=1, source_target_pairs={{0,1},{1,0},{2,3},{3,2},{4,5},{5,4},{6,7},{7,6},{8,9},{9,8},{10,11... | collective-permute-start | bytes 307208 | tf_op jit(solution)/shard_map/ppermute | solution.py:337
  6.8 7.7 %copy-start.10 = (f32[8,361]{1,0:T(8,128)S(1)}, f32[8,361]{1,0:T(8,128)}, u32[]{:S(2)}) copy-start(f32[8,361]{1,0:T(8,128)} %param.25) | copy-start | bytes 34660
  6.8 22.4 %collective-permute-start.5 = (bf16[8,5,5,256]{3,2,1,0:T(8,128)(2,1)}, bf16[8,5,5,256]{3,2,1,0:T(8,128)(2,1)}, u32[]{:S(2)}, u32[]{:S(2)}) collective-permute-start(bf16[8,5,5,256]{3,2,1,0:T(8,128)(2,1)} %get-tuple-element.86), channel_id=1, source_target_pairs={{0,31},{1,30},{2,1},{3,0},{4,3},{5,2},{6,5},{7,4},{8,7},{9,6},{10,... | collective-permute-start | bytes 307208 | tf_op jit(solution)/shard_map/ppermute | solution.py:337
  10.7 7.2 %copy-start.1 = (bf16[8,10,20,256]{3,2,1,0:T(8,128)(2,1)}, bf16[8,10,20,256]{3,2,1,0:T(8,128)(2,1)S(1)}, u32[]{:S(2)}) copy-start(bf16[8,10,20,256]{3,2,1,0:T(8,128)(2,1)S(1)} %copy.47.own) | copy-start | bytes 2457604
  11.5 17.7 %collective-permute-start.1 = (bf16[8,5,5,256]{3,2,1,0:T(8,128)(2,1)}, bf16[8,5,5,256]{3,2,1,0:T(8,128)(2,1)}, u32[]{:S(2)}, u32[]{:S(2)}) collective-permute-start(bf16[8,5,5,256]{3,2,1,0:T(8,128)(2,1)} %get-tuple-element.89), channel_id=1, source_target_pairs={{0,1},{1,0},{2,3},{3,2},{4,5},{5,4},{6,7},{7,6},{8,9},{9,8},{10,11... | collective-permute-start | bytes 307208 | tf_op jit(solution)/shard_map/ppermute | solution.py:337
  13.0 19.9 %collective-permute-start.3 = (bf16[8,5,20,256]{3,2,1,0:T(8,128)(2,1)S(1)}, bf16[8,5,20,256]{3,2,1,0:T(8,128)(2,1)S(1)}, u32[]{:S(2)}, u32[]{:S(2)}) collective-permute-start(bf16[8,5,20,256]{3,2,1,0:T(8,128)(2,1)S(1)} %slice.114), channel_id=1, source_target_pairs={{0,30},{1,31},{2,0},{3,1},{4,2},{5,3},{6,4},{7,5},{8,6},{9,7},{10,... | collective-permute-start | bytes 1228808 | tf_op jit(solution)/shard_map/ppermute | solution.py:337
  13.9 19.0 %collective-permute-start = (bf16[8,5,20,256]{3,2,1,0:T(8,128)(2,1)S(1)}, bf16[8,5,20,256]{3,2,1,0:T(8,128)(2,1)}, u32[]{:S(2)}, u32[]{:S(2)}) collective-permute-start(bf16[8,5,20,256]{3,2,1,0:T(8,128)(2,1)S(1)} %slice.111), channel_id=1, source_target_pairs={{0,30},{1,31},{2,0},{3,1},{4,2},{5,3},{6,4},{7,5},{8,6},{9,7},{10,... | collective-permute-start | bytes 1228808 | tf_op jit(solution)/shard_map/ppermute | solution.py:337
  26.0 1.9 %copy-start.8 = (bf16[8,5,5,256]{3,2,1,0:T(8,128)(2,1)S(1)}, bf16[8,5,5,256]{3,2,1,0:T(8,128)(2,1)}, u32[]{:S(2)}) copy-start(bf16[8,5,5,256]{3,2,1,0:T(8,128)(2,1)} %get-tuple-element.88) | copy-start | bytes 307204
  26.1 2.5 %copy-start.9 = (s32[8,10,20]{2,0,1:T(8,128)S(1)}, s32[8,10,20]{2,0,1:T(8,128)}, u32[]{:S(2)}) copy-start(s32[8,10,20]{2,0,1:T(8,128)} %param.19) | copy-start | bytes 19204
  27.9 5.0 %collective-permute-start.2 = (bf16[8,5,5,256]{3,2,1,0:T(8,128)(2,1)S(1)}, bf16[8,5,5,256]{3,2,1,0:T(8,128)(2,1)S(1)}, u32[]{:S(2)}, u32[]{:S(2)}) collective-permute-start(bf16[8,5,5,256]{3,2,1,0:T(8,128)(2,1)S(1)} %copy-done.8), channel_id=1, source_target_pairs={{0,31},{1,30},{2,1},{3,0},{4,3},{5,2},{6,5},{7,4},{8,7},{9,6},{10,... | collective-permute-start | bytes 307208 | tf_op jit(solution)/shard_map/ppermute | solution.py:337
  32.9 0.7 copy-start.7
  32.9 0.8 copy-start.5
  68.5 26.6 %copy-start.2 = (bf16[2432,256]{1,0:T(8,128)(2,1)S(1)}, bf16[2432,256]{1,0:T(8,128)(2,1)}, u32[]{:S(2)}) copy-start(bf16[2432,256]{1,0:T(8,128)(2,1)} %get-tuple-element.39) | copy-start | bytes 3735556
  93.0 4.0 %collective-permute-start.23 = (bf16[448,256]{1,0:T(8,128)(2,1)S(1)}, bf16[448,256]{1,0:T(8,128)(2,1)S(1)}, u32[]{:S(2)}, u32[]{:S(2)}) collective-permute-start(bf16[448,256]{1,0:T(8,128)(2,1)S(1)} %dynamic-slice_bitcast_fusion.1), channel_id=1, source_target_pairs={{0,2},{1,3},{2,0},{3,1},{4,6},{5,7},{6,4},{7,5},{8,10},{9,11},{10,... | collective-permute-start | bytes 688136 | tf_op jit(solution)/shard_map/ppermute | solution.py:337
  95.1 1.9 %copy-start.6 = (bf16[896,256]{1,0:T(8,128)(2,1)S(1)}, bf16[896,256]{1,0:T(8,128)(2,1)}, u32[]{:S(2)}) copy-start(bf16[896,256]{1,0:T(8,128)(2,1)} %get-tuple-element.41) | copy-start | bytes 1376260
  95.2 21.1 %collective-permute-start.12 = (bf16[1216,256]{1,0:T(8,128)(2,1)S(1)}, bf16[1216,256]{1,0:T(8,128)(2,1)S(1)}, u32[]{:S(2)}, u32[]{:S(2)}) collective-permute-start(bf16[1216,256]{1,0:T(8,128)(2,1)S(1)} %dynamic-slice_bitcast_fusion), channel_id=1, source_target_pairs={{0,2},{1,3},{2,0},{3,1},{4,6},{5,7},{6,4},{7,5},{8,10},{9,11},{10,... | collective-permute-start | bytes 1867784 | tf_op jit(solution)/shard_map/ppermute | solution.py:337
  95.3 12.8 %copy-start.3 = (bf16[8,10,20,256]{3,2,1,0:T(8,128)(2,1)S(1)}, bf16[8,10,20,256]{3,2,1,0:T(8,128)(2,1)}, u32[]{:S(2)}) copy-start(bf16[8,10,20,256]{3,2,1,0:T(8,128)(2,1)} %get-tuple-element.32) | copy-start | bytes 2457604
  97.1 4.4 %collective-permute-start.24 = (bf16[112,256]{1,0:T(8,128)(2,1)S(1)}, bf16[112,256]{1,0:T(8,128)(2,1)S(1)}, u32[]{:S(2)}, u32[]{:S(2)}) collective-permute-start(bf16[112,256]{1,0:T(8,128)(2,1)S(1)} %get-tuple-element.93), channel_id=1, source_target_pairs={{0,1},{1,0},{2,3},{3,2},{4,5},{5,4},{6,7},{7,6},{8,9},{9,8},{10,11... | collective-permute-start | bytes 172040 | tf_op jit(solution)/shard_map/ppermute | solution.py:337
  97.7 4.8 %collective-permute-start.25 = (bf16[112,256]{1,0:T(8,128)(2,1)S(1)}, bf16[112,256]{1,0:T(8,128)(2,1)S(1)}, u32[]{:S(2)}, u32[]{:S(2)}) collective-permute-start(bf16[112,256]{1,0:T(8,128)(2,1)S(1)} %get-tuple-element.95), channel_id=1, source_target_pairs={{0,4},{1,5},{2,6},{3,7},{4,0},{5,1},{6,2},{7,3},{8,12},{9,13},{10,... | collective-permute-start | bytes 172040 | tf_op jit(solution)/shard_map/ppermute | solution.py:337
  98.1 5.5 %collective-permute-start.26 = (bf16[112,256]{1,0:T(8,128)(2,1)S(1)}, bf16[112,256]{1,0:T(8,128)(2,1)S(1)}, u32[]{:S(2)}, u32[]{:S(2)}) collective-permute-start(bf16[112,256]{1,0:T(8,128)(2,1)S(1)} %get-tuple-element.94), channel_id=1, source_target_pairs={{0,5},{1,4},{2,7},{3,6},{4,1},{5,0},{6,3},{7,2},{8,13},{9,12},{10,... | collective-permute-start | bytes 172040 | tf_op jit(solution)/shard_map/ppermute | solution.py:337
  100.8 17.5 %collective-permute-start.11 = (bf16[8,5,5,256]{3,2,1,0:T(8,128)(2,1)S(1)}, bf16[8,5,5,256]{3,2,1,0:T(8,128)(2,1)S(1)}, u32[]{:S(2)}, u32[]{:S(2)}) collective-permute-start(bf16[8,5,5,256]{3,2,1,0:T(8,128)(2,1)S(1)} %get-tuple-element.81), channel_id=1, source_target_pairs={{0,1},{1,0},{2,3},{3,2},{4,5},{5,4},{6,7},{7,6},{8,9},{9,8},{10,11... | collective-permute-start | bytes 307208 | tf_op jit(solution)/shard_map/ppermute | solution.py:337
  103.6 4.5 %collective-permute-start.27 = (bf16[112,256]{1,0:T(8,128)(2,1)S(1)}, bf16[112,256]{1,0:T(8,128)(2,1)S(1)}, u32[]{:S(2)}, u32[]{:S(2)}) collective-permute-start(bf16[112,256]{1,0:T(8,128)(2,1)S(1)} %fusion.9), channel_id=1, source_target_pairs={{0,8},{1,9},{2,10},{3,11},{4,12},{5,13},{6,14},{7,15},{8,0},{9,1},... | collective-permute-start | bytes 172040 | tf_op jit(solution)/shard_map/ppermute | solution.py:337
  103.7 5.1 %collective-permute-start.28 = (bf16[112,256]{1,0:T(8,128)(2,1)S(1)}, bf16[112,256]{1,0:T(8,128)(2,1)S(1)}, u32[]{:S(2)}, u32[]{:S(2)}) collective-permute-start(bf16[112,256]{1,0:T(8,128)(2,1)S(1)} %fusion.9), channel_id=1, source_target_pairs={{0,16},{1,17},{2,18},{3,19},{4,20},{5,21},{6,22},{7,23},{8,24},{9,... | collective-permute-start | bytes 172040 | tf_op jit(solution)/shard_map/ppermute | solution.py:337
  106.7 6.0 %collective-permute-start.29 = (bf16[112,256]{1,0:T(8,128)(2,1)S(1)}, bf16[112,256]{1,0:T(8,128)(2,1)S(1)}, u32[]{:S(2)}, u32[]{:S(2)}) collective-permute-start(bf16[112,256]{1,0:T(8,128)(2,1)S(1)} %fusion.9), channel_id=1, source_target_pairs={{0,24},{1,25},{2,26},{3,27},{4,28},{5,29},{6,30},{7,31},{8,16},{9,... | collective-permute-start | bytes 172040 | tf_op jit(solution)/shard_map/ppermute | solution.py:337
  112.7 5.6 %collective-permute-start.30 = (bf16[112,256]{1,0:T(8,128)(2,1)S(1)}, bf16[112,256]{1,0:T(8,128)(2,1)S(1)}, u32[]{:S(2)}, u32[]{:S(2)}) collective-permute-start(bf16[112,256]{1,0:T(8,128)(2,1)S(1)} %add_convert_fusion.1), channel_id=1, source_target_pairs={{0,1},{1,0},{2,3},{3,2},{4,5},{5,4},{6,7},{7,6},{8,9},{9,8},{10,11... | collective-permute-start | bytes 172040 | tf_op jit(solution)/shard_map/ppermute | solution.py:337
  114.5 6.8 %collective-permute-start.31 = (bf16[112,256]{1,0:T(8,128)(2,1)S(1)}, bf16[112,256]{1,0:T(8,128)(2,1)S(1)}, u32[]{:S(2)}, u32[]{:S(2)}) collective-permute-start(bf16[112,256]{1,0:T(8,128)(2,1)S(1)} %add_convert_fusion.1), channel_id=1, source_target_pairs={{0,4},{1,5},{2,6},{3,7},{4,0},{5,1},{6,2},{7,3},{8,12},{9,13},{10,... | collective-permute-start | bytes 172040 | tf_op jit(solution)/shard_map/ppermute | solution.py:337
  114.5 6.9 %collective-permute-start.32 = (bf16[112,256]{1,0:T(8,128)(2,1)S(1)}, bf16[112,256]{1,0:T(8,128)(2,1)S(1)}, u32[]{:S(2)}, u32[]{:S(2)}) collective-permute-start(bf16[112,256]{1,0:T(8,128)(2,1)S(1)} %add_convert_fusion.1), channel_id=1, source_target_pairs={{0,5},{1,4},{2,7},{3,6},{4,1},{5,0},{6,3},{7,2},{8,13},{9,12},{10,... | collective-permute-start | bytes 172040 | tf_op jit(solution)/shard_map/ppermute | solution.py:337
  116.5 6.4 %collective-permute-start.13 = (bf16[304,256]{1,0:T(8,128)(2,1)S(1)}, bf16[304,256]{1,0:T(8,128)(2,1)S(1)}, u32[]{:S(2)}, u32[]{:S(2)}) collective-permute-start(bf16[304,256]{1,0:T(8,128)(2,1)S(1)} %get-tuple-element.90), channel_id=1, source_target_pairs={{0,1},{1,0},{2,3},{3,2},{4,5},{5,4},{6,7},{7,6},{8,9},{9,8},{10,11... | collective-permute-start | bytes 466952 | tf_op jit(solution)/shard_map/ppermute | solution.py:337
  118.3 6.9 %collective-permute-start.14 = (bf16[304,256]{1,0:T(8,128)(2,1)S(1)}, bf16[304,256]{1,0:T(8,128)(2,1)S(1)}, u32[]{:S(2)}, u32[]{:S(2)}) collective-permute-start(bf16[304,256]{1,0:T(8,128)(2,1)S(1)} %get-tuple-element.92), channel_id=1, source_target_pairs={{0,4},{1,5},{2,6},{3,7},{4,0},{5,1},{6,2},{7,3},{8,12},{9,13},{10,... | collective-permute-start | bytes 466952 | tf_op jit(solution)/shard_map/ppermute | solution.py:337
  118.3 6.9 %collective-permute-start.15 = (bf16[304,256]{1,0:T(8,128)(2,1)S(1)}, bf16[304,256]{1,0:T(8,128)(2,1)S(1)}, u32[]{:S(2)}, u32[]{:S(2)}) collective-permute-start(bf16[304,256]{1,0:T(8,128)(2,1)S(1)} %get-tuple-element.91), channel_id=1, source_target_pairs={{0,5},{1,4},{2,7},{3,6},{4,1},{5,0},{6,3},{7,2},{8,13},{9,12},{10,... | collective-permute-start | bytes 466952 | tf_op jit(solution)/shard_map/ppermute | solution.py:337
  121.4 44.4 %collective-permute-start.9 = (bf16[8,5,5,256]{3,2,1,0:T(8,128)(2,1)S(1)}, bf16[8,5,5,256]{3,2,1,0:T(8,128)(2,1)S(1)}, u32[]{:S(2)}, u32[]{:S(2)}) collective-permute-start(bf16[8,5,5,256]{3,2,1,0:T(8,128)(2,1)S(1)} %get-tuple-element.80), channel_id=1, source_target_pairs={{0,3},{1,2},{2,5},{3,4},{4,7},{5,6},{6,9},{7,8},{8,11},{9,10},{10,... | collective-permute-start | bytes 307208 | tf_op jit(solution)/shard_map/ppermute | solution.py:337
  121.5 44.4 %collective-permute-start.10 = (bf16[8,5,15,256]{3,2,1,0:T(8,128)(2,1)S(1)}, bf16[8,5,15,256]{3,2,1,0:T(8,128)(2,1)S(1)}, u32[]{:S(2)}, u32[]{:S(2)}) collective-permute-start(bf16[8,5,15,256]{3,2,1,0:T(8,128)(2,1)S(1)} %slice.118), channel_id=1, source_target_pairs={{0,2},{1,3},{2,4},{3,5},{4,6},{5,7},{6,8},{7,9},{8,10},{9,11},{10,... | collective-permute-start | bytes 921608 | tf_op jit(solution)/shard_map/ppermute | solution.py:337
  125.3 5.8 %collective-permute-start.16 = (bf16[304,256]{1,0:T(8,128)(2,1)S(1)}, bf16[304,256]{1,0:T(8,128)(2,1)S(1)}, u32[]{:S(2)}, u32[]{:S(2)}) collective-permute-start(bf16[304,256]{1,0:T(8,128)(2,1)S(1)} %fusion.4), channel_id=1, source_target_pairs={{0,8},{1,9},{2,10},{3,11},{4,12},{5,13},{6,14},{7,15},{8,0},{9,1},... | collective-permute-start | bytes 466952 | tf_op jit(solution)/shard_map/ppermute | solution.py:337
  125.4 13.4 %collective-permute-start.17 = (bf16[304,256]{1,0:T(8,128)(2,1)S(1)}, bf16[304,256]{1,0:T(8,128)(2,1)S(1)}, u32[]{:S(2)}, u32[]{:S(2)}) collective-permute-start(bf16[304,256]{1,0:T(8,128)(2,1)S(1)} %fusion.4), channel_id=1, source_target_pairs={{0,16},{1,17},{2,18},{3,19},{4,20},{5,21},{6,22},{7,23},{8,24},{9,... | collective-permute-start | bytes 466952 | tf_op jit(solution)/shard_map/ppermute | solution.py:337
  128.2 10.7 %collective-permute-start.18 = (bf16[304,256]{1,0:T(8,128)(2,1)S(1)}, bf16[304,256]{1,0:T(8,128)(2,1)S(1)}, u32[]{:S(2)}, u32[]{:S(2)}) collective-permute-start(bf16[304,256]{1,0:T(8,128)(2,1)S(1)} %fusion.4), channel_id=1, source_target_pairs={{0,24},{1,25},{2,26},{3,27},{4,28},{5,29},{6,30},{7,31},{8,16},{9,... | collective-permute-start | bytes 466952 | tf_op jit(solution)/shard_map/ppermute | solution.py:337
  138.9 7.8 %collective-permute-start.19 = (bf16[304,256]{1,0:T(8,128)(2,1)S(1)}, bf16[304,256]{1,0:T(8,128)(2,1)S(1)}, u32[]{:S(2)}, u32[]{:S(2)}) collective-permute-start(bf16[304,256]{1,0:T(8,128)(2,1)S(1)} %add_convert_fusion), channel_id=1, source_target_pairs={{0,1},{1,0},{2,3},{3,2},{4,5},{5,4},{6,7},{7,6},{8,9},{9,8},{10,11... | collective-permute-start | bytes 466952 | tf_op jit(solution)/shard_map/ppermute | solution.py:337
  139.6 11.5 %collective-permute-start.20 = (bf16[304,256]{1,0:T(8,128)(2,1)S(1)}, bf16[304,256]{1,0:T(8,128)(2,1)S(1)}, u32[]{:S(2)}, u32[]{:S(2)}) collective-permute-start(bf16[304,256]{1,0:T(8,128)(2,1)S(1)} %add_convert_fusion), channel_id=1, source_target_pairs={{0,4},{1,5},{2,6},{3,7},{4,0},{5,1},{6,2},{7,3},{8,12},{9,13},{10,... | collective-permute-start | bytes 466952 | tf_op jit(solution)/shard_map/ppermute | solution.py:337
  145.3 8.0 %collective-permute-start.21 = (bf16[304,256]{1,0:T(8,128)(2,1)S(1)}, bf16[304,256]{1,0:T(8,128)(2,1)S(1)}, u32[]{:S(2)}, u32[]{:S(2)}) collective-permute-start(bf16[304,256]{1,0:T(8,128)(2,1)S(1)} %add_convert_fusion), channel_id=1, source_target_pairs={{0,5},{1,4},{2,7},{3,6},{4,1},{5,0},{6,3},{7,2},{8,13},{9,12},{10,... | collective-permute-start | bytes 466952 | tf_op jit(solution)/shard_map/ppermute | solution.py:337
  146.8 17.4 %collective-permute-start.7 = (bf16[8,5,15,256]{3,2,1,0:T(8,128)(2,1)S(1)}, bf16[8,5,15,256]{3,2,1,0:T(8,128)(2,1)S(1)}, u32[]{:S(2)}, u32[]{:S(2)}) collective-permute-start(bf16[8,5,15,256]{3,2,1,0:T(8,128)(2,1)S(1)} %get-tuple-element.84), channel_id=1, source_target_pairs={{0,2},{1,3},{2,4},{3,5},{4,6},{5,7},{6,8},{7,9},{8,10},{9,11},{10,... | collective-permute-start | bytes 921608 | tf_op jit(solution)/shard_map/ppermute | solution.py:337
  151.1 8.4 %collective-permute-start.6 = (bf16[8,5,5,256]{3,2,1,0:T(8,128)(2,1)S(1)}, bf16[8,5,5,256]{3,2,1,0:T(8,128)(2,1)S(1)}, u32[]{:S(2)}, u32[]{:S(2)}) collective-permute-start(bf16[8,5,5,256]{3,2,1,0:T(8,128)(2,1)S(1)} %get-tuple-element.82), channel_id=1, source_target_pairs={{0,3},{1,2},{2,5},{3,4},{4,7},{5,6},{6,9},{7,8},{8,11},{9,10},{10,... | collective-permute-start | bytes 307208 | tf_op jit(solution)/shard_map/ppermute | solution.py:337
  153.4 10.8 %collective-permute-start.8 = (bf16[8,5,5,256]{3,2,1,0:T(8,128)(2,1)S(1)}, bf16[8,5,5,256]{3,2,1,0:T(8,128)(2,1)S(1)}, u32[]{:S(2)}, u32[]{:S(2)}) collective-permute-start(bf16[8,5,5,256]{3,2,1,0:T(8,128)(2,1)S(1)} %get-tuple-element.83), channel_id=1, source_target_pairs={{0,1},{1,0},{2,3},{3,2},{4,5},{5,4},{6,7},{7,6},{8,9},{9,8},{10,11... | collective-permute-start | bytes 307208 | tf_op jit(solution)/shard_map/ppermute | solution.py:337
  159.6 6.4 %collective-permute-start.33 = (bf16[448,256]{1,0:T(8,128)(2,1)S(1)}, bf16[448,256]{1,0:T(8,128)(2,1)S(1)}, u32[]{:S(2)}, u32[]{:S(2)}) collective-permute-start(bf16[448,256]{1,0:T(8,128)(2,1)S(1)} %bitcast.105), channel_id=1, source_target_pairs={{0,2},{1,3},{2,0},{3,1},{4,6},{5,7},{6,4},{7,5},{8,10},{9,11},{10,... | collective-permute-start | bytes 688136 | tf_op jit(solution)/shard_map/ppermute | solution.py:337
  164.2 2.7 %collective-permute-start.22 = (bf16[1216,256]{1,0:T(8,128)(2,1)S(1)}, bf16[1216,256]{1,0:T(8,128)(2,1)S(1)}, u32[]{:S(2)}, u32[]{:S(2)}) collective-permute-start(bf16[1216,256]{1,0:T(8,128)(2,1)S(1)} %bitcast.97), channel_id=1, source_target_pairs={{0,2},{1,3},{2,0},{3,1},{4,6},{5,7},{6,4},{7,5},{8,10},{9,11},{10,... | collective-permute-start | bytes 1867784 | tf_op jit(solution)/shard_map/ppermute | solution.py:337

commit v2 on v1

v2 whole, which is shorter than its diff:
```python
import math

import jax
import jax.numpy as jnp
from jax import lax
from jax.experimental import pallas as pl
from jax.experimental.pallas import tpu as pltpu
from jax.sharding import PartitionSpec as P

WIN = 10
SHIFT = 5
EPS = 1e-05
F32 = jnp.float32
BF16 = jnp.bfloat16

SPAN = 2 * WIN - 1
TOK = WIN * WIN
ROWS = 104
KEYS = 128
GROUP = 4
RELS = 384
NEVER = -1e30
PAGES = 8
VMEM_LIMIT = 60 * 1024 * 1024


def dot(a, b):
    return lax.dot_general(a, b, (((1,), (0,)), ((), ())), preferred_element_type=F32)


def dot_bt(a, b):
    return lax.dot_general(a, b, (((1,), (1,)), ((), ())), preferred_element_type=F32)


def dot_at(a, b):
    return lax.dot_general(a, b, (((0,), (0,)), ((), ())), preferred_element_type=F32)


def normalize(x):
    center = x - jnp.sum(x, -1, keepdims=True) * (1.0 / x.shape[-1])
    inv = lax.rsqrt(jnp.sum(center * center, -1, keepdims=True) * (1.0 / x.shape[-1]) + EPS)
    return center * inv, inv


def norm_back(up, normed, inv):
    scale = 1.0 / up.shape[-1]
    mean_up = jnp.sum(up, -1, keepdims=True) * scale
    mean_un = jnp.sum(up * normed, -1, keepdims=True) * scale
    return inv * (up - mean_up - normed * mean_un)


def fold(x):
    return jnp.sum(x.reshape(x.shape[0] // 8, 8, x.shape[1]), 0)


def head_masks(rows, dtype):
    lane = lax.broadcasted_iota(jnp.int32, (rows, KEYS), 1)
    width = KEYS // GROUP
    return [
        ((lane >= k * width) & (lane < (k + 1) * width)).astype(F32).astype(dtype)
        for k in range(GROUP)
    ]


def split_rows(x):
    high = x.astype(BF16)
    return high, (x - high.astype(F32)).astype(BF16)


def page_rows(page, count):
    return pl.ds(page, count, stride=PAGES)


def load_rows(ref, w, rows):
    return jnp.concatenate([ref[t, w, rows, :] for t in range(ref.shape[0])], 1)


def store_rows(ref, w, rows, value):
    for t in range(ref.shape[0]):
        ref[t, w, rows, :] = value[:, t * KEYS : (t + 1) * KEYS]


def only_tokens(x):
    return jnp.where(lax.broadcasted_iota(jnp.int32, x.shape, 0) < TOK, x, 0.0)


def gather_frame(out, own, low, right, corner):
    for w in range(2):
        for r in range(WIN):
            if r < WIN - SHIFT:
                main, side, mr, sr = own, right, r + SHIFT, r
            else:
                main, side, mr, sr = low, corner, r - SHIFT, r - SHIFT
            if w == 0:
                block = main[mr, SHIFT : SHIFT + WIN].astype(F32)
            else:
                block = jnp.concatenate(
                    [main[mr, SHIFT + WIN :].astype(F32), side[sr].astype(F32)], 0
                )
            at = r * WIN * PAGES
            store_rows(
                out, w, slice(at, at + WIN * PAGES), block.reshape(WIN * PAGES, block.shape[-1])
            )


def tenth(n):
    return (n * 205) >> 11


def squeeze_matrix():
    at = lax.broadcasted_iota(jnp.int32, (RELS, 2 * KEYS), 0)
    to = lax.broadcasted_iota(jnp.int32, (RELS, 2 * KEYS), 1)
    hit = (at == to + (SPAN - WIN) * tenth(to)) & (to < SPAN * WIN)
    return hit.astype(F32).astype(BF16)


def bias_kernel(edge, table, out):
    heads = table.shape[0]
    reversed_table = table[...]
    moved = []
    for c in range(WIN):
        shift = WIN - 1 - c
        moved.append(pltpu.roll(reversed_table, RELS - shift, 1) if shift else reversed_table)
    stack = jnp.concatenate(moved, 0)
    high = stack.astype(BF16)
    rest = stack - high.astype(F32)
    middle = rest.astype(BF16)
    least = (rest - middle.astype(F32)).astype(BF16)
    squeeze = squeeze_matrix()
    wide = dot(high, squeeze) + dot(middle, squeeze) + dot(least, squeeze)
    count = WIN * heads
    for r in range(WIN):
        shift = (WIN - 1 - r) * WIN
        rel = pltpu.roll(wide, 2 * KEYS - shift, 1) if shift else wide
        rel = rel[:, :KEYS]
        key = lax.broadcasted_iota(jnp.int32, (count, KEYS), 1)
        row = lax.broadcasted_iota(jnp.int32, (count, KEYS), 0)
        across = (key < TOK // 2) if r >= SHIFT else (key >= TOK // 2)
        key_left = key - WIN * tenth(key) < SHIFT
        own_left = row < SHIFT * heads
        beside = key_left != own_left
        for w in range(2):
            cut_off = across & (edge[0] != 0)
            if w == 1:
                cut_off = cut_off | (beside & (edge[1] != 0))
            value = rel + jnp.where(cut_off, -100.0, 0.0)
            out[w, r * count : (r + 1) * count, :] = jnp.where(key < TOK, value, NEVER)
    for w in range(2):
        out[w, TOK * heads :, :] = jnp.zeros((out.shape[1] - TOK * heads, KEYS), F32)


def attention_kernel(
    own, low, right, corner, qkv_w, bias, g1, b1, qb, vb,
    x_out, xw_out, qkv_out, p_out, o_out,
    xf,
):
    page = pl.program_id(0)

    @pl.when(page == 0)
    def _():
        gather_frame(xf, own, low, right, corner)
        for t in range(xf.shape[0]):
            for w in range(2):
                xf[t, w, TOK * PAGES :, :] = jnp.zeros((xf.shape[2] - TOK * PAGES, KEYS), F32)
                x_out[w * TOK * PAGES : (w + 1) * TOK * PAGES, t * KEYS : (t + 1) * KEYS] = xf[
                    t, w, : TOK * PAGES, :
                ].astype(BF16)

    d = g1.shape[-1]
    heads = d // (KEYS // GROUP)
    scale = (d // heads) ** (-0.5)
    x = jnp.concatenate([only_tokens(load_rows(xf, w, page_rows(page, ROWS))) for w in range(2)], 0)
    for w in range(2):
        xw_out[w, 0] = x[w * ROWS : (w + 1) * ROWS].astype(BF16)
    normed, _ = normalize(x)
    attn_in = (normed * g1[...] + b1[...]).astype(BF16)
    proj = dot(attn_in, qkv_w[...])
    q_all = proj[:, :d] + qb[...]
    k_all = proj[:, d : 2 * d]
    v_all = proj[:, 2 * d :] + vb[...]
    masks = head_masks(KEYS, BF16)
    filler = jnp.zeros((KEYS - ROWS, d), F32)
    for w in range(2):
        rows = slice(w * ROWS, (w + 1) * ROWS)
        q = jnp.concatenate([q_all[rows], filler], 0).astype(BF16)
        k = jnp.concatenate([k_all[rows], filler], 0).astype(BF16)
        v = jnp.concatenate([v_all[rows], filler], 0).astype(BF16)
        qkv_out[w, 0, :, :d] = q
        qkv_out[w, 0, :, d : 2 * d] = k
        qkv_out[w, 0, :, 2 * d :] = v
        parts = []
        for g in range(heads // GROUP):
            lanes = slice(g * KEYS, (g + 1) * KEYS)
            kg, vg = k[:, lanes], v[:, lanes]
            k_stack = jnp.concatenate([kg * m for m in masks], 0)
            v_stack = jnp.concatenate([vg * m for m in masks], 0)
            wide = slice(g * GROUP * KEYS, (g + 1) * GROUP * KEYS)
            s = dot_bt(q[:ROWS, lanes], k_stack)
            probs = []
            for h in range(GROUP):
                rel = bias[w, pl.ds(g * GROUP + h, ROWS, stride=heads), :]
                sh = s[:, h * KEYS : (h + 1) * KEYS] * scale + rel
                e = jnp.exp(sh - jnp.max(sh, -1, keepdims=True))
                probs.append(e * (1.0 / jnp.sum(e, -1, keepdims=True)))
            p = jnp.concatenate(probs, 1).astype(BF16)
            p_out[w, 0, :, wide] = p
            parts.append(dot(p, v_stack))
        store_rows(o_out, w, page_rows(page, TOK), jnp.concatenate(parts, 1)[:TOK])


def mlp_kernel(
    x_in, o_in, t_own, t_low, t_right, t_corner, count,
    proj_w, fc1_w, fc2_w, pb, g2, b2, f1b, f2b,
    frame_out, dy_out, do_out, sums_out,
    tf, fc1_acc, fc2_acc, proj_acc, fc1_sum, small_sum,
):
    step = pl.program_id(0)

    @pl.when(step == 0)
    def _():
        for buf in (fc1_acc, fc2_acc, proj_acc, fc1_sum, small_sum):
            buf[...] = jnp.zeros_like(buf)
        gather_frame(tf, t_own, t_low, t_right, t_corner)

    size, d = x_in.shape
    ff = fc1_w.shape[1] // d
    o = load_rows(o_in, 0, slice(None)).astype(BF16)
    y = x_in[...].astype(F32) + dot(o, proj_w[...]) + pb[...]
    normed2, inv2 = normalize(y)
    c = (normed2 * g2[...] + b2[...]).astype(BF16)
    dr = load_rows(tf, step // 2, pl.ds(pl.multiple_of(step % 2 * size, size), size))
    drb = dr.astype(BF16)
    r = y + f2b[...]
    dc = None
    for j in range(ff):
        at = slice(j * d, (j + 1) * d)
        h = dot(c, fc1_w[:, at]) + f1b[:, at]
        phi = 0.5 * (1.0 + lax.erf(h * math.sqrt(0.5)))
        slope = phi + h * (jnp.exp(h * h * -0.5) * (1.0 / math.sqrt(2.0 * math.pi)))
        gelu = (h * phi).astype(BF16)
        dh_wide = dot_bt(drb, fc2_w[at, :]) * slope
        dh = dh_wide.astype(BF16)
        r = r + dot(gelu, fc2_w[at, :])
        fc2_acc[:, at] += dot_at(drb, gelu)
        fc1_acc[:, at] += dot_at(c, dh)
        fc1_sum[:, at] += fold(dh.astype(F32))
        more = dot_bt(dh, fc1_w[:, at])
        dc = more if dc is None else dc + more
    frame_out[...] = r.reshape(frame_out.shape).astype(BF16)
    dy = dr + norm_back(dc * g2[...], normed2, inv2)
    dz = dy.astype(BF16)
    proj_acc[...] += dot_at(o, dz)
    store_rows(do_out, 0, slice(None), dot_bt(dz, proj_w[...]))
    store_rows(dy_out, 0, slice(None), dy)
    small_sum[0] += fold(dc * normed2)
    small_sum[1] += fold(dc)
    small_sum[2] += fold(dr)
    small_sum[3] += fold(dz.astype(F32))

    @pl.when(step == pl.num_programs(0) - 1)
    def _():
        for j in range(ff):
            sums_out[j * d : (j + 1) * d, :] = fc1_acc[:, j * d : (j + 1) * d].astype(BF16)
            sums_out[(ff + j) * d : (ff + j + 1) * d, :] = fc2_acc[:, j * d : (j + 1) * d].T.astype(
                BF16
            )
        at = 2 * ff * d
        sums_out[at : at + d, :] = proj_acc[...].astype(BF16)
        rows = [jnp.sum(fc1_sum[:, j * d : (j + 1) * d], 0, keepdims=True) for j in range(ff)]
        rows += [jnp.sum(small_sum[k], 0, keepdims=True) for k in range(4)]
        rows.append(jnp.full((1, d), count[0], F32))
        rows.append(jnp.zeros((16 - len(rows), d), F32))
        high, low_part = split_rows(jnp.concatenate(rows, 0))
        at += d
        sums_out[at : at + 16, :] = high
        sums_out[at + 16 : at + 32, :] = low_part
        if sums_out.shape[0] > at + 32:
            sums_out[at + 32 :, :] = jnp.zeros((sums_out.shape[0] - at - 32, d), BF16)


def backward_kernel(last, *refs):
    xw, qkv, p_in, dy_in, do_in, qkv_w, g1, b1 = refs[:8]
    if last:
        before, outs, (dx, qkv_acc, rel_acc, col_sum, small_sum) = refs[8:12], refs[12:17], refs[17:22]
        mixed = refs[22]
    else:
        before, outs, (dx,) = None, refs[8:14], refs[14:]
        qkv_acc, rel_acc, col_sum, small_sum = outs[2:]
    step = pl.program_id(0)

    @pl.when(step == 0)
    def _():
        for k, buf in enumerate((qkv_acc, rel_acc, col_sum, small_sum)):
            buf[...] = before[k][...] if last else jnp.zeros_like(buf)

    d = g1.shape[-1]
    heads = d // (KEYS // GROUP)
    scale = (d // heads) ** (-0.5)
    masks = head_masks(KEYS, BF16)
    row_masks = head_masks(ROWS, F32)
    count = xw.shape[1]
    dqs, dks, dvs = [], [], []
    rel_sum = [None] * heads
    for n in range(count):
        page = step * count + n
        q = qkv[0, n, :, :d]
        k = qkv[0, n, :, d : 2 * d]
        v = qkv[0, n, :, 2 * d :]
        do = only_tokens(load_rows(do_in, 0, page_rows(page, ROWS)))
        dq, dk, dv = [], [], []
        for g in range(heads // GROUP):
            lanes = slice(g * KEYS, (g + 1) * KEYS)
            kg, vg = k[:, lanes], v[:, lanes]
            k_stack = jnp.concatenate([kg * m for m in masks], 0)
            v_stack = jnp.concatenate([vg * m for m in masks], 0)
            dof = do[:, lanes]
            dog = dof.astype(BF16)
            qf = q[:, lanes].astype(F32)[:ROWS]
            q_stack = jnp.concatenate([qf * m for m in row_masks], 0).astype(BF16)
            do_stack = jnp.concatenate([dof * m for m in row_masks], 0).astype(BF16)
            wide = slice(g * GROUP * KEYS, (g + 1) * GROUP * KEYS)
            dp = dot_bt(dog, v_stack)
            p = p_in[0, n, :, wide].astype(F32)
            t = p * dp
            ds = []
            for h in range(GROUP):
                at = slice(h * KEYS, (h + 1) * KEYS)
                th = t[:, at]
                ds.append(th - p[:, at] * jnp.sum(th, -1, keepdims=True))
            for h in range(GROUP):
                at = g * GROUP + h
                rel_sum[at] = ds[h] if n == 0 else rel_sum[at] + ds[h]
            dts = [x * scale for x in ds]
            dt = jnp.concatenate(dts, 1).astype(BF16)
            dt_stack = jnp.concatenate(dts, 0).astype(BF16)
            p_stack = jnp.concatenate(
                [p[:, h * KEYS : (h + 1) * KEYS] for h in range(GROUP)], 0
            ).astype(BF16)
            dq.append(dot(dt, k_stack))
            dk.append(dot_at(dt_stack, q_stack)[:ROWS])
            dv.append(dot_at(p_stack, do_stack)[:ROWS])
        dqs.append(jnp.concatenate(dq, 1))
        dks.append(jnp.concatenate(dk, 1))
        dvs.append(jnp.concatenate(dv, 1))
    for h in range(heads):
        rel_acc[:, h * KEYS : (h + 1) * KEYS] += rel_sum[h]
    joined = jnp.concatenate(
        [jnp.concatenate(dqs, 0), jnp.concatenate(dks, 0), jnp.concatenate(dvs, 0)], 1
    ).astype(BF16)
    x = jnp.concatenate([xw[0, n].astype(F32) for n in range(count)], 0)
    normed, inv = normalize(x)
    attn_in = (normed * g1[...] + b1[...]).astype(BF16)
    qkv_acc[...] += dot_at(attn_in, joined)
    col_sum[...] += fold(joined.astype(F32))
    da = dot_bt(joined, qkv_w[...])
    small_sum[0] += fold(da * normed)
    small_sum[1] += fold(da)
    back = norm_back(da * g1[...], normed, inv)
    for n in range(count):
        rows = page_rows(step * count + n, TOK)
        store_rows(dx, 0, rows, load_rows(dy_in, 0, rows) + back[n * ROWS : n * ROWS + TOK])

    @pl.when(step == pl.num_programs(0) - 1)
    def _():
        frame = load_rows(dx, 0, slice(None)).reshape(WIN, WIN, PAGES, d)
        if not last:
            outs[0][...] = frame[:SHIFT]
            outs[1][...] = frame[SHIFT:].astype(BF16)
            return
        stays, up, left, corner, sums_out = outs
        stays[...] = frame[:SHIFT, :SHIFT]
        up[...] = frame[SHIFT:, :SHIFT].astype(BF16)
        left[...] = frame[:SHIFT, SHIFT:].astype(BF16)
        corner[...] = frame[SHIFT:, SHIFT:].astype(BF16)
        for j in range(3):
            sums_out[j * d : (j + 1) * d, :] = qkv_acc[:, j * d : (j + 1) * d].astype(BF16)
        rel = table_gradient(
            [rel_acc[:, h * KEYS : (h + 1) * KEYS] for h in range(heads)], mixed
        )
        rows = [jnp.sum(small_sum[k], 0, keepdims=True) for k in range(2)]
        rows.append(jnp.sum(col_sum[:, :d], 0, keepdims=True))
        rows.append(jnp.sum(col_sum[:, 2 * d :], 0, keepdims=True))
        rows.append(jnp.zeros((4, d), F32))
        rows.append(rel[:, :d])
        rows.append(jnp.concatenate([rel[:, d:], jnp.zeros((heads, 2 * d - RELS), F32)], 1))
        rows.append(jnp.zeros((8, d), F32))
        high, rest = split_rows(jnp.concatenate(rows, 0))
        at = 3 * d
        sums_out[at : at + 32, :] = high
        sums_out[at + 32 : at + 64, :] = rest
        if sums_out.shape[0] > at + 64:
            sums_out[at + 64 :, :] = jnp.zeros((sums_out.shape[0] - at - 64, d), BF16)


def table_gradient(by_head, mixed):
    heads = len(by_head)
    for h in range(heads):
        mixed[pl.ds(h, ROWS, stride=heads), :] = by_head[h]
    wide = None
    for r in range(WIN):
        part = mixed[r * WIN * heads : (r + 1) * WIN * heads, :]
        part = jnp.concatenate([part, jnp.zeros_like(part)], 1)
        shift = (WIN - 1 - r) * WIN
        part = pltpu.roll(part, shift, 1) if shift else part
        wide = part if wide is None else wide + part
    high, rest = split_rows(wide)
    squeeze = squeeze_matrix()
    moved = dot_bt(high, squeeze) + dot_bt(rest, squeeze)
    total = None
    for c in range(WIN):
        part = moved[c * heads : (c + 1) * heads]
        shift = WIN - 1 - c
        part = pltpu.roll(part, shift, 1) if shift else part
        total = part if total is None else total + part
    at = lax.broadcasted_iota(jnp.int32, (RELS, RELS), 0)
    to = lax.broadcasted_iota(jnp.int32, (RELS, RELS), 1)
    turn = (at + to == SPAN * SPAN - 1).astype(F32).astype(BF16)
    high, rest = split_rows(total)
    return dot(high, turn) + dot(rest, turn)


def collect(places, buf, mine, other, planes):
    core, spot = places[0], places[1]
    size = mine.shape[0] // planes
    for first, pieces in ((core, mine), (1 - core, other)):
        for k in range(planes):
            at = pl.multiple_of((first * planes + (spot ^ k)) * size, 16)
            buf[pl.ds(at, size), :] = pieces[k * size : (k + 1) * size, :].astype(F32)


def finish_mlp_kernel(
    total, planes, places, mine, other,
    fc1, fc2, proj, fc1_b, g2, b2, fc2_b, proj_b, scale_out, buf,
):
    collect(places, buf, mine, other, planes)
    d = proj.shape[0]
    ff = fc1.shape[1] // d
    at = (2 * ff + 1) * d
    rows = buf[at : at + 16, :] + buf[at + 16 : at + 32, :]
    scale = total / rows[ff + 4 : ff + 5, :]
    rows = rows * scale
    scale_out[...] = scale
    for j in range(ff):
        fc1[:, j * d : (j + 1) * d] = buf[j * d : (j + 1) * d, :] * scale
        fc2[j * d : (j + 1) * d, :] = buf[(ff + j) * d : (ff + j + 1) * d, :] * scale
        fc1_b[:, j * d : (j + 1) * d] = rows[j : j + 1]
    proj[...] = buf[2 * ff * d : (2 * ff + 1) * d, :] * scale
    for k, ref in enumerate((g2, b2, fc2_b, proj_b)):
        ref[...] = rows[ff + k : ff + k + 1]


def finish_attention_kernel(
    planes, places, mine, other, scale_in, qkv, g1, b1, q_b, v_b, rel, buf
):
    collect(places, buf, mine, other, planes)
    d = scale_in.shape[1]
    scale = scale_in[...]
    for j in range(3):
        qkv[:, j * d : (j + 1) * d] = buf[j * d : (j + 1) * d, :] * scale
    at = 3 * d
    rows = (buf[at : at + 32, :] + buf[at + 32 : at + 64, :]) * scale
    for k, ref in enumerate((g1, b1, q_b, v_b)):
        ref[...] = rows[k : k + 1]
    heads = rel.shape[0]
    rel[:, :d] = rows[8 : 8 + heads]
    rel[:, d:] = rows[16 : 16 + heads, : rel.shape[1] - d]


def permute(block, target):
    rows, cols = lax.axis_size("rows"), lax.axis_size("cols")
    route = []
    for r in range(rows):
        for c in range(cols):
            tr, tc = target(r, c)
            route.append((r * cols + c, (tr % rows) * cols + tc % cols))
    return lax.ppermute(block, ("rows", "cols"), route)


def tree_sum(parts):
    parts = [p.astype(F32) for p in parts]
    while len(parts) > 1:
        parts = [parts[i] + parts[i + 1] for i in range(0, len(parts), 2)]
    return parts[0].astype(BF16)


def after(values, done):
    return lax.optimization_barrier((values, done))[0]


def spot_index():
    r, c = lax.axis_index("rows"), lax.axis_index("cols")
    return r & 1, ((r >> 1) & 1) * lax.axis_size("cols") + c


def core_hop(r, c):
    return r ^ 1, c


def plane_hop(k):
    cols = lax.axis_size("cols")
    return lambda r, c: (r ^ (2 * (k // cols)), c ^ (k % cols))


def core_scatter(x):
    core, _ = spot_index()
    halves = x.reshape(2, x.shape[0] // 2, x.shape[1])
    mine = lax.dynamic_index_in_dim(halves, core, 0, False)
    other = permute(lax.dynamic_index_in_dim(halves, 1 - core, 0, False), core_hop)
    return tree_sum([mine, other])


def plane_scatter(half):
    planes = 2 * lax.axis_size("cols")
    _, spot = spot_index()
    pieces = half.reshape(planes, half.shape[0] // planes, half.shape[1])
    got = [lax.dynamic_index_in_dim(pieces, spot, 0, False)]
    for k in range(1, planes):
        got.append(
            permute(lax.dynamic_index_in_dim(pieces, spot ^ k, 0, False), plane_hop(k))
        )
    return got


def depth_share(piece):
    got = [piece]
    for k in range(1, lax.axis_size("rows") // 4):
        got.append(permute(piece, lambda r, c, k=k: (r ^ (4 * k), c)))
    return got


def plane_gather(piece):
    got = [piece]
    for k in range(1, 2 * lax.axis_size("cols")):
        got.append(permute(piece, plane_hop(k)))
    return got


def strips(field):
    low = permute(field[:SHIFT], lambda r, c: (r - 1, c))
    right = permute(field[SHIFT:, :SHIFT], lambda r, c: (r, c - 1))
    corner = permute(field[:SHIFT, :SHIFT], lambda r, c: (r - 1, c - 1))
    return low, right, corner


def leave(field):
    upper = permute(field[SHIFT:, :-SHIFT].astype(BF16), lambda r, c: (r + 1, c))
    left = permute(field[:SHIFT, -SHIFT:].astype(BF16), lambda r, c: (r, c + 1))
    corner = permute(field[SHIFT:, -SHIFT:].astype(BF16), lambda r, c: (r + 1, c + 1))
    return corner, upper, left, field[:SHIFT, :-SHIFT]


def whole(a):
    return pl.BlockSpec(a.shape, lambda i: (0,) * len(a.shape), pipeline_mode=pl.Buffered(1))


def held(a):
    return pl.BlockSpec(a.shape, lambda i: (0,) * len(a.shape))


def bias_call(edge, rel_table):
    heads = rel_table.shape[0]
    table = jnp.pad(rel_table[:, ::-1], ((0, 0), (0, RELS - SPAN * SPAN)))
    return pl.pallas_call(
        bias_kernel,
        in_specs=[pl.BlockSpec(memory_space=pltpu.SMEM), pl.BlockSpec(memory_space=pltpu.VMEM)],
        out_shape=jax.ShapeDtypeStruct((2, ROWS * heads, KEYS), F32),
        compiler_params=pltpu.CompilerParams(vmem_limit_bytes=VMEM_LIMIT),
        name="attention_bias",
    )(edge, table)


def loop_params():
    return pltpu.CompilerParams(
        dimension_semantics=("arbitrary",), vmem_limit_bytes=VMEM_LIMIT
    )


def cost(flops):
    return pl.CostEstimate(flops=flops, bytes_accessed=10**7, transcendentals=10**6)


def attention_call(patches, p_strips, qkv_w, bias, g1, b1, q_b, v_b):
    pages, d = patches.shape[2:]
    heads = bias.shape[1] // ROWS
    tokens = 2 * TOK * pages
    shape = jax.ShapeDtypeStruct
    inputs = [patches, *p_strips, qkv_w, bias, g1, b1, q_b, v_b]
    outs = [
        shape((tokens, d), BF16),
        shape((2, pages, ROWS, d), BF16),
        shape((2, pages, KEYS, 3 * d), BF16),
        shape((2, pages, ROWS, heads * KEYS), BF16),
        shape((d // KEYS, 2, TOK * pages, KEYS), F32),
    ]
    paged = lambda a: pl.BlockSpec((2, 1) + a.shape[2:], lambda i: (0, i, 0, 0))
    return pl.pallas_call(
        attention_kernel,
        grid=(pages,),
        in_specs=[whole(a) for a in inputs],
        out_specs=[held(outs[0]), paged(outs[1]), paged(outs[2]), paged(outs[3]), held(outs[4])],
        out_shape=outs,
        scratch_shapes=[pltpu.VMEM((d // KEYS, 2, ROWS * pages, KEYS), F32)],
        compiler_params=loop_params(),
        cost_estimate=cost(10**10),
        name="attention_forward",
    )(*inputs)


def mlp_call(size, x, mixed, masked, t_strips, count, *weights):
    height, width, pages, d = masked.shape
    ff = weights[1].shape[1]
    tokens, chunk = x.shape[0], x.shape[0] // 4
    shape = jax.ShapeDtypeStruct
    blocks = [masked, *t_strips]
    outs = [
        shape((height, width, pages, d), BF16),
        shape((d // KEYS, 2, ROWS * pages, KEYS), F32),
        shape((d // KEYS, 2, ROWS * pages, KEYS), F32),
        shape((size, d), BF16),
    ]
    part = pl.BlockSpec((d // KEYS, 1, chunk, KEYS), lambda i: (0, i // 2, i % 2, 0))
    return pl.pallas_call(
        mlp_kernel,
        grid=(4,),
        in_specs=[pl.BlockSpec((chunk, d), lambda i: (i, 0)), part]
        + [whole(a) for a in blocks]
        + [pl.BlockSpec(memory_space=pltpu.SMEM)]
        + [whole(a) for a in weights],
        out_specs=[
            pl.BlockSpec((SHIFT, WIN, pages, d), lambda i: (i % 2, i // 2, 0, 0)),
            part, part, held(outs[3]),
        ],
        out_shape=outs,
        scratch_shapes=[
            pltpu.VMEM((d // KEYS, 2, TOK * pages, KEYS), F32),
            pltpu.VMEM((d, ff), F32),
            pltpu.VMEM((d, ff), F32),
            pltpu.VMEM((d, d), F32),
            pltpu.VMEM((8, ff), F32),
            pltpu.VMEM((4, 8, d), F32),
        ],
        compiler_params=loop_params(),
        cost_estimate=cost(10**10),
        name="mlp_forward_backward",
    )(x, mixed, *blocks, count, *weights)


def backward_call(w, size, xw, qkv, probs, dy, do, qkv_w, g1, b1, before=()):
    last = w == 1
    pages, d = xw.shape[1], xw.shape[3]
    heads = probs.shape[3] // KEYS
    batch = 2
    shape = jax.ShapeDtypeStruct
    sums = [
        shape((d, 3 * d), F32), shape((ROWS, heads * KEYS), F32), shape((8, 3 * d), F32),
        shape((2, 8, d), F32),
    ]
    dx = pltpu.VMEM((d // KEYS, 1, TOK * pages, KEYS), F32)
    rest = WIN - SHIFT
    if last:
        outs = [
            shape((SHIFT, SHIFT, pages, d), F32), shape((rest, SHIFT, pages, d), BF16),
            shape((SHIFT, rest, pages, d), BF16), shape((rest, rest, pages, d), BF16),
            shape((size, d), BF16),
        ]
        scratch = [dx] + [pltpu.VMEM(a.shape, F32) for a in sums]
        scratch.append(pltpu.VMEM((ROWS * heads, KEYS), F32))
    else:
        outs = [shape((SHIFT, WIN, pages, d), F32), shape((rest, WIN, pages, d), BF16)] + sums
        scratch = [dx]
    paged = lambda a: pl.BlockSpec((1, batch) + a.shape[2:], lambda i: (w, i, 0, 0))
    rows = pl.BlockSpec((d // KEYS, 1, ROWS * pages, KEYS), lambda i: (0, w, 0, 0))
    return pl.pallas_call(
        lambda *refs: backward_kernel(last, *refs),
        grid=(pages // batch,),
        in_specs=[paged(xw), paged(qkv), paged(probs), rows, rows]
        + [whole(a) for a in (qkv_w, g1, b1, *before)],
        out_specs=[held(a) for a in outs],
        out_shape=outs,
        scratch_shapes=scratch,
        compiler_params=loop_params(),
        cost_estimate=cost(10**10),
        name="attention_backward",
    )(xw, qkv, probs, dy, do, qkv_w, g1, b1, *before)


def finish_call(kernel, shapes, places, size, *inputs):
    return pl.pallas_call(
        kernel,
        in_specs=[pl.BlockSpec(memory_space=pltpu.SMEM)]
        + [pl.BlockSpec(memory_space=pltpu.VMEM)] * len(inputs),
        out_shape=[jax.ShapeDtypeStruct(s, F32) for s in shapes],
        scratch_shapes=[pltpu.VMEM((size, inputs[0].shape[1]), F32)],
        compiler_params=pltpu.CompilerParams(vmem_limit_bytes=VMEM_LIMIT),
        name="finish_sums",
    )(places, *inputs)


def shards(
    patches, target, kept_mask, ln1_gain, ln1_bias, qkv_weight, query_bias, value_bias, rel_table,
    proj_weight, proj_bias, ln2_gain, ln2_bias, fc1_weight, fc1_bias, fc2_weight, fc2_bias,
):
    pages, height, width, d = patches.shape
    ff = fc1_weight.shape[1]
    rows, cols = lax.axis_size("rows"), lax.axis_size("cols")
    planes = 2 * cols
    step = 32 * planes
    tokens = pages * height * width
    vec = lambda a: a.reshape(1, -1)

    patches = patches.transpose(1, 2, 0, 3)
    p_strips = strips(patches)
    edge = jnp.stack(
        [lax.axis_index("rows") == rows - 1, lax.axis_index("cols") == cols - 1]
    ).astype(jnp.int32)
    bias = bias_call(edge, rel_table)
    kept = kept_mask.transpose(1, 2, 0)
    masked = target.transpose(1, 2, 0, 3) * kept.astype(BF16)[..., None]
    t_strips = strips(masked)
    count = jnp.sum(kept_mask.astype(F32)).reshape(1)

    g1, b1 = vec(ln1_gain), vec(ln1_bias)
    x, xw, qkv, probs, mixed = attention_call(
        patches, p_strips, qkv_weight, bias, g1, b1, vec(query_bias), vec(value_bias)
    )
    n1 = -(-(2 * ff + d + 32) // step) * step
    n2 = -(-(3 * d + 64) // step) * step
    frame, dy, do, sums = mlp_call(
        n1, x, mixed, masked, t_strips, count, proj_weight, fc1_weight, fc2_weight,
        vec(proj_bias), vec(ln2_gain), vec(ln2_bias), vec(fc1_bias), vec(fc2_bias),
    )

    half = core_scatter(sums)
    got = plane_scatter(half)
    do = after(do, half)
    first = backward_call(0, n2, xw, qkv, probs, dy, do, qkv_weight, g1, b1)
    stays_a, up_a = first[:2]
    got = after(got, first[2])
    piece = tree_sum(got)
    got = depth_share(piece)
    do = after(do, piece)
    stays_b, up_b, left, corner, sums2 = backward_call(
        1, n2, xw, qkv, probs, dy, do, qkv_weight, g1, b1, first[2:]
    )
    got = after(got, sums2)
    half2 = core_scatter(sums2)
    piece = tree_sum(got)
    got2 = plane_scatter(half2)
    mine = jnp.concatenate(plane_gather(piece), 0)
    piece2 = tree_sum(got2)
    got2 = depth_share(piece2)
    other = permute(mine, core_hop)
    piece2 = tree_sum(got2)
    mine2 = jnp.concatenate(plane_gather(piece2), 0)
    other2 = permute(mine2, core_hop)

    places = jnp.stack(spot_index()).astype(jnp.int32)
    total = float(tokens * rows * cols)
    row = (1, d)
    fc1_g, fc2_g, proj_g, fc1_bg, g2_g, b2_g, fc2_bg, proj_bg, scale = finish_call(
        lambda *refs: finish_mlp_kernel(total, planes, *refs),
        [(d, ff), (ff, d), (d, d), (1, ff), row, row, row, row, row],
        places, n1, mine, other,
    )
    qkv_g, g1_g, b1_g, q_bg, v_bg, rel_g = finish_call(
        lambda *refs: finish_attention_kernel(planes, *refs),
        [(d, 3 * d), row, row, row, row, rel_table.shape],
        places, n2, mine2, other2, scale,
    )

    down = lambda r, c: (r + 1, c)
    side = lambda r, c: (r, c + 1)
    across = lambda r, c: (r + 1, c + 1)
    out_up = permute(frame[SHIFT:, :-SHIFT], down)
    out_left = permute(frame[:SHIFT, -SHIFT:], side)
    out_corner = permute(frame[SHIFT:, -SHIFT:], across)
    top = jnp.concatenate([out_corner, out_up], 1)
    bottom = jnp.concatenate([out_left, frame[:SHIFT, :-SHIFT]], 1)
    output = jnp.concatenate([top, bottom], 0)
    up_a, up_b = permute(up_a, down), permute(up_b, down)
    left, corner = permute(left, side), permute(corner, across)
    top = jnp.concatenate([corner, up_a, up_b], 1).astype(F32)
    bottom = jnp.concatenate([left.astype(F32), stays_a, stays_b], 1)
    grad = jnp.concatenate([top, bottom], 0) * scale[0]
    flat = lambda a: a.reshape(-1)
    return (
        output.transpose(2, 0, 1, 3),
        grad.transpose(2, 0, 1, 3),
        flat(g1_g),
        flat(b1_g),
        qkv_g,
        flat(q_bg),
        flat(v_bg),
        rel_g,
        proj_g,
        flat(proj_bg),
        flat(g2_g),
        flat(b2_g),
        fc1_g,
        flat(fc1_bg),
        fc2_g,
        flat(fc2_bg),
    )


def solution(mesh):
    field = P(None, "rows", "cols", None)
    return jax.shard_map(
        shards,
        mesh=mesh,
        in_specs=(field, field, P(None, "rows", "cols")) + (P(),) * 14,
        out_specs=(field, field) + (P(),) * 14,
        check_vma=False,
    )
```

time: 184 us -> 143 us (0.78)
  waiting for transfers between devices: 32.2 us -> 16.5 us
  local copies, waits for them, and re-layouts: 24 us -> 10.6 us
  starting transfers between devices: 48 us -> 39.5 us
  Pallas kernels: 63 us -> 67.3 us
  other arithmetic: 11 us -> 7.29 us
  matrix products: 3.32 us -> 0 us
    ppermute x34 -> x35, waiting for transfers between devices: 32.2 us -> 16.5 us  [permute(): return lax.ppermute(block, ('rows', 'cols'), route)]
    ppermute x34 -> x35, starting transfers between devices: 48 us -> 39.5 us  [permute(): return lax.ppermute(block, ('rows', 'cols'), route)]
    add x5 -> x0, local copies, waits for them, and re-layouts: 4.81 us -> none  [the longest x1 4.57 us: attention_bias(): full = rel[None] + mask[:, :, None, :]]
    pallas_call x4 -> x7, Pallas kernels: 63 us -> 67.3 us  [the longest x2 25.2 us: backward_call(): pl.pallas_call(lambda *refs: backward_kernel(last, *refs), grid=(pages //...]
    slice x13 -> x6, local copies, waits for them, and re-layouts: 7.82 us -> 4.17 us  [the longest x1 1.1 us: shards(): out_up = permute(frame[SHIFT:, :-SHIFT], down)]
    transpose x1 -> x0, local copies, waits for them, and re-layouts: 3.52 us -> none  [attention_bias(): jnp.einsum('hab,ija,klb->ikhjl', grid, hots, hots, precision=HIGH)]
    dot_general x2 -> x0, matrix products: 3.32 us -> none  [attention_bias(): jnp.einsum('hab,ija,klb->ikhjl', grid, hots, hots, precision=HIGH)]
    transpose x0 -> x2, other arithmetic: none -> 2.91 us  [the longest x1 1.95 us: shards(): grad.transpose(2, 0, 1, 3)]
  transfers between devices with their start and end apart: 34 -> 35, of which waited for: 13 -> 11; matrix products, arithmetic and copies ran while one was open for 12% -> 9% of each run, Pallas kernels for 0% -> 35%
where the time goes in v2:
time: 143 us; the launch traced here: 142 us
  Pallas kernels  67.3 us (47%)
  starting transfers between devices  39.5 us (28%)
  waiting for transfers between devices  16.5 us (12%)
  local copies, waits for them, and re-layouts  10.6 us (7%)
  other arithmetic  7.29 us (5%)
    ppermute x35, starting transfers between devices, permute(): return lax.ppermute(block, ('rows', 'cols'), route)  39.5 us
    pallas_call x2, Pallas kernels, backward_call(): pl.pallas_call(lambda *refs: backward_kernel(last, *refs), grid=(pages //...  25.2 us
    pallas_call x1, Pallas kernels, attention_call(): pl.pallas_call(attention_kernel, grid=(pages,), in_specs=[whole(a) for a...  18.9 us
    ppermute x35, waiting for transfers between devices, permute(): return lax.ppermute(block, ('rows', 'cols'), route)  16.5 us
    pallas_call x1, Pallas kernels, mlp_call(): pl.pallas_call(mlp_kernel, grid=(4,), in_specs=[pl.BlockSpec((chunk, d),...  16 us
    pallas_call x2, Pallas kernels, finish_call(): pl.pallas_call(kernel, in_specs=[pl.BlockSpec(memory_space=pltpu.SMEM)] +...  5 us
    unnamed x44, local copies, waits for them, and re-layouts  3.43 us
  transfers between devices with their start and end apart: 35, of which 11 were waited for; matrix products, arithmetic and copies ran while one was open for 9% of the time, Pallas kernels for 35%

profile of v2, /device:TPU:0, one launch (start us, length us, event | category | flops | bytes accessed | tf_op | source)
XLA Modules:
  0.0 142.4 jit_solution(2830120439441275863)
XLA Ops:
  0.7 1.0 fusion.8
  1.7 3.0 %collective-permute-start.1 = (bf16[5,5,8,256]{3,2,1,0:T(8,128)(2,1)S(1)}, bf16[5,5,8,256]{3,2,1,0:T(8,128)(2,1)S(1)}, u32[]{:S(2)}, u32[]{:S(2)}) collective-permute-start(bf16[5,5,8,256]{3,2,1,0:T(8,128)(2,1)S(1)} %get-tuple-element.113), channel_id=1, source_target_pairs={{0,1},{1,0},{2,3},{3,2},{4,5},{5,4},{6,7},{7,6},{8,9},{9,8},{10,11... | collective-permute-start | bytes 307208 | tf_op jit(solution)/shard_map/ppermute | solution.py:476
  4.7 3.7 %collective-permute-start.2 = (bf16[5,5,8,256]{3,2,1,0:T(8,128)(2,1)S(1)}, bf16[5,5,8,256]{3,2,1,0:T(8,128)(2,1)S(1)}, u32[]{:S(2)}, u32[]{:S(2)}) collective-permute-start(bf16[5,5,8,256]{3,2,1,0:T(8,128)(2,1)S(1)} %get-tuple-element.112), channel_id=1, source_target_pairs={{0,31},{1,30},{2,1},{3,0},{4,3},{5,2},{6,5},{7,4},{8,7},{9,6},{10,... | collective-permute-start | bytes 307208 | tf_op jit(solution)/shard_map/ppermute | solution.py:476
  8.4 1.0 slice.40
  9.4 1.2 collective-permute-start
  10.6 0.8 convert_bitcast_fusion
  11.6 0.3 bitcast_multiply_fusion.t_own
  11.9 1.6 %collective-permute-start.4 = (bf16[5,5,8,256]{3,2,1,0:T(8,128)(2,1)S(1)}, bf16[5,5,8,256]{3,2,1,0:T(8,128)(2,1)S(1)}, u32[]{:S(2)}, u32[]{:S(2)}) collective-permute-start(bf16[5,5,8,256]{3,2,1,0:T(8,128)(2,1)S(1)} %get-tuple-element.111), channel_id=1, source_target_pairs={{0,1},{1,0},{2,3},{3,2},{4,5},{5,4},{6,7},{7,6},{8,9},{9,8},{10,11... | collective-permute-start | bytes 307208 | tf_op jit(solution)/shard_map/ppermute | solution.py:476
  13.5 0.2 reverse
  13.8 0.6 pad.4.table
  14.4 0.6 add_convert_fusion.3.edge
  15.0 2.1 %attention_bias.1.bias = f32[2,832,128]{2,1,0:T(8,128)} custom-call(s32[2]{0:T(128)} %add_convert_fusion.3.edge, f32[8,384]{1,0:T(8,128)} %pad.4.table), custom_call_target="tpu_custom_call" | custom-call | tf_op jit(solution)/shard_map/attention_bias/pallas_call | solution.py:563
  17.1 0.6 convert_reduce_fusion
  17.8 0.8 collective-permute-start.3
  18.5 0.6 copy-done.19
  19.3 18.9 %attention_forward.1 = (bf16[1600,256]{1,0:T(8,128)(2,1)}, bf16[2,8,104,256]{3,2,1,0:T(8,128)(2,1)}, bf16[2,8,128,768]{3,2,1,0:T(8,128)(2,1)}, bf16[2,8,104,1024]{3,2,1,0:T(8,128)(2,1)}, f32[2,2,800,128]{3,2,1,0:T(8,128)}) custom-call(bf16[10,20,8,256]{3,2,1,0:T(8,128)(2,1)} %bitcast.72, bf16[5,20,8,256]{3,2,1,0:T(8,128)(2,1)} %copy-done.11, ...), custom_call_target="tpu_custom_call" | custom-call | flops 10000000000 | bytes 10000000 | tf_op jit(solution)/shard_map/attention_forward/pallas_call | solution.py:596
  38.3 0.6 copy-done.18
  38.9 0.1 copy-done.12
  39.0 16.0 %mlp_forward_backward.1 = (bf16[10,20,8,256]{3,2,1,0:T(8,128)(2,1)}, f32[2,2,832,128]{3,2,1,0:T(8,128)}, f32[2,2,832,128]{3,2,1,0:T(8,128)}, bf16[2432,256]{1,0:T(8,128)(2,1)}) custom-call(bf16[1600,256]{1,0:T(8,128)(2,1)} %get-tuple-element.61.x_in, f32[2,2,800,128]{3,2,1,0:T(8,128)} %get-tuple-element.62.o_in, bf16[10,20,8,256]{3,2,1,0:T(8,128)(2,1)} %copy-done, ...), custom_call_target="tpu_custom_call" | custom-call | flops 10000000000 | bytes 10000000 | tf_op jit(solution)/shard_map/mlp_forward_backward/pallas_call | solution.py:622
  55.1 1.2 dynamic-slice_bitcast_fusion
  56.4 0.6 pad_add_fusion.refs_0_
  57.0 1.1 fusion.6
  58.1 0.5 collective-permute-start.7
  58.6 1.0 fusion.5
  59.6 2.5 %collective-permute-start.6 = (bf16[5,5,8,256]{3,2,1,0:T(8,128)(2,1)S(1)}, bf16[5,5,8,256]{3,2,1,0:T(8,128)(2,1)S(1)}, u32[]{:S(2)}, u32[]{:S(2)}) collective-permute-start(bf16[5,5,8,256]{3,2,1,0:T(8,128)(2,1)S(1)} %get-tuple-element.106), channel_id=1, source_target_pairs={{0,3},{1,2},{2,5},{3,4},{4,7},{5,6},{6,9},{7,8},{8,11},{9,10},{10,... | collective-permute-start | bytes 307208 | tf_op jit(solution)/shard_map/ppermute | solution.py:476
  62.1 0.2 fusion.1
  62.3 0.6 collective-permute-start.10
  62.9 0.4 collective-permute-start.11
  63.3 2.6 %collective-permute-start.12 = (bf16[304,256]{1,0:T(8,128)(2,1)S(1)}, bf16[304,256]{1,0:T(8,128)(2,1)S(1)}, u32[]{:S(2)}, u32[]{:S(2)}) collective-permute-start(bf16[304,256]{1,0:T(8,128)(2,1)S(1)} %get-tuple-element.114), channel_id=1, source_target_pairs={{0,5},{1,4},{2,7},{3,6},{4,1},{5,0},{6,3},{7,2},{8,13},{9,12},{10,... | collective-permute-start | bytes 466952 | tf_op jit(solution)/shard_map/ppermute | solution.py:476
  65.8 12.2 %attention_backward.2 = (f32[5,10,8,256]{3,2,1,0:T(8,128)}, bf16[5,10,8,256]{3,2,1,0:T(8,128)(2,1)}, f32[256,768]{1,0:T(8,128)}, f32[104,1024]{1,0:T(8,128)}, f32[8,768]{1,0:T(8,128)}, /*index=5*/f32[2,8,256]{2,1,0:T(8,128)}) custom-call(bf16[2,8,104,256]{3,2,1,0:T(8,128)(2,1)} %get-tuple-element.64.refs_0_, ...), custom_call_target="tpu_custom_call" | custom-call | flops 10000000000 | bytes 10000000 | tf_op jit(solution)/shard_map/attention_backward/pallas_call | solution.py:673
  78.2 2.3 %collective-permute-start.18 = (bf16[304,256]{1,0:T(8,128)(2,1)S(1)}, bf16[304,256]{1,0:T(8,128)(2,1)S(1)}, u32[]{:S(2)}, u32[]{:S(2)}) collective-permute-start(bf16[304,256]{1,0:T(8,128)(2,1)S(1)} %add_convert_fusion.1), channel_id=1, source_target_pairs={{0,16},{1,17},{2,18},{3,19},{4,20},{5,21},{6,22},{7,23},{8,24},{9,... | collective-permute-start | bytes 466952 | tf_op jit(solution)/shard_map/ppermute | solution.py:476
  80.5 2.1 %collective-permute-start.19 = (bf16[304,256]{1,0:T(8,128)(2,1)S(1)}, bf16[304,256]{1,0:T(8,128)(2,1)S(1)}, u32[]{:S(2)}, u32[]{:S(2)}) collective-permute-start(bf16[304,256]{1,0:T(8,128)(2,1)S(1)} %add_convert_fusion.1), channel_id=1, source_target_pairs={{0,24},{1,25},{2,26},{3,27},{4,28},{5,29},{6,30},{7,31},{8,16},{9,... | collective-permute-start | bytes 466952 | tf_op jit(solution)/shard_map/ppermute | solution.py:476
  82.6 13.0 %attention_backward.3 = (f32[5,5,8,256]{3,2,1,0:T(8,128)}, bf16[5,5,8,256]{3,2,1,0:T(8,128)(2,1)}, bf16[5,5,8,256]{3,2,1,0:T(8,128)(2,1)}, bf16[5,5,8,256]{3,2,1,0:T(8,128)(2,1)}, bf16[896,256]{1,0:T(8,128)(2,1)}) custom-call(bf16[2,8,104,256]{3,2,1,0:T(8,128)(2,1)} %get-tuple-element.64.refs_0_, bf16[2,8,128,768]{3,2,1,0:T(8,128)(2,1)} %get-tuple-element.65.refs_1_, ...), custom_call_target="tpu_custom_call" | custom-call | flops 10000000000 | bytes 10000000 | tf_op jit(solution)/shard_map/attention_backward/pallas_call | solution.py:673
  95.6 1.0 dynamic-slice_bitcast_fusion.1
  96.8 0.6 collective-permute-start.20
  97.4 0.4 collective-permute-start.21
  97.8 0.4 collective-permute-done.24
  98.1 2.2 %collective-permute-start.22 = (bf16[304,256]{1,0:T(8,128)(2,1)S(1)}, bf16[304,256]{1,0:T(8,128)(2,1)S(1)}, u32[]{:S(2)}, u32[]{:S(2)}) collective-permute-start(bf16[304,256]{1,0:T(8,128)(2,1)S(1)} %add_convert_fusion), channel_id=1, source_target_pairs={{0,5},{1,4},{2,7},{3,6},{4,1},{5,0},{6,3},{7,2},{8,13},{9,12},{10,... | collective-permute-start | bytes 466952 | tf_op jit(solution)/shard_map/ppermute | solution.py:476
  100.3 1.0 fusion.2
  101.4 2.3 %collective-permute-done.20 = bf16[304,256]{1,0:T(8,128)(2,1)S(1)} collective-permute-done((bf16[304,256]{1,0:T(8,128)(2,1)S(1)}, bf16[304,256]{1,0:T(8,128)(2,1)S(1)}, u32[]{:S(2)}, u32[]{:S(2)}) %collective-permute-start.20) | collective-permute-done | bytes 155680 | tf_op jit(solution)/shard_map/ppermute | solution.py:476
  103.7 0.5 collective-permute-start.25
  104.2 2.9 %collective-permute-done.21 = bf16[304,256]{1,0:T(8,128)(2,1)S(1)} collective-permute-done((bf16[304,256]{1,0:T(8,128)(2,1)S(1)}, bf16[304,256]{1,0:T(8,128)(2,1)S(1)}, u32[]{:S(2)}, u32[]{:S(2)}) %collective-permute-start.21) | collective-permute-done | bytes 155680 | tf_op jit(solution)/shard_map/ppermute | solution.py:476
  107.1 2.7 %collective-permute-start.27 = (bf16[112,256]{1,0:T(8,128)(2,1)S(1)}, bf16[112,256]{1,0:T(8,128)(2,1)S(1)}, u32[]{:S(2)}, u32[]{:S(2)}) collective-permute-start(bf16[112,256]{1,0:T(8,128)(2,1)S(1)} %get-tuple-element.119), channel_id=1, source_target_pairs={{0,5},{1,4},{2,7},{3,6},{4,1},{5,0},{6,3},{7,2},{8,13},{9,12},{10,... | collective-permute-start | bytes 172040 | tf_op jit(solution)/shard_map/ppermute | solution.py:476
  109.9 0.9 collective-permute-start.8
  110.8 0.6 collective-permute-done.26
  111.3 1.4 %collective-permute-done.27 = bf16[112,256]{1,0:T(8,128)(2,1)S(1)} collective-permute-done((bf16[112,256]{1,0:T(8,128)(2,1)S(1)}, bf16[112,256]{1,0:T(8,128)(2,1)S(1)}, u32[]{:S(2)}, u32[]{:S(2)}) %collective-permute-start.27) | collective-permute-done | bytes 57376 | tf_op jit(solution)/shard_map/ppermute | solution.py:476
  112.9 4.1 %collective-permute-start.29 = (bf16[112,256]{1,0:T(8,128)(2,1)S(1)}, bf16[112,256]{1,0:T(8,128)(2,1)S(1)}, u32[]{:S(2)}, u32[]{:S(2)}) collective-permute-start(bf16[112,256]{1,0:T(8,128)(2,1)S(1)} %fusion.4), channel_id=1, source_target_pairs={{0,16},{1,17},{2,18},{3,19},{4,20},{5,21},{6,22},{7,23},{8,24},{9,... | collective-permute-start | bytes 172040 | tf_op jit(solution)/shard_map/ppermute | solution.py:476
  117.0 0.3 collective-permute-start.30
  117.3 1.0 maximum_bitcast_fusion
  118.3 2.4 %collective-permute-start.13 = (bf16[5,5,8,256]{3,2,1,0:T(8,128)(2,1)S(1)}, bf16[5,5,8,256]{3,2,1,0:T(8,128)(2,1)S(1)}, u32[]{:S(2)}, u32[]{:S(2)}) collective-permute-start(bf16[5,5,8,256]{3,2,1,0:T(8,128)(2,1)S(1)} %copy-done.16), channel_id=1, source_target_pairs={{0,3},{1,2},{2,5},{3,4},{4,7},{5,6},{6,9},{7,8},{8,11},{9,10},{10,... | collective-permute-start | bytes 307208 | tf_op jit(solution)/shard_map/ppermute | solution.py:476
  120.7 2.3 %collective-permute-done.30 = bf16[112,256]{1,0:T(8,128)(2,1)S(1)} collective-permute-done((bf16[112,256]{1,0:T(8,128)(2,1)S(1)}, bf16[112,256]{1,0:T(8,128)(2,1)S(1)}, u32[]{:S(2)}, u32[]{:S(2)}) %collective-permute-start.30) | collective-permute-done | bytes 57376 | tf_op jit(solution)/shard_map/ppermute | solution.py:476
  122.9 0.9 collective-permute-start.16
  123.9 2.2 %collective-permute-done.14 = bf16[5,10,8,256]{3,2,1,0:T(8,128)(2,1)S(1)} collective-permute-done((bf16[5,10,8,256]{3,2,1,0:T(8,128)(2,1)S(1)}, bf16[5,10,8,256]{3,2,1,0:T(8,128)(2,1)S(1)}, u32[]{:S(2)}, u32[]{:S(2)}) %collective-permute-start.14) | collective-permute-done | bytes 204832 | tf_op jit(solution)/shard_map/ppermute | solution.py:476
  126.1 0.8 collective-permute-start.31
  126.9 0.9 collective-permute-done.13
  127.8 0.9 collective-permute-done.15
  128.7 2.3 %collective-permute-start.33 = (bf16[112,256]{1,0:T(8,128)(2,1)S(1)}, bf16[112,256]{1,0:T(8,128)(2,1)S(1)}, u32[]{:S(2)}, u32[]{:S(2)}) collective-permute-start(bf16[112,256]{1,0:T(8,128)(2,1)S(1)} %add_convert_fusion.2), channel_id=1, source_target_pairs={{0,5},{1,4},{2,7},{3,6},{4,1},{5,0},{6,3},{7,2},{8,13},{9,12},{10,... | collective-permute-start | bytes 172040 | tf_op jit(solution)/shard_map/ppermute | solution.py:476
  131.1 0.8 collective-permute-done.32
  132.0 1.8 %collective-permute-done.33 = bf16[112,256]{1,0:T(8,128)(2,1)S(1)} collective-permute-done((bf16[112,256]{1,0:T(8,128)(2,1)S(1)}, bf16[112,256]{1,0:T(8,128)(2,1)S(1)}, u32[]{:S(2)}, u32[]{:S(2)}) %collective-permute-start.33) | collective-permute-done | bytes 57376 | tf_op jit(solution)/shard_map/ppermute | solution.py:476
  133.9 0.8 copy-done.5
  134.7 2.9 %finish_sums.2 = (f32[256,1024]{1,0:T(8,128)}, f32[1024,256]{1,0:T(8,128)}, f32[256,256]{1,0:T(8,128)}, f32[1,1024]{1,0:T(1,128)}, f32[1,256]{1,0:T(1,128)}, /*i...) custom-call(s32[2]{0:T(128)} %pad_add_fusion.refs_0_, bf16[1216,256]{1,0:T(8,128)(2,1)} %copy-done.1, ...), custom_call_target="tpu_custom_call" | custom-call | tf_op jit(solution)/shard_map/finish_sums/pallas_call | solution.py:688
  137.7 1.9 %fusion = f32[8,10,20,256]{3,0,2,1:T(8,128)} fusion(f32[5,5,8,256]{3,2,1,0:T(8,128)S(1)} %copy-done.8, f32[5,10,8,256]{3,2,1,0:T(8,128)S(1)} %copy-done.6, f32[5,5,8,256]{3,2,1,0:T(8,128)S(1)} %convert_element_type.121, f32[5,20,8,256]{3,2,1,0:T(8,128)S(1)} %maximum_convert_fusion, f32[256]{0:T(256)} %bitcast.76), kind=kLoop, calls=%fused_computation.1 | loop fusion | flops 1638400 | bytes 3277824 | tf_op jit(solution)/shard_map/transpose | solution.py:788
  139.6 0.7 copy-done.7
  140.3 2.1 %finish_sums.3 = (f32[256,768]{1,0:T(8,128)}, f32[1,256]{1,0:T(1,128)}, f32[1,256]{1,0:T(1,128)}, f32[1,256]{1,0:T(1,128)}, f32[1,256]{1,0:T(1,128)}, /*index=5*/f32[8,361]{1,0:T(8,128)}) custom-call(s32[2]{0:T(128)} %pad_add_fusion.refs_0_, bf16[448,256]{1,0:T(8,128)(2,1)} %copy-done.3, bf16[448,256]{1,0:T(8,128)(2,1)} %copy-done.7, ...), custom_call_target="tpu_custom_call" | custom-call | tf_op jit(solution)/shard_map/finish_sums/pallas_call | solution.py:688
  (86 shorter events, 1.4 us)
Async XLA Ops:
  0.6 10.9 %copy-start.4 = (bf16[8,10,20,256]{3,0,2,1:T(8,128)(2,1)S(1)}, bf16[8,10,20,256]{3,0,2,1:T(8,128)(2,1)}, u32[]{:S(2)}) copy-start(bf16[8,10,20,256]{3,0,2,1:T(8,128)(2,1)} %param.18) | copy-start | bytes 2457604
  1.7 16.1 %collective-permute-start.1 = (bf16[5,5,8,256]{3,2,1,0:T(8,128)(2,1)S(1)}, bf16[5,5,8,256]{3,2,1,0:T(8,128)(2,1)S(1)}, u32[]{:S(2)}, u32[]{:S(2)}) collective-permute-start(bf16[5,5,8,256]{3,2,1,0:T(8,128)(2,1)S(1)} %get-tuple-element.113), channel_id=1, source_target_pairs={{0,1},{1,0},{2,3},{3,2},{4,5},{5,4},{6,7},{7,6},{8,9},{9,8},{10,11... | collective-permute-start | bytes 307208 | tf_op jit(solution)/shard_map/ppermute | solution.py:476
  4.7 13.8 %collective-permute-start.2 = (bf16[5,5,8,256]{3,2,1,0:T(8,128)(2,1)S(1)}, bf16[5,5,8,256]{3,2,1,0:T(8,128)(2,1)S(1)}, u32[]{:S(2)}, u32[]{:S(2)}) collective-permute-start(bf16[5,5,8,256]{3,2,1,0:T(8,128)(2,1)S(1)} %get-tuple-element.112), channel_id=1, source_target_pairs={{0,31},{1,30},{2,1},{3,0},{4,3},{5,2},{6,5},{7,4},{8,7},{9,6},{10,... | collective-permute-start | bytes 307208 | tf_op jit(solution)/shard_map/ppermute | solution.py:476
  9.4 4.1 %copy-start.10 = (f32[8,361]{1,0:T(8,128)S(1)}, f32[8,361]{1,0:T(8,128)}, u32[]{:S(2)}) copy-start(f32[8,361]{1,0:T(8,128)} %param.25) | copy-start | bytes 34660
  9.4 9.1 %collective-permute-start = (bf16[5,20,8,256]{3,2,1,0:T(8,128)(2,1)S(1)}, bf16[5,20,8,256]{3,2,1,0:T(8,128)(2,1)S(1)}, u32[]{:S(2)}, u32[]{:S(2)}) collective-permute-start(bf16[5,20,8,256]{3,2,1,0:T(8,128)(2,1)S(1)} %slice.40), channel_id=1, source_target_pairs={{0,30},{1,31},{2,0},{3,1},{4,2},{5,3},{6,4},{7,5},{8,6},{9,7},{10,... | collective-permute-start | bytes 1228808 | tf_op jit(solution)/shard_map/ppermute | solution.py:476
  11.5 5.6 %copy-start.9 = (s32[8,10,20]{2,0,1:T(8,128)S(1)}, s32[8,10,20]{2,0,1:T(8,128)}, u32[]{:S(2)}) copy-start(s32[8,10,20]{2,0,1:T(8,128)} %param.19) | copy-start | bytes 19204
  11.8 26.4 %copy-start = (bf16[10,20,8,256]{3,2,1,0:T(8,128)(2,1)}, bf16[10,20,8,256]{3,2,1,0:T(8,128)(2,1)S(1)}, u32[]{:S(2)}) copy-start(bf16[10,20,8,256]{3,2,1,0:T(8,128)(2,1)S(1)} %bitcast_multiply_fusion.t_own) | copy-start | bytes 2457604
  11.9 26.3 %collective-permute-start.4 = (bf16[5,5,8,256]{3,2,1,0:T(8,128)(2,1)S(1)}, bf16[5,5,8,256]{3,2,1,0:T(8,128)(2,1)S(1)}, u32[]{:S(2)}, u32[]{:S(2)}) collective-permute-start(bf16[5,5,8,256]{3,2,1,0:T(8,128)(2,1)S(1)} %get-tuple-element.111), channel_id=1, source_target_pairs={{0,1},{1,0},{2,3},{3,2},{4,5},{5,4},{6,7},{7,6},{8,9},{9,8},{10,11... | collective-permute-start | bytes 307208 | tf_op jit(solution)/shard_map/ppermute | solution.py:476
  13.4 24.8 %collective-permute-start.5 = (bf16[5,5,8,256]{3,2,1,0:T(8,128)(2,1)S(1)}, bf16[5,5,8,256]{3,2,1,0:T(8,128)(2,1)S(1)}, u32[]{:S(2)}, u32[]{:S(2)}) collective-permute-start(bf16[5,5,8,256]{3,2,1,0:T(8,128)(2,1)S(1)} %get-tuple-element.110), channel_id=1, source_target_pairs={{0,31},{1,30},{2,1},{3,0},{4,3},{5,2},{6,5},{7,4},{8,7},{9,6},{10,... | collective-permute-start | bytes 307208 | tf_op jit(solution)/shard_map/ppermute | solution.py:476
  17.8 0.8 copy-start.17
  17.8 20.5 %collective-permute-start.3 = (bf16[5,20,8,256]{3,2,1,0:T(8,128)(2,1)S(1)}, bf16[5,20,8,256]{3,2,1,0:T(8,128)(2,1)S(1)}, u32[]{:S(2)}, u32[]{:S(2)}) collective-permute-start(bf16[5,20,8,256]{3,2,1,0:T(8,128)(2,1)S(1)} %slice.43), channel_id=1, source_target_pairs={{0,30},{1,31},{2,0},{3,1},{4,2},{5,3},{6,4},{7,5},{8,6},{9,7},{10,... | collective-permute-start | bytes 1228808 | tf_op jit(solution)/shard_map/ppermute | solution.py:476
  18.5 0.7 copy-start.19
  18.5 0.8 copy-start.11
  38.2 0.6 copy-start.18
  38.2 0.7 copy-start.20
  38.3 0.8 copy-start.12
  55.1 7.0 %copy-start.2 = (bf16[2432,256]{1,0:T(8,128)(2,1)S(1)}, bf16[2432,256]{1,0:T(8,128)(2,1)}, u32[]{:S(2)}) copy-start(bf16[2432,256]{1,0:T(8,128)(2,1)} %get-tuple-element.69) | copy-start | bytes 3735556
  56.3 5.8 %collective-permute-start.9 = (bf16[1216,256]{1,0:T(8,128)(2,1)S(1)}, bf16[1216,256]{1,0:T(8,128)(2,1)S(1)}, u32[]{:S(2)}, u32[]{:S(2)}) collective-permute-start(bf16[1216,256]{1,0:T(8,128)(2,1)S(1)} %dynamic-slice_bitcast_fusion), channel_id=1, source_target_pairs={{0,2},{1,3},{2,0},{3,1},{4,6},{5,7},{6,4},{7,5},{8,10},{9,11},{10,... | collective-permute-start | bytes 1867784 | tf_op jit(solution)/shard_map/ppermute | solution.py:476
  58.1 59.2 %collective-permute-start.7 = (bf16[5,15,8,256]{3,2,1,0:T(8,128)(2,1)S(1)}, bf16[5,15,8,256]{3,2,1,0:T(8,128)(2,1)S(1)}, u32[]{:S(2)}, u32[]{:S(2)}) collective-permute-start(bf16[5,15,8,256]{3,2,1,0:T(8,128)(2,1)S(1)} %get-tuple-element.108), channel_id=1, source_target_pairs={{0,2},{1,3},{2,4},{3,5},{4,6},{5,7},{6,8},{7,9},{8,10},{9,11},{10,... | collective-permute-start | bytes 921608 | tf_op jit(solution)/shard_map/ppermute | solution.py:476
  59.6 53.3 %collective-permute-start.6 = (bf16[5,5,8,256]{3,2,1,0:T(8,128)(2,1)S(1)}, bf16[5,5,8,256]{3,2,1,0:T(8,128)(2,1)S(1)}, u32[]{:S(2)}, u32[]{:S(2)}) collective-permute-start(bf16[5,5,8,256]{3,2,1,0:T(8,128)(2,1)S(1)} %get-tuple-element.106), channel_id=1, source_target_pairs={{0,3},{1,2},{2,5},{3,4},{4,7},{5,6},{6,9},{7,8},{8,11},{9,10},{10,... | collective-permute-start | bytes 307208 | tf_op jit(solution)/shard_map/ppermute | solution.py:476
  62.3 15.7 %collective-permute-start.10 = (bf16[304,256]{1,0:T(8,128)(2,1)S(1)}, bf16[304,256]{1,0:T(8,128)(2,1)S(1)}, u32[]{:S(2)}, u32[]{:S(2)}) collective-permute-start(bf16[304,256]{1,0:T(8,128)(2,1)S(1)} %get-tuple-element.116), channel_id=1, source_target_pairs={{0,1},{1,0},{2,3},{3,2},{4,5},{5,4},{6,7},{7,6},{8,9},{9,8},{10,11... | collective-permute-start | bytes 466952 | tf_op jit(solution)/shard_map/ppermute | solution.py:476
  62.9 15.2 %collective-permute-start.11 = (bf16[304,256]{1,0:T(8,128)(2,1)S(1)}, bf16[304,256]{1,0:T(8,128)(2,1)S(1)}, u32[]{:S(2)}, u32[]{:S(2)}) collective-permute-start(bf16[304,256]{1,0:T(8,128)(2,1)S(1)} %get-tuple-element.115), channel_id=1, source_target_pairs={{0,4},{1,5},{2,6},{3,7},{4,0},{5,1},{6,2},{7,3},{8,12},{9,13},{10,... | collective-permute-start | bytes 466952 | tf_op jit(solution)/shard_map/ppermute | solution.py:476
  63.3 14.8 %collective-permute-start.12 = (bf16[304,256]{1,0:T(8,128)(2,1)S(1)}, bf16[304,256]{1,0:T(8,128)(2,1)S(1)}, u32[]{:S(2)}, u32[]{:S(2)}) collective-permute-start(bf16[304,256]{1,0:T(8,128)(2,1)S(1)} %get-tuple-element.114), channel_id=1, source_target_pairs={{0,5},{1,4},{2,7},{3,6},{4,1},{5,0},{6,3},{7,2},{8,13},{9,12},{10,... | collective-permute-start | bytes 466952 | tf_op jit(solution)/shard_map/ppermute | solution.py:476
  78.2 18.4 %collective-permute-start.17 = (bf16[304,256]{1,0:T(8,128)(2,1)S(1)}, bf16[304,256]{1,0:T(8,128)(2,1)S(1)}, u32[]{:S(2)}, u32[]{:S(2)}) collective-permute-start(bf16[304,256]{1,0:T(8,128)(2,1)S(1)} %add_convert_fusion.1), channel_id=1, source_target_pairs={{0,8},{1,9},{2,10},{3,11},{4,12},{5,13},{6,14},{7,15},{8,0},{9,1},... | collective-permute-start | bytes 466952 | tf_op jit(solution)/shard_map/ppermute | solution.py:476
  78.2 18.4 %collective-permute-start.18 = (bf16[304,256]{1,0:T(8,128)(2,1)S(1)}, bf16[304,256]{1,0:T(8,128)(2,1)S(1)}, u32[]{:S(2)}, u32[]{:S(2)}) collective-permute-start(bf16[304,256]{1,0:T(8,128)(2,1)S(1)} %add_convert_fusion.1), channel_id=1, source_target_pairs={{0,16},{1,17},{2,18},{3,19},{4,20},{5,21},{6,22},{7,23},{8,24},{9,... | collective-permute-start | bytes 466952 | tf_op jit(solution)/shard_map/ppermute | solution.py:476
  80.5 16.2 %collective-permute-start.19 = (bf16[304,256]{1,0:T(8,128)(2,1)S(1)}, bf16[304,256]{1,0:T(8,128)(2,1)S(1)}, u32[]{:S(2)}, u32[]{:S(2)}) collective-permute-start(bf16[304,256]{1,0:T(8,128)(2,1)S(1)} %add_convert_fusion.1), channel_id=1, source_target_pairs={{0,24},{1,25},{2,26},{3,27},{4,28},{5,29},{6,30},{7,31},{8,16},{9,... | collective-permute-start | bytes 466952 | tf_op jit(solution)/shard_map/ppermute | solution.py:476
  96.6 1.6 %collective-permute-start.24 = (bf16[448,256]{1,0:T(8,128)(2,1)S(1)}, bf16[448,256]{1,0:T(8,128)(2,1)S(1)}, u32[]{:S(2)}, u32[]{:S(2)}) collective-permute-start(bf16[448,256]{1,0:T(8,128)(2,1)S(1)} %dynamic-slice_bitcast_fusion.1), channel_id=1, source_target_pairs={{0,2},{1,3},{2,0},{3,1},{4,6},{5,7},{6,4},{7,5},{8,10},{9,11},{10,... | collective-permute-start | bytes 688136 | tf_op jit(solution)/shard_map/ppermute | solution.py:476
  96.8 6.9 %collective-permute-start.20 = (bf16[304,256]{1,0:T(8,128)(2,1)S(1)}, bf16[304,256]{1,0:T(8,128)(2,1)S(1)}, u32[]{:S(2)}, u32[]{:S(2)}) collective-permute-start(bf16[304,256]{1,0:T(8,128)(2,1)S(1)} %add_convert_fusion), channel_id=1, source_target_pairs={{0,1},{1,0},{2,3},{3,2},{4,5},{5,4},{6,7},{7,6},{8,9},{9,8},{10,11... | collective-permute-start | bytes 466952 | tf_op jit(solution)/shard_map/ppermute | solution.py:476
  97.4 9.7 %collective-permute-start.21 = (bf16[304,256]{1,0:T(8,128)(2,1)S(1)}, bf16[304,256]{1,0:T(8,128)(2,1)S(1)}, u32[]{:S(2)}, u32[]{:S(2)}) collective-permute-start(bf16[304,256]{1,0:T(8,128)(2,1)S(1)} %add_convert_fusion), channel_id=1, source_target_pairs={{0,4},{1,5},{2,6},{3,7},{4,0},{5,1},{6,2},{7,3},{8,12},{9,13},{10,... | collective-permute-start | bytes 466952 | tf_op jit(solution)/shard_map/ppermute | solution.py:476
  98.1 9.0 %collective-permute-start.22 = (bf16[304,256]{1,0:T(8,128)(2,1)S(1)}, bf16[304,256]{1,0:T(8,128)(2,1)S(1)}, u32[]{:S(2)}, u32[]{:S(2)}) collective-permute-start(bf16[304,256]{1,0:T(8,128)(2,1)S(1)} %add_convert_fusion), channel_id=1, source_target_pairs={{0,5},{1,4},{2,7},{3,6},{4,1},{5,0},{6,3},{7,2},{8,13},{9,12},{10,... | collective-permute-start | bytes 466952 | tf_op jit(solution)/shard_map/ppermute | solution.py:476
  101.4 16.9 %copy-start.13 = (bf16[5,10,8,256]{3,2,1,0:T(8,128)(2,1)S(1)}, bf16[5,10,8,256]{3,2,1,0:T(8,128)(2,1)}, u32[]{:S(2)}) copy-start(bf16[5,10,8,256]{3,2,1,0:T(8,128)(2,1)} %get-tuple-element.81) | copy-start | bytes 614404
  101.4 16.9 %copy-start.16 = (bf16[5,5,8,256]{3,2,1,0:T(8,128)(2,1)S(1)}, bf16[5,5,8,256]{3,2,1,0:T(8,128)(2,1)}, u32[]{:S(2)}) copy-start(bf16[5,5,8,256]{3,2,1,0:T(8,128)(2,1)} %get-tuple-element.80) | copy-start | bytes 307204
  101.4 19.3 %copy-start.15 = (bf16[5,5,8,256]{3,2,1,0:T(8,128)(2,1)S(1)}, bf16[5,5,8,256]{3,2,1,0:T(8,128)(2,1)}, u32[]{:S(2)}) copy-start(bf16[5,5,8,256]{3,2,1,0:T(8,128)(2,1)} %get-tuple-element.82) | copy-start | bytes 307204
  101.4 21.5 %copy-start.14 = (bf16[5,5,8,256]{3,2,1,0:T(8,128)(2,1)S(1)}, bf16[5,5,8,256]{3,2,1,0:T(8,128)(2,1)}, u32[]{:S(2)}) copy-start(bf16[5,5,8,256]{3,2,1,0:T(8,128)(2,1)} %get-tuple-element.83) | copy-start | bytes 307204
  103.7 6.2 %collective-permute-start.25 = (bf16[112,256]{1,0:T(8,128)(2,1)S(1)}, bf16[112,256]{1,0:T(8,128)(2,1)S(1)}, u32[]{:S(2)}, u32[]{:S(2)}) collective-permute-start(bf16[112,256]{1,0:T(8,128)(2,1)S(1)} %get-tuple-element.118), channel_id=1, source_target_pairs={{0,1},{1,0},{2,3},{3,2},{4,5},{5,4},{6,7},{7,6},{8,9},{9,8},{10,11... | collective-permute-start | bytes 172040 | tf_op jit(solution)/shard_map/ppermute | solution.py:476
  107.1 4.2 %collective-permute-start.26 = (bf16[112,256]{1,0:T(8,128)(2,1)S(1)}, bf16[112,256]{1,0:T(8,128)(2,1)S(1)}, u32[]{:S(2)}, u32[]{:S(2)}) collective-permute-start(bf16[112,256]{1,0:T(8,128)(2,1)S(1)} %get-tuple-element.120), channel_id=1, source_target_pairs={{0,4},{1,5},{2,6},{3,7},{4,0},{5,1},{6,2},{7,3},{8,12},{9,13},{10,... | collective-permute-start | bytes 172040 | tf_op jit(solution)/shard_map/ppermute | solution.py:476
  107.1 5.6 %collective-permute-start.27 = (bf16[112,256]{1,0:T(8,128)(2,1)S(1)}, bf16[112,256]{1,0:T(8,128)(2,1)S(1)}, u32[]{:S(2)}, u32[]{:S(2)}) collective-permute-start(bf16[112,256]{1,0:T(8,128)(2,1)S(1)} %get-tuple-element.119), channel_id=1, source_target_pairs={{0,5},{1,4},{2,7},{3,6},{4,1},{5,0},{6,3},{7,2},{8,13},{9,12},{10,... | collective-permute-start | bytes 172040 | tf_op jit(solution)/shard_map/ppermute | solution.py:476
  109.9 21.2 %copy-start.1 = (bf16[1216,256]{1,0:T(8,128)(2,1)}, bf16[1216,256]{1,0:T(8,128)(2,1)S(1)}, u32[]{:S(2)}) copy-start(bf16[1216,256]{1,0:T(8,128)(2,1)S(1)} %pad_maximum_fusion.refs_1_) | copy-start | bytes 1867780
  109.9 7.1 %collective-permute-start.8 = (bf16[5,5,8,256]{3,2,1,0:T(8,128)(2,1)S(1)}, bf16[5,5,8,256]{3,2,1,0:T(8,128)(2,1)S(1)}, u32[]{:S(2)}, u32[]{:S(2)}) collective-permute-start(bf16[5,5,8,256]{3,2,1,0:T(8,128)(2,1)S(1)} %get-tuple-element.107), channel_id=1, source_target_pairs={{0,1},{1,0},{2,3},{3,2},{4,5},{5,4},{6,7},{7,6},{8,9},{9,8},{10,11... | collective-permute-start | bytes 307208 | tf_op jit(solution)/shard_map/ppermute | solution.py:476
  111.3 22.6 %collective-permute-start.23 = (bf16[1216,256]{1,0:T(8,128)(2,1)S(1)}, bf16[1216,256]{1,0:T(8,128)(2,1)S(1)}, u32[]{:S(2)}, u32[]{:S(2)}) collective-permute-start(bf16[1216,256]{1,0:T(8,128)(2,1)S(1)} %pad_maximum_fusion.refs_1_), channel_id=1, source_target_pairs={{0,2},{1,3},{2,0},{3,1},{4,6},{5,7},{6,4},{7,5},{8,10},{9,11},{10,... | collective-permute-start | bytes 1867784 | tf_op jit(solution)/shard_map/ppermute | solution.py:476
  112.8 5.4 %collective-permute-start.28 = (bf16[112,256]{1,0:T(8,128)(2,1)S(1)}, bf16[112,256]{1,0:T(8,128)(2,1)S(1)}, u32[]{:S(2)}, u32[]{:S(2)}) collective-permute-start(bf16[112,256]{1,0:T(8,128)(2,1)S(1)} %fusion.4), channel_id=1, source_target_pairs={{0,8},{1,9},{2,10},{3,11},{4,12},{5,13},{6,14},{7,15},{8,0},{9,1},... | collective-permute-start | bytes 172040 | tf_op jit(solution)/shard_map/ppermute | solution.py:476
  112.9 7.8 %collective-permute-start.29 = (bf16[112,256]{1,0:T(8,128)(2,1)S(1)}, bf16[112,256]{1,0:T(8,128)(2,1)S(1)}, u32[]{:S(2)}, u32[]{:S(2)}) collective-permute-start(bf16[112,256]{1,0:T(8,128)(2,1)S(1)} %fusion.4), channel_id=1, source_target_pairs={{0,16},{1,17},{2,18},{3,19},{4,20},{5,21},{6,22},{7,23},{8,24},{9,... | collective-permute-start | bytes 172040 | tf_op jit(solution)/shard_map/ppermute | solution.py:476
  117.0 6.0 %collective-permute-start.30 = (bf16[112,256]{1,0:T(8,128)(2,1)S(1)}, bf16[112,256]{1,0:T(8,128)(2,1)S(1)}, u32[]{:S(2)}, u32[]{:S(2)}) collective-permute-start(bf16[112,256]{1,0:T(8,128)(2,1)S(1)} %fusion.4), channel_id=1, source_target_pairs={{0,24},{1,25},{2,26},{3,27},{4,28},{5,29},{6,30},{7,31},{8,16},{9,... | collective-permute-start | bytes 172040 | tf_op jit(solution)/shard_map/ppermute | solution.py:476
  118.2 7.9 %collective-permute-start.14 = (bf16[5,10,8,256]{3,2,1,0:T(8,128)(2,1)S(1)}, bf16[5,10,8,256]{3,2,1,0:T(8,128)(2,1)S(1)}, u32[]{:S(2)}, u32[]{:S(2)}) collective-permute-start(bf16[5,10,8,256]{3,2,1,0:T(8,128)(2,1)S(1)} %copy-done.13), channel_id=1, source_target_pairs={{0,2},{1,3},{2,4},{3,5},{4,6},{5,7},{6,8},{7,9},{8,10},{9,11},{10,... | collective-permute-start | bytes 614408 | tf_op jit(solution)/shard_map/ppermute | solution.py:476
  118.3 9.5 %collective-permute-start.13 = (bf16[5,5,8,256]{3,2,1,0:T(8,128)(2,1)S(1)}, bf16[5,5,8,256]{3,2,1,0:T(8,128)(2,1)S(1)}, u32[]{:S(2)}, u32[]{:S(2)}) collective-permute-start(bf16[5,5,8,256]{3,2,1,0:T(8,128)(2,1)S(1)} %copy-done.16), channel_id=1, source_target_pairs={{0,3},{1,2},{2,5},{3,4},{4,7},{5,6},{6,9},{7,8},{8,11},{9,10},{10,... | collective-permute-start | bytes 307208 | tf_op jit(solution)/shard_map/ppermute | solution.py:476
  120.7 8.0 %collective-permute-start.15 = (bf16[5,5,8,256]{3,2,1,0:T(8,128)(2,1)S(1)}, bf16[5,5,8,256]{3,2,1,0:T(8,128)(2,1)S(1)}, u32[]{:S(2)}, u32[]{:S(2)}) collective-permute-start(bf16[5,5,8,256]{3,2,1,0:T(8,128)(2,1)S(1)} %copy-done.15), channel_id=1, source_target_pairs={{0,2},{1,3},{2,4},{3,5},{4,6},{5,7},{6,8},{7,9},{8,10},{9,11},{10,... | collective-permute-start | bytes 307208 | tf_op jit(solution)/shard_map/ppermute | solution.py:476
  122.9 8.1 %collective-permute-start.16 = (bf16[5,5,8,256]{3,2,1,0:T(8,128)(2,1)S(1)}, bf16[5,5,8,256]{3,2,1,0:T(8,128)(2,1)S(1)}, u32[]{:S(2)}, u32[]{:S(2)}) collective-permute-start(bf16[5,5,8,256]{3,2,1,0:T(8,128)(2,1)S(1)} %copy-done.14), channel_id=1, source_target_pairs={{0,1},{1,0},{2,3},{3,2},{4,5},{5,4},{6,7},{7,6},{8,9},{9,8},{10,11... | collective-permute-start | bytes 307208 | tf_op jit(solution)/shard_map/ppermute | solution.py:476
  123.9 13.8 %copy-start.6 = (f32[5,10,8,256]{3,2,1,0:T(8,128)S(1)}, f32[5,10,8,256]{3,2,1,0:T(8,128)}, u32[]{:S(2)}) copy-start(f32[5,10,8,256]{3,2,1,0:T(8,128)} %get-tuple-element.84) | copy-start | bytes 1228804
  123.9 13.8 %copy-start.8 = (f32[5,5,8,256]{3,2,1,0:T(8,128)S(1)}, f32[5,5,8,256]{3,2,1,0:T(8,128)}, u32[]{:S(2)}) copy-start(f32[5,5,8,256]{3,2,1,0:T(8,128)} %get-tuple-element.85) | copy-start | bytes 614404
  126.1 5.0 %collective-permute-start.31 = (bf16[112,256]{1,0:T(8,128)(2,1)S(1)}, bf16[112,256]{1,0:T(8,128)(2,1)S(1)}, u32[]{:S(2)}, u32[]{:S(2)}) collective-permute-start(bf16[112,256]{1,0:T(8,128)(2,1)S(1)} %add_convert_fusion.2), channel_id=1, source_target_pairs={{0,1},{1,0},{2,3},{3,2},{4,5},{5,4},{6,7},{7,6},{8,9},{9,8},{10,11... | collective-permute-start | bytes 172040 | tf_op jit(solution)/shard_map/ppermute | solution.py:476
  127.8 4.2 %collective-permute-start.32 = (bf16[112,256]{1,0:T(8,128)(2,1)S(1)}, bf16[112,256]{1,0:T(8,128)(2,1)S(1)}, u32[]{:S(2)}, u32[]{:S(2)}) collective-permute-start(bf16[112,256]{1,0:T(8,128)(2,1)S(1)} %add_convert_fusion.2), channel_id=1, source_target_pairs={{0,4},{1,5},{2,6},{3,7},{4,0},{5,1},{6,2},{7,3},{8,12},{9,13},{10,... | collective-permute-start | bytes 172040 | tf_op jit(solution)/shard_map/ppermute | solution.py:476
  128.7 5.1 %collective-permute-start.33 = (bf16[112,256]{1,0:T(8,128)(2,1)S(1)}, bf16[112,256]{1,0:T(8,128)(2,1)S(1)}, u32[]{:S(2)}, u32[]{:S(2)}) collective-permute-start(bf16[112,256]{1,0:T(8,128)(2,1)S(1)} %add_convert_fusion.2), channel_id=1, source_target_pairs={{0,5},{1,4},{2,7},{3,6},{4,1},{5,0},{6,3},{7,2},{8,13},{9,12},{10,... | collective-permute-start | bytes 172040 | tf_op jit(solution)/shard_map/ppermute | solution.py:476
  133.8 5.8 %copy-start.3 = (bf16[448,256]{1,0:T(8,128)(2,1)}, bf16[448,256]{1,0:T(8,128)(2,1)S(1)}, u32[]{:S(2)}) copy-start(bf16[448,256]{1,0:T(8,128)(2,1)S(1)} %pad_maximum_fusion.1.refs_1_) | copy-start | bytes 688132
  133.8 5.8 %collective-permute-start.34 = (bf16[448,256]{1,0:T(8,128)(2,1)S(1)}, bf16[448,256]{1,0:T(8,128)(2,1)S(1)}, u32[]{:S(2)}, u32[]{:S(2)}) collective-permute-start(bf16[448,256]{1,0:T(8,128)(2,1)S(1)} %pad_maximum_fusion.1.refs_1_), channel_id=1, source_target_pairs={{0,2},{1,3},{2,0},{3,1},{4,6},{5,7},{6,4},{7,5},{8,10},{9,11},{10,... | collective-permute-start | bytes 688136 | tf_op jit(solution)/shard_map/ppermute | solution.py:476
  133.9 0.8 copy-start.5
  139.6 0.7 copy-start.7

commit v3 on v2

v3 whole, which is shorter than its diff:
```python
import math

import jax
import jax.numpy as jnp
from jax import lax
from jax.experimental import pallas as pl
from jax.experimental.pallas import tpu as pltpu
from jax.sharding import PartitionSpec as P

WIN = 10
SHIFT = 5
EPS = 1e-05
F32 = jnp.float32
BF16 = jnp.bfloat16

SPAN = 2 * WIN - 1
TOK = WIN * WIN
ROWS = 104
KEYS = 128
GROUP = 4
RELS = 384
NEVER = -1e30
PAGES = 8
VMEM_LIMIT = 20


def dot(a, b):
    return lax.dot_general(a, b, (((1,), (0,)), ((), ())), preferred_element_type=F32)


def dot_bt(a, b):
    return lax.dot_general(a, b, (((1,), (1,)), ((), ())), preferred_element_type=F32)


def dot_at(a, b):
    return lax.dot_general(a, b, (((0,), (0,)), ((), ())), preferred_element_type=F32)


def normalize(x):
    center = x - jnp.sum(x, -1, keepdims=True) * (1.0 / x.shape[-1])
    inv = lax.rsqrt(jnp.sum(center * center, -1, keepdims=True) * (1.0 / x.shape[-1]) + EPS)
    return center * inv, inv


def norm_back(up, normed, inv):
    scale = 1.0 / up.shape[-1]
    mean_up = jnp.sum(up, -1, keepdims=True) * scale
    mean_un = jnp.sum(up * normed, -1, keepdims=True) * scale
    return inv * (up - mean_up - normed * mean_un)


def fold(x):
    return jnp.sum(x.reshape(x.shape[0] // 8, 8, x.shape[1]), 0)


def head_masks(rows, dtype):
    lane = lax.broadcasted_iota(jnp.int32, (rows, KEYS), 1)
    width = KEYS // GROUP
    return [
        ((lane >= k * width) & (lane < (k + 1) * width)).astype(F32).astype(dtype)
        for k in range(GROUP)
    ]


def head_rows(x, masks):
    return jnp.concatenate([x * m for m in masks], 0).astype(BF16)


def own_lanes(stacked):
    lane = lax.broadcasted_iota(jnp.int32, (ROWS, KEYS), 1)
    out = stacked[(GROUP - 1) * ROWS :]
    for h in reversed(range(GROUP - 1)):
        out = jnp.where(lane < (h + 1) * (KEYS // GROUP), stacked[h * ROWS : (h + 1) * ROWS], out)
    return out


def split_rows(x):
    high = x.astype(BF16)
    return high, (x - high.astype(F32)).astype(BF16)


def page_rows(page, count):
    return pl.ds(page, count, stride=PAGES)


def load_rows(ref, w, rows):
    return jnp.concatenate([ref[t, w, rows, :] for t in range(ref.shape[0])], 1)


def store_rows(ref, w, rows, value):
    for t in range(ref.shape[0]):
        ref[t, w, rows, :] = value[:, t * KEYS : (t + 1) * KEYS]


def only_tokens(x):
    return jnp.where(lax.broadcasted_iota(jnp.int32, x.shape, 0) < TOK, x, 0.0)


def gather_frame(out, own, low, right, corner):
    for w in range(2):
        for r in range(WIN):
            if r < WIN - SHIFT:
                main, side, mr, sr = own, right, r + SHIFT, r
            else:
                main, side, mr, sr = low, corner, r - SHIFT, r - SHIFT
            if w == 0:
                block = main[mr, SHIFT : SHIFT + WIN].astype(F32)
            else:
                block = jnp.concatenate(
                    [main[mr, SHIFT + WIN :].astype(F32), side[sr].astype(F32)], 0
                )
            at = r * WIN * PAGES
            store_rows(
                out, w, slice(at, at + WIN * PAGES), block.reshape(WIN * PAGES, block.shape[-1])
            )


def tenth(n):
    return (n * 205) >> 11


def squeeze_matrix():
    at = lax.broadcasted_iota(jnp.int32, (RELS, 2 * KEYS), 0)
    to = lax.broadcasted_iota(jnp.int32, (RELS, 2 * KEYS), 1)
    hit = (at == to + (SPAN - WIN) * tenth(to)) & (to < SPAN * WIN)
    return hit.astype(F32).astype(BF16)


def copy_all(pairs, sems):
    copies = [pltpu.make_async_copy(a, b, sems.at[k]) for k, (a, b) in enumerate(pairs)]
    for copy in copies:
        copy.start()
    for copy in copies:
        copy.wait()


def strips_kernel(field, low, right, corner, sems):
    copy_all(
        (
            (field.at[:SHIFT], low), (field.at[SHIFT:, :SHIFT], right),
            (field.at[:SHIFT, :SHIFT], corner),
        ),
        sems,
    )


def target_kernel(
    target_in, kept_in, table_in, masked, low, right, corner, count, table, target, kept, sems
):
    copy_all(((target_in, target), (kept_in, kept), (table_in, table)), sems)
    rows, cols = target.shape[:2]
    total = jnp.zeros(kept.shape[1:], F32)
    for r in range(rows):
        kept_row = kept[r].astype(F32)
        total = total + kept_row
        for c in range(cols):
            masked[r, c] = (target[r, c].astype(F32) * kept_row[:, c : c + 1]).astype(BF16)
    low[...] = masked[:SHIFT]
    right[...] = masked[SHIFT:, :SHIFT]
    corner[...] = masked[:SHIFT, :SHIFT]
    total = jnp.sum(jnp.sum(total, 1, keepdims=True), 0, keepdims=True)
    count[...] = jnp.broadcast_to(total, count.shape)


def split_halves(places, sums, mine, other):
    size = mine.shape[0]
    core = places[2]
    mine[...] = sums[pl.ds(pl.multiple_of(core * size, 16), size), :]
    other[...] = sums[pl.ds(pl.multiple_of((1 - core) * size, 16), size), :]


def split_kernel(places, mine, other, *outs):
    size = outs[0].shape[0]
    for k, out in enumerate(outs):
        at = pl.ds(pl.multiple_of((places[3] ^ k) * size, 16), size)
        out[...] = (mine[at, :].astype(F32) + other[at, :].astype(F32)).astype(BF16)


def tree_sum(parts):
    while len(parts) > 1:
        parts = [parts[i] + parts[i + 1] for i in range(0, len(parts), 2)]
    return parts[0]


def sum_kernel(*refs):
    refs[-1][...] = tree_sum([ref[...].astype(F32) for ref in refs[:-1]]).astype(BF16)


def join_kernel(*refs):
    out, at = refs[-1], 0
    for ref in refs[:-1]:
        out[at : at + ref.shape[0]] = ref[...]
        at += ref.shape[0]


def side_kernel(out_up, out_side, grad_up, grad_side, out):
    at = 0
    for ref in (out_up, out_side, grad_up, grad_side):
        out[at : at + ref.shape[0]] = ref[:, -SHIFT:]
        at += ref.shape[0]


def turn_matrix():
    at = lax.broadcasted_iota(jnp.int32, (RELS, RELS), 0)
    to = lax.broadcasted_iota(jnp.int32, (RELS, RELS), 1)
    return (at + to == SPAN * SPAN - 1).astype(F32).astype(BF16)


def split_three(x):
    high = x.astype(BF16)
    rest = x - high.astype(F32)
    middle = rest.astype(BF16)
    return high, middle, (rest - middle.astype(F32)).astype(BF16)


def bias_kernel(edge, table, out, padded):
    heads = table.shape[0]
    padded[...] = jnp.zeros_like(padded)
    padded[:, : table.shape[1]] = table[...]
    turn = turn_matrix()
    high, middle, least = split_three(padded[...])
    reversed_table = dot(high, turn) + dot(middle, turn) + dot(least, turn)
    moved = []
    for c in range(WIN):
        shift = WIN - 1 - c
        moved.append(pltpu.roll(reversed_table, RELS - shift, 1) if shift else reversed_table)
    stack = jnp.concatenate(moved, 0)
    high, middle, least = split_three(stack)
    squeeze = squeeze_matrix()
    wide = dot(high, squeeze) + dot(middle, squeeze) + dot(least, squeeze)
    count = WIN * heads
    for r in range(WIN):
        shift = (WIN - 1 - r) * WIN
        rel = pltpu.roll(wide, 2 * KEYS - shift, 1) if shift else wide
        rel = rel[:, :KEYS]
        key = lax.broadcasted_iota(jnp.int32, (count, KEYS), 1)
        row = lax.broadcasted_iota(jnp.int32, (count, KEYS), 0)
        across = (key < TOK // 2) if r >= SHIFT else (key >= TOK // 2)
        key_left = key - WIN * tenth(key) < SHIFT
        own_left = row < SHIFT * heads
        beside = key_left != own_left
        for w in range(2):
            cut_off = across & (edge[0] != 0)
            if w == 1:
                cut_off = cut_off | (beside & (edge[1] != 0))
            value = rel + jnp.where(cut_off, -100.0, 0.0)
            out[w, r * count : (r + 1) * count, :] = jnp.where(key < TOK, value, NEVER)
    for w in range(2):
        out[w, TOK * heads :, :] = jnp.zeros((out.shape[1] - TOK * heads, KEYS), F32)


def attention_kernel(
    own, low, right, corner, qkv_w, bias, g1, b1, qb, vb,
    x_out, xw_out, qkv_out, p_out, o_out,
    xf,
):
    gather_frame(xf, own, low, right, corner)
    for t in range(xf.shape[0]):
        for w in range(2):
            xf[t, w, TOK * PAGES :, :] = jnp.zeros((xf.shape[2] - TOK * PAGES, KEYS), F32)
            x_out[w * TOK * PAGES : (w + 1) * TOK * PAGES, t * KEYS : (t + 1) * KEYS] = xf[
                t, w, : TOK * PAGES, :
            ].astype(BF16)

    @pl.loop(0, PAGES)
    def _(page):
        attention_page(
            page, xf, qkv_w, bias, g1, b1, qb, vb, xw_out, qkv_out, p_out, o_out
        )


def attention_page(page, xf, qkv_w, bias, g1, b1, qb, vb, xw_out, qkv_out, p_out, o_out):
    d = g1.shape[-1]
    heads = d // (KEYS // GROUP)
    scale = (d // heads) ** (-0.5)
    x = jnp.concatenate([only_tokens(load_rows(xf, w, page_rows(page, ROWS))) for w in range(2)], 0)
    for w in range(2):
        xw_out[w, page] = x[w * ROWS : (w + 1) * ROWS].astype(BF16)
    normed, _ = normalize(x)
    attn_in = (normed * g1[...] + b1[...]).astype(BF16)
    proj = dot(attn_in, qkv_w[...])
    q_all = proj[:, :d] + qb[...]
    k_all = proj[:, d : 2 * d]
    v_all = proj[:, 2 * d :] + vb[...]
    masks = head_masks(ROWS, F32)
    filler = jnp.zeros((KEYS - ROWS, d), F32)
    groups = heads // GROUP
    scores, values = [], []
    for w in range(2):
        rows = slice(w * ROWS, (w + 1) * ROWS)
        q = jnp.concatenate([q_all[rows], filler], 0).astype(BF16)
        k = jnp.concatenate([k_all[rows], filler], 0).astype(BF16)
        v = jnp.concatenate([v_all[rows], filler], 0).astype(BF16)
        qkv_out[w, page, :, :d] = q
        qkv_out[w, page, :, d : 2 * d] = k
        qkv_out[w, page, :, 2 * d :] = v
        for g in range(groups):
            lanes = slice(g * KEYS, (g + 1) * KEYS)
            scores.append(dot_bt(head_rows(q_all[rows, lanes], masks), k[:, lanes]))
            values.append(v[:, lanes])
    probs = []
    for n, s in enumerate(scores):
        w, g = divmod(n, groups)
        es = []
        for h in range(GROUP):
            rel = bias[w, pl.ds(g * GROUP + h, ROWS, stride=heads), :]
            sh = s[h * ROWS : (h + 1) * ROWS] * scale + rel
            e = jnp.exp(sh - jnp.max(sh, -1, keepdims=True))
            es.append(e * (1.0 / jnp.sum(e, -1, keepdims=True)))
        p = jnp.concatenate(es, 0).astype(BF16)
        p_out[w, page, g * GROUP * ROWS : (g + 1) * GROUP * ROWS, :] = p
        probs.append(p)
    parts = [own_lanes(dot(p, v)) for p, v in zip(probs, values)]
    for w in range(2):
        joined = jnp.concatenate(parts[w * groups : (w + 1) * groups], 1)
        store_rows(o_out, w, page_rows(page, TOK), joined[:TOK])


def mlp_kernel(
    places, x_in, o_in, t_own, t_low, t_right, t_corner, count,
    proj_w, fc1_w, fc2_w, pb, g2, b2, f1b, f2b,
    stays, up, side, dy_out, do_out, mine, other,
    frame_out, sums_out, tf, fc1_acc, fc2_acc, proj_acc, fc1_sum, small_sum,
):
    for buf in (fc1_acc, fc2_acc, proj_acc, fc1_sum, small_sum):
        buf[...] = jnp.zeros_like(buf)
    gather_frame(tf, t_own, t_low, t_right, t_corner)

    @pl.loop(0, 4)
    def _(step):
        mlp_chunk(
            step, x_in, o_in, proj_w, fc1_w, fc2_w, pb, g2, b2, f1b, f2b, frame_out, dy_out, do_out,
            tf, fc1_acc, fc2_acc, proj_acc, fc1_sum, small_sum,
        )

    d = proj_w.shape[0]
    ff = fc1_w.shape[1] // d
    for j in range(ff):
        sums_out[j * d : (j + 1) * d, :] = fc1_acc[:, j * d : (j + 1) * d].astype(BF16)
        sums_out[(ff + j) * d : (ff + j + 1) * d, :] = fc2_acc[:, j * d : (j + 1) * d].T.astype(
            BF16
        )
    at = 2 * ff * d
    sums_out[at : at + d, :] = proj_acc[...].astype(BF16)
    rows = [jnp.sum(fc1_sum[:, j * d : (j + 1) * d], 0, keepdims=True) for j in range(ff)]
    rows += [jnp.sum(small_sum[k], 0, keepdims=True) for k in range(4)]
    rows.append(count[...])
    rows.append(jnp.zeros((16 - len(rows), d), F32))
    high, low_part = split_rows(jnp.concatenate(rows, 0))
    at += d
    sums_out[at : at + 16, :] = high
    sums_out[at + 16 : at + 32, :] = low_part
    if sums_out.shape[0] > at + 32:
        sums_out[at + 32 :, :] = jnp.zeros((sums_out.shape[0] - at - 32, d), BF16)
    split_halves(places, sums_out, mine, other)
    stays[...] = frame_out[:SHIFT, :-SHIFT]
    up[...] = frame_out[SHIFT:]
    side[...] = frame_out[:SHIFT, -SHIFT:]


def mlp_chunk(
    step, x_in, o_in, proj_w, fc1_w, fc2_w, pb, g2, b2, f1b, f2b, frame_out, dy_out, do_out,
    tf, fc1_acc, fc2_acc, proj_acc, fc1_sum, small_sum,
):
    size, d = x_in.shape[0] // 4, x_in.shape[1]
    ff = fc1_w.shape[1] // d
    w, half = step // 2, step % 2
    rows = pl.ds(pl.multiple_of(half * size, 16), size)
    o = load_rows(o_in, w, rows).astype(BF16)
    y = x_in[pl.ds(pl.multiple_of(step * size, 16), size), :].astype(F32) + dot(o, proj_w[...]) + pb[...]
    normed2, inv2 = normalize(y)
    c = (normed2 * g2[...] + b2[...]).astype(BF16)
    dr = load_rows(tf, w, rows)
    drb = dr.astype(BF16)
    r = y + f2b[...]
    dc = None
    for j in range(ff):
        at = slice(j * d, (j + 1) * d)
        h = dot(c, fc1_w[:, at]) + f1b[:, at]
        phi = 0.5 * (1.0 + lax.erf(h * math.sqrt(0.5)))
        slope = phi + h * (jnp.exp(h * h * -0.5) * (1.0 / math.sqrt(2.0 * math.pi)))
        gelu = (h * phi).astype(BF16)
        dh_wide = dot_bt(drb, fc2_w[at, :]) * slope
        dh = dh_wide.astype(BF16)
        r = r + dot(gelu, fc2_w[at, :])
        fc2_acc[:, at] += dot_at(drb, gelu)
        fc1_acc[:, at] += dot_at(c, dh)
        fc1_sum[:, at] += fold(dh.astype(F32))
        more = dot_bt(dh, fc1_w[:, at])
        dc = more if dc is None else dc + more
    frame_out[pl.ds(half * SHIFT, SHIFT), pl.ds(w * WIN, WIN)] = r.reshape(
        SHIFT, WIN, PAGES, d
    ).astype(BF16)
    dy = dr + norm_back(dc * g2[...], normed2, inv2)
    dz = dy.astype(BF16)
    proj_acc[...] += dot_at(o, dz)
    store_rows(do_out, w, rows, dot_bt(dz, proj_w[...]))
    store_rows(dy_out, w, rows, dy)
    small_sum[0] += fold(dc * normed2)
    small_sum[1] += fold(dc)
    small_sum[2] += fold(dr)
    small_sum[3] += fold(dz.astype(F32))


def backward_kernel(
    places, xw, qkv, p_in, dy_in, do_in, qkv_w, g1, b1,
    stays, side, up, mine, other,
    dx, qkv_acc, rel_acc, col_sum, small_sum, mixed, sums_out,
):
    for buf in (qkv_acc, rel_acc, col_sum, small_sum):
        buf[...] = jnp.zeros_like(buf)

    @pl.loop(0, PAGES)
    def _(page):
        backward_page(
            page, xw, qkv, p_in, dy_in, do_in, qkv_w, g1, b1, dx, qkv_acc, rel_acc, col_sum,
            small_sum,
        )

    d = g1.shape[-1]
    heads = d // (KEYS // GROUP)
    right = load_rows(dx, 1, slice(None)).reshape(WIN, WIN, PAGES, d)
    left = load_rows(dx, 0, slice(None)).reshape(WIN, WIN, PAGES, d)
    stays[:, :WIN] = left[:SHIFT]
    stays[:, WIN:] = right[:SHIFT, :SHIFT]
    side[...] = right[:SHIFT, SHIFT:].astype(BF16)
    up[:, :WIN] = left[SHIFT:].astype(BF16)
    up[:, WIN:] = right[SHIFT:].astype(BF16)
    for j in range(3):
        sums_out[j * d : (j + 1) * d, :] = qkv_acc[:, j * d : (j + 1) * d].astype(BF16)
    rel = table_gradient(
        [rel_acc[:, h * KEYS : (h + 1) * KEYS] for h in range(heads)], mixed
    )
    rows = [jnp.sum(small_sum[k], 0, keepdims=True) for k in range(2)]
    rows.append(jnp.sum(col_sum[:, :d], 0, keepdims=True))
    rows.append(jnp.sum(col_sum[:, 2 * d :], 0, keepdims=True))
    rows.append(jnp.zeros((4, d), F32))
    rows.append(rel[:, :d])
    rows.append(jnp.concatenate([rel[:, d:], jnp.zeros((heads, 2 * d - RELS), F32)], 1))
    rows.append(jnp.zeros((8, d), F32))
    high, rest = split_rows(jnp.concatenate(rows, 0))
    at = 3 * d
    sums_out[at : at + 32, :] = high
    sums_out[at + 32 : at + 64, :] = rest
    if sums_out.shape[0] > at + 64:
        sums_out[at + 64 :, :] = jnp.zeros((sums_out.shape[0] - at - 64, d), BF16)
    split_halves(places, sums_out, mine, other)


def backward_page(
    page, xw, qkv, p_in, dy_in, do_in, qkv_w, g1, b1, dx, qkv_acc, rel_acc, col_sum, small_sum
):
    d = g1.shape[-1]
    heads = d // (KEYS // GROUP)
    scale = (d // heads) ** (-0.5)
    masks = head_masks(ROWS, F32)
    count = 2
    groups = heads // GROUP
    chains = [(n, g) for n in range(count) for g in range(groups)]
    qs, ks, dos, dps = [], [], [], []
    for n, g in chains:
        lanes = slice(g * KEYS, (g + 1) * KEYS)
        qs.append(head_rows(qkv[n, page, :, lanes].astype(F32)[:ROWS], masks))
        ks.append(qkv[n, page, :, d + g * KEYS : d + (g + 1) * KEYS])
        v = qkv[n, page, :, 2 * d + g * KEYS : 2 * d + (g + 1) * KEYS]
        do = only_tokens(do_in[g, n, page_rows(page, ROWS), :])
        dos.append(head_rows(do, masks))
        dps.append(dot_bt(dos[-1], v))
    dts = []
    rel_sum = [None] * heads
    for c, (n, g) in enumerate(chains):
        p = p_in[n, page, g * GROUP * ROWS : (g + 1) * GROUP * ROWS, :].astype(F32)
        t = p * dps[c]
        ds = t - p * jnp.sum(t, -1, keepdims=True)
        for h in range(GROUP):
            at = g * GROUP + h
            part = ds[h * ROWS : (h + 1) * ROWS]
            rel_sum[at] = part if n == 0 else rel_sum[at] + part
        dts.append((ds * scale).astype(BF16))
    dqs, dks, dvs = [], [], []
    for c, (n, g) in enumerate(chains):
        p = p_in[n, page, g * GROUP * ROWS : (g + 1) * GROUP * ROWS, :]
        dqs.append(own_lanes(dot(dts[c], ks[c])))
        dks.append(dot_at(dts[c], qs[c])[:ROWS])
        dvs.append(dot_at(p, dos[c])[:ROWS])
    for h in range(heads):
        rel_acc[:, h * KEYS : (h + 1) * KEYS] += rel_sum[h]
    joined = jnp.concatenate(
        [
            jnp.concatenate([part[n * groups + g] for n in range(count)], 0)
            for part in (dqs, dks, dvs)
            for g in range(groups)
        ],
        1,
    ).astype(BF16)
    x = jnp.concatenate([xw[n, page].astype(F32) for n in range(count)], 0)
    normed, inv = normalize(x)
    attn_in = (normed * g1[...] + b1[...]).astype(BF16)
    qkv_acc[...] += dot_at(attn_in, joined)
    col_sum[...] += fold(joined.astype(F32))
    da = dot_bt(joined, qkv_w[...])
    small_sum[0] += fold(da * normed)
    small_sum[1] += fold(da)
    back = norm_back(da * g1[...], normed, inv)
    for n in range(count):
        rows = page_rows(page, TOK)
        store_rows(dx, n, rows, load_rows(dy_in, n, rows) + back[n * ROWS : n * ROWS + TOK])


def table_gradient(by_head, mixed):
    heads = len(by_head)
    for h in range(heads):
        mixed[pl.ds(h, ROWS, stride=heads), :] = by_head[h]
    wide = None
    for r in range(WIN):
        part = mixed[r * WIN * heads : (r + 1) * WIN * heads, :]
        part = jnp.concatenate([part, jnp.zeros_like(part)], 1)
        shift = (WIN - 1 - r) * WIN
        part = pltpu.roll(part, shift, 1) if shift else part
        wide = part if wide is None else wide + part
    high, rest = split_rows(wide)
    squeeze = squeeze_matrix()
    moved = dot_bt(high, squeeze) + dot_bt(rest, squeeze)
    total = None
    for c in range(WIN):
        part = moved[c * heads : (c + 1) * heads]
        shift = WIN - 1 - c
        part = pltpu.roll(part, shift, 1) if shift else part
        total = part if total is None else total + part
    turn = turn_matrix()
    high, rest = split_rows(total)
    return dot(high, turn) + dot(rest, turn)


def collect(places, buf, mine, other, planes, first, size):
    core, spot = places[2], places[3]
    stride = mine.shape[0] // planes
    for c, pieces in ((core, mine), (1 - core, other)):
        for k in range(planes):
            at = pl.multiple_of((c * planes + (spot ^ k)) * size, 16)
            buf[pl.ds(at, size), :] = pieces[k * stride + first : k * stride + first + size, :].astype(
                F32
            )


def finish_kernel(
    total, planes, sizes, places, mine, other, up, side, stays,
    grad, fc1, fc2, proj, fc1_b, g2, b2, fc2_b, proj_b, qkv, g1, b1, q_b, v_b, rel, buf1, buf2,
):
    collect(places, buf1, mine, other, planes, 0, sizes[0])
    collect(places, buf2, mine, other, planes, sizes[0], sizes[1])
    d = proj.shape[0]
    ff = fc1.shape[1] // d
    at = (2 * ff + 1) * d
    rows = buf1[at : at + 16, :] + buf1[at + 16 : at + 32, :]
    scale = total / rows[ff + 4 : ff + 5, :]
    rows = rows * scale
    wide = scale.reshape(1, 1, 1, d)
    rest = up.shape[0]
    grad[:rest, :SHIFT] = side[: rest].astype(F32) * wide
    grad[:rest, SHIFT:] = up[:, :-SHIFT].astype(F32) * wide
    grad[rest:, :SHIFT] = side[rest:].astype(F32) * wide
    grad[rest:, SHIFT:] = stays[...] * wide
    for j in range(ff):
        fc1[:, j * d : (j + 1) * d] = buf1[j * d : (j + 1) * d, :] * scale
        fc2[j * d : (j + 1) * d, :] = buf1[(ff + j) * d : (ff + j + 1) * d, :] * scale
        fc1_b[:, j * d : (j + 1) * d] = rows[j : j + 1]
    proj[...] = buf1[2 * ff * d : (2 * ff + 1) * d, :] * scale
    for k, ref in enumerate((g2, b2, fc2_b, proj_b)):
        ref[...] = rows[ff + k : ff + k + 1]
    for j in range(3):
        qkv[:, j * d : (j + 1) * d] = buf2[j * d : (j + 1) * d, :] * scale
    at = 3 * d
    rows = (buf2[at : at + 32, :] + buf2[at + 32 : at + 64, :]) * scale
    for k, ref in enumerate((g1, b1, q_b, v_b)):
        ref[...] = rows[k : k + 1]
    heads = rel.shape[0]
    rel[:, :d] = rows[8 : 8 + heads]
    rel[:, d:] = rows[16 : 16 + heads, : rel.shape[1] - d]


def permute(block, target):
    rows, cols = lax.axis_size("rows"), lax.axis_size("cols")
    route = []
    for r in range(rows):
        for c in range(cols):
            tr, tc = target(r, c)
            route.append((r * cols + c, (tr % rows) * cols + tc % cols))
    return lax.ppermute(block, ("rows", "cols"), route)


def after(values, done):
    return lax.optimization_barrier((values, done))[0]


def core_hop(r, c):
    return r ^ 1, c


def plane_hop(k):
    cols = lax.axis_size("cols")
    return lambda r, c: (r ^ (2 * (k // cols)), c ^ (k % cols))


def plane_share(pieces):
    return [pieces[0]] + [permute(p, plane_hop(k)) for k, p in enumerate(pieces) if k]


def depth_share(piece):
    got = [piece]
    for k in range(1, lax.axis_size("rows") // 4):
        got.append(permute(piece, lambda r, c, k=k: (r ^ (4 * k), c)))
    return got


def strip_hops():
    return [lambda r, c: (r - 1, c), lambda r, c: (r, c - 1), lambda r, c: (r - 1, c - 1)]


def in_vmem():
    return pl.BlockSpec(memory_space=pltpu.VMEM)


def in_smem():
    return pl.BlockSpec(memory_space=pltpu.SMEM)


def to_vmem(a):
    return pltpu.with_memory_space_constraint(a, pltpu.VMEM)


def limit(mib):
    return pltpu.CompilerParams(vmem_limit_bytes=mib * 1024 * 1024)


def strip_shapes(field):
    rows, cols, pages, d = field.shape
    return [
        pltpu.VMEM(s, BF16)
        for s in (
            (SHIFT, cols, pages, d), (rows - SHIFT, SHIFT, pages, d), (SHIFT, SHIFT, pages, d)
        )
    ]


def in_hbm():
    return pl.BlockSpec(memory_space=pltpu.HBM)


def to_hbm(a):
    return pltpu.with_memory_space_constraint(a, pltpu.HBM)


def strips_call(field):
    return pl.pallas_call(
        strips_kernel,
        in_specs=[in_hbm()],
        out_specs=[in_vmem()] * 3,
        out_shape=strip_shapes(field),
        scratch_shapes=[pltpu.SemaphoreType.DMA((3,))],
        compiler_params=limit(4),
        name="input_strips",
    )(to_hbm(field))


def target_call(target, kept, table):
    return pl.pallas_call(
        target_kernel,
        in_specs=[in_hbm()] * 3,
        out_specs=[in_vmem()] * 6,
        out_shape=[
            pltpu.VMEM(target.shape, BF16), *strip_shapes(target),
            pltpu.VMEM((1, target.shape[-1]), F32), pltpu.VMEM(table.shape, F32),
        ],
        scratch_shapes=[
            pltpu.VMEM(target.shape, BF16), pltpu.VMEM(kept.shape, kept.dtype),
            pltpu.SemaphoreType.DMA((3,)),
        ],
        compiler_params=limit(8),
        name="masked_target",
    )(*map(to_hbm, (target, kept, table)))


def split_call(places, mine, other):
    planes = 2 * lax.axis_size("cols")
    n, d = mine.shape
    return pl.pallas_call(
        split_kernel,
        in_specs=[in_smem()] + [in_vmem()] * 2,
        out_specs=[in_vmem()] * planes,
        out_shape=[pltpu.VMEM((n // planes, d), BF16)] * planes,
        compiler_params=limit(4),
        name="split_sums",
    )(places, *map(to_vmem, (mine, other)))


def local_call(kernel, rows, parts, name):
    return pl.pallas_call(
        kernel,
        in_specs=[in_vmem()] * len(parts),
        out_specs=in_vmem(),
        out_shape=pltpu.VMEM((rows,) + parts[-1].shape[1:], BF16),
        compiler_params=limit(4),
        name=name,
    )(*map(to_vmem, parts))


def sum_call(parts):
    return local_call(sum_kernel, parts[0].shape[0], parts, "add_pieces")


def join_call(parts):
    return local_call(join_kernel, sum(a.shape[0] for a in parts), parts, "join_pieces")


def side_call(*parts):
    return local_call(side_kernel, sum(a.shape[0] for a in parts), parts, "side_strip")


def bias_call(places, rel_table):
    heads = rel_table.shape[0]
    return pl.pallas_call(
        bias_kernel,
        in_specs=[in_smem(), in_vmem()],
        out_specs=in_vmem(),
        out_shape=pltpu.VMEM((2, ROWS * heads, KEYS), F32),
        scratch_shapes=[pltpu.VMEM((heads, RELS), F32)],
        compiler_params=limit(VMEM_LIMIT),
        name="attention_bias",
    )(places, to_vmem(rel_table))


def cost(flops):
    return pl.CostEstimate(flops=flops, bytes_accessed=10**7, transcendentals=10**6)


def attention_call(patches, p_strips, qkv_w, bias, g1, b1, q_b, v_b):
    pages, d = patches.shape[2:]
    heads = bias.shape[1] // ROWS
    tokens = 2 * TOK * pages
    shape = pltpu.VMEM
    inputs = [patches, *p_strips, qkv_w, bias, g1, b1, q_b, v_b]
    outs = [
        shape((tokens, d), BF16),
        shape((2, pages, ROWS, d), BF16),
        shape((2, pages, KEYS, 3 * d), BF16),
        shape((2, pages, heads * ROWS, KEYS), BF16),
        shape((d // KEYS, 2, TOK * pages, KEYS), F32),
    ]
    return pl.pallas_call(
        attention_kernel,
        in_specs=[in_vmem()] * len(inputs),
        out_specs=[in_vmem()] * len(outs),
        out_shape=outs,
        scratch_shapes=[pltpu.VMEM((d // KEYS, 2, ROWS * pages, KEYS), F32)],
        compiler_params=limit(VMEM_LIMIT),
        cost_estimate=cost(10**10),
        name="attention_forward",
    )(*map(to_vmem, inputs))


def mlp_call(size, places, x, mixed, masked, t_strips, count, *weights):
    height, width, pages, d = masked.shape
    ff = weights[1].shape[1]
    shape = pltpu.VMEM
    inputs = [x, mixed, masked, *t_strips, count, *weights]
    rest = WIN - SHIFT
    outs = [
        shape((SHIFT, width - SHIFT, pages, d), BF16), shape((rest, width, pages, d), BF16),
        shape((SHIFT, SHIFT, pages, d), BF16),
        shape((d // KEYS, 2, ROWS * pages, KEYS), F32),
        shape((d // KEYS, 2, ROWS * pages, KEYS), F32),
        shape((size // 2, d), BF16), shape((size // 2, d), BF16),
    ]
    return pl.pallas_call(
        mlp_kernel,
        in_specs=[in_smem()] + [in_vmem()] * len(inputs),
        out_specs=[in_vmem()] * len(outs),
        out_shape=outs,
        scratch_shapes=[
            pltpu.VMEM((height, width, pages, d), BF16),
            pltpu.VMEM((size, d), BF16),
            pltpu.VMEM((d // KEYS, 2, TOK * pages, KEYS), F32),
            pltpu.VMEM((d, ff), F32),
            pltpu.VMEM((d, ff), F32),
            pltpu.VMEM((d, d), F32),
            pltpu.VMEM((8, ff), F32),
            pltpu.VMEM((4, 8, d), F32),
        ],
        compiler_params=limit(VMEM_LIMIT),
        cost_estimate=cost(10**10),
        name="mlp_forward_backward",
    )(places, *map(to_vmem, inputs))


def backward_call(size, places, xw, qkv, probs, dy, do, qkv_w, g1, b1):
    pages, d = xw.shape[1], xw.shape[3]
    heads = probs.shape[2] // ROWS
    shape = pltpu.VMEM
    inputs = [xw, qkv, probs, dy, do, qkv_w, g1, b1]
    rest = WIN - SHIFT
    outs = [
        shape((SHIFT, 2 * WIN - SHIFT, pages, d), F32), shape((SHIFT, SHIFT, pages, d), BF16),
        shape((rest, 2 * WIN, pages, d), BF16), shape((size // 2, d), BF16),
        shape((size // 2, d), BF16),
    ]
    return pl.pallas_call(
        backward_kernel,
        in_specs=[in_smem()] + [in_vmem()] * len(inputs),
        out_specs=[in_vmem()] * len(outs),
        out_shape=outs,
        scratch_shapes=[
            shape((d // KEYS, 2, TOK * pages, KEYS), F32),
            shape((d, 3 * d), F32),
            shape((ROWS, heads * KEYS), F32),
            shape((8, 3 * d), F32),
            shape((2, 8, d), F32),
            shape((ROWS * heads, KEYS), F32),
            shape((size, d), BF16),
        ],
        compiler_params=limit(VMEM_LIMIT),
        cost_estimate=cost(10**10),
        name="attention_backward",
    )(places, *map(to_vmem, inputs))


def finish_call(total, planes, ff, n1, n2, rel_shape, places, *inputs):
    d = inputs[0].shape[1]
    row = (1, d)
    field = (WIN,) + inputs[2].shape[1:]
    shapes = [field, (d, ff), (ff, d), (d, d), (1, ff), row, row, row, row, (d, 3 * d)]
    shapes += [row, row, row, row, rel_shape]
    sizes = (n1 // (2 * planes), n2 // (2 * planes))
    return pl.pallas_call(
        lambda *refs: finish_kernel(total, planes, sizes, *refs),
        in_specs=[in_smem()] + [in_vmem()] * len(inputs),
        out_shape=[jax.ShapeDtypeStruct(s, F32) for s in shapes],
        scratch_shapes=[pltpu.VMEM((n1, d), F32), pltpu.VMEM((n2, d), F32)],
        compiler_params=limit(VMEM_LIMIT),
        name="finish_sums",
    )(places, *map(to_vmem, inputs))


def shards(
    patches, target, kept_mask, ln1_gain, ln1_bias, qkv_weight, query_bias, value_bias, rel_table,
    proj_weight, proj_bias, ln2_gain, ln2_bias, fc1_weight, fc1_bias, fc2_weight, fc2_bias,
):
    pages, height, width, d = patches.shape
    ff = fc1_weight.shape[1]
    rows, cols = lax.axis_size("rows"), lax.axis_size("cols")
    r, c = lax.axis_index("rows"), lax.axis_index("cols")
    planes = 2 * cols
    step = 32 * planes
    tokens = pages * height * width
    vec = lambda a: a.reshape(1, -1)
    n1 = -(-(2 * ff + d + 32) // step) * step
    n2 = -(-(3 * d + 64) // step) * step

    places = jnp.stack([r == rows - 1, c == cols - 1, r & 1, ((r >> 1) & 1) * cols + c])
    places = places.astype(jnp.int32)
    patches = patches.transpose(1, 2, 0, 3)
    p_strips = [permute(a, hop) for a, hop in zip(strips_call(patches), strip_hops())]
    masked, *t_strips, count, table = target_call(
        target.transpose(1, 2, 0, 3), kept_mask.transpose(1, 0, 2), rel_table
    )
    t_strips = [permute(a, hop) for a, hop in zip(t_strips, strip_hops())]
    bias = bias_call(places, table)

    g1, b1 = vec(ln1_gain), vec(ln1_bias)
    x, xw, qkv, probs, mixed = attention_call(
        patches, p_strips, qkv_weight, bias, g1, b1, vec(query_bias), vec(value_bias)
    )
    out_stays, out_up, out_side, dy, do, mine, other = mlp_call(
        n1, places, x, mixed, masked, t_strips, count, proj_weight, fc1_weight, fc2_weight,
        vec(proj_bias), vec(ln2_gain), vec(ln2_bias), vec(fc1_bias), vec(fc2_bias),
    )

    to_right, to_below = (lambda r, c: (r, c + 1)), (lambda r, c: (r + 1, c))
    out_up = permute(out_up, to_below)

    pieces = split_call(places, mine, permute(other, core_hop))
    got = plane_share(pieces)
    do = after(do, pieces)
    stays, side, up, mine2, other2 = backward_call(
        n2, places, xw, qkv, probs, dy, do, qkv_weight, g1, b1
    )
    got, out_up = after((got, out_up), mine2)
    piece = sum_call(got)
    mine2, other2, up, out_up = after((mine2, other2, up, out_up), piece)
    up = permute(up, to_below)
    pieces2 = split_call(places, mine2, permute(other2, core_hop))
    got = depth_share(piece)
    got2 = plane_share(pieces2)
    piece2 = sum_call(got2)
    side, up = after((side, up), piece2)
    side = permute(side_call(out_up, out_side, up, side), to_right)
    got2 = depth_share(piece2)
    piece = sum_call(got)
    piece2 = sum_call(got2)

    piece = join_call([piece, piece2])
    piece, side = after((piece, side), side)
    mine = join_call(plane_share([piece] * planes))
    other = permute(mine, core_hop)
    rest = WIN - SHIFT
    top = jnp.concatenate([side[:rest], out_up[:, :-SHIFT]], 1)
    bottom = jnp.concatenate([side[rest:WIN], out_stays], 1)
    output = jnp.concatenate([top, bottom], 0)
    mine, output = after((mine, output), output)
    total = float(tokens * rows * cols)
    (
        grad, fc1_g, fc2_g, proj_g, fc1_bg, g2_g, b2_g, fc2_bg, proj_bg, qkv_g, g1_g, b1_g, q_bg,
        v_bg, rel_g,
    ) = finish_call(
        total, planes, ff, n1, n2, rel_table.shape, places, mine, other, up, side[WIN:], stays
    )
    flat = lambda a: a.reshape(-1)
    return (
        output.transpose(2, 0, 1, 3),
        grad.transpose(2, 0, 1, 3),
        flat(g1_g),
        flat(b1_g),
        qkv_g,
        flat(q_bg),
        flat(v_bg),
        rel_g,
        proj_g,
        flat(proj_bg),
        flat(g2_g),
        flat(b2_g),
        fc1_g,
        flat(fc1_bg),
        fc2_g,
        flat(fc2_bg),
    )


def solution(mesh):
    field = P(None, "rows", "cols", None)
    return jax.shard_map(
        shards,
        mesh=mesh,
        in_specs=(field, field, P(None, "rows", "cols")) + (P(),) * 14,
        out_specs=(field, field) + (P(),) * 14,
        check_vma=False,
    )
```

time: 143 us -> 109 us (0.76)
  Pallas kernels: 67.3 us -> 46.1 us
  waiting for transfers between devices: 16.5 us -> 27.8 us
  local copies, waits for them, and re-layouts: 10.6 us -> 0.13 us
  starting transfers between devices: 39.5 us -> 32.6 us
  other arithmetic: 7.29 us -> 1.04 us
    pallas_call x7 -> x16, Pallas kernels: 67.3 us -> 46.1 us  [the longest x1 13.3 us: backward_call(): pl.pallas_call(backward_kernel, in_specs=[in_smem()] + [in_vmem()] * len(...]
    ppermute x35 -> x27, waiting for transfers between devices: 16.5 us -> 27.8 us  [permute(): return lax.ppermute(block, ('rows', 'cols'), route)]
    ppermute x35 -> x27, starting transfers between devices: 39.5 us -> 32.6 us  [permute(): return lax.ppermute(block, ('rows', 'cols'), route)]
    slice x6 -> x3, local copies, waits for them, and re-layouts: 4.17 us -> 0.05 us  [the longest x2 0.04 us: shards(): top = jnp.concatenate([side[:rest], out_up[:, :-SHIFT]], 1)]
    unnamed x44 -> x28, local copies, waits for them, and re-layouts: 3.43 us -> 0.08 us
    transpose x2 -> x0, other arithmetic: 2.91 us -> none  [the longest x1 1.95 us: shards(): grad.transpose(2, 0, 1, 3)]
    convert_element_type x10 -> x0, other arithmetic: 2.85 us -> none  [the longest x6 1.4 us: tree_sum(): return parts[0].astype(BF16)]
    squeeze x4 -> x0, local copies, waits for them, and re-layouts: 2.25 us -> none  [the longest x2 2.17 us: core_scatter(): lax.dynamic_index_in_dim(halves, 1 - core, 0, False)]
  transfers between devices with their start and end apart: 35 -> 27, of which waited for: 11 -> 12; matrix products, arithmetic and copies ran while one was open for 9% -> 1% of each run, Pallas kernels for 35% -> 26%
where the time goes in v3:
time: 109 us
  Pallas kernels  46.1 us (42%)
  starting transfers between devices  32.6 us (30%)
  waiting for transfers between devices  27.8 us (26%)
  between operations  1.11 us (1%)
    ppermute x27, starting transfers between devices, permute(): return lax.ppermute(block, ('rows', 'cols'), route)  32.6 us
    ppermute x27, waiting for transfers between devices, permute(): return lax.ppermute(block, ('rows', 'cols'), route)  27.8 us
    pallas_call x1, Pallas kernels, backward_call(): pl.pallas_call(backward_kernel, in_specs=[in_smem()] + [in_vmem()] * len(...  13.3 us
    pallas_call x1, Pallas kernels, mlp_call(): pl.pallas_call(mlp_kernel, in_specs=[in_smem()] + [in_vmem()] * len(input...  12.3 us
    pallas_call x1, Pallas kernels, attention_call(): pl.pallas_call(attention_kernel, in_specs=[in_vmem()] * len(inputs), out_...  10.4 us
    pallas_call x1, Pallas kernels, finish_call(): pl.pallas_call(lambda *refs: finish_kernel(total, planes, sizes, *refs),...  3.04 us
    pallas_call x1, Pallas kernels, target_call(): pl.pallas_call(target_kernel, in_specs=[in_hbm()] * 3, out_specs=[in_vmem...  2.19 us
  transfers between devices with their start and end apart: 27, of which 12 were waited for; matrix products, arithmetic and copies ran while one was open for 1% of the time, Pallas kernels for 26%

profile of v3, /device:TPU:0, one launch (start us, length us, event | category | flops | bytes accessed | tf_op | source)
XLA Modules:
  0.0 108.9 jit_solution(1049209652094529912)
XLA Ops:
  0.7 1.9 %input_strips.1 = (bf16[5,20,8,256]{3,2,1,0:T(8,128)(2,1)S(1)}, bf16[5,5,8,256]{3,2,1,0:T(8,128)(2,1)}, bf16[5,5,8,256]{3,2,1,0:T(8,128)(2,1)}) custom-call(bf16[10,20,8,256]{3,2,1,0:T(8,128)(2,1)} %bitcast.27), custom_call_target="tpu_custom_call" | custom-call | tf_op jit(solution)/shard_map/input_strips/pallas_call | solution.py:655
  2.6 5.5 %collective-permute-start = (bf16[5,20,8,256]{3,2,1,0:T(8,128)(2,1)S(1)}, bf16[5,20,8,256]{3,2,1,0:T(8,128)(2,1)S(1)}, u32[]{:S(2)}, u32[]{:S(2)}) collective-permute-start(bf16[5,20,8,256]{3,2,1,0:T(8,128)(2,1)S(1)} %get-tuple-element.81), channel_id=1, source_target_pairs={{0,30},{1,31},{2,0},{3,1},{4,2},{5,3},{6,4},{7,5},{8,6},{9,7},{10,... | collective-permute-start | bytes 1228808 | tf_op jit(solution)/shard_map/ppermute | solution.py:589
  8.1 1.5 %collective-permute-start.1 = (bf16[5,5,8,256]{3,2,1,0:T(8,128)(2,1)}, bf16[5,5,8,256]{3,2,1,0:T(8,128)(2,1)}, u32[]{:S(2)}, u32[]{:S(2)}) collective-permute-start(bf16[5,5,8,256]{3,2,1,0:T(8,128)(2,1)} %get-tuple-element.82), channel_id=1, source_target_pairs={{0,1},{1,0},{2,3},{3,2},{4,5},{5,4},{6,7},{7,6},{8,9},{9,8},{10,11... | collective-permute-start | bytes 307208 | tf_op jit(solution)/shard_map/ppermute | solution.py:589
  9.6 0.4 collective-permute-start.2
  9.9 2.2 %masked_target.1 = (bf16[10,20,8,256]{3,2,1,0:T(8,128)(2,1)S(1)}, bf16[5,20,8,256]{3,2,1,0:T(8,128)(2,1)S(1)}, bf16[5,5,8,256]{3,2,1,0:T(8,128)(2,1)}, bf16[5,5,...) custom-call(bf16[10,20,8,256]{3,2,1,0:T(8,128)(2,1)} %bitcast.41, s32[10,8,20]{2,1,0:T(8,128)} %bitcast.42, ...), custom_call_target="tpu_custom_call" | custom-call | tf_op jit(solution)/shard_map/masked_target/pallas_call | solution.py:667
  12.1 1.6 %collective-permute-start.4 = (bf16[5,5,8,256]{3,2,1,0:T(8,128)(2,1)}, bf16[5,5,8,256]{3,2,1,0:T(8,128)(2,1)S(1)}, u32[]{:S(2)}, u32[]{:S(2)}) collective-permute-start(bf16[5,5,8,256]{3,2,1,0:T(8,128)(2,1)} %get-tuple-element.89), channel_id=1, source_target_pairs={{0,1},{1,0},{2,3},{3,2},{4,5},{5,4},{6,7},{7,6},{8,9},{9,8},{10,11... | collective-permute-start | bytes 307208 | tf_op jit(solution)/shard_map/ppermute | solution.py:589
  13.7 0.2 collective-permute-start.5
  13.9 0.1 pad_add_fusion.edge.places.refs_0_
  14.0 1.3 %attention_bias.1.bias = f32[2,832,128]{2,1,0:T(8,128)S(1)} custom-call(s32[4]{0:T(128)S(1)} %pad_add_fusion.edge.places.refs_0_, f32[8,361]{1,0:T(8,128)S(1)} %get-tuple-element.84.table), custom_call_target="tpu_custom_call" | custom-call | tf_op jit(solution)/shard_map/attention_bias/pallas_call | solution.py:722
  15.3 0.0 collective-permute-done.1.right
  15.4 0.6 collective-permute-start.3
  15.9 0.4 collective-permute-done.2.corner
  16.3 0.0 collective-permute-done.low
  16.4 0.0 copy-start.1
  16.4 0.0 copy-start.2
  16.4 0.0 copy-start.4
  16.4 0.0 copy-start.5
  16.4 0.0 copy-start.8
  16.4 0.0 copy-start.9
  16.5 0.0 copy-start.10
  16.5 0.0 copy-start.11
  16.5 10.4 %attention_forward.1 = (bf16[1600,256]{1,0:T(8,128)(2,1)S(1)}, bf16[2,8,104,256]{3,2,1,0:T(8,128)(2,1)S(1)}, bf16[2,8,128,768]{3,2,1,0:T(8,128)(2,1)S(1)}, bf16[...) custom-call(bf16[10,20,8,256]{3,2,1,0:T(8,128)(2,1)S(1)} %bitcast.28, ...), custom_call_target="tpu_custom_call" | custom-call | flops 10000000000 | bytes 10000000 | tf_op jit(solution)/shard_map/attention_forward/pallas_call | solution.py:750
  26.9 0.0 collective-permute-done.4.t_right
  27.1 12.3 %mlp_forward_backward.1 = (bf16[5,15,8,256]{3,2,1,0:T(8,128)(2,1)S(1)}, bf16[5,20,8,256]{3,2,1,0:T(8,128)(2,1)S(1)}, bf16[5,5,8,256]{3,2,1,0:T(8,128)(2,1)S(1)},...) custom-call(s32[4]{0:T(128)S(1)} %pad_add_fusion.edge.places.refs_0_, ...), custom_call_target="tpu_custom_call" | custom-call | flops 10000000000 | bytes 10000000 | tf_op jit(solution)/shard_map/mlp_forward_backward/pallas_call | solution.py:775
  39.4 0.1 collective-permute-start.6
  39.5 0.5 collective-permute-start.10
  40.0 1.5 %collective-permute-done.6.other = bf16[1216,256]{1,0:T(8,128)(2,1)S(1)} collective-permute-done((bf16[1216,256]{1,0:T(8,128)(2,1)S(1)}, bf16[1216,256]{1,0:T(8,128)(2,1)S(1)}, u32[]{:S(2)}, u32[]{:S(2)}) %collective-permute-start.6) | collective-permute-done | bytes 622624 | tf_op jit(solution)/shard_map/ppermute | solution.py:589
  41.5 0.7 split_sums.2
  42.2 1.7 %collective-permute-start.7 = (bf16[304,256]{1,0:T(8,128)(2,1)S(1)}, bf16[304,256]{1,0:T(8,128)(2,1)S(1)}, u32[]{:S(2)}, u32[]{:S(2)}) collective-permute-start(bf16[304,256]{1,0:T(8,128)(2,1)S(1)} %get-tuple-element.95), channel_id=1, source_target_pairs={{0,1},{1,0},{2,3},{3,2},{4,5},{5,4},{6,7},{7,6},{8,9},{9,8},{10,11... | collective-permute-start | bytes 466952 | tf_op jit(solution)/shard_map/ppermute | solution.py:589
  43.9 1.0 collective-permute-start.8
  44.9 0.9 collective-permute-start.9
  45.8 13.3 %attention_backward.1 = (f32[5,15,8,256]{3,2,1,0:T(8,128)S(1)}, bf16[5,5,8,256]{3,2,1,0:T(8,128)(2,1)S(1)}, bf16[5,20,8,256]{3,2,1,0:T(8,128)(2,1)S(1)}, bf16[44...) custom-call(s32[4]{0:T(128)S(1)} %pad_add_fusion.edge.places.refs_0_, bf16[2,8,104,256]{3,2,1,0:T(8,128)(2,1)S(1)} %get-tuple-element.99.xw, ...), custom_call_target="tpu_custom_call" | custom-call | flops 10000000000 | bytes 10000000 | tf_op jit(solution)/shard_map/attention_backward/pallas_call | solution.py:807
  59.1 0.1 add_pieces.4.refs_0_
  59.2 0.1 collective-permute-start.21
  59.2 1.2 %collective-permute-start.14 = (bf16[448,256]{1,0:T(8,128)(2,1)S(1)}, bf16[448,256]{1,0:T(8,128)(2,1)S(1)}, u32[]{:S(2)}, u32[]{:S(2)}) collective-permute-start(bf16[448,256]{1,0:T(8,128)(2,1)S(1)} %get-tuple-element.114), channel_id=1, source_target_pairs={{0,2},{1,3},{2,0},{3,1},{4,6},{5,7},{6,4},{7,5},{8,10},{9,11},{10,... | collective-permute-start | bytes 688136 | tf_op jit(solution)/shard_map/ppermute | solution.py:589
  60.5 1.1 %collective-permute-done.14.other = bf16[448,256]{1,0:T(8,128)(2,1)S(1)} collective-permute-done((bf16[448,256]{1,0:T(8,128)(2,1)S(1)}, bf16[448,256]{1,0:T(8,128)(2,1)S(1)}, u32[]{:S(2)}, u32[]{:S(2)}) %collective-permute-start.14) | collective-permute-done | bytes 229408 | tf_op jit(solution)/shard_map/ppermute | solution.py:589
  61.6 0.6 split_sums.3
  62.2 1.6 %collective-permute-start.15 = (bf16[112,256]{1,0:T(8,128)(2,1)S(1)}, bf16[112,256]{1,0:T(8,128)(2,1)S(1)}, u32[]{:S(2)}, u32[]{:S(2)}) collective-permute-start(bf16[112,256]{1,0:T(8,128)(2,1)S(1)} %get-tuple-element.116), channel_id=1, source_target_pairs={{0,1},{1,0},{2,3},{3,2},{4,5},{5,4},{6,7},{7,6},{8,9},{9,8},{10,11... | collective-permute-start | bytes 172040 | tf_op jit(solution)/shard_map/ppermute | solution.py:589
  63.8 0.5 collective-permute-start.16
  64.3 1.5 %collective-permute-start.17 = (bf16[112,256]{1,0:T(8,128)(2,1)S(1)}, bf16[112,256]{1,0:T(8,128)(2,1)S(1)}, u32[]{:S(2)}, u32[]{:S(2)}) collective-permute-start(bf16[112,256]{1,0:T(8,128)(2,1)S(1)} %get-tuple-element.118), channel_id=1, source_target_pairs={{0,5},{1,4},{2,7},{3,6},{4,1},{5,0},{6,3},{7,2},{8,13},{9,12},{10,... | collective-permute-start | bytes 172040 | tf_op jit(solution)/shard_map/ppermute | solution.py:589
  65.8 0.7 collective-permute-done.15.refs_1_
  66.5 5.3 %collective-permute-done.16.refs_2_ = bf16[112,256]{1,0:T(8,128)(2,1)S(1)} collective-permute-done((bf16[112,256]{1,0:T(8,128)(2,1)S(1)}, bf16[112,256]{1,0:T(8,128)(2,1)S(1)}, u32[]{:S(2)}, u32[]{:S(2)}) %collective-permute-start.16) | collective-permute-done | bytes 57376 | tf_op jit(solution)/shard_map/ppermute | solution.py:589
  71.8 1.7 %collective-permute-start.22 = (bf16[20,5,8,256]{3,2,1,0:T(8,128)(2,1)S(1)}, bf16[20,5,8,256]{3,2,1,0:T(8,128)(2,1)S(1)}, u32[]{:S(2)}, u32[]{:S(2)}) collective-permute-start(bf16[20,5,8,256]{3,2,1,0:T(8,128)(2,1)S(1)} %side_strip.1), channel_id=1, source_target_pairs={{0,1},{1,0},{2,3},{3,2},{4,5},{5,4},{6,7},{7,6},{8,9},{9,8},{10,11... | collective-permute-start | bytes 1228808 | tf_op jit(solution)/shard_map/ppermute | solution.py:589
  73.6 0.1 collective-permute-start.13
  73.7 4.3 %collective-permute-start.11 = (bf16[304,256]{1,0:T(8,128)(2,1)S(1)}, bf16[304,256]{1,0:T(8,128)(2,1)S(1)}, u32[]{:S(2)}, u32[]{:S(2)}) collective-permute-start(bf16[304,256]{1,0:T(8,128)(2,1)S(1)} %add_pieces.4.refs_0_), channel_id=1, source_target_pairs={{0,8},{1,9},{2,10},{3,11},{4,12},{5,13},{6,14},{7,15},{8,0},{9,1},... | collective-permute-start | bytes 466952 | tf_op jit(solution)/shard_map/ppermute | solution.py:589
  78.0 0.1 collective-permute-start.20
  78.1 4.3 %collective-permute-done.13.refs_3_ = bf16[304,256]{1,0:T(8,128)(2,1)S(1)} collective-permute-done((bf16[304,256]{1,0:T(8,128)(2,1)S(1)}, bf16[304,256]{1,0:T(8,128)(2,1)S(1)}, u32[]{:S(2)}, u32[]{:S(2)}) %collective-permute-start.13) | collective-permute-done | bytes 155680 | tf_op jit(solution)/shard_map/ppermute | solution.py:589
  82.4 3.6 %collective-permute-start.19 = (bf16[112,256]{1,0:T(8,128)(2,1)S(1)}, bf16[112,256]{1,0:T(8,128)(2,1)S(1)}, u32[]{:S(2)}, u32[]{:S(2)}) collective-permute-start(bf16[112,256]{1,0:T(8,128)(2,1)S(1)} %add_pieces.6.refs_0_), channel_id=1, source_target_pairs={{0,16},{1,17},{2,18},{3,19},{4,20},{5,21},{6,22},{7,23},{8,24},{9,... | collective-permute-start | bytes 172040 | tf_op jit(solution)/shard_map/ppermute | solution.py:589
  86.0 3.2 %collective-permute-done.12.refs_2_ = bf16[304,256]{1,0:T(8,128)(2,1)S(1)} collective-permute-done((bf16[304,256]{1,0:T(8,128)(2,1)S(1)}, bf16[304,256]{1,0:T(8,128)(2,1)S(1)}, u32[]{:S(2)}, u32[]{:S(2)}) %collective-permute-start.12) | collective-permute-done | bytes 155680 | tf_op jit(solution)/shard_map/ppermute | solution.py:589
  89.2 0.5 collective-permute-start.18
  89.7 0.1 add_pieces.5.refs_0_
  89.8 0.0 collective-permute-done.20.refs_3_
  89.8 1.9 %collective-permute-done.19.refs_2_ = bf16[112,256]{1,0:T(8,128)(2,1)S(1)} collective-permute-done((bf16[112,256]{1,0:T(8,128)(2,1)S(1)}, bf16[112,256]{1,0:T(8,128)(2,1)S(1)}, u32[]{:S(2)}, u32[]{:S(2)}) %collective-permute-start.19) | collective-permute-done | bytes 57376 | tf_op jit(solution)/shard_map/ppermute | solution.py:589
  91.8 1.6 %collective-permute-done.18.refs_1_ = bf16[112,256]{1,0:T(8,128)(2,1)S(1)} collective-permute-done((bf16[112,256]{1,0:T(8,128)(2,1)S(1)}, bf16[112,256]{1,0:T(8,128)(2,1)S(1)}, u32[]{:S(2)}, u32[]{:S(2)}) %collective-permute-start.18) | collective-permute-done | bytes 57376 | tf_op jit(solution)/shard_map/ppermute | solution.py:589
  93.5 0.1 collective-permute-start.25
  93.5 3.0 %collective-permute-start.24 = (bf16[416,256]{1,0:T(8,128)(2,1)S(1)}, bf16[416,256]{1,0:T(8,128)(2,1)S(1)}, u32[]{:S(2)}, u32[]{:S(2)}) collective-permute-start(bf16[416,256]{1,0:T(8,128)(2,1)S(1)} %join_pieces.2.refs_0_), channel_id=1, source_target_pairs={{0,4},{1,5},{2,6},{3,7},{4,0},{5,1},{6,2},{7,3},{8,12},{9,13},{10,... | collective-permute-start | bytes 638984 | tf_op jit(solution)/shard_map/ppermute | solution.py:589
  96.5 0.5 collective-permute-start.23
  97.0 4.5 %collective-permute-done.25.refs_3_ = bf16[416,256]{1,0:T(8,128)(2,1)S(1)} collective-permute-done((bf16[416,256]{1,0:T(8,128)(2,1)S(1)}, bf16[416,256]{1,0:T(8,128)(2,1)S(1)}, u32[]{:S(2)}, u32[]{:S(2)}) %collective-permute-start.25) | collective-permute-done | bytes 213024 | tf_op jit(solution)/shard_map/ppermute | solution.py:589
  101.5 1.8 %collective-permute-done.24.refs_2_ = bf16[416,256]{1,0:T(8,128)(2,1)S(1)} collective-permute-done((bf16[416,256]{1,0:T(8,128)(2,1)S(1)}, bf16[416,256]{1,0:T(8,128)(2,1)S(1)}, u32[]{:S(2)}, u32[]{:S(2)}) %collective-permute-start.24) | collective-permute-done | bytes 213024 | tf_op jit(solution)/shard_map/ppermute | solution.py:589
  103.3 0.1 join_pieces.3.refs_1_
  103.4 0.1 collective-permute-start.26
  103.5 1.0 maximum_maximum_fusion
  104.5 1.3 %collective-permute-done.26.refs_2_ = bf16[1664,256]{1,0:T(8,128)(2,1)S(1)} collective-permute-done((bf16[1664,256]{1,0:T(8,128)(2,1)S(1)}, bf16[1664,256]{1,0:T(8,128)(2,1)S(1)}, u32[]{:S(2)}, u32[]{:S(2)}) %collective-permute-start.26) | collective-permute-done | bytes 852000 | tf_op jit(solution)/shard_map/ppermute | solution.py:589
  105.8 3.0 %finish_sums.1 = (f32[10,20,8,256]{3,2,1,0:T(8,128)}, f32[256,1024]{1,0:T(8,128)}, f32[1024,256]{1,0:T(8,128)}, f32[256,256]{1,0:T(8,128)}, f32[1,1024]{1,0:T(1,...) custom-call(s32[4]{0:T(128)S(1)} %pad_add_fusion.edge.places.refs_0_, ...), custom_call_target="tpu_custom_call" | custom-call | tf_op jit(solution)/shard_map/finish_sums/pallas_call | solution.py:834
  (39 shorter events, 0.2 us)
Async XLA Ops:
  0.6 15.7 %copy-start = (bf16[8,10,20,256]{3,0,2,1:T(8,128)(2,1)S(1)}, bf16[8,10,20,256]{3,0,2,1:T(8,128)(2,1)}, u32[]{:S(2)}) copy-start(bf16[8,10,20,256]{3,0,2,1:T(8,128)(2,1)} %param.17) | copy-start | bytes 2457604
  0.7 15.7 %copy-start.3 = (bf16[256,768]{1,0:T(8,128)(2,1)S(1)}, bf16[256,768]{1,0:T(8,128)(2,1)}, u32[]{:S(2)}) copy-start(bf16[256,768]{1,0:T(8,128)(2,1)} %qkv_w.3) | copy-start | bytes 1179652
  0.7 15.7 %copy-start.7 = (f32[256]{0:T(256)S(1)}, f32[256]{0:T(256)}, u32[]{:S(2)}) copy-start(f32[256]{0:T(256)} %param.24) | copy-start | bytes 3076
  0.7 15.7 %copy-start.6 = (f32[256]{0:T(256)S(1)}, f32[256]{0:T(256)}, u32[]{:S(2)}) copy-start(f32[256]{0:T(256)} %param.23) | copy-start | bytes 3076
  0.7 15.7 %copy-start.13 = (f32[256]{0:T(256)S(1)}, f32[256]{0:T(256)}, u32[]{:S(2)}) copy-start(f32[256]{0:T(256)} %param.21) | copy-start | bytes 3076
  0.7 15.7 %copy-start.12 = (f32[256]{0:T(256)S(1)}, f32[256]{0:T(256)}, u32[]{:S(2)}) copy-start(f32[256]{0:T(256)} %param.20) | copy-start | bytes 3076
  2.6 13.8 %collective-permute-start = (bf16[5,20,8,256]{3,2,1,0:T(8,128)(2,1)S(1)}, bf16[5,20,8,256]{3,2,1,0:T(8,128)(2,1)S(1)}, u32[]{:S(2)}, u32[]{:S(2)}) collective-permute-start(bf16[5,20,8,256]{3,2,1,0:T(8,128)(2,1)S(1)} %get-tuple-element.81), channel_id=1, source_target_pairs={{0,30},{1,31},{2,0},{3,1},{4,2},{5,3},{6,4},{7,5},{8,6},{9,7},{10,... | collective-permute-start | bytes 1228808 | tf_op jit(solution)/shard_map/ppermute | solution.py:589
  8.1 7.3 %collective-permute-start.1 = (bf16[5,5,8,256]{3,2,1,0:T(8,128)(2,1)}, bf16[5,5,8,256]{3,2,1,0:T(8,128)(2,1)}, u32[]{:S(2)}, u32[]{:S(2)}) collective-permute-start(bf16[5,5,8,256]{3,2,1,0:T(8,128)(2,1)} %get-tuple-element.82), channel_id=1, source_target_pairs={{0,1},{1,0},{2,3},{3,2},{4,5},{5,4},{6,7},{7,6},{8,9},{9,8},{10,11... | collective-permute-start | bytes 307208 | tf_op jit(solution)/shard_map/ppermute | solution.py:589
  9.6 6.8 %collective-permute-start.2 = (bf16[5,5,8,256]{3,2,1,0:T(8,128)(2,1)}, bf16[5,5,8,256]{3,2,1,0:T(8,128)(2,1)}, u32[]{:S(2)}, u32[]{:S(2)}) collective-permute-start(bf16[5,5,8,256]{3,2,1,0:T(8,128)(2,1)} %get-tuple-element.83), channel_id=1, source_target_pairs={{0,31},{1,30},{2,1},{3,0},{4,3},{5,2},{6,5},{7,4},{8,7},{9,6},{10,... | collective-permute-start | bytes 307208 | tf_op jit(solution)/shard_map/ppermute | solution.py:589
  12.1 14.8 %collective-permute-start.4 = (bf16[5,5,8,256]{3,2,1,0:T(8,128)(2,1)}, bf16[5,5,8,256]{3,2,1,0:T(8,128)(2,1)S(1)}, u32[]{:S(2)}, u32[]{:S(2)}) collective-permute-start(bf16[5,5,8,256]{3,2,1,0:T(8,128)(2,1)} %get-tuple-element.89), channel_id=1, source_target_pairs={{0,1},{1,0},{2,3},{3,2},{4,5},{5,4},{6,7},{7,6},{8,9},{9,8},{10,11... | collective-permute-start | bytes 307208 | tf_op jit(solution)/shard_map/ppermute | solution.py:589
  13.7 13.3 %collective-permute-start.5 = (bf16[5,5,8,256]{3,2,1,0:T(8,128)(2,1)}, bf16[5,5,8,256]{3,2,1,0:T(8,128)(2,1)S(1)}, u32[]{:S(2)}, u32[]{:S(2)}) collective-permute-start(bf16[5,5,8,256]{3,2,1,0:T(8,128)(2,1)} %get-tuple-element.90), channel_id=1, source_target_pairs={{0,31},{1,30},{2,1},{3,0},{4,3},{5,2},{6,5},{7,4},{8,7},{9,6},{10,... | collective-permute-start | bytes 307208 | tf_op jit(solution)/shard_map/ppermute | solution.py:589
  15.4 11.6 %collective-permute-start.3 = (bf16[5,20,8,256]{3,2,1,0:T(8,128)(2,1)S(1)}, bf16[5,20,8,256]{3,2,1,0:T(8,128)(2,1)S(1)}, u32[]{:S(2)}, u32[]{:S(2)}) collective-permute-start(bf16[5,20,8,256]{3,2,1,0:T(8,128)(2,1)S(1)} %get-tuple-element.88), channel_id=1, source_target_pairs={{0,30},{1,31},{2,0},{3,1},{4,2},{5,3},{6,4},{7,5},{8,6},{9,7},{10,... | collective-permute-start | bytes 1228808 | tf_op jit(solution)/shard_map/ppermute | solution.py:589
  16.4 10.6 %copy-start.1 = (bf16[256,1024]{1,0:T(8,128)(2,1)S(1)}, bf16[256,1024]{1,0:T(8,128)(2,1)}, u32[]{:S(2)}) copy-start(bf16[256,1024]{1,0:T(8,128)(2,1)} %fc1_w.1) | copy-start | bytes 1572868
  16.4 10.6 %copy-start.2 = (bf16[1024,256]{1,0:T(8,128)(2,1)S(1)}, bf16[1024,256]{1,0:T(8,128)(2,1)}, u32[]{:S(2)}) copy-start(bf16[1024,256]{1,0:T(8,128)(2,1)} %fc2_w.1) | copy-start | bytes 1572868
  16.4 10.6 %copy-start.4 = (bf16[256,256]{1,0:T(8,128)(2,1)S(1)}, bf16[256,256]{1,0:T(8,128)(2,1)}, u32[]{:S(2)}) copy-start(bf16[256,256]{1,0:T(8,128)(2,1)} %proj_w.1) | copy-start | bytes 393220
  16.4 10.6 %copy-start.5 = (f32[1024]{0:T(1024)S(1)}, f32[1024]{0:T(1024)}, u32[]{:S(2)}) copy-start(f32[1024]{0:T(1024)} %param.31) | copy-start | bytes 12292
  16.4 10.6 %copy-start.8 = (f32[256]{0:T(256)S(1)}, f32[256]{0:T(256)}, u32[]{:S(2)}) copy-start(f32[256]{0:T(256)} %param.27) | copy-start | bytes 3076
  16.4 10.6 %copy-start.9 = (f32[256]{0:T(256)S(1)}, f32[256]{0:T(256)}, u32[]{:S(2)}) copy-start(f32[256]{0:T(256)} %param.28) | copy-start | bytes 3076
  16.5 10.6 %copy-start.10 = (f32[256]{0:T(256)S(1)}, f32[256]{0:T(256)}, u32[]{:S(2)}) copy-start(f32[256]{0:T(256)} %param.29) | copy-start | bytes 3076
  16.5 10.6 %copy-start.11 = (f32[256]{0:T(256)S(1)}, f32[256]{0:T(256)}, u32[]{:S(2)}) copy-start(f32[256]{0:T(256)} %param.33) | copy-start | bytes 3076
  39.4 2.1 %collective-permute-start.6 = (bf16[1216,256]{1,0:T(8,128)(2,1)S(1)}, bf16[1216,256]{1,0:T(8,128)(2,1)S(1)}, u32[]{:S(2)}, u32[]{:S(2)}) collective-permute-start(bf16[1216,256]{1,0:T(8,128)(2,1)S(1)} %get-tuple-element.93), channel_id=1, source_target_pairs={{0,2},{1,3},{2,0},{3,1},{4,6},{5,7},{6,4},{7,5},{8,10},{9,11},{10,... | collective-permute-start | bytes 1867784 | tf_op jit(solution)/shard_map/ppermute | solution.py:589
  39.5 19.6 %collective-permute-start.10 = (bf16[5,20,8,256]{3,2,1,0:T(8,128)(2,1)S(1)}, bf16[5,20,8,256]{3,2,1,0:T(8,128)(2,1)S(1)}, u32[]{:S(2)}, u32[]{:S(2)}) collective-permute-start(bf16[5,20,8,256]{3,2,1,0:T(8,128)(2,1)S(1)} %get-tuple-element.98), channel_id=1, source_target_pairs={{0,2},{1,3},{2,4},{3,5},{4,6},{5,7},{6,8},{7,9},{8,10},{9,11},{10,... | collective-permute-start | bytes 1228808 | tf_op jit(solution)/shard_map/ppermute | solution.py:589
  42.2 16.9 %collective-permute-start.7 = (bf16[304,256]{1,0:T(8,128)(2,1)S(1)}, bf16[304,256]{1,0:T(8,128)(2,1)S(1)}, u32[]{:S(2)}, u32[]{:S(2)}) collective-permute-start(bf16[304,256]{1,0:T(8,128)(2,1)S(1)} %get-tuple-element.95), channel_id=1, source_target_pairs={{0,1},{1,0},{2,3},{3,2},{4,5},{5,4},{6,7},{7,6},{8,9},{9,8},{10,11... | collective-permute-start | bytes 466952 | tf_op jit(solution)/shard_map/ppermute | solution.py:589
  43.9 15.1 %collective-permute-start.8 = (bf16[304,256]{1,0:T(8,128)(2,1)S(1)}, bf16[304,256]{1,0:T(8,128)(2,1)S(1)}, u32[]{:S(2)}, u32[]{:S(2)}) collective-permute-start(bf16[304,256]{1,0:T(8,128)(2,1)S(1)} %get-tuple-element.96), channel_id=1, source_target_pairs={{0,4},{1,5},{2,6},{3,7},{4,0},{5,1},{6,2},{7,3},{8,12},{9,13},{10,... | collective-permute-start | bytes 466952 | tf_op jit(solution)/shard_map/ppermute | solution.py:589
  44.9 14.2 %collective-permute-start.9 = (bf16[304,256]{1,0:T(8,128)(2,1)S(1)}, bf16[304,256]{1,0:T(8,128)(2,1)S(1)}, u32[]{:S(2)}, u32[]{:S(2)}) collective-permute-start(bf16[304,256]{1,0:T(8,128)(2,1)S(1)} %get-tuple-element.97), channel_id=1, source_target_pairs={{0,5},{1,4},{2,7},{3,6},{4,1},{5,0},{6,3},{7,2},{8,13},{9,12},{10,... | collective-permute-start | bytes 466952 | tf_op jit(solution)/shard_map/ppermute | solution.py:589
  59.2 12.6 %collective-permute-start.21 = (bf16[5,20,8,256]{3,2,1,0:T(8,128)(2,1)S(1)}, bf16[5,20,8,256]{3,2,1,0:T(8,128)(2,1)S(1)}, u32[]{:S(2)}, u32[]{:S(2)}) collective-permute-start(bf16[5,20,8,256]{3,2,1,0:T(8,128)(2,1)S(1)} %get-tuple-element.122), channel_id=1, source_target_pairs={{0,2},{1,3},{2,4},{3,5},{4,6},{5,7},{6,8},{7,9},{8,10},{9,11},{10,... | collective-permute-start | bytes 1228808 | tf_op jit(solution)/shard_map/ppermute | solution.py:589
  59.2 2.4 %collective-permute-start.14 = (bf16[448,256]{1,0:T(8,128)(2,1)S(1)}, bf16[448,256]{1,0:T(8,128)(2,1)S(1)}, u32[]{:S(2)}, u32[]{:S(2)}) collective-permute-start(bf16[448,256]{1,0:T(8,128)(2,1)S(1)} %get-tuple-element.114), channel_id=1, source_target_pairs={{0,2},{1,3},{2,0},{3,1},{4,6},{5,7},{6,4},{7,5},{8,10},{9,11},{10,... | collective-permute-start | bytes 688136 | tf_op jit(solution)/shard_map/ppermute | solution.py:589
  62.2 4.3 %collective-permute-start.15 = (bf16[112,256]{1,0:T(8,128)(2,1)S(1)}, bf16[112,256]{1,0:T(8,128)(2,1)S(1)}, u32[]{:S(2)}, u32[]{:S(2)}) collective-permute-start(bf16[112,256]{1,0:T(8,128)(2,1)S(1)} %get-tuple-element.116), channel_id=1, source_target_pairs={{0,1},{1,0},{2,3},{3,2},{4,5},{5,4},{6,7},{7,6},{8,9},{9,8},{10,11... | collective-permute-start | bytes 172040 | tf_op jit(solution)/shard_map/ppermute | solution.py:589
  63.8 8.0 %collective-permute-start.16 = (bf16[112,256]{1,0:T(8,128)(2,1)S(1)}, bf16[112,256]{1,0:T(8,128)(2,1)S(1)}, u32[]{:S(2)}, u32[]{:S(2)}) collective-permute-start(bf16[112,256]{1,0:T(8,128)(2,1)S(1)} %get-tuple-element.117), channel_id=1, source_target_pairs={{0,4},{1,5},{2,6},{3,7},{4,0},{5,1},{6,2},{7,3},{8,12},{9,13},{10,... | collective-permute-start | bytes 172040 | tf_op jit(solution)/shard_map/ppermute | solution.py:589
  64.3 7.5 %collective-permute-start.17 = (bf16[112,256]{1,0:T(8,128)(2,1)S(1)}, bf16[112,256]{1,0:T(8,128)(2,1)S(1)}, u32[]{:S(2)}, u32[]{:S(2)}) collective-permute-start(bf16[112,256]{1,0:T(8,128)(2,1)S(1)} %get-tuple-element.118), channel_id=1, source_target_pairs={{0,5},{1,4},{2,7},{3,6},{4,1},{5,0},{6,3},{7,2},{8,13},{9,12},{10,... | collective-permute-start | bytes 172040 | tf_op jit(solution)/shard_map/ppermute | solution.py:589
  71.8 21.6 %collective-permute-start.22 = (bf16[20,5,8,256]{3,2,1,0:T(8,128)(2,1)S(1)}, bf16[20,5,8,256]{3,2,1,0:T(8,128)(2,1)S(1)}, u32[]{:S(2)}, u32[]{:S(2)}) collective-permute-start(bf16[20,5,8,256]{3,2,1,0:T(8,128)(2,1)S(1)} %side_strip.1), channel_id=1, source_target_pairs={{0,1},{1,0},{2,3},{3,2},{4,5},{5,4},{6,7},{7,6},{8,9},{9,8},{10,11... | collective-permute-start | bytes 1228808 | tf_op jit(solution)/shard_map/ppermute | solution.py:589
  73.6 8.8 %collective-permute-start.13 = (bf16[304,256]{1,0:T(8,128)(2,1)S(1)}, bf16[304,256]{1,0:T(8,128)(2,1)S(1)}, u32[]{:S(2)}, u32[]{:S(2)}) collective-permute-start(bf16[304,256]{1,0:T(8,128)(2,1)S(1)} %add_pieces.4.refs_0_), channel_id=1, source_target_pairs={{0,24},{1,25},{2,26},{3,27},{4,28},{5,29},{6,30},{7,31},{8,16},{9,... | collective-permute-start | bytes 466952 | tf_op jit(solution)/shard_map/ppermute | solution.py:589
  73.7 15.5 %collective-permute-start.12 = (bf16[304,256]{1,0:T(8,128)(2,1)S(1)}, bf16[304,256]{1,0:T(8,128)(2,1)S(1)}, u32[]{:S(2)}, u32[]{:S(2)}) collective-permute-start(bf16[304,256]{1,0:T(8,128)(2,1)S(1)} %add_pieces.4.refs_0_), channel_id=1, source_target_pairs={{0,16},{1,17},{2,18},{3,19},{4,20},{5,21},{6,22},{7,23},{8,24},{9,... | collective-permute-start | bytes 466952 | tf_op jit(solution)/shard_map/ppermute | solution.py:589
  73.7 16.0 %collective-permute-start.11 = (bf16[304,256]{1,0:T(8,128)(2,1)S(1)}, bf16[304,256]{1,0:T(8,128)(2,1)S(1)}, u32[]{:S(2)}, u32[]{:S(2)}) collective-permute-start(bf16[304,256]{1,0:T(8,128)(2,1)S(1)} %add_pieces.4.refs_0_), channel_id=1, source_target_pairs={{0,8},{1,9},{2,10},{3,11},{4,12},{5,13},{6,14},{7,15},{8,0},{9,1},... | collective-permute-start | bytes 466952 | tf_op jit(solution)/shard_map/ppermute | solution.py:589
  78.0 11.9 %collective-permute-start.20 = (bf16[112,256]{1,0:T(8,128)(2,1)S(1)}, bf16[112,256]{1,0:T(8,128)(2,1)S(1)}, u32[]{:S(2)}, u32[]{:S(2)}) collective-permute-start(bf16[112,256]{1,0:T(8,128)(2,1)S(1)} %add_pieces.6.refs_0_), channel_id=1, source_target_pairs={{0,24},{1,25},{2,26},{3,27},{4,28},{5,29},{6,30},{7,31},{8,16},{9,... | collective-permute-start | bytes 172040 | tf_op jit(solution)/shard_map/ppermute | solution.py:589
  82.4 9.4 %collective-permute-start.19 = (bf16[112,256]{1,0:T(8,128)(2,1)S(1)}, bf16[112,256]{1,0:T(8,128)(2,1)S(1)}, u32[]{:S(2)}, u32[]{:S(2)}) collective-permute-start(bf16[112,256]{1,0:T(8,128)(2,1)S(1)} %add_pieces.6.refs_0_), channel_id=1, source_target_pairs={{0,16},{1,17},{2,18},{3,19},{4,20},{5,21},{6,22},{7,23},{8,24},{9,... | collective-permute-start | bytes 172040 | tf_op jit(solution)/shard_map/ppermute | solution.py:589
  89.2 4.2 %collective-permute-start.18 = (bf16[112,256]{1,0:T(8,128)(2,1)S(1)}, bf16[112,256]{1,0:T(8,128)(2,1)S(1)}, u32[]{:S(2)}, u32[]{:S(2)}) collective-permute-start(bf16[112,256]{1,0:T(8,128)(2,1)S(1)} %add_pieces.6.refs_0_), channel_id=1, source_target_pairs={{0,8},{1,9},{2,10},{3,11},{4,12},{5,13},{6,14},{7,15},{8,0},{9,1},... | collective-permute-start | bytes 172040 | tf_op jit(solution)/shard_map/ppermute | solution.py:589
  93.5 8.0 %collective-permute-start.25 = (bf16[416,256]{1,0:T(8,128)(2,1)S(1)}, bf16[416,256]{1,0:T(8,128)(2,1)S(1)}, u32[]{:S(2)}, u32[]{:S(2)}) collective-permute-start(bf16[416,256]{1,0:T(8,128)(2,1)S(1)} %join_pieces.2.refs_0_), channel_id=1, source_target_pairs={{0,5},{1,4},{2,7},{3,6},{4,1},{5,0},{6,3},{7,2},{8,13},{9,12},{10,... | collective-permute-start | bytes 638984 | tf_op jit(solution)/shard_map/ppermute | solution.py:589
  93.5 9.8 %collective-permute-start.24 = (bf16[416,256]{1,0:T(8,128)(2,1)S(1)}, bf16[416,256]{1,0:T(8,128)(2,1)S(1)}, u32[]{:S(2)}, u32[]{:S(2)}) collective-permute-start(bf16[416,256]{1,0:T(8,128)(2,1)S(1)} %join_pieces.2.refs_0_), channel_id=1, source_target_pairs={{0,4},{1,5},{2,6},{3,7},{4,0},{5,1},{6,2},{7,3},{8,12},{9,13},{10,... | collective-permute-start | bytes 638984 | tf_op jit(solution)/shard_map/ppermute | solution.py:589
  96.5 6.8 %collective-permute-start.23 = (bf16[416,256]{1,0:T(8,128)(2,1)S(1)}, bf16[416,256]{1,0:T(8,128)(2,1)S(1)}, u32[]{:S(2)}, u32[]{:S(2)}) collective-permute-start(bf16[416,256]{1,0:T(8,128)(2,1)S(1)} %join_pieces.2.refs_0_), channel_id=1, source_target_pairs={{0,1},{1,0},{2,3},{3,2},{4,5},{5,4},{6,7},{7,6},{8,9},{9,8},{10,11... | collective-permute-start | bytes 638984 | tf_op jit(solution)/shard_map/ppermute | solution.py:589
  103.4 2.4 %collective-permute-start.26 = (bf16[1664,256]{1,0:T(8,128)(2,1)S(1)}, bf16[1664,256]{1,0:T(8,128)(2,1)S(1)}, u32[]{:S(2)}, u32[]{:S(2)}) collective-permute-start(bf16[1664,256]{1,0:T(8,128)(2,1)S(1)} %join_pieces.3.refs_1_), channel_id=1, source_target_pairs={{0,2},{1,3},{2,0},{3,1},{4,6},{5,7},{6,4},{7,5},{8,10},{9,11},{10,... | collective-permute-start | bytes 2555912 | tf_op jit(solution)/shard_map/ppermute | solution.py:589

commit v4 on v3

--- a/solution.py
+++ b/solution.py
@@ -21,6 +21,8 @@
 RELS = 384
 NEVER = -1e30
 PAGES = 8
+BACK_AT_ONCE = 1
+AT_ONCE = 4
 VMEM_LIMIT = 20
 
 
@@ -193,19 +195,6 @@
         at += ref.shape[0]
 
 
-def side_kernel(out_up, out_side, grad_up, grad_side, out):
-    at = 0
-    for ref in (out_up, out_side, grad_up, grad_side):
-        out[at : at + ref.shape[0]] = ref[:, -SHIFT:]
-        at += ref.shape[0]
-
-
-def turn_matrix():
-    at = lax.broadcasted_iota(jnp.int32, (RELS, RELS), 0)
-    to = lax.broadcasted_iota(jnp.int32, (RELS, RELS), 1)
-    return (at + to == SPAN * SPAN - 1).astype(F32).astype(BF16)
-
-
 def split_three(x):
     high = x.astype(BF16)
     rest = x - high.astype(F32)
@@ -217,13 +206,11 @@
     heads = table.shape[0]
     padded[...] = jnp.zeros_like(padded)
     padded[:, : table.shape[1]] = table[...]
-    turn = turn_matrix()
-    high, middle, least = split_three(padded[...])
-    reversed_table = dot(high, turn) + dot(middle, turn) + dot(least, turn)
+    offsets = padded[...]
     moved = []
     for c in range(WIN):
         shift = WIN - 1 - c
-        moved.append(pltpu.roll(reversed_table, RELS - shift, 1) if shift else reversed_table)
+        moved.append(pltpu.roll(offsets, RELS - shift, 1) if shift else offsets)
     stack = jnp.concatenate(moved, 0)
     high, middle, least = split_three(stack)
     squeeze = squeeze_matrix()
@@ -233,20 +220,20 @@
         shift = (WIN - 1 - r) * WIN
         rel = pltpu.roll(wide, 2 * KEYS - shift, 1) if shift else wide
         rel = rel[:, :KEYS]
-        key = lax.broadcasted_iota(jnp.int32, (count, KEYS), 1)
+        query = lax.broadcasted_iota(jnp.int32, (count, KEYS), 1)
         row = lax.broadcasted_iota(jnp.int32, (count, KEYS), 0)
-        across = (key < TOK // 2) if r >= SHIFT else (key >= TOK // 2)
-        key_left = key - WIN * tenth(key) < SHIFT
+        across = (query < TOK // 2) if r >= SHIFT else (query >= TOK // 2)
+        query_left = query - WIN * tenth(query) < SHIFT
         own_left = row < SHIFT * heads
-        beside = key_left != own_left
+        beside = query_left != own_left
         for w in range(2):
             cut_off = across & (edge[0] != 0)
             if w == 1:
                 cut_off = cut_off | (beside & (edge[1] != 0))
             value = rel + jnp.where(cut_off, -100.0, 0.0)
-            out[w, r * count : (r + 1) * count, :] = jnp.where(key < TOK, value, NEVER)
+            out[w, r * count : (r + 1) * count, :] = value
     for w in range(2):
-        out[w, TOK * heads :, :] = jnp.zeros((out.shape[1] - TOK * heads, KEYS), F32)
+        out[w, TOK * heads :, :] = jnp.full((out.shape[1] - TOK * heads, KEYS), NEVER, F32)
 
 
 def attention_kernel(
@@ -262,20 +249,14 @@
                 t, w, : TOK * PAGES, :
             ].astype(BF16)
 
-    @pl.loop(0, PAGES)
-    def _(page):
-        attention_page(
-            page, xf, qkv_w, bias, g1, b1, qb, vb, xw_out, qkv_out, p_out, o_out
-        )
-
-
-def attention_page(page, xf, qkv_w, bias, g1, b1, qb, vb, xw_out, qkv_out, p_out, o_out):
     d = g1.shape[-1]
     heads = d // (KEYS // GROUP)
     scale = (d // heads) ** (-0.5)
-    x = jnp.concatenate([only_tokens(load_rows(xf, w, page_rows(page, ROWS))) for w in range(2)], 0)
-    for w in range(2):
-        xw_out[w, page] = x[w * ROWS : (w + 1) * ROWS].astype(BF16)
+    windows = [(page, w) for page in range(PAGES) for w in range(2)]
+    x = jnp.concatenate(
+        [only_tokens(load_rows(xf, w, page_rows(page, ROWS))) for page, w in windows], 0
+    )
+    xw_out[...] = x.astype(BF16)
     normed, _ = normalize(x)
     attn_in = (normed * g1[...] + b1[...]).astype(BF16)
     proj = dot(attn_in, qkv_w[...])
@@ -285,53 +266,52 @@
     masks = head_masks(ROWS, F32)
     filler = jnp.zeros((KEYS - ROWS, d), F32)
     groups = heads // GROUP
-    scores, values = [], []
-    for w in range(2):
-        rows = slice(w * ROWS, (w + 1) * ROWS)
-        q = jnp.concatenate([q_all[rows], filler], 0).astype(BF16)
-        k = jnp.concatenate([k_all[rows], filler], 0).astype(BF16)
-        v = jnp.concatenate([v_all[rows], filler], 0).astype(BF16)
-        qkv_out[w, page, :, :d] = q
-        qkv_out[w, page, :, d : 2 * d] = k
-        qkv_out[w, page, :, 2 * d :] = v
-        for g in range(groups):
-            lanes = slice(g * KEYS, (g + 1) * KEYS)
-            scores.append(dot_bt(head_rows(q_all[rows, lanes], masks), k[:, lanes]))
-            values.append(v[:, lanes])
-    probs = []
-    for n, s in enumerate(scores):
-        w, g = divmod(n, groups)
-        es = []
-        for h in range(GROUP):
-            rel = bias[w, pl.ds(g * GROUP + h, ROWS, stride=heads), :]
-            sh = s[h * ROWS : (h + 1) * ROWS] * scale + rel
-            e = jnp.exp(sh - jnp.max(sh, -1, keepdims=True))
-            es.append(e * (1.0 / jnp.sum(e, -1, keepdims=True)))
-        p = jnp.concatenate(es, 0).astype(BF16)
-        p_out[w, page, g * GROUP * ROWS : (g + 1) * GROUP * ROWS, :] = p
-        probs.append(p)
-    parts = [own_lanes(dot(p, v)) for p, v in zip(probs, values)]
-    for w in range(2):
-        joined = jnp.concatenate(parts[w * groups : (w + 1) * groups], 1)
-        store_rows(o_out, w, page_rows(page, TOK), joined[:TOK])
+    for start in range(0, len(windows), AT_ONCE):
+        scores, values = [], []
+        some = windows[start : start + AT_ONCE]
+        for n, (page, w) in enumerate(some):
+            rows = slice((start + n) * ROWS, (start + n + 1) * ROWS)
+            q = jnp.concatenate([q_all[rows], filler], 0).astype(BF16)
+            k = jnp.concatenate([k_all[rows], filler], 0).astype(BF16)
+            v = jnp.concatenate([v_all[rows], filler], 0).astype(BF16)
+            qkv_out[w, page, :, :d] = q
+            qkv_out[w, page, :, d : 2 * d] = k
+            qkv_out[w, page, :, 2 * d :] = v
+            for g in range(groups):
+                lanes = slice(g * KEYS, (g + 1) * KEYS)
+                scores.append(dot_bt(head_rows(k_all[rows, lanes], masks), q[:, lanes]))
+                values.append(head_rows(v_all[rows, lanes], masks))
+        probs = []
+        for n, s in enumerate(scores):
+            page, w = some[n // groups]
+            g = n % groups
+            es = []
+            for h in range(GROUP):
+                rel = bias[w, pl.ds(g * GROUP + h, ROWS, stride=heads), :]
+                sh = s[h * ROWS : (h + 1) * ROWS] * scale + rel
+                e = jnp.exp(sh - jnp.max(sh, 0, keepdims=True))
+                es.append(e * (1.0 / jnp.sum(e, 0, keepdims=True)))
+            p = jnp.concatenate(es, 0).astype(BF16)
+            p_out[w, page, g * GROUP * ROWS : (g + 1) * GROUP * ROWS, :] = p
+            probs.append(p)
+        parts = [dot_at(p, v)[:ROWS] for p, v in zip(probs, values)]
+        for n, (page, w) in enumerate(some):
+            joined = jnp.concatenate(parts[n * groups : (n + 1) * groups], 1)
+            store_rows(o_out, w, page_rows(page, TOK), joined[:TOK])
 
 
 def mlp_kernel(
     places, x_in, o_in, t_own, t_low, t_right, t_corner, count,
     proj_w, fc1_w, fc2_w, pb, g2, b2, f1b, f2b,
-    stays, up, side, dy_out, do_out, mine, other,
+    stays, up, side, corner, dy_out, do_out, mine, other,
     frame_out, sums_out, tf, fc1_acc, fc2_acc, proj_acc, fc1_sum, small_sum,
 ):
-    for buf in (fc1_acc, fc2_acc, proj_acc, fc1_sum, small_sum):
-        buf[...] = jnp.zeros_like(buf)
     gather_frame(tf, t_own, t_low, t_right, t_corner)
 
-    @pl.loop(0, 4)
-    def _(step):
-        mlp_chunk(
-            step, x_in, o_in, proj_w, fc1_w, fc2_w, pb, g2, b2, f1b, f2b, frame_out, dy_out, do_out,
-            tf, fc1_acc, fc2_acc, proj_acc, fc1_sum, small_sum,
-        )
+    mlp_step(
+        x_in, o_in, proj_w, fc1_w, fc2_w, pb, g2, b2, f1b, f2b, frame_out, dy_out, do_out,
+        tf, fc1_acc, fc2_acc, proj_acc, fc1_sum, small_sum,
+    )
 
     d = proj_w.shape[0]
     ff = fc1_w.shape[1] // d
@@ -354,23 +334,27 @@
         sums_out[at + 32 :, :] = jnp.zeros((sums_out.shape[0] - at - 32, d), BF16)
     split_halves(places, sums_out, mine, other)
     stays[...] = frame_out[:SHIFT, :-SHIFT]
-    up[...] = frame_out[SHIFT:]
+    up[...] = frame_out[SHIFT:, :-SHIFT]
     side[...] = frame_out[:SHIFT, -SHIFT:]
-
-
-def mlp_chunk(
-    step, x_in, o_in, proj_w, fc1_w, fc2_w, pb, g2, b2, f1b, f2b, frame_out, dy_out, do_out,
+    corner[...] = frame_out[SHIFT:, -SHIFT:]
+
+
+def both_windows(ref):
+    return jnp.concatenate([load_rows(ref, w, slice(0, TOK * PAGES)) for w in range(2)], 0)
+
+
+def mlp_step(
+    x_in, o_in, proj_w, fc1_w, fc2_w, pb, g2, b2, f1b, f2b, frame_out, dy_out, do_out,
     tf, fc1_acc, fc2_acc, proj_acc, fc1_sum, small_sum,
 ):
-    size, d = x_in.shape[0] // 4, x_in.shape[1]
+    d = x_in.shape[1]
     ff = fc1_w.shape[1] // d
-    w, half = step // 2, step % 2
-    rows = pl.ds(pl.multiple_of(half * size, 16), size)
-    o = load_rows(o_in, w, rows).astype(BF16)
-    y = x_in[pl.ds(pl.multiple_of(step * size, 16), size), :].astype(F32) + dot(o, proj_w[...]) + pb[...]
+    tokens = TOK * PAGES
+    o = both_windows(o_in).astype(BF16)
+    y = x_in[...].astype(F32) + dot(o, proj_w[...]) + pb[...]
     normed2, inv2 = normalize(y)
     c = (normed2 * g2[...] + b2[...]).astype(BF16)
-    dr = load_rows(tf, w, rows)
+    dr = both_windows(tf)
     drb = dr.astype(BF16)
     r = y + f2b[...]
     dc = None
@@ -383,49 +367,64 @@
         dh_wide = dot_bt(drb, fc2_w[at, :]) * slope
         dh = dh_wide.astype(BF16)
         r = r + dot(gelu, fc2_w[at, :])
-        fc2_acc[:, at] += dot_at(drb, gelu)
-        fc1_acc[:, at] += dot_at(c, dh)
-        fc1_sum[:, at] += fold(dh.astype(F32))
+        fc2_acc[:, at] = dot_at(drb, gelu)
+        fc1_acc[:, at] = dot_at(c, dh)
+        fc1_sum[:, at] = fold(dh.astype(F32))
         more = dot_bt(dh, fc1_w[:, at])
         dc = more if dc is None else dc + more
-    frame_out[pl.ds(half * SHIFT, SHIFT), pl.ds(w * WIN, WIN)] = r.reshape(
-        SHIFT, WIN, PAGES, d
-    ).astype(BF16)
+    for w in range(2):
+        frame_out[:, w * WIN : (w + 1) * WIN] = (
+            r[w * tokens : (w + 1) * tokens].reshape(WIN, WIN, PAGES, d).astype(BF16)
+        )
     dy = dr + norm_back(dc * g2[...], normed2, inv2)
     dz = dy.astype(BF16)
-    proj_acc[...] += dot_at(o, dz)
-    store_rows(do_out, w, rows, dot_bt(dz, proj_w[...]))
-    store_rows(dy_out, w, rows, dy)
-    small_sum[0] += fold(dc * normed2)
-    small_sum[1] += fold(dc)
-    small_sum[2] += fold(dr)
-    small_sum[3] += fold(dz.astype(F32))
+    proj_acc[...] = dot_at(o, dz)
+    do = dot_bt(dz, proj_w[...])
+    for w in range(2):
+        rows = slice(w * tokens, (w + 1) * tokens)
+        store_rows(do_out, w, slice(0, tokens), do[rows])
+        store_rows(dy_out, w, slice(0, tokens), dy[rows])
+    small_sum[0] = fold(dc * normed2)
+    small_sum[1] = fold(dc)
+    small_sum[2] = fold(dr)
+    small_sum[3] = fold(dz.astype(F32))
 
 
 def backward_kernel(
-    places, xw, qkv, p_in, dy_in, do_in, qkv_w, g1, b1,
-    stays, side, up, mine, other,
-    dx, qkv_acc, rel_acc, col_sum, small_sum, mixed, sums_out,
+    places, xw, qkv, p_in, dy_in, do_in, qkv_w, g1, b1, out_side, out_corner,
+    stays, side, corner, up, mine, other,
+    dx, qkv_acc, rel_acc, col_sum, small_sum, mixed, sums_out, joined_all,
 ):
-    for buf in (qkv_acc, rel_acc, col_sum, small_sum):
-        buf[...] = jnp.zeros_like(buf)
-
-    @pl.loop(0, PAGES)
-    def _(page):
-        backward_page(
-            page, xw, qkv, p_in, dy_in, do_in, qkv_w, g1, b1, dx, qkv_acc, rel_acc, col_sum,
-            small_sum,
-        )
+    rel_acc[...] = jnp.zeros_like(rel_acc)
+    for page in range(0, PAGES, BACK_AT_ONCE):
+        backward_pages(range(page, page + BACK_AT_ONCE), qkv, p_in, do_in, joined_all, rel_acc)
 
     d = g1.shape[-1]
     heads = d // (KEYS // GROUP)
+    joined = joined_all[...]
+    normed, inv = normalize(xw[...].astype(F32))
+    attn_in = (normed * g1[...] + b1[...]).astype(BF16)
+    qkv_acc[...] = dot_at(attn_in, joined)
+    col_sum[...] = fold(joined.astype(F32))
+    da = dot_bt(joined, qkv_w[...])
+    small_sum[0] = fold(da * normed)
+    small_sum[1] = fold(da)
+    back = norm_back(da * g1[...], normed, inv)
+    for page in range(PAGES):
+        rows = page_rows(page, TOK)
+        for w in range(2):
+            at = (2 * page + w) * ROWS
+            store_rows(dx, w, rows, load_rows(dy_in, w, rows) + back[at : at + TOK])
     right = load_rows(dx, 1, slice(None)).reshape(WIN, WIN, PAGES, d)
     left = load_rows(dx, 0, slice(None)).reshape(WIN, WIN, PAGES, d)
     stays[:, :WIN] = left[:SHIFT]
     stays[:, WIN:] = right[:SHIFT, :SHIFT]
-    side[...] = right[:SHIFT, SHIFT:].astype(BF16)
+    side[:SHIFT] = out_side[...]
+    side[SHIFT:] = right[:SHIFT, SHIFT:].astype(BF16)
+    corner[: WIN - SHIFT] = out_corner[...]
+    corner[WIN - SHIFT :] = right[SHIFT:, SHIFT:].astype(BF16)
     up[:, :WIN] = left[SHIFT:].astype(BF16)
-    up[:, WIN:] = right[SHIFT:].astype(BF16)
+    up[:, WIN:] = right[SHIFT:, :SHIFT].astype(BF16)
     for j in range(3):
         sums_out[j * d : (j + 1) * d, :] = qkv_acc[:, j * d : (j + 1) * d].astype(BF16)
     rel = table_gradient(
@@ -447,64 +446,53 @@
     split_halves(places, sums_out, mine, other)
 
 
-def backward_page(
-    page, xw, qkv, p_in, dy_in, do_in, qkv_w, g1, b1, dx, qkv_acc, rel_acc, col_sum, small_sum
-):
-    d = g1.shape[-1]
+def backward_pages(pages, qkv, p_in, do_in, joined_all, rel_acc):
+    d = qkv.shape[-1] // 3
     heads = d // (KEYS // GROUP)
+    groups = heads // GROUP
     scale = (d // heads) ** (-0.5)
     masks = head_masks(ROWS, F32)
-    count = 2
-    groups = heads // GROUP
-    chains = [(n, g) for n in range(count) for g in range(groups)]
-    qs, ks, dos, dps = [], [], [], []
-    for n, g in chains:
+    chains = [(page, w, g) for page in pages for w in range(2) for g in range(groups)]
+    queries, keys, dos, dps = [], [], [], []
+    filler = jnp.zeros((KEYS - ROWS, KEYS), F32)
+    for page, w, g in chains:
         lanes = slice(g * KEYS, (g + 1) * KEYS)
-        qs.append(head_rows(qkv[n, page, :, lanes].astype(F32)[:ROWS], masks))
-        ks.append(qkv[n, page, :, d + g * KEYS : d + (g + 1) * KEYS])
-        v = qkv[n, page, :, 2 * d + g * KEYS : 2 * d + (g + 1) * KEYS]
-        do = only_tokens(do_in[g, n, page_rows(page, ROWS), :])
-        dos.append(head_rows(do, masks))
-        dps.append(dot_bt(dos[-1], v))
+        queries.append(qkv[w, page, :, lanes])
+        k = qkv[w, page, :, d + g * KEYS : d + (g + 1) * KEYS]
+        v = qkv[w, page, :, 2 * d + g * KEYS : 2 * d + (g + 1) * KEYS]
+        keys.append(head_rows(k.astype(F32)[:ROWS], masks))
+        do = only_tokens(do_in[g, w, page_rows(page, ROWS), :])
+        dos.append(jnp.concatenate([do, filler], 0).astype(BF16))
+        dps.append(dot_bt(head_rows(v.astype(F32)[:ROWS], masks), dos[-1]))
     dts = []
     rel_sum = [None] * heads
-    for c, (n, g) in enumerate(chains):
-        p = p_in[n, page, g * GROUP * ROWS : (g + 1) * GROUP * ROWS, :].astype(F32)
+    for c, (page, w, g) in enumerate(chains):
+        p = p_in[w, page, g * GROUP * ROWS : (g + 1) * GROUP * ROWS, :].astype(F32)
         t = p * dps[c]
-        ds = t - p * jnp.sum(t, -1, keepdims=True)
+        ds = []
         for h in range(GROUP):
-            at = g * GROUP + h
-            part = ds[h * ROWS : (h + 1) * ROWS]
-            rel_sum[at] = part if n == 0 else rel_sum[at] + part
-        dts.append((ds * scale).astype(BF16))
-    dqs, dks, dvs = [], [], []
-    for c, (n, g) in enumerate(chains):
-        p = p_in[n, page, g * GROUP * ROWS : (g + 1) * GROUP * ROWS, :]
-        dqs.append(own_lanes(dot(dts[c], ks[c])))
-        dks.append(dot_at(dts[c], qs[c])[:ROWS])
-        dvs.append(dot_at(p, dos[c])[:ROWS])
+            at = slice(h * ROWS, (h + 1) * ROWS)
+            part = t[at] - p[at] * jnp.sum(t[at], 0, keepdims=True)
+            head = g * GROUP + h
+            rel_sum[head] = part if rel_sum[head] is None else rel_sum[head] + part
+            ds.append(part * scale)
+        dts.append(jnp.concatenate(ds, 0).astype(BF16))
     for h in range(heads):
         rel_acc[:, h * KEYS : (h + 1) * KEYS] += rel_sum[h]
-    joined = jnp.concatenate(
-        [
-            jnp.concatenate([part[n * groups + g] for n in range(count)], 0)
-            for part in (dqs, dks, dvs)
-            for g in range(groups)
-        ],
-        1,
-    ).astype(BF16)
-    x = jnp.concatenate([xw[n, page].astype(F32) for n in range(count)], 0)
-    normed, inv = normalize(x)
-    attn_in = (normed * g1[...] + b1[...]).astype(BF16)
-    qkv_acc[...] += dot_at(attn_in, joined)
-    col_sum[...] += fold(joined.astype(F32))
-    da = dot_bt(joined, qkv_w[...])
-    small_sum[0] += fold(da * normed)
-    small_sum[1] += fold(da)
-    back = norm_back(da * g1[...], normed, inv)
-    for n in range(count):
-        rows = page_rows(page, TOK)
-        store_rows(dx, n, rows, load_rows(dy_in, n, rows) + back[n * ROWS : n * ROWS + TOK])
+    parts = {}
+    for c, (page, w, g) in enumerate(chains):
+        p = p_in[w, page, g * GROUP * ROWS : (g + 1) * GROUP * ROWS, :]
+        parts[0, page, w, g] = dot_at(dts[c], keys[c])[:ROWS]
+        parts[1, page, w, g] = own_lanes(dot(dts[c], queries[c]))
+        parts[2, page, w, g] = own_lanes(dot(p, dos[c]))
+    for page in pages:
+        for k in range(3):
+            for g in range(groups):
+                joined = jnp.concatenate([parts[k, page, w, g] for w in range(2)], 0)
+                at = k * d + g * KEYS
+                joined_all[2 * page * ROWS : 2 * (page + 1) * ROWS, at : at + KEYS] = joined.astype(
+                    BF16
+                )
 
 
 def table_gradient(by_head, mixed):
@@ -527,9 +515,7 @@
         shift = WIN - 1 - c
         part = pltpu.roll(part, shift, 1) if shift else part
         total = part if total is None else total + part
-    turn = turn_matrix()
-    high, rest = split_rows(total)
-    return dot(high, turn) + dot(rest, turn)
+    return total
 
 
 def collect(places, buf, mine, other, planes, first, size):
@@ -544,7 +530,7 @@
 
 
 def finish_kernel(
-    total, planes, sizes, places, mine, other, up, side, stays,
+    total, planes, sizes, places, mine, other, up, side, corner, stays,
     grad, fc1, fc2, proj, fc1_b, g2, b2, fc2_b, proj_b, qkv, g1, b1, q_b, v_b, rel, buf1, buf2,
 ):
     collect(places, buf1, mine, other, planes, 0, sizes[0])
@@ -557,9 +543,9 @@
     rows = rows * scale
     wide = scale.reshape(1, 1, 1, d)
     rest = up.shape[0]
-    grad[:rest, :SHIFT] = side[: rest].astype(F32) * wide
-    grad[:rest, SHIFT:] = up[:, :-SHIFT].astype(F32) * wide
-    grad[rest:, :SHIFT] = side[rest:].astype(F32) * wide
+    grad[:rest, :SHIFT] = corner[rest:].astype(F32) * wide
+    grad[:rest, SHIFT:] = up[...].astype(F32) * wide
+    grad[rest:, :SHIFT] = side[SHIFT:].astype(F32) * wide
     grad[rest:, SHIFT:] = stays[...] * wide
     for j in range(ff):
         fc1[:, j * d : (j + 1) * d] = buf1[j * d : (j + 1) * d, :] * scale
@@ -606,11 +592,12 @@
     return [pieces[0]] + [permute(p, plane_hop(k)) for k, p in enumerate(pieces) if k]
 
 
-def depth_share(piece):
-    got = [piece]
-    for k in range(1, lax.axis_size("rows") // 4):
-        got.append(permute(piece, lambda r, c, k=k: (r ^ (4 * k), c)))
-    return got
+def depth_sum(piece):
+    hop = 4
+    while hop < lax.axis_size("rows"):
+        piece = sum_call([piece, permute(piece, lambda r, c, hop=hop: (r ^ hop, c))])
+        hop *= 2
+    return piece
 
 
 def strip_hops():
@@ -713,10 +700,6 @@
     return local_call(join_kernel, sum(a.shape[0] for a in parts), parts, "join_pieces")
 
 
-def side_call(*parts):
-    return local_call(side_kernel, sum(a.shape[0] for a in parts), parts, "side_strip")
-
-
 def bias_call(places, rel_table):
     heads = rel_table.shape[0]
     return pl.pallas_call(
@@ -742,7 +725,7 @@
     inputs = [patches, *p_strips, qkv_w, bias, g1, b1, q_b, v_b]
     outs = [
         shape((tokens, d), BF16),
-        shape((2, pages, ROWS, d), BF16),
+        shape((2 * pages * ROWS, d), BF16),
         shape((2, pages, KEYS, 3 * d), BF16),
         shape((2, pages, heads * ROWS, KEYS), BF16),
         shape((d // KEYS, 2, TOK * pages, KEYS), F32),
@@ -766,8 +749,8 @@
     inputs = [x, mixed, masked, *t_strips, count, *weights]
     rest = WIN - SHIFT
     outs = [
-        shape((SHIFT, width - SHIFT, pages, d), BF16), shape((rest, width, pages, d), BF16),
-        shape((SHIFT, SHIFT, pages, d), BF16),
+        shape((SHIFT, width - SHIFT, pages, d), BF16), shape((rest, width - SHIFT, pages, d), BF16),
+        shape((SHIFT, SHIFT, pages, d), BF16), shape((rest, SHIFT, pages, d), BF16),
         shape((d // KEYS, 2, ROWS * pages, KEYS), F32),
         shape((d // KEYS, 2, ROWS * pages, KEYS), F32),
         shape((size // 2, d), BF16), shape((size // 2, d), BF16),
@@ -793,15 +776,16 @@
     )(places, *map(to_vmem, inputs))
 
 
-def backward_call(size, places, xw, qkv, probs, dy, do, qkv_w, g1, b1):
-    pages, d = xw.shape[1], xw.shape[3]
+def backward_call(size, places, xw, qkv, probs, dy, do, *more):
+    pages, d = probs.shape[1], xw.shape[1]
     heads = probs.shape[2] // ROWS
     shape = pltpu.VMEM
-    inputs = [xw, qkv, probs, dy, do, qkv_w, g1, b1]
+    inputs = [xw, qkv, probs, dy, do, *more]
     rest = WIN - SHIFT
     outs = [
-        shape((SHIFT, 2 * WIN - SHIFT, pages, d), F32), shape((SHIFT, SHIFT, pages, d), BF16),
-        shape((rest, 2 * WIN, pages, d), BF16), shape((size // 2, d), BF16),
+        shape((SHIFT, 2 * WIN - SHIFT, pages, d), F32), shape((2 * SHIFT, SHIFT, pages, d), BF16),
+        shape((2 * rest, SHIFT, pages, d), BF16),
+        shape((rest, 2 * WIN - SHIFT, pages, d), BF16), shape((size // 2, d), BF16),
         shape((size // 2, d), BF16),
     ]
     return pl.pallas_call(
@@ -817,6 +801,7 @@
             shape((2, 8, d), F32),
             shape((ROWS * heads, KEYS), F32),
             shape((size, d), BF16),
+            shape((2 * pages * ROWS, 3 * d), BF16),
         ],
         compiler_params=limit(VMEM_LIMIT),
         cost_estimate=cost(10**10),
@@ -827,7 +812,7 @@
 def finish_call(total, planes, ff, n1, n2, rel_shape, places, *inputs):
     d = inputs[0].shape[1]
     row = (1, d)
-    field = (WIN,) + inputs[2].shape[1:]
+    field = (WIN, 2 * WIN) + inputs[2].shape[2:]
     shapes = [field, (d, ff), (ff, d), (d, d), (1, ff), row, row, row, row, (d, 3 * d)]
     shapes += [row, row, row, row, rel_shape]
     sizes = (n1 // (2 * planes), n2 // (2 * planes))
@@ -870,41 +855,36 @@
     x, xw, qkv, probs, mixed = attention_call(
         patches, p_strips, qkv_weight, bias, g1, b1, vec(query_bias), vec(value_bias)
     )
-    out_stays, out_up, out_side, dy, do, mine, other = mlp_call(
+    out_stays, out_up, out_side, out_corner, dy, do, mine, other = mlp_call(
         n1, places, x, mixed, masked, t_strips, count, proj_weight, fc1_weight, fc2_weight,
         vec(proj_bias), vec(ln2_gain), vec(ln2_bias), vec(fc1_bias), vec(fc2_bias),
     )
 
     to_right, to_below = (lambda r, c: (r, c + 1)), (lambda r, c: (r + 1, c))
+    across = lambda r, c: (r + 1, c + 1)
     out_up = permute(out_up, to_below)
 
     pieces = split_call(places, mine, permute(other, core_hop))
     got = plane_share(pieces)
     do = after(do, pieces)
-    stays, side, up, mine2, other2 = backward_call(
-        n2, places, xw, qkv, probs, dy, do, qkv_weight, g1, b1
+    stays, side, corner, up, mine2, other2 = backward_call(
+        n2, places, xw, qkv, probs, dy, do, qkv_weight, g1, b1, out_side, out_corner
     )
     got, out_up = after((got, out_up), mine2)
     piece = sum_call(got)
     mine2, other2, up, out_up = after((mine2, other2, up, out_up), piece)
-    up = permute(up, to_below)
+
     pieces2 = split_call(places, mine2, permute(other2, core_hop))
-    got = depth_share(piece)
-    got2 = plane_share(pieces2)
-    piece2 = sum_call(got2)
-    side, up = after((side, up), piece2)
-    side = permute(side_call(out_up, out_side, up, side), to_right)
-    got2 = depth_share(piece2)
-    piece = sum_call(got)
-    piece2 = sum_call(got2)
-
+    piece2 = sum_call(plane_share(pieces2))
+    up, side, corner = after((up, side, corner), piece2)
     piece = join_call([piece, piece2])
-    piece, side = after((piece, side), side)
+    up, side, corner = permute(up, to_below), permute(side, to_right), permute(corner, across)
+    piece = depth_sum(piece)
+    piece, up, side, corner = after((piece, up, side, corner), up)
     mine = join_call(plane_share([piece] * planes))
     other = permute(mine, core_hop)
-    rest = WIN - SHIFT
-    top = jnp.concatenate([side[:rest], out_up[:, :-SHIFT]], 1)
-    bottom = jnp.concatenate([side[rest:WIN], out_stays], 1)
+    top = jnp.concatenate([corner[: WIN - SHIFT], out_up], 1)
+    bottom = jnp.concatenate([side[:SHIFT], out_stays], 1)
     output = jnp.concatenate([top, bottom], 0)
     mine, output = after((mine, output), output)
     total = float(tokens * rows * cols)
@@ -912,7 +892,7 @@
         grad, fc1_g, fc2_g, proj_g, fc1_bg, g2_g, b2_g, fc2_bg, proj_bg, qkv_g, g1_g, b1_g, q_bg,
         v_bg, rel_g,
     ) = finish_call(
-        total, planes, ff, n1, n2, rel_table.shape, places, mine, other, up, side[WIN:], stays
+        total, planes, ff, n1, n2, rel_table.shape, places, mine, other, up, side, corner, stays
     )
     flat = lambda a: a.reshape(-1)
     return (

time: 109 us -> 97.1 us (0.89)
  Pallas kernels: 46.1 us -> 35.6 us
  starting transfers between devices: 32.6 us -> 25.9 us
  waiting for transfers between devices: 27.8 us -> 33 us
    ppermute x27 -> x24, starting transfers between devices: 32.6 us -> 25.9 us  [permute(): return lax.ppermute(block, ('rows', 'cols'), route)]
    ppermute x27 -> x24, waiting for transfers between devices: 27.8 us -> 33 us  [permute(): return lax.ppermute(block, ('rows', 'cols'), route)]
    pallas_call x1, Pallas kernels: 13.3 us -> 9.26 us  [backward_call(): pl.pallas_call(backward_kernel, in_specs=[in_smem()] + [in_vmem()] * len(...]
    pallas_call x1, Pallas kernels: 10.4 us -> 7.29 us  [attention_call(): pl.pallas_call(attention_kernel, in_specs=[in_vmem()] * len(inputs), out_...]
    pallas_call x1, Pallas kernels: 12.3 us -> 9.33 us  [mlp_call(): pl.pallas_call(mlp_kernel, in_specs=[in_smem()] + [in_vmem()] * len(input...]
  transfers between devices with their start and end apart: 27 -> 24, of which waited for: 12 -> 15; matrix products, arithmetic and copies ran while one was open for 1% -> 1% of each run, Pallas kernels for 26% -> 21%
where the time goes in v4:
time: 97.1 us; the launch traced here: 96.9 us
  Pallas kernels  35.6 us (37%)
  waiting for transfers between devices  33 us (34%)
  starting transfers between devices  25.9 us (27%)
  between operations  1.21 us (1%)
  other arithmetic  1.05 us (1%)
    ppermute x24, waiting for transfers between devices, permute(): return lax.ppermute(block, ('rows', 'cols'), route)  33 us
    ppermute x24, starting transfers between devices, permute(): return lax.ppermute(block, ('rows', 'cols'), route)  25.9 us
    pallas_call x1, Pallas kernels, mlp_call(): pl.pallas_call(mlp_kernel, in_specs=[in_smem()] + [in_vmem()] * len(input...  9.33 us
    pallas_call x1, Pallas kernels, backward_call(): pl.pallas_call(backward_kernel, in_specs=[in_smem()] + [in_vmem()] * len(...  9.26 us
    pallas_call x1, Pallas kernels, attention_call(): pl.pallas_call(attention_kernel, in_specs=[in_vmem()] * len(inputs), out_...  7.29 us
    pallas_call x1, Pallas kernels, finish_call(): pl.pallas_call(lambda *refs: finish_kernel(total, planes, sizes, *refs),...  3.04 us
    pallas_call x1, Pallas kernels, target_call(): pl.pallas_call(target_kernel, in_specs=[in_hbm()] * 3, out_specs=[in_vmem...  2.19 us
  transfers between devices with their start and end apart: 24, of which 15 were waited for; matrix products, arithmetic and copies ran while one was open for 1% of the time, Pallas kernels for 21%

profile of v4, /device:TPU:0, one launch (start us, length us, event | category | flops | bytes accessed | tf_op | source)
XLA Modules:
  0.0 96.9 jit_solution(5225347903724786018)
XLA Ops:
  0.7 1.9 %input_strips.1 = (bf16[5,20,8,256]{3,2,1,0:T(8,128)(2,1)S(1)}, bf16[5,5,8,256]{3,2,1,0:T(8,128)(2,1)}, bf16[5,5,8,256]{3,2,1,0:T(8,128)(2,1)}) custom-call(bf16[10,20,8,256]{3,2,1,0:T(8,128)(2,1)} %bitcast.27), custom_call_target="tpu_custom_call" | custom-call | tf_op jit(solution)/shard_map/input_strips/pallas_call | solution.py:642
  2.6 5.5 %collective-permute-start = (bf16[5,20,8,256]{3,2,1,0:T(8,128)(2,1)S(1)}, bf16[5,20,8,256]{3,2,1,0:T(8,128)(2,1)S(1)}, u32[]{:S(2)}, u32[]{:S(2)}) collective-permute-start(bf16[5,20,8,256]{3,2,1,0:T(8,128)(2,1)S(1)} %get-tuple-element.86), channel_id=1, source_target_pairs={{0,30},{1,31},{2,0},{3,1},{4,2},{5,3},{6,4},{7,5},{8,6},{9,7},{10,... | collective-permute-start | bytes 1228808 | tf_op jit(solution)/shard_map/ppermute | solution.py:575
  8.1 1.5 %collective-permute-start.1 = (bf16[5,5,8,256]{3,2,1,0:T(8,128)(2,1)}, bf16[5,5,8,256]{3,2,1,0:T(8,128)(2,1)}, u32[]{:S(2)}, u32[]{:S(2)}) collective-permute-start(bf16[5,5,8,256]{3,2,1,0:T(8,128)(2,1)} %get-tuple-element.87), channel_id=1, source_target_pairs={{0,1},{1,0},{2,3},{3,2},{4,5},{5,4},{6,7},{7,6},{8,9},{9,8},{10,11... | collective-permute-start | bytes 307208 | tf_op jit(solution)/shard_map/ppermute | solution.py:575
  9.6 0.4 collective-permute-start.2
  9.9 2.2 %masked_target.1 = (bf16[10,20,8,256]{3,2,1,0:T(8,128)(2,1)S(1)}, bf16[5,20,8,256]{3,2,1,0:T(8,128)(2,1)S(1)}, bf16[5,5,8,256]{3,2,1,0:T(8,128)(2,1)}, bf16[5,5,...) custom-call(bf16[10,20,8,256]{3,2,1,0:T(8,128)(2,1)} %bitcast.41, s32[10,8,20]{2,1,0:T(8,128)} %bitcast.42, ...), custom_call_target="tpu_custom_call" | custom-call | tf_op jit(solution)/shard_map/masked_target/pallas_call | solution.py:654
  12.1 1.6 %collective-permute-start.4 = (bf16[5,5,8,256]{3,2,1,0:T(8,128)(2,1)}, bf16[5,5,8,256]{3,2,1,0:T(8,128)(2,1)S(1)}, u32[]{:S(2)}, u32[]{:S(2)}) collective-permute-start(bf16[5,5,8,256]{3,2,1,0:T(8,128)(2,1)} %get-tuple-element.94), channel_id=1, source_target_pairs={{0,1},{1,0},{2,3},{3,2},{4,5},{5,4},{6,7},{7,6},{8,9},{9,8},{10,11... | collective-permute-start | bytes 307208 | tf_op jit(solution)/shard_map/ppermute | solution.py:575
  13.7 0.2 collective-permute-start.5
  13.9 0.1 pad_add_fusion.edge.places.refs_0_
  14.0 1.1 %attention_bias.1.bias = f32[2,832,128]{2,1,0:T(8,128)S(1)} custom-call(s32[4]{0:T(128)S(1)} %pad_add_fusion.edge.places.refs_0_, f32[8,361]{1,0:T(8,128)S(1)} %get-tuple-element.89.table), custom_call_target="tpu_custom_call" | custom-call | tf_op jit(solution)/shard_map/attention_bias/pallas_call | solution.py:705
  15.1 0.3 collective-permute-done.1.right
  15.3 0.3 collective-permute-start.3
  15.7 0.7 collective-permute-done.2.corner
  16.3 0.0 collective-permute-done.low
  16.4 0.0 copy-start.1
  16.4 0.0 copy-start.2
  16.4 0.0 copy-start.4
  16.4 0.0 copy-start.5
  16.4 0.0 copy-start.8
  16.4 0.0 copy-start.9
  16.5 0.0 copy-start.10
  16.5 0.0 copy-start.11
  16.5 7.3 %attention_forward.1 = (bf16[1600,256]{1,0:T(8,128)(2,1)S(1)}, bf16[1664,256]{1,0:T(8,128)(2,1)S(1)}, bf16[2,8,128,768]{3,2,1,0:T(8,128)(2,1)S(1)}, bf16[2,8,832...) custom-call(bf16[10,20,8,256]{3,2,1,0:T(8,128)(2,1)S(1)} %bitcast.28, ...), custom_call_target="tpu_custom_call" | custom-call | flops 10000000000 | bytes 10000000 | tf_op jit(solution)/shard_map/attention_forward/pallas_call | solution.py:733
  23.8 0.0 collective-permute-done.4.t_right
  23.8 0.0 collective-permute-done.3.t_low
  23.9 9.3 %mlp_forward_backward.1 = (bf16[5,15,8,256]{3,2,1,0:T(8,128)(2,1)S(1)}, bf16[5,15,8,256]{3,2,1,0:T(8,128)(2,1)S(1)}, bf16[5,5,8,256]{3,2,1,0:T(8,128)(2,1)S(1)},...) custom-call(s32[4]{0:T(128)S(1)} %pad_add_fusion.edge.places.refs_0_, ...), custom_call_target="tpu_custom_call" | custom-call | flops 10000000000 | bytes 10000000 | tf_op jit(solution)/shard_map/mlp_forward_backward/pallas_call | solution.py:758
  33.2 0.1 collective-permute-start.6
  33.3 0.5 collective-permute-start.10
  33.8 1.5 %collective-permute-done.6.other = bf16[1216,256]{1,0:T(8,128)(2,1)S(1)} collective-permute-done((bf16[1216,256]{1,0:T(8,128)(2,1)S(1)}, bf16[1216,256]{1,0:T(8,128)(2,1)S(1)}, u32[]{:S(2)}, u32[]{:S(2)}) %collective-permute-start.6) | collective-permute-done | bytes 622624 | tf_op jit(solution)/shard_map/ppermute | solution.py:575
  35.4 0.7 split_sums.2
  36.1 1.7 %collective-permute-start.7 = (bf16[304,256]{1,0:T(8,128)(2,1)S(1)}, bf16[304,256]{1,0:T(8,128)(2,1)S(1)}, u32[]{:S(2)}, u32[]{:S(2)}) collective-permute-start(bf16[304,256]{1,0:T(8,128)(2,1)S(1)} %get-tuple-element.100), channel_id=1, source_target_pairs={{0,1},{1,0},{2,3},{3,2},{4,5},{5,4},{6,7},{7,6},{8,9},{9,8},{10,11... | collective-permute-start | bytes 466952 | tf_op jit(solution)/shard_map/ppermute | solution.py:575
  37.8 0.7 collective-permute-start.8
  38.5 1.1 %collective-permute-start.9 = (bf16[304,256]{1,0:T(8,128)(2,1)S(1)}, bf16[304,256]{1,0:T(8,128)(2,1)S(1)}, u32[]{:S(2)}, u32[]{:S(2)}) collective-permute-start(bf16[304,256]{1,0:T(8,128)(2,1)S(1)} %get-tuple-element.102), channel_id=1, source_target_pairs={{0,5},{1,4},{2,7},{3,6},{4,1},{5,0},{6,3},{7,2},{8,13},{9,12},{10,... | collective-permute-start | bytes 466952 | tf_op jit(solution)/shard_map/ppermute | solution.py:575
  39.6 9.3 %attention_backward.1 = (f32[5,15,8,256]{3,2,1,0:T(8,128)S(1)}, bf16[10,5,8,256]{3,2,1,0:T(8,128)(2,1)S(1)}, bf16[10,5,8,256]{3,2,1,0:T(8,128)(2,1)S(1)}, bf16[5...) custom-call(s32[4]{0:T(128)S(1)} %pad_add_fusion.edge.places.refs_0_, ...), custom_call_target="tpu_custom_call" | custom-call | flops 10000000000 | bytes 10000000 | tf_op jit(solution)/shard_map/attention_backward/pallas_call | solution.py:791
  48.9 0.0 collective-permute-done.10
  48.9 0.1 collective-permute-done.8.refs_2_
  49.0 0.1 add_pieces.4.refs_0_
  49.1 0.1 collective-permute-start.11
  49.2 1.5 %collective-permute-done.11.other = bf16[448,256]{1,0:T(8,128)(2,1)S(1)} collective-permute-done((bf16[448,256]{1,0:T(8,128)(2,1)S(1)}, bf16[448,256]{1,0:T(8,128)(2,1)S(1)}, u32[]{:S(2)}, u32[]{:S(2)}) %collective-permute-start.11) | collective-permute-done | bytes 229408 | tf_op jit(solution)/shard_map/ppermute | solution.py:575
  50.7 0.6 split_sums.3
  51.3 1.8 %collective-permute-start.12 = (bf16[112,256]{1,0:T(8,128)(2,1)S(1)}, bf16[112,256]{1,0:T(8,128)(2,1)S(1)}, u32[]{:S(2)}, u32[]{:S(2)}) collective-permute-start(bf16[112,256]{1,0:T(8,128)(2,1)S(1)} %get-tuple-element.123), channel_id=1, source_target_pairs={{0,1},{1,0},{2,3},{3,2},{4,5},{5,4},{6,7},{7,6},{8,9},{9,8},{10,11... | collective-permute-start | bytes 172040 | tf_op jit(solution)/shard_map/ppermute | solution.py:575
  53.1 0.5 collective-permute-start.13
  53.6 1.2 %collective-permute-start.14 = (bf16[112,256]{1,0:T(8,128)(2,1)S(1)}, bf16[112,256]{1,0:T(8,128)(2,1)S(1)}, u32[]{:S(2)}, u32[]{:S(2)}) collective-permute-start(bf16[112,256]{1,0:T(8,128)(2,1)S(1)} %get-tuple-element.125), channel_id=1, source_target_pairs={{0,5},{1,4},{2,7},{3,6},{4,1},{5,0},{6,3},{7,2},{8,13},{9,12},{10,... | collective-permute-start | bytes 172040 | tf_op jit(solution)/shard_map/ppermute | solution.py:575
  54.8 0.7 collective-permute-done.12.refs_1_
  55.5 2.4 %collective-permute-done.13.refs_2_ = bf16[112,256]{1,0:T(8,128)(2,1)S(1)} collective-permute-done((bf16[112,256]{1,0:T(8,128)(2,1)S(1)}, bf16[112,256]{1,0:T(8,128)(2,1)S(1)}, u32[]{:S(2)}, u32[]{:S(2)}) %collective-permute-start.13) | collective-permute-done | bytes 57376 | tf_op jit(solution)/shard_map/ppermute | solution.py:575
  57.9 0.8 collective-permute-done.14.refs_3_
  58.7 0.1 collective-permute-start.15
  58.8 0.1 collective-permute-start.17
  58.9 5.8 %collective-permute-done.15.refs_1_ = bf16[416,256]{1,0:T(8,128)(2,1)S(1)} collective-permute-done((bf16[416,256]{1,0:T(8,128)(2,1)S(1)}, bf16[416,256]{1,0:T(8,128)(2,1)S(1)}, u32[]{:S(2)}, u32[]{:S(2)}) %collective-permute-start.15) | collective-permute-done | bytes 213024 | tf_op jit(solution)/shard_map/ppermute | solution.py:575
  64.6 0.1 add_pieces.6.refs_0_
  64.7 1.5 %collective-permute-start.16 = (bf16[416,256]{1,0:T(8,128)(2,1)S(1)}, bf16[416,256]{1,0:T(8,128)(2,1)S(1)}, u32[]{:S(2)}, u32[]{:S(2)}) collective-permute-start(bf16[416,256]{1,0:T(8,128)(2,1)S(1)} %add_pieces.6.refs_0_), channel_id=1, source_target_pairs={{0,16},{1,17},{2,18},{3,19},{4,20},{5,21},{6,22},{7,23},{8,24},{9,... | collective-permute-start | bytes 638984 | tf_op jit(solution)/shard_map/ppermute | solution.py:575
  66.1 1.5 %collective-permute-start.18 = (bf16[10,5,8,256]{3,2,1,0:T(8,128)(2,1)S(1)}, bf16[10,5,8,256]{3,2,1,0:T(8,128)(2,1)S(1)}, u32[]{:S(2)}, u32[]{:S(2)}) collective-permute-start(bf16[10,5,8,256]{3,2,1,0:T(8,128)(2,1)S(1)} %get-tuple-element.130), channel_id=1, source_target_pairs={{0,1},{1,0},{2,3},{3,2},{4,5},{5,4},{6,7},{7,6},{8,9},{9,8},{10,11... | collective-permute-start | bytes 614408 | tf_op jit(solution)/shard_map/ppermute | solution.py:575
  67.6 7.1 %collective-permute-done.16.refs_1_ = bf16[416,256]{1,0:T(8,128)(2,1)S(1)} collective-permute-done((bf16[416,256]{1,0:T(8,128)(2,1)S(1)}, bf16[416,256]{1,0:T(8,128)(2,1)S(1)}, u32[]{:S(2)}, u32[]{:S(2)}) %collective-permute-start.16) | collective-permute-done | bytes 213024 | tf_op jit(solution)/shard_map/ppermute | solution.py:575
  74.8 0.1 add_pieces.7.refs_0_
  74.8 1.7 %collective-permute-done.19.refs_5_ = bf16[10,5,8,256]{3,2,1,0:T(8,128)(2,1)S(1)} collective-permute-done((bf16[10,5,8,256]{3,2,1,0:T(8,128)(2,1)S(1)}, bf16[10,5,8,256]{3,2,1,0:T(8,128)(2,1)S(1)}, u32[]{:S(2)}, u32[]{:S(2)}) %collective-permute-start.19) | collective-permute-done | bytes 204832 | tf_op jit(solution)/shard_map/ppermute | solution.py:575
  76.5 4.5 %collective-permute-start.22 = (bf16[416,256]{1,0:T(8,128)(2,1)S(1)}, bf16[416,256]{1,0:T(8,128)(2,1)S(1)}, u32[]{:S(2)}, u32[]{:S(2)}) collective-permute-start(bf16[416,256]{1,0:T(8,128)(2,1)S(1)} %add_pieces.7.refs_0_), channel_id=1, source_target_pairs={{0,5},{1,4},{2,7},{3,6},{4,1},{5,0},{6,3},{7,2},{8,13},{9,12},{10,... | collective-permute-start | bytes 638984 | tf_op jit(solution)/shard_map/ppermute | solution.py:575
  81.0 1.1 %collective-permute-start.20 = (bf16[416,256]{1,0:T(8,128)(2,1)S(1)}, bf16[416,256]{1,0:T(8,128)(2,1)S(1)}, u32[]{:S(2)}, u32[]{:S(2)}) collective-permute-start(bf16[416,256]{1,0:T(8,128)(2,1)S(1)} %add_pieces.7.refs_0_), channel_id=1, source_target_pairs={{0,1},{1,0},{2,3},{3,2},{4,5},{5,4},{6,7},{7,6},{8,9},{9,8},{10,11... | collective-permute-start | bytes 638984 | tf_op jit(solution)/shard_map/ppermute | solution.py:575
  82.1 5.1 %collective-permute-done.22.refs_3_ = bf16[416,256]{1,0:T(8,128)(2,1)S(1)} collective-permute-done((bf16[416,256]{1,0:T(8,128)(2,1)S(1)}, bf16[416,256]{1,0:T(8,128)(2,1)S(1)}, u32[]{:S(2)}, u32[]{:S(2)}) %collective-permute-start.22) | collective-permute-done | bytes 213024 | tf_op jit(solution)/shard_map/ppermute | solution.py:575
  87.2 3.2 %collective-permute-done.21.refs_2_ = bf16[416,256]{1,0:T(8,128)(2,1)S(1)} collective-permute-done((bf16[416,256]{1,0:T(8,128)(2,1)S(1)}, bf16[416,256]{1,0:T(8,128)(2,1)S(1)}, u32[]{:S(2)}, u32[]{:S(2)}) %collective-permute-start.21) | collective-permute-done | bytes 213024 | tf_op jit(solution)/shard_map/ppermute | solution.py:575
  90.4 0.8 collective-permute-done.20.refs_1_
  91.2 0.1 join_pieces.3.refs_1_
  91.3 0.1 collective-permute-start.23
  91.4 1.0 %maximum_maximum_fusion = bf16[10,20,8,256]{3,2,1,0:T(8,128)(2,1)} fusion(bf16[5,15,8,256]{3,2,1,0:T(8,128)(2,1)S(1)} %get-tuple-element.136, bf16[5,5,8,256]{3,2,1,0:T(8,128)(2,1)S(1)} %slice.7, bf16[5,15,8,256]{3,2,1,0:T(8,128)(2,1)S(1)} %collective-permute-done.10, bf16[5,5,8,256]{3,2,1,0:T(8,128)(2,1)S(1)} %slice.6), kind=kLoop, calls=%fused_computation | loop fusion | flops 1228800 | bytes 1638400 | tf_op jit(solution)/shard_map/concatenate | solution.py:888
  92.4 1.4 %collective-permute-done.23.refs_2_ = bf16[1664,256]{1,0:T(8,128)(2,1)S(1)} collective-permute-done((bf16[1664,256]{1,0:T(8,128)(2,1)S(1)}, bf16[1664,256]{1,0:T(8,128)(2,1)S(1)}, u32[]{:S(2)}, u32[]{:S(2)}) %collective-permute-start.23) | collective-permute-done | bytes 852000 | tf_op jit(solution)/shard_map/ppermute | solution.py:575
  93.7 3.0 %finish_sums.1 = (f32[10,20,8,256]{3,2,1,0:T(8,128)}, f32[256,1024]{1,0:T(8,128)}, f32[1024,256]{1,0:T(8,128)}, f32[256,256]{1,0:T(8,128)}, f32[1,1024]{1,0:T(1,...) custom-call(s32[4]{0:T(128)S(1)} %pad_add_fusion.edge.places.refs_0_, ...), custom_call_target="tpu_custom_call" | custom-call | tf_op jit(solution)/shard_map/finish_sums/pallas_call | solution.py:819
  (31 shorter events, 0.1 us)
Async XLA Ops:
  0.6 15.7 %copy-start = (bf16[8,10,20,256]{3,0,2,1:T(8,128)(2,1)S(1)}, bf16[8,10,20,256]{3,0,2,1:T(8,128)(2,1)}, u32[]{:S(2)}) copy-start(bf16[8,10,20,256]{3,0,2,1:T(8,128)(2,1)} %param.17) | copy-start | bytes 2457604
  0.7 15.7 %copy-start.3 = (bf16[256,768]{1,0:T(8,128)(2,1)S(1)}, bf16[256,768]{1,0:T(8,128)(2,1)}, u32[]{:S(2)}) copy-start(bf16[256,768]{1,0:T(8,128)(2,1)} %qkv_w.3) | copy-start | bytes 1179652
  0.7 15.7 %copy-start.7 = (f32[256]{0:T(256)S(1)}, f32[256]{0:T(256)}, u32[]{:S(2)}) copy-start(f32[256]{0:T(256)} %param.24) | copy-start | bytes 3076
  0.7 15.7 %copy-start.6 = (f32[256]{0:T(256)S(1)}, f32[256]{0:T(256)}, u32[]{:S(2)}) copy-start(f32[256]{0:T(256)} %param.23) | copy-start | bytes 3076
  0.7 15.7 %copy-start.13 = (f32[256]{0:T(256)S(1)}, f32[256]{0:T(256)}, u32[]{:S(2)}) copy-start(f32[256]{0:T(256)} %param.21) | copy-start | bytes 3076
  0.7 15.7 %copy-start.12 = (f32[256]{0:T(256)S(1)}, f32[256]{0:T(256)}, u32[]{:S(2)}) copy-start(f32[256]{0:T(256)} %param.20) | copy-start | bytes 3076
  2.6 13.8 %collective-permute-start = (bf16[5,20,8,256]{3,2,1,0:T(8,128)(2,1)S(1)}, bf16[5,20,8,256]{3,2,1,0:T(8,128)(2,1)S(1)}, u32[]{:S(2)}, u32[]{:S(2)}) collective-permute-start(bf16[5,20,8,256]{3,2,1,0:T(8,128)(2,1)S(1)} %get-tuple-element.86), channel_id=1, source_target_pairs={{0,30},{1,31},{2,0},{3,1},{4,2},{5,3},{6,4},{7,5},{8,6},{9,7},{10,... | collective-permute-start | bytes 1228808 | tf_op jit(solution)/shard_map/ppermute | solution.py:575
  8.1 7.3 %collective-permute-start.1 = (bf16[5,5,8,256]{3,2,1,0:T(8,128)(2,1)}, bf16[5,5,8,256]{3,2,1,0:T(8,128)(2,1)}, u32[]{:S(2)}, u32[]{:S(2)}) collective-permute-start(bf16[5,5,8,256]{3,2,1,0:T(8,128)(2,1)} %get-tuple-element.87), channel_id=1, source_target_pairs={{0,1},{1,0},{2,3},{3,2},{4,5},{5,4},{6,7},{7,6},{8,9},{9,8},{10,11... | collective-permute-start | bytes 307208 | tf_op jit(solution)/shard_map/ppermute | solution.py:575
  9.6 6.8 %collective-permute-start.2 = (bf16[5,5,8,256]{3,2,1,0:T(8,128)(2,1)}, bf16[5,5,8,256]{3,2,1,0:T(8,128)(2,1)}, u32[]{:S(2)}, u32[]{:S(2)}) collective-permute-start(bf16[5,5,8,256]{3,2,1,0:T(8,128)(2,1)} %get-tuple-element.88), channel_id=1, source_target_pairs={{0,31},{1,30},{2,1},{3,0},{4,3},{5,2},{6,5},{7,4},{8,7},{9,6},{10,... | collective-permute-start | bytes 307208 | tf_op jit(solution)/shard_map/ppermute | solution.py:575
  12.1 11.7 %collective-permute-start.4 = (bf16[5,5,8,256]{3,2,1,0:T(8,128)(2,1)}, bf16[5,5,8,256]{3,2,1,0:T(8,128)(2,1)S(1)}, u32[]{:S(2)}, u32[]{:S(2)}) collective-permute-start(bf16[5,5,8,256]{3,2,1,0:T(8,128)(2,1)} %get-tuple-element.94), channel_id=1, source_target_pairs={{0,1},{1,0},{2,3},{3,2},{4,5},{5,4},{6,7},{7,6},{8,9},{9,8},{10,11... | collective-permute-start | bytes 307208 | tf_op jit(solution)/shard_map/ppermute | solution.py:575
  13.7 10.1 %collective-permute-start.5 = (bf16[5,5,8,256]{3,2,1,0:T(8,128)(2,1)}, bf16[5,5,8,256]{3,2,1,0:T(8,128)(2,1)S(1)}, u32[]{:S(2)}, u32[]{:S(2)}) collective-permute-start(bf16[5,5,8,256]{3,2,1,0:T(8,128)(2,1)} %get-tuple-element.95), channel_id=1, source_target_pairs={{0,31},{1,30},{2,1},{3,0},{4,3},{5,2},{6,5},{7,4},{8,7},{9,6},{10,... | collective-permute-start | bytes 307208 | tf_op jit(solution)/shard_map/ppermute | solution.py:575
  15.3 8.5 %collective-permute-start.3 = (bf16[5,20,8,256]{3,2,1,0:T(8,128)(2,1)S(1)}, bf16[5,20,8,256]{3,2,1,0:T(8,128)(2,1)S(1)}, u32[]{:S(2)}, u32[]{:S(2)}) collective-permute-start(bf16[5,20,8,256]{3,2,1,0:T(8,128)(2,1)S(1)} %get-tuple-element.93), channel_id=1, source_target_pairs={{0,30},{1,31},{2,0},{3,1},{4,2},{5,3},{6,4},{7,5},{8,6},{9,7},{10,... | collective-permute-start | bytes 1228808 | tf_op jit(solution)/shard_map/ppermute | solution.py:575
  16.4 7.4 %copy-start.1 = (bf16[256,1024]{1,0:T(8,128)(2,1)S(1)}, bf16[256,1024]{1,0:T(8,128)(2,1)}, u32[]{:S(2)}) copy-start(bf16[256,1024]{1,0:T(8,128)(2,1)} %fc1_w.1) | copy-start | bytes 1572868
  16.4 7.4 %copy-start.2 = (bf16[1024,256]{1,0:T(8,128)(2,1)S(1)}, bf16[1024,256]{1,0:T(8,128)(2,1)}, u32[]{:S(2)}) copy-start(bf16[1024,256]{1,0:T(8,128)(2,1)} %fc2_w.1) | copy-start | bytes 1572868
  16.4 7.4 %copy-start.4 = (bf16[256,256]{1,0:T(8,128)(2,1)S(1)}, bf16[256,256]{1,0:T(8,128)(2,1)}, u32[]{:S(2)}) copy-start(bf16[256,256]{1,0:T(8,128)(2,1)} %proj_w.1) | copy-start | bytes 393220
  16.4 7.4 %copy-start.5 = (f32[1024]{0:T(1024)S(1)}, f32[1024]{0:T(1024)}, u32[]{:S(2)}) copy-start(f32[1024]{0:T(1024)} %param.31) | copy-start | bytes 12292
  16.4 7.4 %copy-start.8 = (f32[256]{0:T(256)S(1)}, f32[256]{0:T(256)}, u32[]{:S(2)}) copy-start(f32[256]{0:T(256)} %param.27) | copy-start | bytes 3076
  16.4 7.4 %copy-start.9 = (f32[256]{0:T(256)S(1)}, f32[256]{0:T(256)}, u32[]{:S(2)}) copy-start(f32[256]{0:T(256)} %param.28) | copy-start | bytes 3076
  16.5 7.4 %copy-start.10 = (f32[256]{0:T(256)S(1)}, f32[256]{0:T(256)}, u32[]{:S(2)}) copy-start(f32[256]{0:T(256)} %param.29) | copy-start | bytes 3076
  16.5 7.4 %copy-start.11 = (f32[256]{0:T(256)S(1)}, f32[256]{0:T(256)}, u32[]{:S(2)}) copy-start(f32[256]{0:T(256)} %param.33) | copy-start | bytes 3076
  33.2 2.1 %collective-permute-start.6 = (bf16[1216,256]{1,0:T(8,128)(2,1)S(1)}, bf16[1216,256]{1,0:T(8,128)(2,1)S(1)}, u32[]{:S(2)}, u32[]{:S(2)}) collective-permute-start(bf16[1216,256]{1,0:T(8,128)(2,1)S(1)} %get-tuple-element.98), channel_id=1, source_target_pairs={{0,2},{1,3},{2,0},{3,1},{4,6},{5,7},{6,4},{7,5},{8,10},{9,11},{10,... | collective-permute-start | bytes 1867784 | tf_op jit(solution)/shard_map/ppermute | solution.py:575
  33.3 15.6 %collective-permute-start.10 = (bf16[5,15,8,256]{3,2,1,0:T(8,128)(2,1)S(1)}, bf16[5,15,8,256]{3,2,1,0:T(8,128)(2,1)S(1)}, u32[]{:S(2)}, u32[]{:S(2)}) collective-permute-start(bf16[5,15,8,256]{3,2,1,0:T(8,128)(2,1)S(1)} %get-tuple-element.103), channel_id=1, source_target_pairs={{0,2},{1,3},{2,4},{3,5},{4,6},{5,7},{6,8},{7,9},{8,10},{9,11},{10,... | collective-permute-start | bytes 921608 | tf_op jit(solution)/shard_map/ppermute | solution.py:575
  36.1 12.8 %collective-permute-start.7 = (bf16[304,256]{1,0:T(8,128)(2,1)S(1)}, bf16[304,256]{1,0:T(8,128)(2,1)S(1)}, u32[]{:S(2)}, u32[]{:S(2)}) collective-permute-start(bf16[304,256]{1,0:T(8,128)(2,1)S(1)} %get-tuple-element.100), channel_id=1, source_target_pairs={{0,1},{1,0},{2,3},{3,2},{4,5},{5,4},{6,7},{7,6},{8,9},{9,8},{10,11... | collective-permute-start | bytes 466952 | tf_op jit(solution)/shard_map/ppermute | solution.py:575
  37.8 11.3 %collective-permute-start.8 = (bf16[304,256]{1,0:T(8,128)(2,1)S(1)}, bf16[304,256]{1,0:T(8,128)(2,1)S(1)}, u32[]{:S(2)}, u32[]{:S(2)}) collective-permute-start(bf16[304,256]{1,0:T(8,128)(2,1)S(1)} %get-tuple-element.101), channel_id=1, source_target_pairs={{0,4},{1,5},{2,6},{3,7},{4,0},{5,1},{6,2},{7,3},{8,12},{9,13},{10,... | collective-permute-start | bytes 466952 | tf_op jit(solution)/shard_map/ppermute | solution.py:575
  38.5 10.5 %collective-permute-start.9 = (bf16[304,256]{1,0:T(8,128)(2,1)S(1)}, bf16[304,256]{1,0:T(8,128)(2,1)S(1)}, u32[]{:S(2)}, u32[]{:S(2)}) collective-permute-start(bf16[304,256]{1,0:T(8,128)(2,1)S(1)} %get-tuple-element.102), channel_id=1, source_target_pairs={{0,5},{1,4},{2,7},{3,6},{4,1},{5,0},{6,3},{7,2},{8,13},{9,12},{10,... | collective-permute-start | bytes 466952 | tf_op jit(solution)/shard_map/ppermute | solution.py:575
  49.1 1.6 %collective-permute-start.11 = (bf16[448,256]{1,0:T(8,128)(2,1)S(1)}, bf16[448,256]{1,0:T(8,128)(2,1)S(1)}, u32[]{:S(2)}, u32[]{:S(2)}) collective-permute-start(bf16[448,256]{1,0:T(8,128)(2,1)S(1)} %get-tuple-element.121), channel_id=1, source_target_pairs={{0,2},{1,3},{2,0},{3,1},{4,6},{5,7},{6,4},{7,5},{8,10},{9,11},{10,... | collective-permute-start | bytes 688136 | tf_op jit(solution)/shard_map/ppermute | solution.py:575
  51.3 4.2 %collective-permute-start.12 = (bf16[112,256]{1,0:T(8,128)(2,1)S(1)}, bf16[112,256]{1,0:T(8,128)(2,1)S(1)}, u32[]{:S(2)}, u32[]{:S(2)}) collective-permute-start(bf16[112,256]{1,0:T(8,128)(2,1)S(1)} %get-tuple-element.123), channel_id=1, source_target_pairs={{0,1},{1,0},{2,3},{3,2},{4,5},{5,4},{6,7},{7,6},{8,9},{9,8},{10,11... | collective-permute-start | bytes 172040 | tf_op jit(solution)/shard_map/ppermute | solution.py:575
  53.1 4.8 %collective-permute-start.13 = (bf16[112,256]{1,0:T(8,128)(2,1)S(1)}, bf16[112,256]{1,0:T(8,128)(2,1)S(1)}, u32[]{:S(2)}, u32[]{:S(2)}) collective-permute-start(bf16[112,256]{1,0:T(8,128)(2,1)S(1)} %get-tuple-element.124), channel_id=1, source_target_pairs={{0,4},{1,5},{2,6},{3,7},{4,0},{5,1},{6,2},{7,3},{8,12},{9,13},{10,... | collective-permute-start | bytes 172040 | tf_op jit(solution)/shard_map/ppermute | solution.py:575
  53.6 5.1 %collective-permute-start.14 = (bf16[112,256]{1,0:T(8,128)(2,1)S(1)}, bf16[112,256]{1,0:T(8,128)(2,1)S(1)}, u32[]{:S(2)}, u32[]{:S(2)}) collective-permute-start(bf16[112,256]{1,0:T(8,128)(2,1)S(1)} %get-tuple-element.125), channel_id=1, source_target_pairs={{0,5},{1,4},{2,7},{3,6},{4,1},{5,0},{6,3},{7,2},{8,13},{9,12},{10,... | collective-permute-start | bytes 172040 | tf_op jit(solution)/shard_map/ppermute | solution.py:575
  58.7 5.9 %collective-permute-start.15 = (bf16[416,256]{1,0:T(8,128)(2,1)S(1)}, bf16[416,256]{1,0:T(8,128)(2,1)S(1)}, u32[]{:S(2)}, u32[]{:S(2)}) collective-permute-start(bf16[416,256]{1,0:T(8,128)(2,1)S(1)} %join_pieces.2.refs_0_), channel_id=1, source_target_pairs={{0,8},{1,9},{2,10},{3,11},{4,12},{5,13},{6,14},{7,15},{8,0},{9,1},... | collective-permute-start | bytes 638984 | tf_op jit(solution)/shard_map/ppermute | solution.py:575
  58.8 17.7 %collective-permute-start.17 = (bf16[5,15,8,256]{3,2,1,0:T(8,128)(2,1)S(1)}, bf16[5,15,8,256]{3,2,1,0:T(8,128)(2,1)S(1)}, u32[]{:S(2)}, u32[]{:S(2)}) collective-permute-start(bf16[5,15,8,256]{3,2,1,0:T(8,128)(2,1)S(1)} %get-tuple-element.129), channel_id=1, source_target_pairs={{0,2},{1,3},{2,4},{3,5},{4,6},{5,7},{6,8},{7,9},{8,10},{9,11},{10,... | collective-permute-start | bytes 921608 | tf_op jit(solution)/shard_map/ppermute | solution.py:575
  64.7 10.1 %collective-permute-start.16 = (bf16[416,256]{1,0:T(8,128)(2,1)S(1)}, bf16[416,256]{1,0:T(8,128)(2,1)S(1)}, u32[]{:S(2)}, u32[]{:S(2)}) collective-permute-start(bf16[416,256]{1,0:T(8,128)(2,1)S(1)} %add_pieces.6.refs_0_), channel_id=1, source_target_pairs={{0,16},{1,17},{2,18},{3,19},{4,20},{5,21},{6,22},{7,23},{8,24},{9,... | collective-permute-start | bytes 638984 | tf_op jit(solution)/shard_map/ppermute | solution.py:575
  66.1 8.7 %collective-permute-start.18 = (bf16[10,5,8,256]{3,2,1,0:T(8,128)(2,1)S(1)}, bf16[10,5,8,256]{3,2,1,0:T(8,128)(2,1)S(1)}, u32[]{:S(2)}, u32[]{:S(2)}) collective-permute-start(bf16[10,5,8,256]{3,2,1,0:T(8,128)(2,1)S(1)} %get-tuple-element.130), channel_id=1, source_target_pairs={{0,1},{1,0},{2,3},{3,2},{4,5},{5,4},{6,7},{7,6},{8,9},{9,8},{10,11... | collective-permute-start | bytes 614408 | tf_op jit(solution)/shard_map/ppermute | solution.py:575
  67.6 8.9 %collective-permute-start.19 = (bf16[10,5,8,256]{3,2,1,0:T(8,128)(2,1)S(1)}, bf16[10,5,8,256]{3,2,1,0:T(8,128)(2,1)S(1)}, u32[]{:S(2)}, u32[]{:S(2)}) collective-permute-start(bf16[10,5,8,256]{3,2,1,0:T(8,128)(2,1)S(1)} %get-tuple-element.131), channel_id=1, source_target_pairs={{0,3},{1,2},{2,5},{3,4},{4,7},{5,6},{6,9},{7,8},{8,11},{9,10},{10,... | collective-permute-start | bytes 614408 | tf_op jit(solution)/shard_map/ppermute | solution.py:575
  76.5 10.7 %collective-permute-start.22 = (bf16[416,256]{1,0:T(8,128)(2,1)S(1)}, bf16[416,256]{1,0:T(8,128)(2,1)S(1)}, u32[]{:S(2)}, u32[]{:S(2)}) collective-permute-start(bf16[416,256]{1,0:T(8,128)(2,1)S(1)} %add_pieces.7.refs_0_), channel_id=1, source_target_pairs={{0,5},{1,4},{2,7},{3,6},{4,1},{5,0},{6,3},{7,2},{8,13},{9,12},{10,... | collective-permute-start | bytes 638984 | tf_op jit(solution)/shard_map/ppermute | solution.py:575
  81.0 9.4 %collective-permute-start.21 = (bf16[416,256]{1,0:T(8,128)(2,1)S(1)}, bf16[416,256]{1,0:T(8,128)(2,1)S(1)}, u32[]{:S(2)}, u32[]{:S(2)}) collective-permute-start(bf16[416,256]{1,0:T(8,128)(2,1)S(1)} %add_pieces.7.refs_0_), channel_id=1, source_target_pairs={{0,4},{1,5},{2,6},{3,7},{4,0},{5,1},{6,2},{7,3},{8,12},{9,13},{10,... | collective-permute-start | bytes 638984 | tf_op jit(solution)/shard_map/ppermute | solution.py:575
  81.0 10.2 %collective-permute-start.20 = (bf16[416,256]{1,0:T(8,128)(2,1)S(1)}, bf16[416,256]{1,0:T(8,128)(2,1)S(1)}, u32[]{:S(2)}, u32[]{:S(2)}) collective-permute-start(bf16[416,256]{1,0:T(8,128)(2,1)S(1)} %add_pieces.7.refs_0_), channel_id=1, source_target_pairs={{0,1},{1,0},{2,3},{3,2},{4,5},{5,4},{6,7},{7,6},{8,9},{9,8},{10,11... | collective-permute-start | bytes 638984 | tf_op jit(solution)/shard_map/ppermute | solution.py:575
  91.3 2.4 %collective-permute-start.23 = (bf16[1664,256]{1,0:T(8,128)(2,1)S(1)}, bf16[1664,256]{1,0:T(8,128)(2,1)S(1)}, u32[]{:S(2)}, u32[]{:S(2)}) collective-permute-start(bf16[1664,256]{1,0:T(8,128)(2,1)S(1)} %join_pieces.3.refs_1_), channel_id=1, source_target_pairs={{0,2},{1,3},{2,0},{3,1},{4,6},{5,7},{6,4},{7,5},{8,10},{9,11},{10,... | collective-permute-start | bytes 2555912 | tf_op jit(solution)/shard_map/ppermute | solution.py:575

commit v5 on v4

--- a/solution.py
+++ b/solution.py
@@ -164,17 +164,23 @@
     count[...] = jnp.broadcast_to(total, count.shape)
 
 
-def split_halves(places, sums, mine, other):
+def core_and_spot():
+    r, c = lax.axis_index("rows"), lax.axis_index("cols")
+    return r & 1, ((r >> 1) & 1) * lax.axis_size("cols") + c
+
+
+def split_halves(sums, mine, other):
     size = mine.shape[0]
-    core = places[2]
+    core, _ = core_and_spot()
     mine[...] = sums[pl.ds(pl.multiple_of(core * size, 16), size), :]
     other[...] = sums[pl.ds(pl.multiple_of((1 - core) * size, 16), size), :]
 
 
-def split_kernel(places, mine, other, *outs):
+def split_kernel(mine, other, *outs):
     size = outs[0].shape[0]
+    _, spot = core_and_spot()
     for k, out in enumerate(outs):
-        at = pl.ds(pl.multiple_of((places[3] ^ k) * size, 16), size)
+        at = pl.ds(pl.multiple_of((spot ^ k) * size, 16), size)
         out[...] = (mine[at, :].astype(F32) + other[at, :].astype(F32)).astype(BF16)
 
 
@@ -202,8 +208,10 @@
     return high, middle, (rest - middle.astype(F32)).astype(BF16)
 
 
-def bias_kernel(edge, table, out, padded):
+def bias_kernel(table, out, padded):
     heads = table.shape[0]
+    last_row = lax.axis_index("rows") == lax.axis_size("rows") - 1
+    last_col = lax.axis_index("cols") == lax.axis_size("cols") - 1
     padded[...] = jnp.zeros_like(padded)
     padded[:, : table.shape[1]] = table[...]
     offsets = padded[...]
@@ -227,9 +235,9 @@
         own_left = row < SHIFT * heads
         beside = query_left != own_left
         for w in range(2):
-            cut_off = across & (edge[0] != 0)
+            cut_off = across & last_row
             if w == 1:
-                cut_off = cut_off | (beside & (edge[1] != 0))
+                cut_off = cut_off | (beside & last_col)
             value = rel + jnp.where(cut_off, -100.0, 0.0)
             out[w, r * count : (r + 1) * count, :] = value
     for w in range(2):
@@ -301,9 +309,9 @@
 
 
 def mlp_kernel(
-    places, x_in, o_in, t_own, t_low, t_right, t_corner, count,
+    x_in, o_in, t_own, t_low, t_right, t_corner, count,
     proj_w, fc1_w, fc2_w, pb, g2, b2, f1b, f2b,
-    stays, up, side, corner, dy_out, do_out, mine, other,
+    stays, up, side, corner, dy_out, do_out, rows_out, mine, other,
     frame_out, sums_out, tf, fc1_acc, fc2_acc, proj_acc, fc1_sum, small_sum,
 ):
     gather_frame(tf, t_own, t_low, t_right, t_corner)
@@ -317,22 +325,18 @@
     ff = fc1_w.shape[1] // d
     for j in range(ff):
         sums_out[j * d : (j + 1) * d, :] = fc1_acc[:, j * d : (j + 1) * d].astype(BF16)
-        sums_out[(ff + j) * d : (ff + j + 1) * d, :] = fc2_acc[:, j * d : (j + 1) * d].T.astype(
-            BF16
-        )
+        sums_out[(ff + j) * d : (ff + j + 1) * d, :] = fc2_acc[j * d : (j + 1) * d, :].astype(BF16)
     at = 2 * ff * d
     sums_out[at : at + d, :] = proj_acc[...].astype(BF16)
     rows = [jnp.sum(fc1_sum[:, j * d : (j + 1) * d], 0, keepdims=True) for j in range(ff)]
     rows += [jnp.sum(small_sum[k], 0, keepdims=True) for k in range(4)]
     rows.append(count[...])
     rows.append(jnp.zeros((16 - len(rows), d), F32))
-    high, low_part = split_rows(jnp.concatenate(rows, 0))
+    rows_out[...] = jnp.concatenate(rows, 0)
     at += d
-    sums_out[at : at + 16, :] = high
-    sums_out[at + 16 : at + 32, :] = low_part
-    if sums_out.shape[0] > at + 32:
-        sums_out[at + 32 :, :] = jnp.zeros((sums_out.shape[0] - at - 32, d), BF16)
-    split_halves(places, sums_out, mine, other)
+    if sums_out.shape[0] > at:
+        sums_out[at:, :] = jnp.zeros((sums_out.shape[0] - at, d), BF16)
+    split_halves(sums_out, mine, other)
     stays[...] = frame_out[:SHIFT, :-SHIFT]
     up[...] = frame_out[SHIFT:, :-SHIFT]
     side[...] = frame_out[:SHIFT, -SHIFT:]
@@ -367,7 +371,7 @@
         dh_wide = dot_bt(drb, fc2_w[at, :]) * slope
         dh = dh_wide.astype(BF16)
         r = r + dot(gelu, fc2_w[at, :])
-        fc2_acc[:, at] = dot_at(drb, gelu)
+        fc2_acc[at, :] = dot_at(gelu, drb)
         fc1_acc[:, at] = dot_at(c, dh)
         fc1_sum[:, at] = fold(dh.astype(F32))
         more = dot_bt(dh, fc1_w[:, at])
@@ -391,7 +395,7 @@
 
 
 def backward_kernel(
-    places, xw, qkv, p_in, dy_in, do_in, qkv_w, g1, b1, out_side, out_corner,
+    xw, qkv, p_in, dy_in, do_in, qkv_w, g1, b1, out_side, mlp_rows,
     stays, side, corner, up, mine, other,
     dx, qkv_acc, rel_acc, col_sum, small_sum, mixed, sums_out, joined_all,
 ):
@@ -421,8 +425,7 @@
     stays[:, WIN:] = right[:SHIFT, :SHIFT]
     side[:SHIFT] = out_side[...]
     side[SHIFT:] = right[:SHIFT, SHIFT:].astype(BF16)
-    corner[: WIN - SHIFT] = out_corner[...]
-    corner[WIN - SHIFT :] = right[SHIFT:, SHIFT:].astype(BF16)
+    corner[...] = right[SHIFT:, SHIFT:].astype(BF16)
     up[:, :WIN] = left[SHIFT:].astype(BF16)
     up[:, WIN:] = right[SHIFT:, :SHIFT].astype(BF16)
     for j in range(3):
@@ -433,17 +436,16 @@
     rows = [jnp.sum(small_sum[k], 0, keepdims=True) for k in range(2)]
     rows.append(jnp.sum(col_sum[:, :d], 0, keepdims=True))
     rows.append(jnp.sum(col_sum[:, 2 * d :], 0, keepdims=True))
-    rows.append(jnp.zeros((4, d), F32))
+    rows.append(mlp_rows[:12])
     rows.append(rel[:, :d])
     rows.append(jnp.concatenate([rel[:, d:], jnp.zeros((heads, 2 * d - RELS), F32)], 1))
-    rows.append(jnp.zeros((8, d), F32))
     high, rest = split_rows(jnp.concatenate(rows, 0))
     at = 3 * d
     sums_out[at : at + 32, :] = high
     sums_out[at + 32 : at + 64, :] = rest
     if sums_out.shape[0] > at + 64:
         sums_out[at + 64 :, :] = jnp.zeros((sums_out.shape[0] - at - 64, d), BF16)
-    split_halves(places, sums_out, mine, other)
+    split_halves(sums_out, mine, other)
 
 
 def backward_pages(pages, qkv, p_in, do_in, joined_all, rel_acc):
@@ -518,8 +520,8 @@
     return total
 
 
-def collect(places, buf, mine, other, planes, first, size):
-    core, spot = places[2], places[3]
+def collect(buf, mine, other, planes, first, size):
+    core, spot = core_and_spot()
     stride = mine.shape[0] // planes
     for c, pieces in ((core, mine), (1 - core, other)):
         for k in range(planes):
@@ -530,39 +532,37 @@
 
 
 def finish_kernel(
-    total, planes, sizes, places, mine, other, up, side, corner, stays,
+    total, planes, sizes, mine, other, up, side, corner, stays,
     grad, fc1, fc2, proj, fc1_b, g2, b2, fc2_b, proj_b, qkv, g1, b1, q_b, v_b, rel, buf1, buf2,
 ):
-    collect(places, buf1, mine, other, planes, 0, sizes[0])
-    collect(places, buf2, mine, other, planes, sizes[0], sizes[1])
+    collect(buf1, mine, other, planes, 0, sizes[0])
+    collect(buf2, mine, other, planes, sizes[0], sizes[1])
     d = proj.shape[0]
     ff = fc1.shape[1] // d
-    at = (2 * ff + 1) * d
-    rows = buf1[at : at + 16, :] + buf1[at + 16 : at + 32, :]
-    scale = total / rows[ff + 4 : ff + 5, :]
+    at = 3 * d
+    rows = buf2[at : at + 32, :] + buf2[at + 32 : at + 64, :]
+    scale = total / rows[ff + 8 : ff + 9, :]
     rows = rows * scale
     wide = scale.reshape(1, 1, 1, d)
     rest = up.shape[0]
-    grad[:rest, :SHIFT] = corner[rest:].astype(F32) * wide
+    grad[:rest, :SHIFT] = corner[...].astype(F32) * wide
     grad[:rest, SHIFT:] = up[...].astype(F32) * wide
     grad[rest:, :SHIFT] = side[SHIFT:].astype(F32) * wide
     grad[rest:, SHIFT:] = stays[...] * wide
     for j in range(ff):
         fc1[:, j * d : (j + 1) * d] = buf1[j * d : (j + 1) * d, :] * scale
         fc2[j * d : (j + 1) * d, :] = buf1[(ff + j) * d : (ff + j + 1) * d, :] * scale
-        fc1_b[:, j * d : (j + 1) * d] = rows[j : j + 1]
+        fc1_b[:, j * d : (j + 1) * d] = rows[4 + j : 5 + j]
     proj[...] = buf1[2 * ff * d : (2 * ff + 1) * d, :] * scale
     for k, ref in enumerate((g2, b2, fc2_b, proj_b)):
-        ref[...] = rows[ff + k : ff + k + 1]
+        ref[...] = rows[ff + 4 + k : ff + 5 + k]
     for j in range(3):
         qkv[:, j * d : (j + 1) * d] = buf2[j * d : (j + 1) * d, :] * scale
-    at = 3 * d
-    rows = (buf2[at : at + 32, :] + buf2[at + 32 : at + 64, :]) * scale
     for k, ref in enumerate((g1, b1, q_b, v_b)):
         ref[...] = rows[k : k + 1]
     heads = rel.shape[0]
-    rel[:, :d] = rows[8 : 8 + heads]
-    rel[:, d:] = rows[16 : 16 + heads, : rel.shape[1] - d]
+    rel[:, :d] = rows[16 : 16 + heads]
+    rel[:, d:] = rows[16 + heads : 16 + 2 * heads, : rel.shape[1] - d]
 
 
 def permute(block, target):
@@ -606,10 +606,6 @@
 
 def in_vmem():
     return pl.BlockSpec(memory_space=pltpu.VMEM)
-
-
-def in_smem():
-    return pl.BlockSpec(memory_space=pltpu.SMEM)
 
 
 def to_vmem(a):
@@ -668,17 +664,17 @@
     )(*map(to_hbm, (target, kept, table)))
 
 
-def split_call(places, mine, other):
+def split_call(mine, other):
     planes = 2 * lax.axis_size("cols")
     n, d = mine.shape
     return pl.pallas_call(
         split_kernel,
-        in_specs=[in_smem()] + [in_vmem()] * 2,
+        in_specs=[in_vmem()] * 2,
         out_specs=[in_vmem()] * planes,
         out_shape=[pltpu.VMEM((n // planes, d), BF16)] * planes,
         compiler_params=limit(4),
         name="split_sums",
-    )(places, *map(to_vmem, (mine, other)))
+    )(*map(to_vmem, (mine, other)))
 
 
 def local_call(kernel, rows, parts, name):
@@ -700,17 +696,17 @@
     return local_call(join_kernel, sum(a.shape[0] for a in parts), parts, "join_pieces")
 
 
-def bias_call(places, rel_table):
+def bias_call(rel_table):
     heads = rel_table.shape[0]
     return pl.pallas_call(
         bias_kernel,
-        in_specs=[in_smem(), in_vmem()],
+        in_specs=[in_vmem()],
         out_specs=in_vmem(),
         out_shape=pltpu.VMEM((2, ROWS * heads, KEYS), F32),
         scratch_shapes=[pltpu.VMEM((heads, RELS), F32)],
         compiler_params=limit(VMEM_LIMIT),
         name="attention_bias",
-    )(places, to_vmem(rel_table))
+    )(to_vmem(rel_table))
 
 
 def cost(flops):
@@ -742,7 +738,7 @@
     )(*map(to_vmem, inputs))
 
 
-def mlp_call(size, places, x, mixed, masked, t_strips, count, *weights):
+def mlp_call(size, x, mixed, masked, t_strips, count, *weights):
     height, width, pages, d = masked.shape
     ff = weights[1].shape[1]
     shape = pltpu.VMEM
@@ -753,11 +749,11 @@
         shape((SHIFT, SHIFT, pages, d), BF16), shape((rest, SHIFT, pages, d), BF16),
         shape((d // KEYS, 2, ROWS * pages, KEYS), F32),
         shape((d // KEYS, 2, ROWS * pages, KEYS), F32),
-        shape((size // 2, d), BF16), shape((size // 2, d), BF16),
+        shape((16, d), F32), shape((size // 2, d), BF16), shape((size // 2, d), BF16),
     ]
     return pl.pallas_call(
         mlp_kernel,
-        in_specs=[in_smem()] + [in_vmem()] * len(inputs),
+        in_specs=[in_vmem()] * len(inputs),
         out_specs=[in_vmem()] * len(outs),
         out_shape=outs,
         scratch_shapes=[
@@ -765,7 +761,7 @@
             pltpu.VMEM((size, d), BF16),
             pltpu.VMEM((d // KEYS, 2, TOK * pages, KEYS), F32),
             pltpu.VMEM((d, ff), F32),
-            pltpu.VMEM((d, ff), F32),
+            pltpu.VMEM((ff, d), F32),
             pltpu.VMEM((d, d), F32),
             pltpu.VMEM((8, ff), F32),
             pltpu.VMEM((4, 8, d), F32),
@@ -773,10 +769,10 @@
         compiler_params=limit(VMEM_LIMIT),
         cost_estimate=cost(10**10),
         name="mlp_forward_backward",
-    )(places, *map(to_vmem, inputs))
-
-
-def backward_call(size, places, xw, qkv, probs, dy, do, *more):
+    )(*map(to_vmem, inputs))
+
+
+def backward_call(size, xw, qkv, probs, dy, do, *more):
     pages, d = probs.shape[1], xw.shape[1]
     heads = probs.shape[2] // ROWS
     shape = pltpu.VMEM
@@ -784,13 +780,13 @@
     rest = WIN - SHIFT
     outs = [
         shape((SHIFT, 2 * WIN - SHIFT, pages, d), F32), shape((2 * SHIFT, SHIFT, pages, d), BF16),
-        shape((2 * rest, SHIFT, pages, d), BF16),
+        shape((rest, SHIFT, pages, d), BF16),
         shape((rest, 2 * WIN - SHIFT, pages, d), BF16), shape((size // 2, d), BF16),
         shape((size // 2, d), BF16),
     ]
     return pl.pallas_call(
         backward_kernel,
-        in_specs=[in_smem()] + [in_vmem()] * len(inputs),
+        in_specs=[in_vmem()] * len(inputs),
         out_specs=[in_vmem()] * len(outs),
         out_shape=outs,
         scratch_shapes=[
@@ -806,10 +802,10 @@
         compiler_params=limit(VMEM_LIMIT),
         cost_estimate=cost(10**10),
         name="attention_backward",
-    )(places, *map(to_vmem, inputs))
-
-
-def finish_call(total, planes, ff, n1, n2, rel_shape, places, *inputs):
+    )(*map(to_vmem, inputs))
+
+
+def finish_call(total, planes, ff, n1, n2, rel_shape, *inputs):
     d = inputs[0].shape[1]
     row = (1, d)
     field = (WIN, 2 * WIN) + inputs[2].shape[2:]
@@ -818,12 +814,12 @@
     sizes = (n1 // (2 * planes), n2 // (2 * planes))
     return pl.pallas_call(
         lambda *refs: finish_kernel(total, planes, sizes, *refs),
-        in_specs=[in_smem()] + [in_vmem()] * len(inputs),
+        in_specs=[in_vmem()] * len(inputs),
         out_shape=[jax.ShapeDtypeStruct(s, F32) for s in shapes],
         scratch_shapes=[pltpu.VMEM((n1, d), F32), pltpu.VMEM((n2, d), F32)],
         compiler_params=limit(VMEM_LIMIT),
         name="finish_sums",
-    )(places, *map(to_vmem, inputs))
+    )(*map(to_vmem, inputs))
 
 
 def shards(
@@ -833,48 +829,47 @@
     pages, height, width, d = patches.shape
     ff = fc1_weight.shape[1]
     rows, cols = lax.axis_size("rows"), lax.axis_size("cols")
-    r, c = lax.axis_index("rows"), lax.axis_index("cols")
     planes = 2 * cols
     step = 32 * planes
     tokens = pages * height * width
     vec = lambda a: a.reshape(1, -1)
-    n1 = -(-(2 * ff + d + 32) // step) * step
+    n1 = -(-(2 * ff + d) // step) * step
     n2 = -(-(3 * d + 64) // step) * step
 
-    places = jnp.stack([r == rows - 1, c == cols - 1, r & 1, ((r >> 1) & 1) * cols + c])
-    places = places.astype(jnp.int32)
     patches = patches.transpose(1, 2, 0, 3)
     p_strips = [permute(a, hop) for a, hop in zip(strips_call(patches), strip_hops())]
     masked, *t_strips, count, table = target_call(
         target.transpose(1, 2, 0, 3), kept_mask.transpose(1, 0, 2), rel_table
     )
     t_strips = [permute(a, hop) for a, hop in zip(t_strips, strip_hops())]
-    bias = bias_call(places, table)
+    bias = bias_call(table)
 
     g1, b1 = vec(ln1_gain), vec(ln1_bias)
     x, xw, qkv, probs, mixed = attention_call(
         patches, p_strips, qkv_weight, bias, g1, b1, vec(query_bias), vec(value_bias)
     )
-    out_stays, out_up, out_side, out_corner, dy, do, mine, other = mlp_call(
-        n1, places, x, mixed, masked, t_strips, count, proj_weight, fc1_weight, fc2_weight,
+    out_stays, out_up, out_side, out_corner, dy, do, mlp_rows, mine, other = mlp_call(
+        n1, x, mixed, masked, t_strips, count, proj_weight, fc1_weight, fc2_weight,
         vec(proj_bias), vec(ln2_gain), vec(ln2_bias), vec(fc1_bias), vec(fc2_bias),
     )
 
     to_right, to_below = (lambda r, c: (r, c + 1)), (lambda r, c: (r + 1, c))
     across = lambda r, c: (r + 1, c + 1)
-    out_up = permute(out_up, to_below)
-
-    pieces = split_call(places, mine, permute(other, core_hop))
+    out_up, out_corner = permute(out_up, to_below), permute(out_corner, across)
+
+    pieces = split_call(mine, permute(other, core_hop))
     got = plane_share(pieces)
     do = after(do, pieces)
     stays, side, corner, up, mine2, other2 = backward_call(
-        n2, places, xw, qkv, probs, dy, do, qkv_weight, g1, b1, out_side, out_corner
-    )
-    got, out_up = after((got, out_up), mine2)
+        n2, xw, qkv, probs, dy, do, qkv_weight, g1, b1, out_side, mlp_rows
+    )
+    got, out_up, out_corner = after((got, out_up, out_corner), mine2)
     piece = sum_call(got)
-    mine2, other2, up, out_up = after((mine2, other2, up, out_up), piece)
-
-    pieces2 = split_call(places, mine2, permute(other2, core_hop))
+    mine2, other2, up, out_up, out_corner = after(
+        (mine2, other2, up, out_up, out_corner), piece
+    )
+
+    pieces2 = split_call(mine2, permute(other2, core_hop))
     piece2 = sum_call(plane_share(pieces2))
     up, side, corner = after((up, side, corner), piece2)
     piece = join_call([piece, piece2])
@@ -883,7 +878,7 @@
     piece, up, side, corner = after((piece, up, side, corner), up)
     mine = join_call(plane_share([piece] * planes))
     other = permute(mine, core_hop)
-    top = jnp.concatenate([corner[: WIN - SHIFT], out_up], 1)
+    top = jnp.concatenate([out_corner, out_up], 1)
     bottom = jnp.concatenate([side[:SHIFT], out_stays], 1)
     output = jnp.concatenate([top, bottom], 0)
     mine, output = after((mine, output), output)
@@ -892,7 +887,7 @@
         grad, fc1_g, fc2_g, proj_g, fc1_bg, g2_g, b2_g, fc2_bg, proj_bg, qkv_g, g1_g, b1_g, q_bg,
         v_bg, rel_g,
     ) = finish_call(
-        total, planes, ff, n1, n2, rel_table.shape, places, mine, other, up, side, corner, stays
+        total, planes, ff, n1, n2, rel_table.shape, mine, other, up, side, corner, stays
     )
     flat = lambda a: a.reshape(-1)
     return (

time: 97.1 us -> 90.9 us (0.936)
  Pallas kernels: 35.6 us -> 30 us
    pallas_call x5, Pallas kernels: 21 us -> 18.2 us  [the longest x1 8.75 us: backward_call(): pl.pallas_call(backward_kernel, in_specs=[in_vmem()] * len(inputs), out_s...]
    pallas_call x1, Pallas kernels: 7.29 us -> 6.28 us  [attention_call(): pl.pallas_call(attention_kernel, in_specs=[in_vmem()] * len(inputs), out_...]
    ppermute x24 -> x25, starting transfers between devices: 25.9 us -> 25.5 us  [permute(): return lax.ppermute(block, ('rows', 'cols'), route)]
    ppermute x24 -> x25, waiting for transfers between devices: 33 us -> 32.9 us  [permute(): return lax.ppermute(block, ('rows', 'cols'), route)]
  transfers between devices with their start and end apart: 24 -> 25, of which waited for: 15 -> 14; matrix products, arithmetic and copies ran while one was open for 1% -> 1% of each run, Pallas kernels for 21% -> 19%
where the time goes in v5:
time: 90.9 us; the launch traced here: 90.8 us
  waiting for transfers between devices  32.9 us (36%)
  Pallas kernels  30 us (33%)
  starting transfers between devices  25.5 us (28%)
  between operations  1.2 us (1%)
  other arithmetic  0.97 us (1%)
    ppermute x25, waiting for transfers between devices, permute(): return lax.ppermute(block, ('rows', 'cols'), route)  32.9 us
    ppermute x25, starting transfers between devices, permute(): return lax.ppermute(block, ('rows', 'cols'), route)  25.5 us
    pallas_call x1, Pallas kernels, backward_call(): pl.pallas_call(backward_kernel, in_specs=[in_vmem()] * len(inputs), out_s...  8.75 us
    pallas_call x1, Pallas kernels, mlp_call(): pl.pallas_call(mlp_kernel, in_specs=[in_vmem()] * len(inputs), out_specs=...  8.67 us
    pallas_call x1, Pallas kernels, attention_call(): pl.pallas_call(attention_kernel, in_specs=[in_vmem()] * len(inputs), out_...  6.28 us
    pallas_call x1, Pallas kernels, finish_call(): pl.pallas_call(lambda *refs: finish_kernel(total, planes, sizes, *refs),...  2.54 us
  transfers between devices with their start and end apart: 25, of which 14 were waited for; matrix products, arithmetic and copies ran while one was open for 1% of the time, Pallas kernels for 19%

profile of v5, /device:TPU:0, one launch (start us, length us, event | category | flops | bytes accessed | tf_op | source)
XLA Modules:
  0.0 90.8 jit_solution(7977758162977654992)
XLA Ops:
  0.7 1.2 %input_strips.1 = (bf16[5,20,8,256]{3,2,1,0:T(8,128)(2,1)S(1)}, bf16[5,5,8,256]{3,2,1,0:T(8,128)(2,1)S(1)}, bf16[5,5,8,256]{3,2,1,0:T(8,128)(2,1)S(1)}) custom-call(bf16[10,20,8,256]{3,2,1,0:T(8,128)(2,1)} %bitcast.23), custom_call_target="tpu_custom_call" | custom-call | tf_op jit(solution)/shard_map/input_strips/pallas_call | solution.py:638
  1.9 5.5 %collective-permute-start = (bf16[5,20,8,256]{3,2,1,0:T(8,128)(2,1)S(1)}, bf16[5,20,8,256]{3,2,1,0:T(8,128)(2,1)S(1)}, u32[]{:S(2)}, u32[]{:S(2)}) collective-permute-start(bf16[5,20,8,256]{3,2,1,0:T(8,128)(2,1)S(1)} %get-tuple-element.89), channel_id=1, source_target_pairs={{0,30},{1,31},{2,0},{3,1},{4,2},{5,3},{6,4},{7,5},{8,6},{9,7},{10,... | collective-permute-start | bytes 1228808 | tf_op jit(solution)/shard_map/ppermute | solution.py:575
  7.4 1.5 %collective-permute-start.1 = (bf16[5,5,8,256]{3,2,1,0:T(8,128)(2,1)S(1)}, bf16[5,5,8,256]{3,2,1,0:T(8,128)(2,1)S(1)}, u32[]{:S(2)}, u32[]{:S(2)}) collective-permute-start(bf16[5,5,8,256]{3,2,1,0:T(8,128)(2,1)S(1)} %get-tuple-element.90), channel_id=1, source_target_pairs={{0,1},{1,0},{2,3},{3,2},{4,5},{5,4},{6,7},{7,6},{8,9},{9,8},{10,11... | collective-permute-start | bytes 307208 | tf_op jit(solution)/shard_map/ppermute | solution.py:575
  8.9 0.4 collective-permute-start.2
  9.3 1.6 %masked_target.1 = (bf16[10,20,8,256]{3,2,1,0:T(8,128)(2,1)S(1)}, bf16[5,20,8,256]{3,2,1,0:T(8,128)(2,1)S(1)}, bf16[5,5,8,256]{3,2,1,0:T(8,128)(2,1)S(1)}, bf16[...) custom-call(bf16[10,20,8,256]{3,2,1,0:T(8,128)(2,1)} %bitcast.37, ...), custom_call_target="tpu_custom_call" | custom-call | tf_op jit(solution)/shard_map/masked_target/pallas_call | solution.py:650
  10.9 1.6 %collective-permute-start.4 = (bf16[5,5,8,256]{3,2,1,0:T(8,128)(2,1)S(1)}, bf16[5,5,8,256]{3,2,1,0:T(8,128)(2,1)S(1)}, u32[]{:S(2)}, u32[]{:S(2)}) collective-permute-start(bf16[5,5,8,256]{3,2,1,0:T(8,128)(2,1)S(1)} %get-tuple-element.97), channel_id=1, source_target_pairs={{0,1},{1,0},{2,3},{3,2},{4,5},{5,4},{6,7},{7,6},{8,9},{9,8},{10,11... | collective-permute-start | bytes 307208 | tf_op jit(solution)/shard_map/ppermute | solution.py:575
  12.4 0.2 collective-permute-start.5
  12.7 0.5 attention_bias.1.bias
  13.2 1.2 %collective-permute-done.1.right = bf16[5,5,8,256]{3,2,1,0:T(8,128)(2,1)S(1)} collective-permute-done((bf16[5,5,8,256]{3,2,1,0:T(8,128)(2,1)S(1)}, bf16[5,5,8,256]{3,2,1,0:T(8,128)(2,1)S(1)}, u32[]{:S(2)}, u32[]{:S(2)}) %collective-permute-start.1) | collective-permute-done | bytes 102432 | tf_op jit(solution)/shard_map/ppermute | solution.py:575
  14.4 0.0 collective-permute-start.3
  14.4 1.3 %collective-permute-done.2.corner = bf16[5,5,8,256]{3,2,1,0:T(8,128)(2,1)S(1)} collective-permute-done((bf16[5,5,8,256]{3,2,1,0:T(8,128)(2,1)S(1)}, bf16[5,5,8,256]{3,2,1,0:T(8,128)(2,1)S(1)}, u32[]{:S(2)}, u32[]{:S(2)}) %collective-permute-start.2) | collective-permute-done | bytes 102432 | tf_op jit(solution)/shard_map/ppermute | solution.py:575
  15.7 0.0 collective-permute-done.low
  15.7 0.0 copy-start.1
  15.7 0.0 copy-start.2
  15.7 0.0 copy-start.4
  15.7 0.0 copy-start.5
  15.8 0.0 copy-start.8
  15.8 0.0 copy-start.9
  15.8 0.0 copy-start.10
  15.8 0.0 copy-start.11
  15.8 6.3 %attention_forward.1 = (bf16[1600,256]{1,0:T(8,128)(2,1)S(1)}, bf16[1664,256]{1,0:T(8,128)(2,1)S(1)}, bf16[2,8,128,768]{3,2,1,0:T(8,128)(2,1)S(1)}, bf16[2,8,832...) custom-call(bf16[10,20,8,256]{3,2,1,0:T(8,128)(2,1)S(1)} %bitcast.24, ...), custom_call_target="tpu_custom_call" | custom-call | flops 10000000000 | bytes 10000000 | tf_op jit(solution)/shard_map/attention_forward/pallas_call | solution.py:729
  22.1 0.0 collective-permute-done.4.t_right
  22.1 0.0 collective-permute-done.5.t_corner
  22.2 8.7 %mlp_forward_backward.1 = (bf16[5,15,8,256]{3,2,1,0:T(8,128)(2,1)S(1)}, bf16[5,15,8,256]{3,2,1,0:T(8,128)(2,1)S(1)}, bf16[5,5,8,256]{3,2,1,0:T(8,128)(2,1)S(1)},...) custom-call(bf16[1600,256]{1,0:T(8,128)(2,1)S(1)} %get-tuple-element, ...), custom_call_target="tpu_custom_call" | custom-call | flops 10000000000 | bytes 10000000 | tf_op jit(solution)/shard_map/mlp_forward_backward/pallas_call | solution.py:754
  30.9 0.1 collective-permute-start.6
  31.0 1.3 %collective-permute-start.11 = (bf16[5,5,8,256]{3,2,1,0:T(8,128)(2,1)S(1)}, bf16[5,5,8,256]{3,2,1,0:T(8,128)(2,1)S(1)}, u32[]{:S(2)}, u32[]{:S(2)}) collective-permute-start(bf16[5,5,8,256]{3,2,1,0:T(8,128)(2,1)S(1)} %get-tuple-element.107), channel_id=1, source_target_pairs={{0,3},{1,2},{2,5},{3,4},{4,7},{5,6},{6,9},{7,8},{8,11},{9,10},{10,... | collective-permute-start | bytes 307208 | tf_op jit(solution)/shard_map/ppermute | solution.py:575
  32.3 0.0 collective-permute-start.10
  32.3 0.6 collective-permute-done.6.other
  32.9 0.1 split_sums.2
  33.1 1.4 %collective-permute-start.7 = (bf16[288,256]{1,0:T(8,128)(2,1)S(1)}, bf16[288,256]{1,0:T(8,128)(2,1)S(1)}, u32[]{:S(2)}, u32[]{:S(2)}) collective-permute-start(bf16[288,256]{1,0:T(8,128)(2,1)S(1)} %get-tuple-element.103), channel_id=1, source_target_pairs={{0,1},{1,0},{2,3},{3,2},{4,5},{5,4},{6,7},{7,6},{8,9},{9,8},{10,11... | collective-permute-start | bytes 442376 | tf_op jit(solution)/shard_map/ppermute | solution.py:575
  34.5 2.2 %collective-permute-start.9 = (bf16[288,256]{1,0:T(8,128)(2,1)S(1)}, bf16[288,256]{1,0:T(8,128)(2,1)S(1)}, u32[]{:S(2)}, u32[]{:S(2)}) collective-permute-start(bf16[288,256]{1,0:T(8,128)(2,1)S(1)} %get-tuple-element.105), channel_id=1, source_target_pairs={{0,5},{1,4},{2,7},{3,6},{4,1},{5,0},{6,3},{7,2},{8,13},{9,12},{10,... | collective-permute-start | bytes 442376 | tf_op jit(solution)/shard_map/ppermute | solution.py:575
  36.6 8.8 %attention_backward.1 = (f32[5,15,8,256]{3,2,1,0:T(8,128)S(1)}, bf16[10,5,8,256]{3,2,1,0:T(8,128)(2,1)S(1)}, bf16[5,5,8,256]{3,2,1,0:T(8,128)(2,1)S(1)}, bf16[5,...) custom-call(bf16[1664,256]{1,0:T(8,128)(2,1)S(1)} %get-tuple-element.108.xw, ...), custom_call_target="tpu_custom_call" | custom-call | flops 10000000000 | bytes 10000000 | tf_op jit(solution)/shard_map/attention_backward/pallas_call | solution.py:787
  45.4 0.0 collective-permute-done.10
  45.4 0.0 collective-permute-done.7.refs_1_
  45.4 2.4 %collective-permute-done.8.refs_2_ = bf16[288,256]{1,0:T(8,128)(2,1)S(1)} collective-permute-done((bf16[288,256]{1,0:T(8,128)(2,1)S(1)}, bf16[288,256]{1,0:T(8,128)(2,1)S(1)}, u32[]{:S(2)}, u32[]{:S(2)}) %collective-permute-start.8) | collective-permute-done | bytes 147488 | tf_op jit(solution)/shard_map/ppermute | solution.py:575
  47.9 0.0 collective-permute-done.9.refs_3_
  47.9 0.1 add_pieces.4.refs_0_
  47.9 0.1 collective-permute-start.12
  48.0 1.5 %collective-permute-done.12.other = bf16[448,256]{1,0:T(8,128)(2,1)S(1)} collective-permute-done((bf16[448,256]{1,0:T(8,128)(2,1)S(1)}, bf16[448,256]{1,0:T(8,128)(2,1)S(1)}, u32[]{:S(2)}, u32[]{:S(2)}) %collective-permute-start.12) | collective-permute-done | bytes 229408 | tf_op jit(solution)/shard_map/ppermute | solution.py:575
  49.5 0.1 split_sums.3
  49.6 0.5 collective-permute-start.13
  50.1 0.0 collective-permute-start.14
  50.1 3.0 %collective-permute-start.15 = (bf16[112,256]{1,0:T(8,128)(2,1)S(1)}, bf16[112,256]{1,0:T(8,128)(2,1)S(1)}, u32[]{:S(2)}, u32[]{:S(2)}) collective-permute-start(bf16[112,256]{1,0:T(8,128)(2,1)S(1)} %get-tuple-element.130), channel_id=1, source_target_pairs={{0,5},{1,4},{2,7},{3,6},{4,1},{5,0},{6,3},{7,2},{8,13},{9,12},{10,... | collective-permute-start | bytes 172040 | tf_op jit(solution)/shard_map/ppermute | solution.py:575
  53.1 0.8 collective-permute-done.13.refs_1_
  53.9 1.4 %collective-permute-done.14.refs_2_ = bf16[112,256]{1,0:T(8,128)(2,1)S(1)} collective-permute-done((bf16[112,256]{1,0:T(8,128)(2,1)S(1)}, bf16[112,256]{1,0:T(8,128)(2,1)S(1)}, u32[]{:S(2)}, u32[]{:S(2)}) %collective-permute-start.14) | collective-permute-done | bytes 57376 | tf_op jit(solution)/shard_map/ppermute | solution.py:575
  55.4 0.1 collective-permute-start.16
  55.5 0.1 collective-permute-start.18
  55.6 5.7 %collective-permute-done.16.refs_1_ = bf16[400,256]{1,0:T(8,128)(2,1)S(1)} collective-permute-done((bf16[400,256]{1,0:T(8,128)(2,1)S(1)}, bf16[400,256]{1,0:T(8,128)(2,1)S(1)}, u32[]{:S(2)}, u32[]{:S(2)}) %collective-permute-start.16) | collective-permute-done | bytes 204832 | tf_op jit(solution)/shard_map/ppermute | solution.py:575
  61.3 0.9 %collective-permute-start.17 = (bf16[400,256]{1,0:T(8,128)(2,1)S(1)}, bf16[400,256]{1,0:T(8,128)(2,1)S(1)}, u32[]{:S(2)}, u32[]{:S(2)}) collective-permute-start(bf16[400,256]{1,0:T(8,128)(2,1)S(1)} %add_pieces.6.refs_0_), channel_id=1, source_target_pairs={{0,16},{1,17},{2,18},{3,19},{4,20},{5,21},{6,22},{7,23},{8,24},{9,... | collective-permute-start | bytes 614408 | tf_op jit(solution)/shard_map/ppermute | solution.py:575
  62.3 1.1 %collective-permute-start.19 = (bf16[10,5,8,256]{3,2,1,0:T(8,128)(2,1)S(1)}, bf16[10,5,8,256]{3,2,1,0:T(8,128)(2,1)S(1)}, u32[]{:S(2)}, u32[]{:S(2)}) collective-permute-start(bf16[10,5,8,256]{3,2,1,0:T(8,128)(2,1)S(1)} %get-tuple-element.135), channel_id=1, source_target_pairs={{0,1},{1,0},{2,3},{3,2},{4,5},{5,4},{6,7},{7,6},{8,9},{9,8},{10,11... | collective-permute-start | bytes 614408 | tf_op jit(solution)/shard_map/ppermute | solution.py:575
  63.4 7.7 %collective-permute-done.17.refs_1_ = bf16[400,256]{1,0:T(8,128)(2,1)S(1)} collective-permute-done((bf16[400,256]{1,0:T(8,128)(2,1)S(1)}, bf16[400,256]{1,0:T(8,128)(2,1)S(1)}, u32[]{:S(2)}, u32[]{:S(2)}) %collective-permute-start.17) | collective-permute-done | bytes 204832 | tf_op jit(solution)/shard_map/ppermute | solution.py:575
  71.2 0.7 collective-permute-done.20.refs_4_
  71.9 0.0 collective-permute-done.19.refs_3_
  71.9 0.0 collective-permute-done.18.refs_2_
  71.9 4.5 %collective-permute-start.23 = (bf16[400,256]{1,0:T(8,128)(2,1)S(1)}, bf16[400,256]{1,0:T(8,128)(2,1)S(1)}, u32[]{:S(2)}, u32[]{:S(2)}) collective-permute-start(bf16[400,256]{1,0:T(8,128)(2,1)S(1)} %add_pieces.7.refs_0_), channel_id=1, source_target_pairs={{0,5},{1,4},{2,7},{3,6},{4,1},{5,0},{6,3},{7,2},{8,13},{9,12},{10,... | collective-permute-start | bytes 614408 | tf_op jit(solution)/shard_map/ppermute | solution.py:575
  76.3 1.1 %collective-permute-start.21 = (bf16[400,256]{1,0:T(8,128)(2,1)S(1)}, bf16[400,256]{1,0:T(8,128)(2,1)S(1)}, u32[]{:S(2)}, u32[]{:S(2)}) collective-permute-start(bf16[400,256]{1,0:T(8,128)(2,1)S(1)} %add_pieces.7.refs_0_), channel_id=1, source_target_pairs={{0,1},{1,0},{2,3},{3,2},{4,5},{5,4},{6,7},{7,6},{8,9},{9,8},{10,11... | collective-permute-start | bytes 614408 | tf_op jit(solution)/shard_map/ppermute | solution.py:575
  77.4 4.9 %collective-permute-done.23.refs_3_ = bf16[400,256]{1,0:T(8,128)(2,1)S(1)} collective-permute-done((bf16[400,256]{1,0:T(8,128)(2,1)S(1)}, bf16[400,256]{1,0:T(8,128)(2,1)S(1)}, u32[]{:S(2)}, u32[]{:S(2)}) %collective-permute-start.23) | collective-permute-done | bytes 204832 | tf_op jit(solution)/shard_map/ppermute | solution.py:575
  82.3 2.9 %collective-permute-done.22.refs_2_ = bf16[400,256]{1,0:T(8,128)(2,1)S(1)} collective-permute-done((bf16[400,256]{1,0:T(8,128)(2,1)S(1)}, bf16[400,256]{1,0:T(8,128)(2,1)S(1)}, u32[]{:S(2)}, u32[]{:S(2)}) %collective-permute-start.22) | collective-permute-done | bytes 204832 | tf_op jit(solution)/shard_map/ppermute | solution.py:575
  85.2 0.4 collective-permute-done.21.refs_1_
  85.6 0.1 join_pieces.3.refs_0_
  85.7 0.1 collective-permute-start.24
  85.8 1.0 %maximum_maximum_fusion = bf16[10,20,8,256]{3,2,1,0:T(8,128)(2,1)} fusion(bf16[5,15,8,256]{3,2,1,0:T(8,128)(2,1)S(1)} %get-tuple-element.141, bf16[5,5,8,256]{3,2,1,0:T(8,128)(2,1)S(1)} %slice.3, bf16[5,15,8,256]{3,2,1,0:T(8,128)(2,1)S(1)} %collective-permute-done.10, bf16[5,5,8,256]{3,2,1,0:T(8,128)(2,1)S(1)} %collective-permute-done.11), kind=kLoop, calls=%fused_computation | loop fusion | flops 1228800 | bytes 1638400 | tf_op jit(solution)/shard_map/concatenate | solution.py:883
  86.7 1.3 %collective-permute-done.24.refs_1_ = bf16[1600,256]{1,0:T(8,128)(2,1)S(1)} collective-permute-done((bf16[1600,256]{1,0:T(8,128)(2,1)S(1)}, bf16[1600,256]{1,0:T(8,128)(2,1)S(1)}, u32[]{:S(2)}, u32[]{:S(2)}) %collective-permute-start.24) | collective-permute-done | bytes 819232 | tf_op jit(solution)/shard_map/ppermute | solution.py:575
  88.1 2.5 %finish_sums.1 = (f32[10,20,8,256]{3,2,1,0:T(8,128)}, f32[256,1024]{1,0:T(8,128)}, f32[1024,256]{1,0:T(8,128)}, f32[256,256]{1,0:T(8,128)}, f32[1,1024]{1,0:T(1,...) custom-call(bf16[1600,256]{1,0:T(8,128)(2,1)S(1)} %join_pieces.3.ref, ...), custom_call_target="tpu_custom_call" | custom-call | tf_op jit(solution)/shard_map/finish_sums/pallas_call | solution.py:815
  (31 shorter events, 0.2 us)
Async XLA Ops:
  0.6 15.0 %copy-start = (bf16[8,10,20,256]{3,0,2,1:T(8,128)(2,1)S(1)}, bf16[8,10,20,256]{3,0,2,1:T(8,128)(2,1)}, u32[]{:S(2)}) copy-start(bf16[8,10,20,256]{3,0,2,1:T(8,128)(2,1)} %param.17) | copy-start | bytes 2457604
  0.7 15.0 %copy-start.3 = (bf16[256,768]{1,0:T(8,128)(2,1)S(1)}, bf16[256,768]{1,0:T(8,128)(2,1)}, u32[]{:S(2)}) copy-start(bf16[256,768]{1,0:T(8,128)(2,1)} %qkv_w.3) | copy-start | bytes 1179652
  0.7 15.0 %copy-start.7 = (f32[256]{0:T(256)S(1)}, f32[256]{0:T(256)}, u32[]{:S(2)}) copy-start(f32[256]{0:T(256)} %param.24) | copy-start | bytes 3076
  0.7 15.0 %copy-start.6 = (f32[256]{0:T(256)S(1)}, f32[256]{0:T(256)}, u32[]{:S(2)}) copy-start(f32[256]{0:T(256)} %param.23) | copy-start | bytes 3076
  0.7 15.0 %copy-start.13 = (f32[256]{0:T(256)S(1)}, f32[256]{0:T(256)}, u32[]{:S(2)}) copy-start(f32[256]{0:T(256)} %param.21) | copy-start | bytes 3076
  0.7 15.0 %copy-start.12 = (f32[256]{0:T(256)S(1)}, f32[256]{0:T(256)}, u32[]{:S(2)}) copy-start(f32[256]{0:T(256)} %param.20) | copy-start | bytes 3076
  1.9 13.8 %collective-permute-start = (bf16[5,20,8,256]{3,2,1,0:T(8,128)(2,1)S(1)}, bf16[5,20,8,256]{3,2,1,0:T(8,128)(2,1)S(1)}, u32[]{:S(2)}, u32[]{:S(2)}) collective-permute-start(bf16[5,20,8,256]{3,2,1,0:T(8,128)(2,1)S(1)} %get-tuple-element.89), channel_id=1, source_target_pairs={{0,30},{1,31},{2,0},{3,1},{4,2},{5,3},{6,4},{7,5},{8,6},{9,7},{10,... | collective-permute-start | bytes 1228808 | tf_op jit(solution)/shard_map/ppermute | solution.py:575
  7.4 7.0 %collective-permute-start.1 = (bf16[5,5,8,256]{3,2,1,0:T(8,128)(2,1)S(1)}, bf16[5,5,8,256]{3,2,1,0:T(8,128)(2,1)S(1)}, u32[]{:S(2)}, u32[]{:S(2)}) collective-permute-start(bf16[5,5,8,256]{3,2,1,0:T(8,128)(2,1)S(1)} %get-tuple-element.90), channel_id=1, source_target_pairs={{0,1},{1,0},{2,3},{3,2},{4,5},{5,4},{6,7},{7,6},{8,9},{9,8},{10,11... | collective-permute-start | bytes 307208 | tf_op jit(solution)/shard_map/ppermute | solution.py:575
  8.9 6.8 %collective-permute-start.2 = (bf16[5,5,8,256]{3,2,1,0:T(8,128)(2,1)S(1)}, bf16[5,5,8,256]{3,2,1,0:T(8,128)(2,1)S(1)}, u32[]{:S(2)}, u32[]{:S(2)}) collective-permute-start(bf16[5,5,8,256]{3,2,1,0:T(8,128)(2,1)S(1)} %get-tuple-element.91), channel_id=1, source_target_pairs={{0,31},{1,30},{2,1},{3,0},{4,3},{5,2},{6,5},{7,4},{8,7},{9,6},{10,... | collective-permute-start | bytes 307208 | tf_op jit(solution)/shard_map/ppermute | solution.py:575
  10.9 11.2 %collective-permute-start.4 = (bf16[5,5,8,256]{3,2,1,0:T(8,128)(2,1)S(1)}, bf16[5,5,8,256]{3,2,1,0:T(8,128)(2,1)S(1)}, u32[]{:S(2)}, u32[]{:S(2)}) collective-permute-start(bf16[5,5,8,256]{3,2,1,0:T(8,128)(2,1)S(1)} %get-tuple-element.97), channel_id=1, source_target_pairs={{0,1},{1,0},{2,3},{3,2},{4,5},{5,4},{6,7},{7,6},{8,9},{9,8},{10,11... | collective-permute-start | bytes 307208 | tf_op jit(solution)/shard_map/ppermute | solution.py:575
  12.4 9.7 %collective-permute-start.5 = (bf16[5,5,8,256]{3,2,1,0:T(8,128)(2,1)S(1)}, bf16[5,5,8,256]{3,2,1,0:T(8,128)(2,1)S(1)}, u32[]{:S(2)}, u32[]{:S(2)}) collective-permute-start(bf16[5,5,8,256]{3,2,1,0:T(8,128)(2,1)S(1)} %get-tuple-element.98), channel_id=1, source_target_pairs={{0,31},{1,30},{2,1},{3,0},{4,3},{5,2},{6,5},{7,4},{8,7},{9,6},{10,... | collective-permute-start | bytes 307208 | tf_op jit(solution)/shard_map/ppermute | solution.py:575
  14.4 7.8 %collective-permute-start.3 = (bf16[5,20,8,256]{3,2,1,0:T(8,128)(2,1)S(1)}, bf16[5,20,8,256]{3,2,1,0:T(8,128)(2,1)S(1)}, u32[]{:S(2)}, u32[]{:S(2)}) collective-permute-start(bf16[5,20,8,256]{3,2,1,0:T(8,128)(2,1)S(1)} %get-tuple-element.96), channel_id=1, source_target_pairs={{0,30},{1,31},{2,0},{3,1},{4,2},{5,3},{6,4},{7,5},{8,6},{9,7},{10,... | collective-permute-start | bytes 1228808 | tf_op jit(solution)/shard_map/ppermute | solution.py:575
  15.7 6.4 %copy-start.1 = (bf16[256,1024]{1,0:T(8,128)(2,1)S(1)}, bf16[256,1024]{1,0:T(8,128)(2,1)}, u32[]{:S(2)}) copy-start(bf16[256,1024]{1,0:T(8,128)(2,1)} %fc1_w.1) | copy-start | bytes 1572868
  15.7 6.4 %copy-start.2 = (bf16[1024,256]{1,0:T(8,128)(2,1)S(1)}, bf16[1024,256]{1,0:T(8,128)(2,1)}, u32[]{:S(2)}) copy-start(bf16[1024,256]{1,0:T(8,128)(2,1)} %fc2_w.1) | copy-start | bytes 1572868
  15.7 6.4 %copy-start.4 = (bf16[256,256]{1,0:T(8,128)(2,1)S(1)}, bf16[256,256]{1,0:T(8,128)(2,1)}, u32[]{:S(2)}) copy-start(bf16[256,256]{1,0:T(8,128)(2,1)} %proj_w.1) | copy-start | bytes 393220
  15.7 6.4 %copy-start.5 = (f32[1024]{0:T(1024)S(1)}, f32[1024]{0:T(1024)}, u32[]{:S(2)}) copy-start(f32[1024]{0:T(1024)} %param.31) | copy-start | bytes 12292
  15.8 6.4 %copy-start.8 = (f32[256]{0:T(256)S(1)}, f32[256]{0:T(256)}, u32[]{:S(2)}) copy-start(f32[256]{0:T(256)} %param.27) | copy-start | bytes 3076
  15.8 6.4 %copy-start.9 = (f32[256]{0:T(256)S(1)}, f32[256]{0:T(256)}, u32[]{:S(2)}) copy-start(f32[256]{0:T(256)} %param.28) | copy-start | bytes 3076
  15.8 6.4 %copy-start.10 = (f32[256]{0:T(256)S(1)}, f32[256]{0:T(256)}, u32[]{:S(2)}) copy-start(f32[256]{0:T(256)} %param.29) | copy-start | bytes 3076
  15.8 6.4 %copy-start.11 = (f32[256]{0:T(256)S(1)}, f32[256]{0:T(256)}, u32[]{:S(2)}) copy-start(f32[256]{0:T(256)} %param.33) | copy-start | bytes 3076
  30.9 2.1 %collective-permute-start.6 = (bf16[1152,256]{1,0:T(8,128)(2,1)S(1)}, bf16[1152,256]{1,0:T(8,128)(2,1)S(1)}, u32[]{:S(2)}, u32[]{:S(2)}) collective-permute-start(bf16[1152,256]{1,0:T(8,128)(2,1)S(1)} %get-tuple-element.101), channel_id=1, source_target_pairs={{0,2},{1,3},{2,0},{3,1},{4,6},{5,7},{6,4},{7,5},{8,10},{9,11},{10,... | collective-permute-start | bytes 1769480 | tf_op jit(solution)/shard_map/ppermute | solution.py:575
  31.0 14.4 %collective-permute-start.11 = (bf16[5,5,8,256]{3,2,1,0:T(8,128)(2,1)S(1)}, bf16[5,5,8,256]{3,2,1,0:T(8,128)(2,1)S(1)}, u32[]{:S(2)}, u32[]{:S(2)}) collective-permute-start(bf16[5,5,8,256]{3,2,1,0:T(8,128)(2,1)S(1)} %get-tuple-element.107), channel_id=1, source_target_pairs={{0,3},{1,2},{2,5},{3,4},{4,7},{5,6},{6,9},{7,8},{8,11},{9,10},{10,... | collective-permute-start | bytes 307208 | tf_op jit(solution)/shard_map/ppermute | solution.py:575
  32.3 13.1 %collective-permute-start.10 = (bf16[5,15,8,256]{3,2,1,0:T(8,128)(2,1)S(1)}, bf16[5,15,8,256]{3,2,1,0:T(8,128)(2,1)S(1)}, u32[]{:S(2)}, u32[]{:S(2)}) collective-permute-start(bf16[5,15,8,256]{3,2,1,0:T(8,128)(2,1)S(1)} %get-tuple-element.106), channel_id=1, source_target_pairs={{0,2},{1,3},{2,4},{3,5},{4,6},{5,7},{6,8},{7,9},{8,10},{9,11},{10,... | collective-permute-start | bytes 921608 | tf_op jit(solution)/shard_map/ppermute | solution.py:575
  33.1 12.3 %collective-permute-start.7 = (bf16[288,256]{1,0:T(8,128)(2,1)S(1)}, bf16[288,256]{1,0:T(8,128)(2,1)S(1)}, u32[]{:S(2)}, u32[]{:S(2)}) collective-permute-start(bf16[288,256]{1,0:T(8,128)(2,1)S(1)} %get-tuple-element.103), channel_id=1, source_target_pairs={{0,1},{1,0},{2,3},{3,2},{4,5},{5,4},{6,7},{7,6},{8,9},{9,8},{10,11... | collective-permute-start | bytes 442376 | tf_op jit(solution)/shard_map/ppermute | solution.py:575
  34.5 13.4 %collective-permute-start.8 = (bf16[288,256]{1,0:T(8,128)(2,1)S(1)}, bf16[288,256]{1,0:T(8,128)(2,1)S(1)}, u32[]{:S(2)}, u32[]{:S(2)}) collective-permute-start(bf16[288,256]{1,0:T(8,128)(2,1)S(1)} %get-tuple-element.104), channel_id=1, source_target_pairs={{0,4},{1,5},{2,6},{3,7},{4,0},{5,1},{6,2},{7,3},{8,12},{9,13},{10,... | collective-permute-start | bytes 442376 | tf_op jit(solution)/shard_map/ppermute | solution.py:575
  34.5 13.4 %collective-permute-start.9 = (bf16[288,256]{1,0:T(8,128)(2,1)S(1)}, bf16[288,256]{1,0:T(8,128)(2,1)S(1)}, u32[]{:S(2)}, u32[]{:S(2)}) collective-permute-start(bf16[288,256]{1,0:T(8,128)(2,1)S(1)} %get-tuple-element.105), channel_id=1, source_target_pairs={{0,5},{1,4},{2,7},{3,6},{4,1},{5,0},{6,3},{7,2},{8,13},{9,12},{10,... | collective-permute-start | bytes 442376 | tf_op jit(solution)/shard_map/ppermute | solution.py:575
  47.9 1.6 %collective-permute-start.12 = (bf16[448,256]{1,0:T(8,128)(2,1)S(1)}, bf16[448,256]{1,0:T(8,128)(2,1)S(1)}, u32[]{:S(2)}, u32[]{:S(2)}) collective-permute-start(bf16[448,256]{1,0:T(8,128)(2,1)S(1)} %get-tuple-element.126), channel_id=1, source_target_pairs={{0,2},{1,3},{2,0},{3,1},{4,6},{5,7},{6,4},{7,5},{8,10},{9,11},{10,... | collective-permute-start | bytes 688136 | tf_op jit(solution)/shard_map/ppermute | solution.py:575
  49.6 4.4 %collective-permute-start.13 = (bf16[112,256]{1,0:T(8,128)(2,1)S(1)}, bf16[112,256]{1,0:T(8,128)(2,1)S(1)}, u32[]{:S(2)}, u32[]{:S(2)}) collective-permute-start(bf16[112,256]{1,0:T(8,128)(2,1)S(1)} %get-tuple-element.128), channel_id=1, source_target_pairs={{0,1},{1,0},{2,3},{3,2},{4,5},{5,4},{6,7},{7,6},{8,9},{9,8},{10,11... | collective-permute-start | bytes 172040 | tf_op jit(solution)/shard_map/ppermute | solution.py:575
  50.1 5.3 %collective-permute-start.14 = (bf16[112,256]{1,0:T(8,128)(2,1)S(1)}, bf16[112,256]{1,0:T(8,128)(2,1)S(1)}, u32[]{:S(2)}, u32[]{:S(2)}) collective-permute-start(bf16[112,256]{1,0:T(8,128)(2,1)S(1)} %get-tuple-element.129), channel_id=1, source_target_pairs={{0,4},{1,5},{2,6},{3,7},{4,0},{5,1},{6,2},{7,3},{8,12},{9,13},{10,... | collective-permute-start | bytes 172040 | tf_op jit(solution)/shard_map/ppermute | solution.py:575
  50.1 5.3 %collective-permute-start.15 = (bf16[112,256]{1,0:T(8,128)(2,1)S(1)}, bf16[112,256]{1,0:T(8,128)(2,1)S(1)}, u32[]{:S(2)}, u32[]{:S(2)}) collective-permute-start(bf16[112,256]{1,0:T(8,128)(2,1)S(1)} %get-tuple-element.130), channel_id=1, source_target_pairs={{0,5},{1,4},{2,7},{3,6},{4,1},{5,0},{6,3},{7,2},{8,13},{9,12},{10,... | collective-permute-start | bytes 172040 | tf_op jit(solution)/shard_map/ppermute | solution.py:575
  55.4 5.8 %collective-permute-start.16 = (bf16[400,256]{1,0:T(8,128)(2,1)S(1)}, bf16[400,256]{1,0:T(8,128)(2,1)S(1)}, u32[]{:S(2)}, u32[]{:S(2)}) collective-permute-start(bf16[400,256]{1,0:T(8,128)(2,1)S(1)} %join_pieces.2.refs_0_), channel_id=1, source_target_pairs={{0,8},{1,9},{2,10},{3,11},{4,12},{5,13},{6,14},{7,15},{8,0},{9,1},... | collective-permute-start | bytes 614408 | tf_op jit(solution)/shard_map/ppermute | solution.py:575
  55.5 16.4 %collective-permute-start.18 = (bf16[5,15,8,256]{3,2,1,0:T(8,128)(2,1)S(1)}, bf16[5,15,8,256]{3,2,1,0:T(8,128)(2,1)S(1)}, u32[]{:S(2)}, u32[]{:S(2)}) collective-permute-start(bf16[5,15,8,256]{3,2,1,0:T(8,128)(2,1)S(1)} %get-tuple-element.134), channel_id=1, source_target_pairs={{0,2},{1,3},{2,4},{3,5},{4,6},{5,7},{6,8},{7,9},{8,10},{9,11},{10,... | collective-permute-start | bytes 921608 | tf_op jit(solution)/shard_map/ppermute | solution.py:575
  61.3 9.8 %collective-permute-start.17 = (bf16[400,256]{1,0:T(8,128)(2,1)S(1)}, bf16[400,256]{1,0:T(8,128)(2,1)S(1)}, u32[]{:S(2)}, u32[]{:S(2)}) collective-permute-start(bf16[400,256]{1,0:T(8,128)(2,1)S(1)} %add_pieces.6.refs_0_), channel_id=1, source_target_pairs={{0,16},{1,17},{2,18},{3,19},{4,20},{5,21},{6,22},{7,23},{8,24},{9,... | collective-permute-start | bytes 614408 | tf_op jit(solution)/shard_map/ppermute | solution.py:575
  62.3 9.6 %collective-permute-start.19 = (bf16[10,5,8,256]{3,2,1,0:T(8,128)(2,1)S(1)}, bf16[10,5,8,256]{3,2,1,0:T(8,128)(2,1)S(1)}, u32[]{:S(2)}, u32[]{:S(2)}) collective-permute-start(bf16[10,5,8,256]{3,2,1,0:T(8,128)(2,1)S(1)} %get-tuple-element.135), channel_id=1, source_target_pairs={{0,1},{1,0},{2,3},{3,2},{4,5},{5,4},{6,7},{7,6},{8,9},{9,8},{10,11... | collective-permute-start | bytes 614408 | tf_op jit(solution)/shard_map/ppermute | solution.py:575
  63.4 8.5 %collective-permute-start.20 = (bf16[5,5,8,256]{3,2,1,0:T(8,128)(2,1)S(1)}, bf16[5,5,8,256]{3,2,1,0:T(8,128)(2,1)S(1)}, u32[]{:S(2)}, u32[]{:S(2)}) collective-permute-start(bf16[5,5,8,256]{3,2,1,0:T(8,128)(2,1)S(1)} %get-tuple-element.136), channel_id=1, source_target_pairs={{0,3},{1,2},{2,5},{3,4},{4,7},{5,6},{6,9},{7,8},{8,11},{9,10},{10,... | collective-permute-start | bytes 307208 | tf_op jit(solution)/shard_map/ppermute | solution.py:575
  71.9 10.4 %collective-permute-start.23 = (bf16[400,256]{1,0:T(8,128)(2,1)S(1)}, bf16[400,256]{1,0:T(8,128)(2,1)S(1)}, u32[]{:S(2)}, u32[]{:S(2)}) collective-permute-start(bf16[400,256]{1,0:T(8,128)(2,1)S(1)} %add_pieces.7.refs_0_), channel_id=1, source_target_pairs={{0,5},{1,4},{2,7},{3,6},{4,1},{5,0},{6,3},{7,2},{8,13},{9,12},{10,... | collective-permute-start | bytes 614408 | tf_op jit(solution)/shard_map/ppermute | solution.py:575
  76.3 8.8 %collective-permute-start.22 = (bf16[400,256]{1,0:T(8,128)(2,1)S(1)}, bf16[400,256]{1,0:T(8,128)(2,1)S(1)}, u32[]{:S(2)}, u32[]{:S(2)}) collective-permute-start(bf16[400,256]{1,0:T(8,128)(2,1)S(1)} %add_pieces.7.refs_0_), channel_id=1, source_target_pairs={{0,4},{1,5},{2,6},{3,7},{4,0},{5,1},{6,2},{7,3},{8,12},{9,13},{10,... | collective-permute-start | bytes 614408 | tf_op jit(solution)/shard_map/ppermute | solution.py:575
  76.3 9.3 %collective-permute-start.21 = (bf16[400,256]{1,0:T(8,128)(2,1)S(1)}, bf16[400,256]{1,0:T(8,128)(2,1)S(1)}, u32[]{:S(2)}, u32[]{:S(2)}) collective-permute-start(bf16[400,256]{1,0:T(8,128)(2,1)S(1)} %add_pieces.7.refs_0_), channel_id=1, source_target_pairs={{0,1},{1,0},{2,3},{3,2},{4,5},{5,4},{6,7},{7,6},{8,9},{9,8},{10,11... | collective-permute-start | bytes 614408 | tf_op jit(solution)/shard_map/ppermute | solution.py:575
  85.7 2.4 %collective-permute-start.24 = (bf16[1600,256]{1,0:T(8,128)(2,1)S(1)}, bf16[1600,256]{1,0:T(8,128)(2,1)S(1)}, u32[]{:S(2)}, u32[]{:S(2)}) collective-permute-start(bf16[1600,256]{1,0:T(8,128)(2,1)S(1)} %join_pieces.3.refs_0_), channel_id=1, source_target_pairs={{0,2},{1,3},{2,0},{3,1},{4,6},{5,7},{6,4},{7,5},{8,10},{9,11},{10,... | collective-permute-start | bytes 2457608 | tf_op jit(solution)/shard_map/ppermute | solution.py:575

commit v6 on v5

--- a/solution.py
+++ b/solution.py
@@ -21,6 +21,7 @@
 RELS = 384
 NEVER = -1e30
 PAGES = 8
+VECTORS = 32
 BACK_AT_ONCE = 1
 AT_ONCE = 4
 VMEM_LIMIT = 20
@@ -428,8 +429,12 @@
     corner[...] = right[SHIFT:, SHIFT:].astype(BF16)
     up[:, :WIN] = left[SHIFT:].astype(BF16)
     up[:, WIN:] = right[SHIFT:, :SHIFT].astype(BF16)
-    for j in range(3):
-        sums_out[j * d : (j + 1) * d, :] = qkv_acc[:, j * d : (j + 1) * d].astype(BF16)
+    half = sums_out.shape[0] // 2
+    part = 3 * d // 2
+    for j in range(6):
+        at = j // 3 * half + j % 3 * (d // 2)
+        rows = slice(j % 2 * (d // 2), (j % 2 + 1) * (d // 2))
+        sums_out[at : at + d // 2, :] = qkv_acc[rows, j // 2 * d : (j // 2 + 1) * d].astype(BF16)
     rel = table_gradient(
         [rel_acc[:, h * KEYS : (h + 1) * KEYS] for h in range(heads)], mixed
     )
@@ -440,11 +445,13 @@
     rows.append(rel[:, :d])
     rows.append(jnp.concatenate([rel[:, d:], jnp.zeros((heads, 2 * d - RELS), F32)], 1))
     high, rest = split_rows(jnp.concatenate(rows, 0))
-    at = 3 * d
-    sums_out[at : at + 32, :] = high
-    sums_out[at + 32 : at + 64, :] = rest
-    if sums_out.shape[0] > at + 64:
-        sums_out[at + 64 :, :] = jnp.zeros((sums_out.shape[0] - at - 64, d), BF16)
+    for start in (0, half):
+        at = start + part
+        sums_out[at : at + VECTORS, :] = high
+        sums_out[at + VECTORS : at + 2 * VECTORS, :] = rest
+        at += 2 * VECTORS
+        if at < start + half:
+            sums_out[at : start + half, :] = jnp.zeros((start + half - at, d), BF16)
     split_halves(sums_out, mine, other)
 
 
@@ -531,24 +538,35 @@
             )
 
 
+def gradient_kernel(total, planes, count_row, first, size, mine, up, side, corner, stays, grad):
+    _, spot = core_and_spot()
+    stride = mine.shape[0] // planes
+    count = 0.0
+    for row in (count_row, count_row + VECTORS):
+        piece, at = row // size, row % size
+        start = (spot ^ piece) * stride + first + at // 16 * 16
+        block = mine[pl.ds(pl.multiple_of(start, 16), 16), :].astype(F32)
+        count = count + block[at % 16 : at % 16 + 1]
+    wide = (total / count).reshape(1, 1, 1, count.shape[1])
+    rest = up.shape[0]
+    grad[:rest, :SHIFT] = corner[...].astype(F32) * wide
+    grad[:rest, SHIFT:] = up[...].astype(F32) * wide
+    grad[rest:, :SHIFT] = side[SHIFT:].astype(F32) * wide
+    grad[rest:, SHIFT:] = stays[...] * wide
+
+
 def finish_kernel(
-    total, planes, sizes, mine, other, up, side, corner, stays,
-    grad, fc1, fc2, proj, fc1_b, g2, b2, fc2_b, proj_b, qkv, g1, b1, q_b, v_b, rel, buf1, buf2,
+    total, planes, sizes, mine, other,
+    fc1, fc2, proj, fc1_b, g2, b2, fc2_b, proj_b, qkv, g1, b1, q_b, v_b, rel, buf1, buf2,
 ):
     collect(buf1, mine, other, planes, 0, sizes[0])
     collect(buf2, mine, other, planes, sizes[0], sizes[1])
     d = proj.shape[0]
     ff = fc1.shape[1] // d
-    at = 3 * d
-    rows = buf2[at : at + 32, :] + buf2[at + 32 : at + 64, :]
+    half, at = buf2.shape[0] // 2, 3 * d // 2
+    rows = buf2[at : at + VECTORS, :] + buf2[at + VECTORS : at + 2 * VECTORS, :]
     scale = total / rows[ff + 8 : ff + 9, :]
     rows = rows * scale
-    wide = scale.reshape(1, 1, 1, d)
-    rest = up.shape[0]
-    grad[:rest, :SHIFT] = corner[...].astype(F32) * wide
-    grad[:rest, SHIFT:] = up[...].astype(F32) * wide
-    grad[rest:, :SHIFT] = side[SHIFT:].astype(F32) * wide
-    grad[rest:, SHIFT:] = stays[...] * wide
     for j in range(ff):
         fc1[:, j * d : (j + 1) * d] = buf1[j * d : (j + 1) * d, :] * scale
         fc2[j * d : (j + 1) * d, :] = buf1[(ff + j) * d : (ff + j + 1) * d, :] * scale
@@ -556,8 +574,10 @@
     proj[...] = buf1[2 * ff * d : (2 * ff + 1) * d, :] * scale
     for k, ref in enumerate((g2, b2, fc2_b, proj_b)):
         ref[...] = rows[ff + 4 + k : ff + 5 + k]
-    for j in range(3):
-        qkv[:, j * d : (j + 1) * d] = buf2[j * d : (j + 1) * d, :] * scale
+    for j in range(6):
+        at = j // 3 * half + j % 3 * (d // 2)
+        part = slice(j % 2 * (d // 2), (j % 2 + 1) * (d // 2))
+        qkv[part, j // 2 * d : (j // 2 + 1) * d] = buf2[at : at + d // 2, :] * scale
     for k, ref in enumerate((g1, b1, q_b, v_b)):
         ref[...] = rows[k : k + 1]
     heads = rel.shape[0]
@@ -805,11 +825,23 @@
     )(*map(to_vmem, inputs))
 
 
+def gradient_call(total, planes, ff, n1, n2, *inputs):
+    d = inputs[0].shape[1]
+    first, size = n1 // (2 * planes), n2 // (2 * planes)
+    count_row = 3 * d // 2 + ff // d + 8
+    return pl.pallas_call(
+        lambda *refs: gradient_kernel(total, planes, count_row, first, size, *refs),
+        in_specs=[in_vmem()] * len(inputs),
+        out_shape=jax.ShapeDtypeStruct((WIN, 2 * WIN) + inputs[1].shape[2:], F32),
+        compiler_params=limit(VMEM_LIMIT),
+        name="input_gradient",
+    )(*map(to_vmem, inputs))
+
+
 def finish_call(total, planes, ff, n1, n2, rel_shape, *inputs):
     d = inputs[0].shape[1]
     row = (1, d)
-    field = (WIN, 2 * WIN) + inputs[2].shape[2:]
-    shapes = [field, (d, ff), (ff, d), (d, d), (1, ff), row, row, row, row, (d, 3 * d)]
+    shapes = [(d, ff), (ff, d), (d, d), (1, ff), row, row, row, row, (d, 3 * d)]
     shapes += [row, row, row, row, rel_shape]
     sizes = (n1 // (2 * planes), n2 // (2 * planes))
     return pl.pallas_call(
@@ -834,7 +866,7 @@
     tokens = pages * height * width
     vec = lambda a: a.reshape(1, -1)
     n1 = -(-(2 * ff + d) // step) * step
-    n2 = -(-(3 * d + 64) // step) * step
+    n2 = -(-(3 * d + 4 * VECTORS) // step) * step
 
     patches = patches.transpose(1, 2, 0, 3)
     p_strips = [permute(a, hop) for a, hop in zip(strips_call(patches), strip_hops())]
@@ -883,11 +915,13 @@
     output = jnp.concatenate([top, bottom], 0)
     mine, output = after((mine, output), output)
     total = float(tokens * rows * cols)
+    grad = gradient_call(total, planes, ff, n1, n2, mine, up, side, corner, stays)
+    other, grad = after((other, grad), grad)
     (
-        grad, fc1_g, fc2_g, proj_g, fc1_bg, g2_g, b2_g, fc2_bg, proj_bg, qkv_g, g1_g, b1_g, q_bg,
+        fc1_g, fc2_g, proj_g, fc1_bg, g2_g, b2_g, fc2_bg, proj_bg, qkv_g, g1_g, b1_g, q_bg,
         v_bg, rel_g,
     ) = finish_call(
-        total, planes, ff, n1, n2, rel_table.shape, mine, other, up, side, corner, stays
+        total, planes, ff, n1, n2, rel_table.shape, mine, other
     )
     flat = lambda a: a.reshape(-1)
     return (

time: 90.9 us -> 90.2 us (level)
  waiting for transfers between devices: 32.9 us -> 31.6 us
    pallas_call x0 -> x1, Pallas kernels: none -> 1.3 us  [gradient_call(): pl.pallas_call(lambda *refs: gradient_kernel(total, planes, count_row, fi...]
    ppermute x25, waiting for transfers between devices: 32.9 us -> 31.6 us  [permute(): return lax.ppermute(block, ('rows', 'cols'), route)]
  transfers between devices with their start and end apart: 25 -> 25, of which waited for: 14 -> 13; matrix products, arithmetic and copies ran while one was open for 1% -> 1% of each run, Pallas kernels for 19% -> 21%
where the time goes in v6:
time: 90.2 us; the launch traced here: 90.1 us
  waiting for transfers between devices  31.6 us (35%)
  Pallas kernels  30.8 us (34%)
  starting transfers between devices  25.5 us (28%)
  between operations  1.04 us (1%)
  other arithmetic  0.97 us (1%)
    ppermute x25, waiting for transfers between devices, permute(): return lax.ppermute(block, ('rows', 'cols'), route)  31.6 us
    ppermute x25, starting transfers between devices, permute(): return lax.ppermute(block, ('rows', 'cols'), route)  25.5 us
    pallas_call x1, Pallas kernels, backward_call(): pl.pallas_call(backward_kernel, in_specs=[in_vmem()] * len(inputs), out_s...  8.74 us
    pallas_call x1, Pallas kernels, mlp_call(): pl.pallas_call(mlp_kernel, in_specs=[in_vmem()] * len(inputs), out_specs=...  8.67 us
    pallas_call x1, Pallas kernels, attention_call(): pl.pallas_call(attention_kernel, in_specs=[in_vmem()] * len(inputs), out_...  6.28 us
    pallas_call x1, Pallas kernels, finish_call(): pl.pallas_call(lambda *refs: finish_kernel(total, planes, sizes, *refs),...  2 us
  transfers between devices with their start and end apart: 25, of which 13 were waited for; matrix products, arithmetic and copies ran while one was open for 1% of the time, Pallas kernels for 21%

profile of v6, /device:TPU:0, one launch (start us, length us, event | category | flops | bytes accessed | tf_op | source)
XLA Modules:
  0.0 90.1 jit_solution(14048595040006611681)
XLA Ops:
  0.7 1.2 %input_strips.1 = (bf16[5,20,8,256]{3,2,1,0:T(8,128)(2,1)S(1)}, bf16[5,5,8,256]{3,2,1,0:T(8,128)(2,1)S(1)}, bf16[5,5,8,256]{3,2,1,0:T(8,128)(2,1)S(1)}) custom-call(bf16[10,20,8,256]{3,2,1,0:T(8,128)(2,1)} %bitcast.23), custom_call_target="tpu_custom_call" | custom-call | tf_op jit(solution)/shard_map/input_strips/pallas_call | solution.py:658
  1.9 5.5 %collective-permute-start = (bf16[5,20,8,256]{3,2,1,0:T(8,128)(2,1)S(1)}, bf16[5,20,8,256]{3,2,1,0:T(8,128)(2,1)S(1)}, u32[]{:S(2)}, u32[]{:S(2)}) collective-permute-start(bf16[5,20,8,256]{3,2,1,0:T(8,128)(2,1)S(1)} %get-tuple-element.90), channel_id=1, source_target_pairs={{0,30},{1,31},{2,0},{3,1},{4,2},{5,3},{6,4},{7,5},{8,6},{9,7},{10,... | collective-permute-start | bytes 1228808 | tf_op jit(solution)/shard_map/ppermute | solution.py:595
  7.4 1.5 %collective-permute-start.1 = (bf16[5,5,8,256]{3,2,1,0:T(8,128)(2,1)S(1)}, bf16[5,5,8,256]{3,2,1,0:T(8,128)(2,1)S(1)}, u32[]{:S(2)}, u32[]{:S(2)}) collective-permute-start(bf16[5,5,8,256]{3,2,1,0:T(8,128)(2,1)S(1)} %get-tuple-element.91), channel_id=1, source_target_pairs={{0,1},{1,0},{2,3},{3,2},{4,5},{5,4},{6,7},{7,6},{8,9},{9,8},{10,11... | collective-permute-start | bytes 307208 | tf_op jit(solution)/shard_map/ppermute | solution.py:595
  8.9 0.4 collective-permute-start.2
  9.3 1.6 %masked_target.1 = (bf16[10,20,8,256]{3,2,1,0:T(8,128)(2,1)S(1)}, bf16[5,20,8,256]{3,2,1,0:T(8,128)(2,1)S(1)}, bf16[5,5,8,256]{3,2,1,0:T(8,128)(2,1)S(1)}, bf16[...) custom-call(bf16[10,20,8,256]{3,2,1,0:T(8,128)(2,1)} %bitcast.38, ...), custom_call_target="tpu_custom_call" | custom-call | tf_op jit(solution)/shard_map/masked_target/pallas_call | solution.py:670
  10.9 1.6 %collective-permute-start.4 = (bf16[5,5,8,256]{3,2,1,0:T(8,128)(2,1)S(1)}, bf16[5,5,8,256]{3,2,1,0:T(8,128)(2,1)S(1)}, u32[]{:S(2)}, u32[]{:S(2)}) collective-permute-start(bf16[5,5,8,256]{3,2,1,0:T(8,128)(2,1)S(1)} %get-tuple-element.98), channel_id=1, source_target_pairs={{0,1},{1,0},{2,3},{3,2},{4,5},{5,4},{6,7},{7,6},{8,9},{9,8},{10,11... | collective-permute-start | bytes 307208 | tf_op jit(solution)/shard_map/ppermute | solution.py:595
  12.4 0.2 collective-permute-start.5
  12.7 0.5 attention_bias.1.bias
  13.2 1.2 %collective-permute-done.1.right = bf16[5,5,8,256]{3,2,1,0:T(8,128)(2,1)S(1)} collective-permute-done((bf16[5,5,8,256]{3,2,1,0:T(8,128)(2,1)S(1)}, bf16[5,5,8,256]{3,2,1,0:T(8,128)(2,1)S(1)}, u32[]{:S(2)}, u32[]{:S(2)}) %collective-permute-start.1) | collective-permute-done | bytes 102432 | tf_op jit(solution)/shard_map/ppermute | solution.py:595
  14.4 1.3 %collective-permute-done.2.corner = bf16[5,5,8,256]{3,2,1,0:T(8,128)(2,1)S(1)} collective-permute-done((bf16[5,5,8,256]{3,2,1,0:T(8,128)(2,1)S(1)}, bf16[5,5,8,256]{3,2,1,0:T(8,128)(2,1)S(1)}, u32[]{:S(2)}, u32[]{:S(2)}) %collective-permute-start.2) | collective-permute-done | bytes 102432 | tf_op jit(solution)/shard_map/ppermute | solution.py:595
  15.7 0.0 collective-permute-done.low
  15.7 0.0 copy-start.1
  15.7 0.0 copy-start.2
  15.7 0.0 copy-start.4
  15.7 0.0 copy-start.5
  15.8 0.0 copy-start.8
  15.8 0.0 copy-start.9
  15.8 0.0 copy-start.10
  15.8 0.0 copy-start.11
  15.8 6.3 %attention_forward.1 = (bf16[1600,256]{1,0:T(8,128)(2,1)S(1)}, bf16[1664,256]{1,0:T(8,128)(2,1)S(1)}, bf16[2,8,128,768]{3,2,1,0:T(8,128)(2,1)S(1)}, bf16[2,8,832...) custom-call(bf16[10,20,8,256]{3,2,1,0:T(8,128)(2,1)S(1)} %bitcast.24, ...), custom_call_target="tpu_custom_call" | custom-call | flops 10000000000 | bytes 10000000 | tf_op jit(solution)/shard_map/attention_forward/pallas_call | solution.py:749
  22.1 0.0 collective-permute-done.4.t_right
  22.1 0.0 collective-permute-done.3.t_low
  22.2 8.7 %mlp_forward_backward.1 = (bf16[5,15,8,256]{3,2,1,0:T(8,128)(2,1)S(1)}, bf16[5,15,8,256]{3,2,1,0:T(8,128)(2,1)S(1)}, bf16[5,5,8,256]{3,2,1,0:T(8,128)(2,1)S(1)},...) custom-call(bf16[1600,256]{1,0:T(8,128)(2,1)S(1)} %get-tuple-element, ...), custom_call_target="tpu_custom_call" | custom-call | flops 10000000000 | bytes 10000000 | tf_op jit(solution)/shard_map/mlp_forward_backward/pallas_call | solution.py:774
  30.9 0.1 collective-permute-start.6
  31.0 1.3 %collective-permute-start.11 = (bf16[5,5,8,256]{3,2,1,0:T(8,128)(2,1)S(1)}, bf16[5,5,8,256]{3,2,1,0:T(8,128)(2,1)S(1)}, u32[]{:S(2)}, u32[]{:S(2)}) collective-permute-start(bf16[5,5,8,256]{3,2,1,0:T(8,128)(2,1)S(1)} %get-tuple-element.108), channel_id=1, source_target_pairs={{0,3},{1,2},{2,5},{3,4},{4,7},{5,6},{6,9},{7,8},{8,11},{9,10},{10,... | collective-permute-start | bytes 307208 | tf_op jit(solution)/shard_map/ppermute | solution.py:595
  32.3 0.0 collective-permute-start.10
  32.3 0.6 collective-permute-done.6.other
  32.9 0.1 split_sums.2
  33.1 1.4 %collective-permute-start.7 = (bf16[288,256]{1,0:T(8,128)(2,1)S(1)}, bf16[288,256]{1,0:T(8,128)(2,1)S(1)}, u32[]{:S(2)}, u32[]{:S(2)}) collective-permute-start(bf16[288,256]{1,0:T(8,128)(2,1)S(1)} %get-tuple-element.104), channel_id=1, source_target_pairs={{0,1},{1,0},{2,3},{3,2},{4,5},{5,4},{6,7},{7,6},{8,9},{9,8},{10,11... | collective-permute-start | bytes 442376 | tf_op jit(solution)/shard_map/ppermute | solution.py:595
  34.5 2.2 %collective-permute-start.9 = (bf16[288,256]{1,0:T(8,128)(2,1)S(1)}, bf16[288,256]{1,0:T(8,128)(2,1)S(1)}, u32[]{:S(2)}, u32[]{:S(2)}) collective-permute-start(bf16[288,256]{1,0:T(8,128)(2,1)S(1)} %get-tuple-element.106), channel_id=1, source_target_pairs={{0,5},{1,4},{2,7},{3,6},{4,1},{5,0},{6,3},{7,2},{8,13},{9,12},{10,... | collective-permute-start | bytes 442376 | tf_op jit(solution)/shard_map/ppermute | solution.py:595
  36.6 8.7 %attention_backward.1 = (f32[5,15,8,256]{3,2,1,0:T(8,128)S(1)}, bf16[10,5,8,256]{3,2,1,0:T(8,128)(2,1)S(1)}, bf16[5,5,8,256]{3,2,1,0:T(8,128)(2,1)S(1)}, bf16[5,...) custom-call(bf16[1664,256]{1,0:T(8,128)(2,1)S(1)} %get-tuple-element.109.xw, ...), custom_call_target="tpu_custom_call" | custom-call | flops 10000000000 | bytes 10000000 | tf_op jit(solution)/shard_map/attention_backward/pallas_call | solution.py:807
  45.4 0.0 collective-permute-done.11
  45.4 0.0 collective-permute-done.10
  45.4 2.4 %collective-permute-done.8.refs_2_ = bf16[288,256]{1,0:T(8,128)(2,1)S(1)} collective-permute-done((bf16[288,256]{1,0:T(8,128)(2,1)S(1)}, bf16[288,256]{1,0:T(8,128)(2,1)S(1)}, u32[]{:S(2)}, u32[]{:S(2)}) %collective-permute-start.8) | collective-permute-done | bytes 147488 | tf_op jit(solution)/shard_map/ppermute | solution.py:595
  47.9 0.0 collective-permute-done.9.refs_3_
  47.9 0.1 add_pieces.4.refs_0_
  47.9 0.1 collective-permute-start.12
  48.0 1.5 %collective-permute-done.12.other = bf16[448,256]{1,0:T(8,128)(2,1)S(1)} collective-permute-done((bf16[448,256]{1,0:T(8,128)(2,1)S(1)}, bf16[448,256]{1,0:T(8,128)(2,1)S(1)}, u32[]{:S(2)}, u32[]{:S(2)}) %collective-permute-start.12) | collective-permute-done | bytes 229408 | tf_op jit(solution)/shard_map/ppermute | solution.py:595
  49.5 0.1 split_sums.3
  49.6 0.5 collective-permute-start.13
  50.1 0.0 collective-permute-start.14
  50.1 3.0 %collective-permute-start.15 = (bf16[112,256]{1,0:T(8,128)(2,1)S(1)}, bf16[112,256]{1,0:T(8,128)(2,1)S(1)}, u32[]{:S(2)}, u32[]{:S(2)}) collective-permute-start(bf16[112,256]{1,0:T(8,128)(2,1)S(1)} %get-tuple-element.131), channel_id=1, source_target_pairs={{0,5},{1,4},{2,7},{3,6},{4,1},{5,0},{6,3},{7,2},{8,13},{9,12},{10,... | collective-permute-start | bytes 172040 | tf_op jit(solution)/shard_map/ppermute | solution.py:595
  53.1 0.8 collective-permute-done.13.refs_1_
  53.9 1.4 %collective-permute-done.14.refs_2_ = bf16[112,256]{1,0:T(8,128)(2,1)S(1)} collective-permute-done((bf16[112,256]{1,0:T(8,128)(2,1)S(1)}, bf16[112,256]{1,0:T(8,128)(2,1)S(1)}, u32[]{:S(2)}, u32[]{:S(2)}) %collective-permute-start.14) | collective-permute-done | bytes 57376 | tf_op jit(solution)/shard_map/ppermute | solution.py:595
  55.4 0.1 collective-permute-start.16
  55.5 0.1 collective-permute-start.18
  55.6 5.7 %collective-permute-done.16.refs_1_ = bf16[400,256]{1,0:T(8,128)(2,1)S(1)} collective-permute-done((bf16[400,256]{1,0:T(8,128)(2,1)S(1)}, bf16[400,256]{1,0:T(8,128)(2,1)S(1)}, u32[]{:S(2)}, u32[]{:S(2)}) %collective-permute-start.16) | collective-permute-done | bytes 204832 | tf_op jit(solution)/shard_map/ppermute | solution.py:595
  61.3 0.9 %collective-permute-start.17 = (bf16[400,256]{1,0:T(8,128)(2,1)S(1)}, bf16[400,256]{1,0:T(8,128)(2,1)S(1)}, u32[]{:S(2)}, u32[]{:S(2)}) collective-permute-start(bf16[400,256]{1,0:T(8,128)(2,1)S(1)} %add_pieces.6.refs_0_), channel_id=1, source_target_pairs={{0,16},{1,17},{2,18},{3,19},{4,20},{5,21},{6,22},{7,23},{8,24},{9,... | collective-permute-start | bytes 614408 | tf_op jit(solution)/shard_map/ppermute | solution.py:595
  62.2 1.1 %collective-permute-start.19 = (bf16[10,5,8,256]{3,2,1,0:T(8,128)(2,1)S(1)}, bf16[10,5,8,256]{3,2,1,0:T(8,128)(2,1)S(1)}, u32[]{:S(2)}, u32[]{:S(2)}) collective-permute-start(bf16[10,5,8,256]{3,2,1,0:T(8,128)(2,1)S(1)} %get-tuple-element.136), channel_id=1, source_target_pairs={{0,1},{1,0},{2,3},{3,2},{4,5},{5,4},{6,7},{7,6},{8,9},{9,8},{10,11... | collective-permute-start | bytes 614408 | tf_op jit(solution)/shard_map/ppermute | solution.py:595
  63.4 0.0 collective-permute-start.20
  63.4 7.8 %collective-permute-done.17.refs_1_ = bf16[400,256]{1,0:T(8,128)(2,1)S(1)} collective-permute-done((bf16[400,256]{1,0:T(8,128)(2,1)S(1)}, bf16[400,256]{1,0:T(8,128)(2,1)S(1)}, u32[]{:S(2)}, u32[]{:S(2)}) %collective-permute-start.17) | collective-permute-done | bytes 204832 | tf_op jit(solution)/shard_map/ppermute | solution.py:595
  71.2 0.6 collective-permute-done.20.refs_3_
  71.9 4.5 %collective-permute-start.23 = (bf16[400,256]{1,0:T(8,128)(2,1)S(1)}, bf16[400,256]{1,0:T(8,128)(2,1)S(1)}, u32[]{:S(2)}, u32[]{:S(2)}) collective-permute-start(bf16[400,256]{1,0:T(8,128)(2,1)S(1)} %add_pieces.7.refs_0_), channel_id=1, source_target_pairs={{0,5},{1,4},{2,7},{3,6},{4,1},{5,0},{6,3},{7,2},{8,13},{9,12},{10,... | collective-permute-start | bytes 614408 | tf_op jit(solution)/shard_map/ppermute | solution.py:595
  76.3 0.0 collective-permute-start.22
  76.3 1.1 %collective-permute-start.21 = (bf16[400,256]{1,0:T(8,128)(2,1)S(1)}, bf16[400,256]{1,0:T(8,128)(2,1)S(1)}, u32[]{:S(2)}, u32[]{:S(2)}) collective-permute-start(bf16[400,256]{1,0:T(8,128)(2,1)S(1)} %add_pieces.7.refs_0_), channel_id=1, source_target_pairs={{0,1},{1,0},{2,3},{3,2},{4,5},{5,4},{6,7},{7,6},{8,9},{9,8},{10,11... | collective-permute-start | bytes 614408 | tf_op jit(solution)/shard_map/ppermute | solution.py:595
  77.4 4.9 %collective-permute-done.23.refs_3_ = bf16[400,256]{1,0:T(8,128)(2,1)S(1)} collective-permute-done((bf16[400,256]{1,0:T(8,128)(2,1)S(1)}, bf16[400,256]{1,0:T(8,128)(2,1)S(1)}, u32[]{:S(2)}, u32[]{:S(2)}) %collective-permute-start.23) | collective-permute-done | bytes 204832 | tf_op jit(solution)/shard_map/ppermute | solution.py:595
  82.3 2.9 %collective-permute-done.22.refs_2_ = bf16[400,256]{1,0:T(8,128)(2,1)S(1)} collective-permute-done((bf16[400,256]{1,0:T(8,128)(2,1)S(1)}, bf16[400,256]{1,0:T(8,128)(2,1)S(1)}, u32[]{:S(2)}, u32[]{:S(2)}) %collective-permute-start.22) | collective-permute-done | bytes 204832 | tf_op jit(solution)/shard_map/ppermute | solution.py:595
  85.2 0.4 collective-permute-done.21.refs_1_
  85.6 0.1 join_pieces.3.refs_0_
  85.7 0.1 collective-permute-start.24
  85.8 1.0 %maximum_maximum_fusion = bf16[10,20,8,256]{3,2,1,0:T(8,128)(2,1)} fusion(bf16[5,15,8,256]{3,2,1,0:T(8,128)(2,1)S(1)} %get-tuple-element.142, bf16[5,5,8,256]{3,2,1,0:T(8,128)(2,1)S(1)} %slice.3, bf16[5,15,8,256]{3,2,1,0:T(8,128)(2,1)S(1)} %collective-permute-done.10, bf16[5,5,8,256]{3,2,1,0:T(8,128)(2,1)S(1)} %collective-permute-done.11), kind=kLoop, calls=%fused_computation | loop fusion | flops 1228800 | bytes 1638400 | tf_op jit(solution)/shard_map/concatenate | solution.py:915
  86.7 1.3 %input_gradient.1 = f32[10,20,8,256]{3,2,1,0:T(8,128)} custom-call(bf16[1600,256]{1,0:T(8,128)(2,1)S(1)} %join_pieces.3.refs_0_, bf16[5,15,8,256]{3,2,1,0:T(8,128)(2,1)S(1)} %collective-permute-done.18.refs_1_, bf16[10,5,8,256]{3,2,1,0:T(8,128)(2,1)S(1)} %collective-permute-done.19.refs_2_, bf16[5,5,8,256]{3,2,1,0:T(8,128)(2,1)S(1)} %collective-permute-done.20.refs_3_, ...), custom_call_target="tpu_custom_call" | custom-call | tf_op jit(solution)/shard_map/input_gradient/pallas_call | solution.py:832
  88.0 0.0 collective-permute-done.24.refs_1_
  88.1 2.0 %finish_sums.1 = (f32[256,1024]{1,0:T(8,128)}, f32[1024,256]{1,0:T(8,128)}, f32[256,256]{1,0:T(8,128)}, f32[1,1024]{1,0:T(1,128)}, f32[1,256]{1,0:T(1,128)}, /*i...) custom-call(bf16[1600,256]{1,0:T(8,128)(2,1)S(1)} %join_pieces.3.ref, ...), custom_call_target="tpu_custom_call" | custom-call | tf_op jit(solution)/shard_map/finish_sums/pallas_call | solution.py:847
  (32 shorter events, 0.2 us)
Async XLA Ops:
  0.6 15.0 %copy-start = (bf16[8,10,20,256]{3,0,2,1:T(8,128)(2,1)S(1)}, bf16[8,10,20,256]{3,0,2,1:T(8,128)(2,1)}, u32[]{:S(2)}) copy-start(bf16[8,10,20,256]{3,0,2,1:T(8,128)(2,1)} %param.17) | copy-start | bytes 2457604
  0.7 15.0 %copy-start.3 = (bf16[256,768]{1,0:T(8,128)(2,1)S(1)}, bf16[256,768]{1,0:T(8,128)(2,1)}, u32[]{:S(2)}) copy-start(bf16[256,768]{1,0:T(8,128)(2,1)} %qkv_w.3) | copy-start | bytes 1179652
  0.7 15.0 %copy-start.7 = (f32[256]{0:T(256)S(1)}, f32[256]{0:T(256)}, u32[]{:S(2)}) copy-start(f32[256]{0:T(256)} %param.24) | copy-start | bytes 3076
  0.7 15.0 %copy-start.6 = (f32[256]{0:T(256)S(1)}, f32[256]{0:T(256)}, u32[]{:S(2)}) copy-start(f32[256]{0:T(256)} %param.23) | copy-start | bytes 3076
  0.7 15.0 %copy-start.13 = (f32[256]{0:T(256)S(1)}, f32[256]{0:T(256)}, u32[]{:S(2)}) copy-start(f32[256]{0:T(256)} %param.21) | copy-start | bytes 3076
  0.7 15.0 %copy-start.12 = (f32[256]{0:T(256)S(1)}, f32[256]{0:T(256)}, u32[]{:S(2)}) copy-start(f32[256]{0:T(256)} %param.20) | copy-start | bytes 3076
  1.9 13.8 %collective-permute-start = (bf16[5,20,8,256]{3,2,1,0:T(8,128)(2,1)S(1)}, bf16[5,20,8,256]{3,2,1,0:T(8,128)(2,1)S(1)}, u32[]{:S(2)}, u32[]{:S(2)}) collective-permute-start(bf16[5,20,8,256]{3,2,1,0:T(8,128)(2,1)S(1)} %get-tuple-element.90), channel_id=1, source_target_pairs={{0,30},{1,31},{2,0},{3,1},{4,2},{5,3},{6,4},{7,5},{8,6},{9,7},{10,... | collective-permute-start | bytes 1228808 | tf_op jit(solution)/shard_map/ppermute | solution.py:595
  7.4 7.0 %collective-permute-start.1 = (bf16[5,5,8,256]{3,2,1,0:T(8,128)(2,1)S(1)}, bf16[5,5,8,256]{3,2,1,0:T(8,128)(2,1)S(1)}, u32[]{:S(2)}, u32[]{:S(2)}) collective-permute-start(bf16[5,5,8,256]{3,2,1,0:T(8,128)(2,1)S(1)} %get-tuple-element.91), channel_id=1, source_target_pairs={{0,1},{1,0},{2,3},{3,2},{4,5},{5,4},{6,7},{7,6},{8,9},{9,8},{10,11... | collective-permute-start | bytes 307208 | tf_op jit(solution)/shard_map/ppermute | solution.py:595
  8.9 6.8 %collective-permute-start.2 = (bf16[5,5,8,256]{3,2,1,0:T(8,128)(2,1)S(1)}, bf16[5,5,8,256]{3,2,1,0:T(8,128)(2,1)S(1)}, u32[]{:S(2)}, u32[]{:S(2)}) collective-permute-start(bf16[5,5,8,256]{3,2,1,0:T(8,128)(2,1)S(1)} %get-tuple-element.92), channel_id=1, source_target_pairs={{0,31},{1,30},{2,1},{3,0},{4,3},{5,2},{6,5},{7,4},{8,7},{9,6},{10,... | collective-permute-start | bytes 307208 | tf_op jit(solution)/shard_map/ppermute | solution.py:595
  10.9 11.2 %collective-permute-start.4 = (bf16[5,5,8,256]{3,2,1,0:T(8,128)(2,1)S(1)}, bf16[5,5,8,256]{3,2,1,0:T(8,128)(2,1)S(1)}, u32[]{:S(2)}, u32[]{:S(2)}) collective-permute-start(bf16[5,5,8,256]{3,2,1,0:T(8,128)(2,1)S(1)} %get-tuple-element.98), channel_id=1, source_target_pairs={{0,1},{1,0},{2,3},{3,2},{4,5},{5,4},{6,7},{7,6},{8,9},{9,8},{10,11... | collective-permute-start | bytes 307208 | tf_op jit(solution)/shard_map/ppermute | solution.py:595
  12.4 9.7 %collective-permute-start.5 = (bf16[5,5,8,256]{3,2,1,0:T(8,128)(2,1)S(1)}, bf16[5,5,8,256]{3,2,1,0:T(8,128)(2,1)S(1)}, u32[]{:S(2)}, u32[]{:S(2)}) collective-permute-start(bf16[5,5,8,256]{3,2,1,0:T(8,128)(2,1)S(1)} %get-tuple-element.99), channel_id=1, source_target_pairs={{0,31},{1,30},{2,1},{3,0},{4,3},{5,2},{6,5},{7,4},{8,7},{9,6},{10,... | collective-permute-start | bytes 307208 | tf_op jit(solution)/shard_map/ppermute | solution.py:595
  14.4 7.8 %collective-permute-start.3 = (bf16[5,20,8,256]{3,2,1,0:T(8,128)(2,1)S(1)}, bf16[5,20,8,256]{3,2,1,0:T(8,128)(2,1)S(1)}, u32[]{:S(2)}, u32[]{:S(2)}) collective-permute-start(bf16[5,20,8,256]{3,2,1,0:T(8,128)(2,1)S(1)} %get-tuple-element.97), channel_id=1, source_target_pairs={{0,30},{1,31},{2,0},{3,1},{4,2},{5,3},{6,4},{7,5},{8,6},{9,7},{10,... | collective-permute-start | bytes 1228808 | tf_op jit(solution)/shard_map/ppermute | solution.py:595
  15.7 6.4 %copy-start.1 = (bf16[256,1024]{1,0:T(8,128)(2,1)S(1)}, bf16[256,1024]{1,0:T(8,128)(2,1)}, u32[]{:S(2)}) copy-start(bf16[256,1024]{1,0:T(8,128)(2,1)} %fc1_w.1) | copy-start | bytes 1572868
  15.7 6.4 %copy-start.2 = (bf16[1024,256]{1,0:T(8,128)(2,1)S(1)}, bf16[1024,256]{1,0:T(8,128)(2,1)}, u32[]{:S(2)}) copy-start(bf16[1024,256]{1,0:T(8,128)(2,1)} %fc2_w.1) | copy-start | bytes 1572868
  15.7 6.4 %copy-start.4 = (bf16[256,256]{1,0:T(8,128)(2,1)S(1)}, bf16[256,256]{1,0:T(8,128)(2,1)}, u32[]{:S(2)}) copy-start(bf16[256,256]{1,0:T(8,128)(2,1)} %proj_w.1) | copy-start | bytes 393220
  15.7 6.4 %copy-start.5 = (f32[1024]{0:T(1024)S(1)}, f32[1024]{0:T(1024)}, u32[]{:S(2)}) copy-start(f32[1024]{0:T(1024)} %param.31) | copy-start | bytes 12292
  15.8 6.4 %copy-start.8 = (f32[256]{0:T(256)S(1)}, f32[256]{0:T(256)}, u32[]{:S(2)}) copy-start(f32[256]{0:T(256)} %param.27) | copy-start | bytes 3076
  15.8 6.4 %copy-start.9 = (f32[256]{0:T(256)S(1)}, f32[256]{0:T(256)}, u32[]{:S(2)}) copy-start(f32[256]{0:T(256)} %param.28) | copy-start | bytes 3076
  15.8 6.4 %copy-start.10 = (f32[256]{0:T(256)S(1)}, f32[256]{0:T(256)}, u32[]{:S(2)}) copy-start(f32[256]{0:T(256)} %param.29) | copy-start | bytes 3076
  15.8 6.4 %copy-start.11 = (f32[256]{0:T(256)S(1)}, f32[256]{0:T(256)}, u32[]{:S(2)}) copy-start(f32[256]{0:T(256)} %param.33) | copy-start | bytes 3076
  30.9 2.1 %collective-permute-start.6 = (bf16[1152,256]{1,0:T(8,128)(2,1)S(1)}, bf16[1152,256]{1,0:T(8,128)(2,1)S(1)}, u32[]{:S(2)}, u32[]{:S(2)}) collective-permute-start(bf16[1152,256]{1,0:T(8,128)(2,1)S(1)} %get-tuple-element.102), channel_id=1, source_target_pairs={{0,2},{1,3},{2,0},{3,1},{4,6},{5,7},{6,4},{7,5},{8,10},{9,11},{10,... | collective-permute-start | bytes 1769480 | tf_op jit(solution)/shard_map/ppermute | solution.py:595
  31.0 14.4 %collective-permute-start.11 = (bf16[5,5,8,256]{3,2,1,0:T(8,128)(2,1)S(1)}, bf16[5,5,8,256]{3,2,1,0:T(8,128)(2,1)S(1)}, u32[]{:S(2)}, u32[]{:S(2)}) collective-permute-start(bf16[5,5,8,256]{3,2,1,0:T(8,128)(2,1)S(1)} %get-tuple-element.108), channel_id=1, source_target_pairs={{0,3},{1,2},{2,5},{3,4},{4,7},{5,6},{6,9},{7,8},{8,11},{9,10},{10,... | collective-permute-start | bytes 307208 | tf_op jit(solution)/shard_map/ppermute | solution.py:595
  32.3 13.1 %collective-permute-start.10 = (bf16[5,15,8,256]{3,2,1,0:T(8,128)(2,1)S(1)}, bf16[5,15,8,256]{3,2,1,0:T(8,128)(2,1)S(1)}, u32[]{:S(2)}, u32[]{:S(2)}) collective-permute-start(bf16[5,15,8,256]{3,2,1,0:T(8,128)(2,1)S(1)} %get-tuple-element.107), channel_id=1, source_target_pairs={{0,2},{1,3},{2,4},{3,5},{4,6},{5,7},{6,8},{7,9},{8,10},{9,11},{10,... | collective-permute-start | bytes 921608 | tf_op jit(solution)/shard_map/ppermute | solution.py:595
  33.1 12.3 %collective-permute-start.7 = (bf16[288,256]{1,0:T(8,128)(2,1)S(1)}, bf16[288,256]{1,0:T(8,128)(2,1)S(1)}, u32[]{:S(2)}, u32[]{:S(2)}) collective-permute-start(bf16[288,256]{1,0:T(8,128)(2,1)S(1)} %get-tuple-element.104), channel_id=1, source_target_pairs={{0,1},{1,0},{2,3},{3,2},{4,5},{5,4},{6,7},{7,6},{8,9},{9,8},{10,11... | collective-permute-start | bytes 442376 | tf_op jit(solution)/shard_map/ppermute | solution.py:595
  34.5 13.4 %collective-permute-start.8 = (bf16[288,256]{1,0:T(8,128)(2,1)S(1)}, bf16[288,256]{1,0:T(8,128)(2,1)S(1)}, u32[]{:S(2)}, u32[]{:S(2)}) collective-permute-start(bf16[288,256]{1,0:T(8,128)(2,1)S(1)} %get-tuple-element.105), channel_id=1, source_target_pairs={{0,4},{1,5},{2,6},{3,7},{4,0},{5,1},{6,2},{7,3},{8,12},{9,13},{10,... | collective-permute-start | bytes 442376 | tf_op jit(solution)/shard_map/ppermute | solution.py:595
  34.5 13.4 %collective-permute-start.9 = (bf16[288,256]{1,0:T(8,128)(2,1)S(1)}, bf16[288,256]{1,0:T(8,128)(2,1)S(1)}, u32[]{:S(2)}, u32[]{:S(2)}) collective-permute-start(bf16[288,256]{1,0:T(8,128)(2,1)S(1)} %get-tuple-element.106), channel_id=1, source_target_pairs={{0,5},{1,4},{2,7},{3,6},{4,1},{5,0},{6,3},{7,2},{8,13},{9,12},{10,... | collective-permute-start | bytes 442376 | tf_op jit(solution)/shard_map/ppermute | solution.py:595
  47.9 1.6 %collective-permute-start.12 = (bf16[448,256]{1,0:T(8,128)(2,1)S(1)}, bf16[448,256]{1,0:T(8,128)(2,1)S(1)}, u32[]{:S(2)}, u32[]{:S(2)}) collective-permute-start(bf16[448,256]{1,0:T(8,128)(2,1)S(1)} %get-tuple-element.127), channel_id=1, source_target_pairs={{0,2},{1,3},{2,0},{3,1},{4,6},{5,7},{6,4},{7,5},{8,10},{9,11},{10,... | collective-permute-start | bytes 688136 | tf_op jit(solution)/shard_map/ppermute | solution.py:595
  49.6 4.4 %collective-permute-start.13 = (bf16[112,256]{1,0:T(8,128)(2,1)S(1)}, bf16[112,256]{1,0:T(8,128)(2,1)S(1)}, u32[]{:S(2)}, u32[]{:S(2)}) collective-permute-start(bf16[112,256]{1,0:T(8,128)(2,1)S(1)} %get-tuple-element.129), channel_id=1, source_target_pairs={{0,1},{1,0},{2,3},{3,2},{4,5},{5,4},{6,7},{7,6},{8,9},{9,8},{10,11... | collective-permute-start | bytes 172040 | tf_op jit(solution)/shard_map/ppermute | solution.py:595
  50.1 5.3 %collective-permute-start.14 = (bf16[112,256]{1,0:T(8,128)(2,1)S(1)}, bf16[112,256]{1,0:T(8,128)(2,1)S(1)}, u32[]{:S(2)}, u32[]{:S(2)}) collective-permute-start(bf16[112,256]{1,0:T(8,128)(2,1)S(1)} %get-tuple-element.130), channel_id=1, source_target_pairs={{0,4},{1,5},{2,6},{3,7},{4,0},{5,1},{6,2},{7,3},{8,12},{9,13},{10,... | collective-permute-start | bytes 172040 | tf_op jit(solution)/shard_map/ppermute | solution.py:595
  50.1 5.3 %collective-permute-start.15 = (bf16[112,256]{1,0:T(8,128)(2,1)S(1)}, bf16[112,256]{1,0:T(8,128)(2,1)S(1)}, u32[]{:S(2)}, u32[]{:S(2)}) collective-permute-start(bf16[112,256]{1,0:T(8,128)(2,1)S(1)} %get-tuple-element.131), channel_id=1, source_target_pairs={{0,5},{1,4},{2,7},{3,6},{4,1},{5,0},{6,3},{7,2},{8,13},{9,12},{10,... | collective-permute-start | bytes 172040 | tf_op jit(solution)/shard_map/ppermute | solution.py:595
  55.4 5.8 %collective-permute-start.16 = (bf16[400,256]{1,0:T(8,128)(2,1)S(1)}, bf16[400,256]{1,0:T(8,128)(2,1)S(1)}, u32[]{:S(2)}, u32[]{:S(2)}) collective-permute-start(bf16[400,256]{1,0:T(8,128)(2,1)S(1)} %join_pieces.2.refs_0_), channel_id=1, source_target_pairs={{0,8},{1,9},{2,10},{3,11},{4,12},{5,13},{6,14},{7,15},{8,0},{9,1},... | collective-permute-start | bytes 614408 | tf_op jit(solution)/shard_map/ppermute | solution.py:595
  55.5 16.3 %collective-permute-start.18 = (bf16[5,15,8,256]{3,2,1,0:T(8,128)(2,1)S(1)}, bf16[5,15,8,256]{3,2,1,0:T(8,128)(2,1)S(1)}, u32[]{:S(2)}, u32[]{:S(2)}) collective-permute-start(bf16[5,15,8,256]{3,2,1,0:T(8,128)(2,1)S(1)} %get-tuple-element.135), channel_id=1, source_target_pairs={{0,2},{1,3},{2,4},{3,5},{4,6},{5,7},{6,8},{7,9},{8,10},{9,11},{10,... | collective-permute-start | bytes 921608 | tf_op jit(solution)/shard_map/ppermute | solution.py:595
  61.3 9.8 %collective-permute-start.17 = (bf16[400,256]{1,0:T(8,128)(2,1)S(1)}, bf16[400,256]{1,0:T(8,128)(2,1)S(1)}, u32[]{:S(2)}, u32[]{:S(2)}) collective-permute-start(bf16[400,256]{1,0:T(8,128)(2,1)S(1)} %add_pieces.6.refs_0_), channel_id=1, source_target_pairs={{0,16},{1,17},{2,18},{3,19},{4,20},{5,21},{6,22},{7,23},{8,24},{9,... | collective-permute-start | bytes 614408 | tf_op jit(solution)/shard_map/ppermute | solution.py:595
  62.2 9.6 %collective-permute-start.19 = (bf16[10,5,8,256]{3,2,1,0:T(8,128)(2,1)S(1)}, bf16[10,5,8,256]{3,2,1,0:T(8,128)(2,1)S(1)}, u32[]{:S(2)}, u32[]{:S(2)}) collective-permute-start(bf16[10,5,8,256]{3,2,1,0:T(8,128)(2,1)S(1)} %get-tuple-element.136), channel_id=1, source_target_pairs={{0,1},{1,0},{2,3},{3,2},{4,5},{5,4},{6,7},{7,6},{8,9},{9,8},{10,11... | collective-permute-start | bytes 614408 | tf_op jit(solution)/shard_map/ppermute | solution.py:595
  63.4 8.5 %collective-permute-start.20 = (bf16[5,5,8,256]{3,2,1,0:T(8,128)(2,1)S(1)}, bf16[5,5,8,256]{3,2,1,0:T(8,128)(2,1)S(1)}, u32[]{:S(2)}, u32[]{:S(2)}) collective-permute-start(bf16[5,5,8,256]{3,2,1,0:T(8,128)(2,1)S(1)} %get-tuple-element.137), channel_id=1, source_target_pairs={{0,3},{1,2},{2,5},{3,4},{4,7},{5,6},{6,9},{7,8},{8,11},{9,10},{10,... | collective-permute-start | bytes 307208 | tf_op jit(solution)/shard_map/ppermute | solution.py:595
  71.9 10.5 %collective-permute-start.23 = (bf16[400,256]{1,0:T(8,128)(2,1)S(1)}, bf16[400,256]{1,0:T(8,128)(2,1)S(1)}, u32[]{:S(2)}, u32[]{:S(2)}) collective-permute-start(bf16[400,256]{1,0:T(8,128)(2,1)S(1)} %add_pieces.7.refs_0_), channel_id=1, source_target_pairs={{0,5},{1,4},{2,7},{3,6},{4,1},{5,0},{6,3},{7,2},{8,13},{9,12},{10,... | collective-permute-start | bytes 614408 | tf_op jit(solution)/shard_map/ppermute | solution.py:595
  76.3 8.8 %collective-permute-start.22 = (bf16[400,256]{1,0:T(8,128)(2,1)S(1)}, bf16[400,256]{1,0:T(8,128)(2,1)S(1)}, u32[]{:S(2)}, u32[]{:S(2)}) collective-permute-start(bf16[400,256]{1,0:T(8,128)(2,1)S(1)} %add_pieces.7.refs_0_), channel_id=1, source_target_pairs={{0,4},{1,5},{2,6},{3,7},{4,0},{5,1},{6,2},{7,3},{8,12},{9,13},{10,... | collective-permute-start | bytes 614408 | tf_op jit(solution)/shard_map/ppermute | solution.py:595
  76.3 9.3 %collective-permute-start.21 = (bf16[400,256]{1,0:T(8,128)(2,1)S(1)}, bf16[400,256]{1,0:T(8,128)(2,1)S(1)}, u32[]{:S(2)}, u32[]{:S(2)}) collective-permute-start(bf16[400,256]{1,0:T(8,128)(2,1)S(1)} %add_pieces.7.refs_0_), channel_id=1, source_target_pairs={{0,1},{1,0},{2,3},{3,2},{4,5},{5,4},{6,7},{7,6},{8,9},{9,8},{10,11... | collective-permute-start | bytes 614408 | tf_op jit(solution)/shard_map/ppermute | solution.py:595
  85.7 2.4 %collective-permute-start.24 = (bf16[1600,256]{1,0:T(8,128)(2,1)S(1)}, bf16[1600,256]{1,0:T(8,128)(2,1)S(1)}, u32[]{:S(2)}, u32[]{:S(2)}) collective-permute-start(bf16[1600,256]{1,0:T(8,128)(2,1)S(1)} %join_pieces.3.refs_0_), channel_id=1, source_target_pairs={{0,2},{1,3},{2,0},{3,1},{4,6},{5,7},{6,4},{7,5},{8,10},{9,11},{10,... | collective-permute-start | bytes 2457608 | tf_op jit(solution)/shard_map/ppermute | solution.py:595

commit v7 on v6

--- a/solution.py
+++ b/solution.py
@@ -16,6 +16,7 @@
 SPAN = 2 * WIN - 1
 TOK = WIN * WIN
 ROWS = 104
+PAD_ROWS = ROWS + 1
 KEYS = 128
 GROUP = 4
 RELS = 384
@@ -420,8 +421,8 @@
         for w in range(2):
             at = (2 * page + w) * ROWS
             store_rows(dx, w, rows, load_rows(dy_in, w, rows) + back[at : at + TOK])
-    right = load_rows(dx, 1, slice(None)).reshape(WIN, WIN, PAGES, d)
-    left = load_rows(dx, 0, slice(None)).reshape(WIN, WIN, PAGES, d)
+    right = load_rows(dx, 1, slice(0, TOK * PAGES)).reshape(WIN, WIN, PAGES, d)
+    left = load_rows(dx, 0, slice(0, TOK * PAGES)).reshape(WIN, WIN, PAGES, d)
     stays[:, :WIN] = left[:SHIFT]
     stays[:, WIN:] = right[:SHIFT, :SHIFT]
     side[:SHIFT] = out_side[...]
@@ -722,7 +723,7 @@
         bias_kernel,
         in_specs=[in_vmem()],
         out_specs=in_vmem(),
-        out_shape=pltpu.VMEM((2, ROWS * heads, KEYS), F32),
+        out_shape=pltpu.VMEM((2, PAD_ROWS * heads, KEYS), F32),
         scratch_shapes=[pltpu.VMEM((heads, RELS), F32)],
         compiler_params=limit(VMEM_LIMIT),
         name="attention_bias",
@@ -744,14 +745,14 @@
         shape((2 * pages * ROWS, d), BF16),
         shape((2, pages, KEYS, 3 * d), BF16),
         shape((2, pages, heads * ROWS, KEYS), BF16),
-        shape((d // KEYS, 2, TOK * pages, KEYS), F32),
+        shape((d // KEYS, 2, PAD_ROWS * pages, KEYS), F32),
     ]
     return pl.pallas_call(
         attention_kernel,
         in_specs=[in_vmem()] * len(inputs),
         out_specs=[in_vmem()] * len(outs),
         out_shape=outs,
-        scratch_shapes=[pltpu.VMEM((d // KEYS, 2, ROWS * pages, KEYS), F32)],
+        scratch_shapes=[pltpu.VMEM((d // KEYS, 2, PAD_ROWS * pages, KEYS), F32)],
         compiler_params=limit(VMEM_LIMIT),
         cost_estimate=cost(10**10),
         name="attention_forward",
@@ -767,8 +768,8 @@
     outs = [
         shape((SHIFT, width - SHIFT, pages, d), BF16), shape((rest, width - SHIFT, pages, d), BF16),
         shape((SHIFT, SHIFT, pages, d), BF16), shape((rest, SHIFT, pages, d), BF16),
-        shape((d // KEYS, 2, ROWS * pages, KEYS), F32),
-        shape((d // KEYS, 2, ROWS * pages, KEYS), F32),
+        shape((d // KEYS, 2, PAD_ROWS * pages, KEYS), F32),
+        shape((d // KEYS, 2, PAD_ROWS * pages, KEYS), F32),
         shape((16, d), F32), shape((size // 2, d), BF16), shape((size // 2, d), BF16),
     ]
     return pl.pallas_call(
@@ -779,7 +780,7 @@
         scratch_shapes=[
             pltpu.VMEM((height, width, pages, d), BF16),
             pltpu.VMEM((size, d), BF16),
-            pltpu.VMEM((d // KEYS, 2, TOK * pages, KEYS), F32),
+            pltpu.VMEM((d // KEYS, 2, PAD_ROWS * pages, KEYS), F32),
             pltpu.VMEM((d, ff), F32),
             pltpu.VMEM((ff, d), F32),
             pltpu.VMEM((d, d), F32),
@@ -810,12 +811,12 @@
         out_specs=[in_vmem()] * len(outs),
         out_shape=outs,
         scratch_shapes=[
-            shape((d // KEYS, 2, TOK * pages, KEYS), F32),
+            shape((d // KEYS, 2, PAD_ROWS * pages, KEYS), F32),
             shape((d, 3 * d), F32),
             shape((ROWS, heads * KEYS), F32),
             shape((8, 3 * d), F32),
             shape((2, 8, d), F32),
-            shape((ROWS * heads, KEYS), F32),
+            shape((PAD_ROWS * heads, KEYS), F32),
             shape((size, d), BF16),
             shape((2 * pages * ROWS, 3 * d), BF16),
         ],

time: 90.2 us -> 90.2 us (level)
  no operation moved by 1% of the time
where the time goes in v7:
time: 90.2 us; the launch traced here: 90 us
  waiting for transfers between devices  31.8 us (35%)
  Pallas kernels  30.6 us (34%)
  starting transfers between devices  25.6 us (28%)
  between operations  1.04 us (1%)
  other arithmetic  0.97 us (1%)
    ppermute x25, waiting for transfers between devices, permute(): return lax.ppermute(block, ('rows', 'cols'), route)  31.8 us
    ppermute x25, starting transfers between devices, permute(): return lax.ppermute(block, ('rows', 'cols'), route)  25.6 us
    pallas_call x1, Pallas kernels, mlp_call(): pl.pallas_call(mlp_kernel, in_specs=[in_vmem()] * len(inputs), out_specs=...  8.59 us
    pallas_call x1, Pallas kernels, backward_call(): pl.pallas_call(backward_kernel, in_specs=[in_vmem()] * len(inputs), out_s...  8.58 us
    pallas_call x1, Pallas kernels, attention_call(): pl.pallas_call(attention_kernel, in_specs=[in_vmem()] * len(inputs), out_...  6.28 us
    pallas_call x1, Pallas kernels, finish_call(): pl.pallas_call(lambda *refs: finish_kernel(total, planes, sizes, *refs),...  2 us
  transfers between devices with their start and end apart: 25, of which 13 were waited for; matrix products, arithmetic and copies ran while one was open for 1% of the time, Pallas kernels for 21%

profile of v7, /device:TPU:0, one launch (start us, length us, event | category | flops | bytes accessed | tf_op | source)
XLA Modules:
  0.0 90.0 jit_solution(2500137611259532667)
XLA Ops:
  0.7 1.2 %input_strips.1 = (bf16[5,20,8,256]{3,2,1,0:T(8,128)(2,1)S(1)}, bf16[5,5,8,256]{3,2,1,0:T(8,128)(2,1)S(1)}, bf16[5,5,8,256]{3,2,1,0:T(8,128)(2,1)S(1)}) custom-call(bf16[10,20,8,256]{3,2,1,0:T(8,128)(2,1)} %bitcast.23), custom_call_target="tpu_custom_call" | custom-call | tf_op jit(solution)/shard_map/input_strips/pallas_call | solution.py:659
  1.9 5.5 %collective-permute-start = (bf16[5,20,8,256]{3,2,1,0:T(8,128)(2,1)S(1)}, bf16[5,20,8,256]{3,2,1,0:T(8,128)(2,1)S(1)}, u32[]{:S(2)}, u32[]{:S(2)}) collective-permute-start(bf16[5,20,8,256]{3,2,1,0:T(8,128)(2,1)S(1)} %get-tuple-element.90), channel_id=1, source_target_pairs={{0,30},{1,31},{2,0},{3,1},{4,2},{5,3},{6,4},{7,5},{8,6},{9,7},{10,... | collective-permute-start | bytes 1228808 | tf_op jit(solution)/shard_map/ppermute | solution.py:596
  7.4 1.5 %collective-permute-start.1 = (bf16[5,5,8,256]{3,2,1,0:T(8,128)(2,1)S(1)}, bf16[5,5,8,256]{3,2,1,0:T(8,128)(2,1)S(1)}, u32[]{:S(2)}, u32[]{:S(2)}) collective-permute-start(bf16[5,5,8,256]{3,2,1,0:T(8,128)(2,1)S(1)} %get-tuple-element.91), channel_id=1, source_target_pairs={{0,1},{1,0},{2,3},{3,2},{4,5},{5,4},{6,7},{7,6},{8,9},{9,8},{10,11... | collective-permute-start | bytes 307208 | tf_op jit(solution)/shard_map/ppermute | solution.py:596
  8.9 0.4 collective-permute-start.2
  9.3 1.6 %masked_target.1 = (bf16[10,20,8,256]{3,2,1,0:T(8,128)(2,1)S(1)}, bf16[5,20,8,256]{3,2,1,0:T(8,128)(2,1)S(1)}, bf16[5,5,8,256]{3,2,1,0:T(8,128)(2,1)S(1)}, bf16[...) custom-call(bf16[10,20,8,256]{3,2,1,0:T(8,128)(2,1)} %bitcast.38, ...), custom_call_target="tpu_custom_call" | custom-call | tf_op jit(solution)/shard_map/masked_target/pallas_call | solution.py:671
  10.9 1.6 %collective-permute-start.4 = (bf16[5,5,8,256]{3,2,1,0:T(8,128)(2,1)S(1)}, bf16[5,5,8,256]{3,2,1,0:T(8,128)(2,1)S(1)}, u32[]{:S(2)}, u32[]{:S(2)}) collective-permute-start(bf16[5,5,8,256]{3,2,1,0:T(8,128)(2,1)S(1)} %get-tuple-element.98), channel_id=1, source_target_pairs={{0,1},{1,0},{2,3},{3,2},{4,5},{5,4},{6,7},{7,6},{8,9},{9,8},{10,11... | collective-permute-start | bytes 307208 | tf_op jit(solution)/shard_map/ppermute | solution.py:596
  12.4 0.2 collective-permute-start.5
  12.7 0.5 attention_bias.1.bias
  13.2 1.2 %collective-permute-done.1.right = bf16[5,5,8,256]{3,2,1,0:T(8,128)(2,1)S(1)} collective-permute-done((bf16[5,5,8,256]{3,2,1,0:T(8,128)(2,1)S(1)}, bf16[5,5,8,256]{3,2,1,0:T(8,128)(2,1)S(1)}, u32[]{:S(2)}, u32[]{:S(2)}) %collective-permute-start.1) | collective-permute-done | bytes 102432 | tf_op jit(solution)/shard_map/ppermute | solution.py:596
  14.4 1.3 %collective-permute-done.2.corner = bf16[5,5,8,256]{3,2,1,0:T(8,128)(2,1)S(1)} collective-permute-done((bf16[5,5,8,256]{3,2,1,0:T(8,128)(2,1)S(1)}, bf16[5,5,8,256]{3,2,1,0:T(8,128)(2,1)S(1)}, u32[]{:S(2)}, u32[]{:S(2)}) %collective-permute-start.2) | collective-permute-done | bytes 102432 | tf_op jit(solution)/shard_map/ppermute | solution.py:596
  15.7 0.0 collective-permute-done.low
  15.7 0.0 copy-start.1
  15.7 0.0 copy-start.2
  15.7 0.0 copy-start.4
  15.7 0.0 copy-start.5
  15.8 0.0 copy-start.8
  15.8 0.0 copy-start.9
  15.8 0.0 copy-start.10
  15.8 0.0 copy-start.11
  15.8 6.3 %attention_forward.1 = (bf16[1600,256]{1,0:T(8,128)(2,1)S(1)}, bf16[1664,256]{1,0:T(8,128)(2,1)S(1)}, bf16[2,8,128,768]{3,2,1,0:T(8,128)(2,1)S(1)}, bf16[2,8,832...) custom-call(bf16[10,20,8,256]{3,2,1,0:T(8,128)(2,1)S(1)} %bitcast.24, ...), custom_call_target="tpu_custom_call" | custom-call | flops 10000000000 | bytes 10000000 | tf_op jit(solution)/shard_map/attention_forward/pallas_call | solution.py:750
  22.1 0.0 collective-permute-done.4.t_right
  22.2 8.6 %mlp_forward_backward.1 = (bf16[5,15,8,256]{3,2,1,0:T(8,128)(2,1)S(1)}, bf16[5,15,8,256]{3,2,1,0:T(8,128)(2,1)S(1)}, bf16[5,5,8,256]{3,2,1,0:T(8,128)(2,1)S(1)},...) custom-call(bf16[1600,256]{1,0:T(8,128)(2,1)S(1)} %get-tuple-element, ...), custom_call_target="tpu_custom_call" | custom-call | flops 10000000000 | bytes 10000000 | tf_op jit(solution)/shard_map/mlp_forward_backward/pallas_call | solution.py:775
  30.8 0.1 collective-permute-start.6
  30.9 1.4 %collective-permute-start.11 = (bf16[5,5,8,256]{3,2,1,0:T(8,128)(2,1)S(1)}, bf16[5,5,8,256]{3,2,1,0:T(8,128)(2,1)S(1)}, u32[]{:S(2)}, u32[]{:S(2)}) collective-permute-start(bf16[5,5,8,256]{3,2,1,0:T(8,128)(2,1)S(1)} %get-tuple-element.108), channel_id=1, source_target_pairs={{0,3},{1,2},{2,5},{3,4},{4,7},{5,6},{6,9},{7,8},{8,11},{9,10},{10,... | collective-permute-start | bytes 307208 | tf_op jit(solution)/shard_map/ppermute | solution.py:596
  32.2 0.6 collective-permute-done.6.other
  32.9 0.1 split_sums.2
  33.0 1.4 %collective-permute-start.7 = (bf16[288,256]{1,0:T(8,128)(2,1)S(1)}, bf16[288,256]{1,0:T(8,128)(2,1)S(1)}, u32[]{:S(2)}, u32[]{:S(2)}) collective-permute-start(bf16[288,256]{1,0:T(8,128)(2,1)S(1)} %get-tuple-element.104), channel_id=1, source_target_pairs={{0,1},{1,0},{2,3},{3,2},{4,5},{5,4},{6,7},{7,6},{8,9},{9,8},{10,11... | collective-permute-start | bytes 442376 | tf_op jit(solution)/shard_map/ppermute | solution.py:596
  34.4 0.0 collective-permute-start.8
  34.4 2.1 %collective-permute-start.9 = (bf16[288,256]{1,0:T(8,128)(2,1)S(1)}, bf16[288,256]{1,0:T(8,128)(2,1)S(1)}, u32[]{:S(2)}, u32[]{:S(2)}) collective-permute-start(bf16[288,256]{1,0:T(8,128)(2,1)S(1)} %get-tuple-element.106), channel_id=1, source_target_pairs={{0,5},{1,4},{2,7},{3,6},{4,1},{5,0},{6,3},{7,2},{8,13},{9,12},{10,... | collective-permute-start | bytes 442376 | tf_op jit(solution)/shard_map/ppermute | solution.py:596
  36.6 8.6 %attention_backward.1 = (f32[5,15,8,256]{3,2,1,0:T(8,128)S(1)}, bf16[10,5,8,256]{3,2,1,0:T(8,128)(2,1)S(1)}, bf16[5,5,8,256]{3,2,1,0:T(8,128)(2,1)S(1)}, bf16[5,...) custom-call(bf16[1664,256]{1,0:T(8,128)(2,1)S(1)} %get-tuple-element.109.xw, ...), custom_call_target="tpu_custom_call" | custom-call | flops 10000000000 | bytes 10000000 | tf_op jit(solution)/shard_map/attention_backward/pallas_call | solution.py:808
  45.2 0.0 collective-permute-done.11
  45.2 0.0 collective-permute-done.10
  45.2 2.6 %collective-permute-done.8.refs_2_ = bf16[288,256]{1,0:T(8,128)(2,1)S(1)} collective-permute-done((bf16[288,256]{1,0:T(8,128)(2,1)S(1)}, bf16[288,256]{1,0:T(8,128)(2,1)S(1)}, u32[]{:S(2)}, u32[]{:S(2)}) %collective-permute-start.8) | collective-permute-done | bytes 147488 | tf_op jit(solution)/shard_map/ppermute | solution.py:596
  47.8 0.1 add_pieces.4.refs_0_
  47.9 0.1 collective-permute-start.12
  48.0 1.5 %collective-permute-done.12.other = bf16[448,256]{1,0:T(8,128)(2,1)S(1)} collective-permute-done((bf16[448,256]{1,0:T(8,128)(2,1)S(1)}, bf16[448,256]{1,0:T(8,128)(2,1)S(1)}, u32[]{:S(2)}, u32[]{:S(2)}) %collective-permute-start.12) | collective-permute-done | bytes 229408 | tf_op jit(solution)/shard_map/ppermute | solution.py:596
  49.4 0.1 split_sums.3
  49.5 0.5 collective-permute-start.13
  50.0 0.0 collective-permute-start.14
  50.0 3.0 %collective-permute-start.15 = (bf16[112,256]{1,0:T(8,128)(2,1)S(1)}, bf16[112,256]{1,0:T(8,128)(2,1)S(1)}, u32[]{:S(2)}, u32[]{:S(2)}) collective-permute-start(bf16[112,256]{1,0:T(8,128)(2,1)S(1)} %get-tuple-element.131), channel_id=1, source_target_pairs={{0,5},{1,4},{2,7},{3,6},{4,1},{5,0},{6,3},{7,2},{8,13},{9,12},{10,... | collective-permute-start | bytes 172040 | tf_op jit(solution)/shard_map/ppermute | solution.py:596
  53.1 0.8 collective-permute-done.13.refs_1_
  53.9 1.4 %collective-permute-done.14.refs_2_ = bf16[112,256]{1,0:T(8,128)(2,1)S(1)} collective-permute-done((bf16[112,256]{1,0:T(8,128)(2,1)S(1)}, bf16[112,256]{1,0:T(8,128)(2,1)S(1)}, u32[]{:S(2)}, u32[]{:S(2)}) %collective-permute-start.14) | collective-permute-done | bytes 57376 | tf_op jit(solution)/shard_map/ppermute | solution.py:596
  55.3 0.0 collective-permute-done.15.refs_3_
  55.4 0.1 collective-permute-start.16
  55.5 0.1 collective-permute-start.18
  55.5 5.7 %collective-permute-done.16.refs_1_ = bf16[400,256]{1,0:T(8,128)(2,1)S(1)} collective-permute-done((bf16[400,256]{1,0:T(8,128)(2,1)S(1)}, bf16[400,256]{1,0:T(8,128)(2,1)S(1)}, u32[]{:S(2)}, u32[]{:S(2)}) %collective-permute-start.16) | collective-permute-done | bytes 204832 | tf_op jit(solution)/shard_map/ppermute | solution.py:596
  61.3 0.8 collective-permute-start.17
  62.1 1.1 %collective-permute-start.19 = (bf16[10,5,8,256]{3,2,1,0:T(8,128)(2,1)S(1)}, bf16[10,5,8,256]{3,2,1,0:T(8,128)(2,1)S(1)}, u32[]{:S(2)}, u32[]{:S(2)}) collective-permute-start(bf16[10,5,8,256]{3,2,1,0:T(8,128)(2,1)S(1)} %get-tuple-element.136), channel_id=1, source_target_pairs={{0,1},{1,0},{2,3},{3,2},{4,5},{5,4},{6,7},{7,6},{8,9},{9,8},{10,11... | collective-permute-start | bytes 614408 | tf_op jit(solution)/shard_map/ppermute | solution.py:596
  63.2 7.9 %collective-permute-done.17.refs_1_ = bf16[400,256]{1,0:T(8,128)(2,1)S(1)} collective-permute-done((bf16[400,256]{1,0:T(8,128)(2,1)S(1)}, bf16[400,256]{1,0:T(8,128)(2,1)S(1)}, u32[]{:S(2)}, u32[]{:S(2)}) %collective-permute-start.17) | collective-permute-done | bytes 204832 | tf_op jit(solution)/shard_map/ppermute | solution.py:596
  71.1 0.3 collective-permute-done.20.refs_3_
  71.5 0.0 collective-permute-done.19.refs_2_
  71.5 0.0 collective-permute-done.18.refs_1_
  71.5 4.6 %collective-permute-start.23 = (bf16[400,256]{1,0:T(8,128)(2,1)S(1)}, bf16[400,256]{1,0:T(8,128)(2,1)S(1)}, u32[]{:S(2)}, u32[]{:S(2)}) collective-permute-start(bf16[400,256]{1,0:T(8,128)(2,1)S(1)} %add_pieces.7.refs_0_), channel_id=1, source_target_pairs={{0,5},{1,4},{2,7},{3,6},{4,1},{5,0},{6,3},{7,2},{8,13},{9,12},{10,... | collective-permute-start | bytes 614408 | tf_op jit(solution)/shard_map/ppermute | solution.py:596
  76.1 0.0 collective-permute-start.22
  76.1 1.1 %collective-permute-start.21 = (bf16[400,256]{1,0:T(8,128)(2,1)S(1)}, bf16[400,256]{1,0:T(8,128)(2,1)S(1)}, u32[]{:S(2)}, u32[]{:S(2)}) collective-permute-start(bf16[400,256]{1,0:T(8,128)(2,1)S(1)} %add_pieces.7.refs_0_), channel_id=1, source_target_pairs={{0,1},{1,0},{2,3},{3,2},{4,5},{5,4},{6,7},{7,6},{8,9},{9,8},{10,11... | collective-permute-start | bytes 614408 | tf_op jit(solution)/shard_map/ppermute | solution.py:596
  77.2 4.9 %collective-permute-done.23.refs_3_ = bf16[400,256]{1,0:T(8,128)(2,1)S(1)} collective-permute-done((bf16[400,256]{1,0:T(8,128)(2,1)S(1)}, bf16[400,256]{1,0:T(8,128)(2,1)S(1)}, u32[]{:S(2)}, u32[]{:S(2)}) %collective-permute-start.23) | collective-permute-done | bytes 204832 | tf_op jit(solution)/shard_map/ppermute | solution.py:596
  82.1 2.9 %collective-permute-done.22.refs_2_ = bf16[400,256]{1,0:T(8,128)(2,1)S(1)} collective-permute-done((bf16[400,256]{1,0:T(8,128)(2,1)S(1)}, bf16[400,256]{1,0:T(8,128)(2,1)S(1)}, u32[]{:S(2)}, u32[]{:S(2)}) %collective-permute-start.22) | collective-permute-done | bytes 204832 | tf_op jit(solution)/shard_map/ppermute | solution.py:596
  85.0 0.5 collective-permute-done.21.refs_1_
  85.5 0.1 join_pieces.3.refs_0_
  85.6 0.1 collective-permute-start.24
  85.7 1.0 %maximum_maximum_fusion = bf16[10,20,8,256]{3,2,1,0:T(8,128)(2,1)} fusion(bf16[5,15,8,256]{3,2,1,0:T(8,128)(2,1)S(1)} %get-tuple-element.142, bf16[5,5,8,256]{3,2,1,0:T(8,128)(2,1)S(1)} %slice.3, bf16[5,15,8,256]{3,2,1,0:T(8,128)(2,1)S(1)} %collective-permute-done.10, bf16[5,5,8,256]{3,2,1,0:T(8,128)(2,1)S(1)} %collective-permute-done.11), kind=kLoop, calls=%fused_computation | loop fusion | flops 1228800 | bytes 1638400 | tf_op jit(solution)/shard_map/concatenate | solution.py:916
  86.7 1.3 %input_gradient.1 = f32[10,20,8,256]{3,2,1,0:T(8,128)} custom-call(bf16[1600,256]{1,0:T(8,128)(2,1)S(1)} %join_pieces.3.refs_0_, bf16[5,15,8,256]{3,2,1,0:T(8,128)(2,1)S(1)} %collective-permute-done.18.refs_1_, bf16[10,5,8,256]{3,2,1,0:T(8,128)(2,1)S(1)} %collective-permute-done.19.refs_2_, bf16[5,5,8,256]{3,2,1,0:T(8,128)(2,1)S(1)} %collective-permute-done.20.refs_3_, ...), custom_call_target="tpu_custom_call" | custom-call | tf_op jit(solution)/shard_map/input_gradient/pallas_call | solution.py:833
  88.0 0.0 collective-permute-done.24.refs_1_
  88.0 2.0 %finish_sums.1 = (f32[256,1024]{1,0:T(8,128)}, f32[1024,256]{1,0:T(8,128)}, f32[256,256]{1,0:T(8,128)}, f32[1,1024]{1,0:T(1,128)}, f32[1,256]{1,0:T(1,128)}, /*i...) custom-call(bf16[1600,256]{1,0:T(8,128)(2,1)S(1)} %join_pieces.3.ref, ...), custom_call_target="tpu_custom_call" | custom-call | tf_op jit(solution)/shard_map/finish_sums/pallas_call | solution.py:848
  (32 shorter events, 0.2 us)
Async XLA Ops:
  0.6 15.0 %copy-start = (bf16[8,10,20,256]{3,0,2,1:T(8,128)(2,1)S(1)}, bf16[8,10,20,256]{3,0,2,1:T(8,128)(2,1)}, u32[]{:S(2)}) copy-start(bf16[8,10,20,256]{3,0,2,1:T(8,128)(2,1)} %param.17) | copy-start | bytes 2457604
  0.7 15.0 %copy-start.3 = (bf16[256,768]{1,0:T(8,128)(2,1)S(1)}, bf16[256,768]{1,0:T(8,128)(2,1)}, u32[]{:S(2)}) copy-start(bf16[256,768]{1,0:T(8,128)(2,1)} %qkv_w.3) | copy-start | bytes 1179652
  0.7 15.0 %copy-start.7 = (f32[256]{0:T(256)S(1)}, f32[256]{0:T(256)}, u32[]{:S(2)}) copy-start(f32[256]{0:T(256)} %param.24) | copy-start | bytes 3076
  0.7 15.0 %copy-start.6 = (f32[256]{0:T(256)S(1)}, f32[256]{0:T(256)}, u32[]{:S(2)}) copy-start(f32[256]{0:T(256)} %param.23) | copy-start | bytes 3076
  0.7 15.0 %copy-start.13 = (f32[256]{0:T(256)S(1)}, f32[256]{0:T(256)}, u32[]{:S(2)}) copy-start(f32[256]{0:T(256)} %param.21) | copy-start | bytes 3076
  0.7 15.0 %copy-start.12 = (f32[256]{0:T(256)S(1)}, f32[256]{0:T(256)}, u32[]{:S(2)}) copy-start(f32[256]{0:T(256)} %param.20) | copy-start | bytes 3076
  1.9 13.8 %collective-permute-start = (bf16[5,20,8,256]{3,2,1,0:T(8,128)(2,1)S(1)}, bf16[5,20,8,256]{3,2,1,0:T(8,128)(2,1)S(1)}, u32[]{:S(2)}, u32[]{:S(2)}) collective-permute-start(bf16[5,20,8,256]{3,2,1,0:T(8,128)(2,1)S(1)} %get-tuple-element.90), channel_id=1, source_target_pairs={{0,30},{1,31},{2,0},{3,1},{4,2},{5,3},{6,4},{7,5},{8,6},{9,7},{10,... | collective-permute-start | bytes 1228808 | tf_op jit(solution)/shard_map/ppermute | solution.py:596
  7.4 7.0 %collective-permute-start.1 = (bf16[5,5,8,256]{3,2,1,0:T(8,128)(2,1)S(1)}, bf16[5,5,8,256]{3,2,1,0:T(8,128)(2,1)S(1)}, u32[]{:S(2)}, u32[]{:S(2)}) collective-permute-start(bf16[5,5,8,256]{3,2,1,0:T(8,128)(2,1)S(1)} %get-tuple-element.91), channel_id=1, source_target_pairs={{0,1},{1,0},{2,3},{3,2},{4,5},{5,4},{6,7},{7,6},{8,9},{9,8},{10,11... | collective-permute-start | bytes 307208 | tf_op jit(solution)/shard_map/ppermute | solution.py:596
  8.9 6.8 %collective-permute-start.2 = (bf16[5,5,8,256]{3,2,1,0:T(8,128)(2,1)S(1)}, bf16[5,5,8,256]{3,2,1,0:T(8,128)(2,1)S(1)}, u32[]{:S(2)}, u32[]{:S(2)}) collective-permute-start(bf16[5,5,8,256]{3,2,1,0:T(8,128)(2,1)S(1)} %get-tuple-element.92), channel_id=1, source_target_pairs={{0,31},{1,30},{2,1},{3,0},{4,3},{5,2},{6,5},{7,4},{8,7},{9,6},{10,... | collective-permute-start | bytes 307208 | tf_op jit(solution)/shard_map/ppermute | solution.py:596
  10.9 11.2 %collective-permute-start.4 = (bf16[5,5,8,256]{3,2,1,0:T(8,128)(2,1)S(1)}, bf16[5,5,8,256]{3,2,1,0:T(8,128)(2,1)S(1)}, u32[]{:S(2)}, u32[]{:S(2)}) collective-permute-start(bf16[5,5,8,256]{3,2,1,0:T(8,128)(2,1)S(1)} %get-tuple-element.98), channel_id=1, source_target_pairs={{0,1},{1,0},{2,3},{3,2},{4,5},{5,4},{6,7},{7,6},{8,9},{9,8},{10,11... | collective-permute-start | bytes 307208 | tf_op jit(solution)/shard_map/ppermute | solution.py:596
  12.4 9.7 %collective-permute-start.5 = (bf16[5,5,8,256]{3,2,1,0:T(8,128)(2,1)S(1)}, bf16[5,5,8,256]{3,2,1,0:T(8,128)(2,1)S(1)}, u32[]{:S(2)}, u32[]{:S(2)}) collective-permute-start(bf16[5,5,8,256]{3,2,1,0:T(8,128)(2,1)S(1)} %get-tuple-element.99), channel_id=1, source_target_pairs={{0,31},{1,30},{2,1},{3,0},{4,3},{5,2},{6,5},{7,4},{8,7},{9,6},{10,... | collective-permute-start | bytes 307208 | tf_op jit(solution)/shard_map/ppermute | solution.py:596
  14.4 7.8 %collective-permute-start.3 = (bf16[5,20,8,256]{3,2,1,0:T(8,128)(2,1)S(1)}, bf16[5,20,8,256]{3,2,1,0:T(8,128)(2,1)S(1)}, u32[]{:S(2)}, u32[]{:S(2)}) collective-permute-start(bf16[5,20,8,256]{3,2,1,0:T(8,128)(2,1)S(1)} %get-tuple-element.97), channel_id=1, source_target_pairs={{0,30},{1,31},{2,0},{3,1},{4,2},{5,3},{6,4},{7,5},{8,6},{9,7},{10,... | collective-permute-start | bytes 1228808 | tf_op jit(solution)/shard_map/ppermute | solution.py:596
  15.7 6.4 %copy-start.1 = (bf16[256,1024]{1,0:T(8,128)(2,1)S(1)}, bf16[256,1024]{1,0:T(8,128)(2,1)}, u32[]{:S(2)}) copy-start(bf16[256,1024]{1,0:T(8,128)(2,1)} %fc1_w.1) | copy-start | bytes 1572868
  15.7 6.4 %copy-start.2 = (bf16[1024,256]{1,0:T(8,128)(2,1)S(1)}, bf16[1024,256]{1,0:T(8,128)(2,1)}, u32[]{:S(2)}) copy-start(bf16[1024,256]{1,0:T(8,128)(2,1)} %fc2_w.1) | copy-start | bytes 1572868
  15.7 6.4 %copy-start.4 = (bf16[256,256]{1,0:T(8,128)(2,1)S(1)}, bf16[256,256]{1,0:T(8,128)(2,1)}, u32[]{:S(2)}) copy-start(bf16[256,256]{1,0:T(8,128)(2,1)} %proj_w.1) | copy-start | bytes 393220
  15.7 6.4 %copy-start.5 = (f32[1024]{0:T(1024)S(1)}, f32[1024]{0:T(1024)}, u32[]{:S(2)}) copy-start(f32[1024]{0:T(1024)} %param.31) | copy-start | bytes 12292
  15.8 6.4 %copy-start.8 = (f32[256]{0:T(256)S(1)}, f32[256]{0:T(256)}, u32[]{:S(2)}) copy-start(f32[256]{0:T(256)} %param.27) | copy-start | bytes 3076
  15.8 6.4 %copy-start.9 = (f32[256]{0:T(256)S(1)}, f32[256]{0:T(256)}, u32[]{:S(2)}) copy-start(f32[256]{0:T(256)} %param.28) | copy-start | bytes 3076
  15.8 6.4 %copy-start.10 = (f32[256]{0:T(256)S(1)}, f32[256]{0:T(256)}, u32[]{:S(2)}) copy-start(f32[256]{0:T(256)} %param.29) | copy-start | bytes 3076
  15.8 6.4 %copy-start.11 = (f32[256]{0:T(256)S(1)}, f32[256]{0:T(256)}, u32[]{:S(2)}) copy-start(f32[256]{0:T(256)} %param.33) | copy-start | bytes 3076
  30.8 2.1 %collective-permute-start.6 = (bf16[1152,256]{1,0:T(8,128)(2,1)S(1)}, bf16[1152,256]{1,0:T(8,128)(2,1)S(1)}, u32[]{:S(2)}, u32[]{:S(2)}) collective-permute-start(bf16[1152,256]{1,0:T(8,128)(2,1)S(1)} %get-tuple-element.102), channel_id=1, source_target_pairs={{0,2},{1,3},{2,0},{3,1},{4,6},{5,7},{6,4},{7,5},{8,10},{9,11},{10,... | collective-permute-start | bytes 1769480 | tf_op jit(solution)/shard_map/ppermute | solution.py:596
  30.9 14.3 %collective-permute-start.11 = (bf16[5,5,8,256]{3,2,1,0:T(8,128)(2,1)S(1)}, bf16[5,5,8,256]{3,2,1,0:T(8,128)(2,1)S(1)}, u32[]{:S(2)}, u32[]{:S(2)}) collective-permute-start(bf16[5,5,8,256]{3,2,1,0:T(8,128)(2,1)S(1)} %get-tuple-element.108), channel_id=1, source_target_pairs={{0,3},{1,2},{2,5},{3,4},{4,7},{5,6},{6,9},{7,8},{8,11},{9,10},{10,... | collective-permute-start | bytes 307208 | tf_op jit(solution)/shard_map/ppermute | solution.py:596
  32.2 12.9 %collective-permute-start.10 = (bf16[5,15,8,256]{3,2,1,0:T(8,128)(2,1)S(1)}, bf16[5,15,8,256]{3,2,1,0:T(8,128)(2,1)S(1)}, u32[]{:S(2)}, u32[]{:S(2)}) collective-permute-start(bf16[5,15,8,256]{3,2,1,0:T(8,128)(2,1)S(1)} %get-tuple-element.107), channel_id=1, source_target_pairs={{0,2},{1,3},{2,4},{3,5},{4,6},{5,7},{6,8},{7,9},{8,10},{9,11},{10,... | collective-permute-start | bytes 921608 | tf_op jit(solution)/shard_map/ppermute | solution.py:596
  33.0 12.2 %collective-permute-start.7 = (bf16[288,256]{1,0:T(8,128)(2,1)S(1)}, bf16[288,256]{1,0:T(8,128)(2,1)S(1)}, u32[]{:S(2)}, u32[]{:S(2)}) collective-permute-start(bf16[288,256]{1,0:T(8,128)(2,1)S(1)} %get-tuple-element.104), channel_id=1, source_target_pairs={{0,1},{1,0},{2,3},{3,2},{4,5},{5,4},{6,7},{7,6},{8,9},{9,8},{10,11... | collective-permute-start | bytes 442376 | tf_op jit(solution)/shard_map/ppermute | solution.py:596
  34.4 13.4 %collective-permute-start.8 = (bf16[288,256]{1,0:T(8,128)(2,1)S(1)}, bf16[288,256]{1,0:T(8,128)(2,1)S(1)}, u32[]{:S(2)}, u32[]{:S(2)}) collective-permute-start(bf16[288,256]{1,0:T(8,128)(2,1)S(1)} %get-tuple-element.105), channel_id=1, source_target_pairs={{0,4},{1,5},{2,6},{3,7},{4,0},{5,1},{6,2},{7,3},{8,12},{9,13},{10,... | collective-permute-start | bytes 442376 | tf_op jit(solution)/shard_map/ppermute | solution.py:596
  34.4 13.4 %collective-permute-start.9 = (bf16[288,256]{1,0:T(8,128)(2,1)S(1)}, bf16[288,256]{1,0:T(8,128)(2,1)S(1)}, u32[]{:S(2)}, u32[]{:S(2)}) collective-permute-start(bf16[288,256]{1,0:T(8,128)(2,1)S(1)} %get-tuple-element.106), channel_id=1, source_target_pairs={{0,5},{1,4},{2,7},{3,6},{4,1},{5,0},{6,3},{7,2},{8,13},{9,12},{10,... | collective-permute-start | bytes 442376 | tf_op jit(solution)/shard_map/ppermute | solution.py:596
  47.9 1.6 %collective-permute-start.12 = (bf16[448,256]{1,0:T(8,128)(2,1)S(1)}, bf16[448,256]{1,0:T(8,128)(2,1)S(1)}, u32[]{:S(2)}, u32[]{:S(2)}) collective-permute-start(bf16[448,256]{1,0:T(8,128)(2,1)S(1)} %get-tuple-element.127), channel_id=1, source_target_pairs={{0,2},{1,3},{2,0},{3,1},{4,6},{5,7},{6,4},{7,5},{8,10},{9,11},{10,... | collective-permute-start | bytes 688136 | tf_op jit(solution)/shard_map/ppermute | solution.py:596
  49.5 4.4 %collective-permute-start.13 = (bf16[112,256]{1,0:T(8,128)(2,1)S(1)}, bf16[112,256]{1,0:T(8,128)(2,1)S(1)}, u32[]{:S(2)}, u32[]{:S(2)}) collective-permute-start(bf16[112,256]{1,0:T(8,128)(2,1)S(1)} %get-tuple-element.129), channel_id=1, source_target_pairs={{0,1},{1,0},{2,3},{3,2},{4,5},{5,4},{6,7},{7,6},{8,9},{9,8},{10,11... | collective-permute-start | bytes 172040 | tf_op jit(solution)/shard_map/ppermute | solution.py:596
  50.0 5.3 %collective-permute-start.14 = (bf16[112,256]{1,0:T(8,128)(2,1)S(1)}, bf16[112,256]{1,0:T(8,128)(2,1)S(1)}, u32[]{:S(2)}, u32[]{:S(2)}) collective-permute-start(bf16[112,256]{1,0:T(8,128)(2,1)S(1)} %get-tuple-element.130), channel_id=1, source_target_pairs={{0,4},{1,5},{2,6},{3,7},{4,0},{5,1},{6,2},{7,3},{8,12},{9,13},{10,... | collective-permute-start | bytes 172040 | tf_op jit(solution)/shard_map/ppermute | solution.py:596
  50.0 5.3 %collective-permute-start.15 = (bf16[112,256]{1,0:T(8,128)(2,1)S(1)}, bf16[112,256]{1,0:T(8,128)(2,1)S(1)}, u32[]{:S(2)}, u32[]{:S(2)}) collective-permute-start(bf16[112,256]{1,0:T(8,128)(2,1)S(1)} %get-tuple-element.131), channel_id=1, source_target_pairs={{0,5},{1,4},{2,7},{3,6},{4,1},{5,0},{6,3},{7,2},{8,13},{9,12},{10,... | collective-permute-start | bytes 172040 | tf_op jit(solution)/shard_map/ppermute | solution.py:596
  55.4 5.8 %collective-permute-start.16 = (bf16[400,256]{1,0:T(8,128)(2,1)S(1)}, bf16[400,256]{1,0:T(8,128)(2,1)S(1)}, u32[]{:S(2)}, u32[]{:S(2)}) collective-permute-start(bf16[400,256]{1,0:T(8,128)(2,1)S(1)} %join_pieces.2.refs_0_), channel_id=1, source_target_pairs={{0,8},{1,9},{2,10},{3,11},{4,12},{5,13},{6,14},{7,15},{8,0},{9,1},... | collective-permute-start | bytes 614408 | tf_op jit(solution)/shard_map/ppermute | solution.py:596
  55.5 16.0 %collective-permute-start.18 = (bf16[5,15,8,256]{3,2,1,0:T(8,128)(2,1)S(1)}, bf16[5,15,8,256]{3,2,1,0:T(8,128)(2,1)S(1)}, u32[]{:S(2)}, u32[]{:S(2)}) collective-permute-start(bf16[5,15,8,256]{3,2,1,0:T(8,128)(2,1)S(1)} %get-tuple-element.135), channel_id=1, source_target_pairs={{0,2},{1,3},{2,4},{3,5},{4,6},{5,7},{6,8},{7,9},{8,10},{9,11},{10,... | collective-permute-start | bytes 921608 | tf_op jit(solution)/shard_map/ppermute | solution.py:596
  61.3 9.8 %collective-permute-start.17 = (bf16[400,256]{1,0:T(8,128)(2,1)S(1)}, bf16[400,256]{1,0:T(8,128)(2,1)S(1)}, u32[]{:S(2)}, u32[]{:S(2)}) collective-permute-start(bf16[400,256]{1,0:T(8,128)(2,1)S(1)} %add_pieces.6.refs_0_), channel_id=1, source_target_pairs={{0,16},{1,17},{2,18},{3,19},{4,20},{5,21},{6,22},{7,23},{8,24},{9,... | collective-permute-start | bytes 614408 | tf_op jit(solution)/shard_map/ppermute | solution.py:596
  62.1 9.4 %collective-permute-start.19 = (bf16[10,5,8,256]{3,2,1,0:T(8,128)(2,1)S(1)}, bf16[10,5,8,256]{3,2,1,0:T(8,128)(2,1)S(1)}, u32[]{:S(2)}, u32[]{:S(2)}) collective-permute-start(bf16[10,5,8,256]{3,2,1,0:T(8,128)(2,1)S(1)} %get-tuple-element.136), channel_id=1, source_target_pairs={{0,1},{1,0},{2,3},{3,2},{4,5},{5,4},{6,7},{7,6},{8,9},{9,8},{10,11... | collective-permute-start | bytes 614408 | tf_op jit(solution)/shard_map/ppermute | solution.py:596
  63.2 8.3 %collective-permute-start.20 = (bf16[5,5,8,256]{3,2,1,0:T(8,128)(2,1)S(1)}, bf16[5,5,8,256]{3,2,1,0:T(8,128)(2,1)S(1)}, u32[]{:S(2)}, u32[]{:S(2)}) collective-permute-start(bf16[5,5,8,256]{3,2,1,0:T(8,128)(2,1)S(1)} %get-tuple-element.137), channel_id=1, source_target_pairs={{0,3},{1,2},{2,5},{3,4},{4,7},{5,6},{6,9},{7,8},{8,11},{9,10},{10,... | collective-permute-start | bytes 307208 | tf_op jit(solution)/shard_map/ppermute | solution.py:596
  71.5 10.6 %collective-permute-start.23 = (bf16[400,256]{1,0:T(8,128)(2,1)S(1)}, bf16[400,256]{1,0:T(8,128)(2,1)S(1)}, u32[]{:S(2)}, u32[]{:S(2)}) collective-permute-start(bf16[400,256]{1,0:T(8,128)(2,1)S(1)} %add_pieces.7.refs_0_), channel_id=1, source_target_pairs={{0,5},{1,4},{2,7},{3,6},{4,1},{5,0},{6,3},{7,2},{8,13},{9,12},{10,... | collective-permute-start | bytes 614408 | tf_op jit(solution)/shard_map/ppermute | solution.py:596
  76.1 8.9 %collective-permute-start.22 = (bf16[400,256]{1,0:T(8,128)(2,1)S(1)}, bf16[400,256]{1,0:T(8,128)(2,1)S(1)}, u32[]{:S(2)}, u32[]{:S(2)}) collective-permute-start(bf16[400,256]{1,0:T(8,128)(2,1)S(1)} %add_pieces.7.refs_0_), channel_id=1, source_target_pairs={{0,4},{1,5},{2,6},{3,7},{4,0},{5,1},{6,2},{7,3},{8,12},{9,13},{10,... | collective-permute-start | bytes 614408 | tf_op jit(solution)/shard_map/ppermute | solution.py:596
  76.1 9.4 %collective-permute-start.21 = (bf16[400,256]{1,0:T(8,128)(2,1)S(1)}, bf16[400,256]{1,0:T(8,128)(2,1)S(1)}, u32[]{:S(2)}, u32[]{:S(2)}) collective-permute-start(bf16[400,256]{1,0:T(8,128)(2,1)S(1)} %add_pieces.7.refs_0_), channel_id=1, source_target_pairs={{0,1},{1,0},{2,3},{3,2},{4,5},{5,4},{6,7},{7,6},{8,9},{9,8},{10,11... | collective-permute-start | bytes 614408 | tf_op jit(solution)/shard_map/ppermute | solution.py:596
  85.6 2.4 %collective-permute-start.24 = (bf16[1600,256]{1,0:T(8,128)(2,1)S(1)}, bf16[1600,256]{1,0:T(8,128)(2,1)S(1)}, u32[]{:S(2)}, u32[]{:S(2)}) collective-permute-start(bf16[1600,256]{1,0:T(8,128)(2,1)S(1)} %join_pieces.3.refs_0_), channel_id=1, source_target_pairs={{0,2},{1,3},{2,0},{3,1},{4,6},{5,7},{6,4},{7,5},{8,10},{9,11},{10,... | collective-permute-start | bytes 2457608 | tf_op jit(solution)/shard_map/ppermute | solution.py:596
